TPU v7x, 1024 devices: a whole 4x4x32 slice. The times are simulated.
1024 devices in a mesh: dp: 256 (over y, x_lo, z), tower: 4 (over x_hi, core).
Axes of the slice: x: 4 (x_hi: 2, x_lo: 2; x = x_hi * 2 + x_lo), y: 4, z: 32, core: 2. Of those that a mesh axis runs over, the one named last changes fastest.
Arguments:
- image_feats: bfloat16 [32768, 1152], P('dp'), may hold values from -6 to 6
- text_feats: bfloat16 [32768, 1152], P('dp'), may hold values from -6 to 6
- image_proj: bfloat16 [1152, 1152], P(None, 'tower'), may hold values from -0.1875 to 0.1875
- text_proj: bfloat16 [1152, 1152], P(None, 'tower'), may hold values from -0.1875 to 0.1875
- logit_scale: float32 [1], replicated, may hold values from 2 to 5
- logit_bias: float32 [1], replicated, may hold values from -3 to -1
Outputs:
- pair_loss: float32 [32768], P('dp')
- image_grad: float32 [4, 331776], P('tower', 'dp')
- text_grad: float32 [4, 331776], P('tower', 'dp')
All inputs are finite; a program needn't handle non-finite values.
Results may differ from a plain program's by a relative error of at most 0.0043.
Values may be sent and summed in bfloat16 or wider, within the bound.
No kernel may reach another device: no remote copies, remote signals or barrier semaphores. Data moves between devices by JAX's collectives and lax.ppermute only.
A program may use at most 32 MiB of HBM per device.

v0:
```python
import jax
import jax.numpy as jnp
from jax import lax
from jax.sharding import PartitionSpec as P

CYCLE = 4


def passed_along(block, axis, distance):
    devices = range(lax.axis_size(axis))
    route = [((i - distance) % len(devices), i) for i in devices]
    return lax.ppermute(block, axis, route)


def unit_rows(z):
    norm = jnp.sqrt(jnp.sum(z * z, axis=-1, keepdims=True) + 1e-06)
    return (z / norm, norm)


def outer_rows(left, right):
    return lax.dot_general(
        left, right, (((1,), (1,)), ((), ())), preferred_element_type=jnp.float32
    )


def inner_rows(left, right):
    return lax.dot_general(
        left, right, (((0,), (0,)), ((), ())), preferred_element_type=jnp.float32
    )


def norm_back(grad, unit, norm):
    return ((grad - unit * jnp.sum(unit * grad, axis=-1, keepdims=True)) / norm).astype(
        jnp.bfloat16
    )


def pair_scores(ub, block, scale, bias):
    partial_scores = outer_rows(ub, block)
    return scale * partial_scores + bias


def shards(image_feats, text_feats, image_proj, text_proj, logit_scale, logit_bias):
    rows = image_feats.shape[0]
    width = image_proj.shape[1]
    img_cols = jnp.dot(image_feats, image_proj, preferred_element_type=jnp.float32)
    txt_cols = jnp.dot(text_feats, text_proj, preferred_element_type=jnp.float32)
    img_full, txt_full = (
        lax.all_gather(img_cols, "tower", axis=1, tiled=True),
        lax.all_gather(txt_cols, "tower", axis=1, tiled=True),
    )
    ui, ni = unit_rows(img_full)
    ut, nt = unit_rows(txt_full)
    ub = ui.astype(jnp.bfloat16)
    vb = ut.astype(jnp.bfloat16)
    scale = logit_scale[0]
    bias = logit_bias[0]
    eye = jnp.eye(rows, dtype=jnp.float32)
    scores = pair_scores(ub, vb, scale, bias)
    loss = jnp.sum(jax.nn.softplus((1.0 - 2.0 * eye) * scores), axis=-1)
    weights = (jax.nn.sigmoid(scores) - eye).astype(jnp.bfloat16)
    du = jnp.dot(weights, vb, preferred_element_type=jnp.float32)
    dv = inner_rows(weights, ub)
    block = vb
    carried = jnp.zeros_like(dv)
    for step in range(1, CYCLE + 1):
        block = passed_along(block, "dp", 1)
        scores = pair_scores(ub, block, scale, bias)
        loss = loss + jnp.sum(jax.nn.softplus(scores), axis=-1)
        weights = jax.nn.sigmoid(scores).astype(jnp.bfloat16)
        du = du + jnp.dot(weights, block, preferred_element_type=jnp.float32)
        partial_grad = inner_rows(weights, ub)
        if step == 1:
            carried = partial_grad
        else:
            carried = passed_along(carried, "dp", 1) + partial_grad
    returned = passed_along(carried, "dp", -CYCLE)
    du = scale * du
    dv = scale * (dv + returned)
    start = lax.axis_index("tower") * width
    dzi = lax.dynamic_slice_in_dim(norm_back(du, ui, ni), start, width, 1)
    dzt = lax.dynamic_slice_in_dim(norm_back(dv, ut, nt), start, width, 1)
    pieces = lax.axis_size("dp")
    grad_i = inner_rows(image_feats, dzi).reshape(pieces, -1)
    grad_t = inner_rows(text_feats, dzt).reshape(pieces, -1)
    share = grad_i.shape[1]
    terms = jnp.concatenate((grad_i, grad_t), axis=1)
    summed = lax.psum_scatter(terms, "dp", scatter_dimension=0, tiled=True)
    image_grad = summed[:, :share]
    text_grad = summed[:, share:]
    return (loss, image_grad, text_grad)


def solution(mesh):
    in_specs = (P("dp", None), P("dp", None), P(None, "tower"), P(None, "tower"), P(), P())
    out_specs = (P("dp"), P("tower", "dp"), P("tower", "dp"))
    return jax.shard_map(shards, mesh=mesh, in_specs=in_specs, out_specs=out_specs, check_vma=False)
```

profile of v0, /device:TPU:6, one launch (start us, length us, event | category | flops | bytes accessed | tf_op | source)
XLA Modules:
  0.0 2417.5 jit_solution(6345591822124410522)
XLA Ops:
  7.2 0.0 copy-start
  7.2 0.0 copy-start.1
  7.2 0.0 copy-start.3
  7.2 0.0 all-reduce.3.cloned.1.call-start
  7.2 1.0 copy-done
  8.3 1.3 fusion.32
  9.6 8.6 all_gather.7
  18.2 0.2 multiply_reduce_fusion.2
  18.4 0.1 fusion.28
  18.5 3.8 collective-permute-start
  22.3 0.0 copy-done.1
  22.3 0.0 copy-done.3
  22.3 0.3 fusion.31
  22.7 8.9 all_gather.6
  31.5 0.2 multiply_reduce_fusion.3
  31.7 0.1 fusion.29
  33.1 0.4 fusion.16
  33.5 11.6 collective-permute-done
  45.0 0.3 fusion.17
  45.4 1.1 fusion.23
  46.4 1.9 collective-permute-start.4
  48.4 1.9 collective-permute-start.1
  50.3 1.1 fusion.26
  51.4 0.2 fusion.27
  51.6 21.0 collective-permute-done.1
  72.7 1.9 collective-permute-start.2
  74.6 1.3 fusion.18
  75.9 0.0 collective-permute-done.4
  75.9 1.3 convolution_add_fusion.4
  77.2 1.9 collective-permute-start.5
  79.2 0.2 convolution_add_fusion.3
  79.4 7.4 collective-permute-done.2
  86.8 1.9 collective-permute-start.3
  88.7 0.4 fusion.19
  89.1 0.2 fusion.24
  89.3 10.1 collective-permute-done.5
  99.4 0.1 add.139
  99.5 1.9 collective-permute-start.6
  101.4 1.2 convolution_add_fusion.2
  102.6 2.6 collective-permute-done.3
  105.2 0.3 fusion.20
  105.6 0.2 fusion.25
  105.8 11.1 collective-permute-done.6
  116.9 0.9 add.140
  117.8 6.0 collective-permute-start.7
  123.8 0.2 convolution_add_fusion.1
  124.1 0.3 multiply_reduce_fusion.1
  124.4 1.4 convolution_bitcast_fusion.1
  125.8 1.9 copy.36
  127.7 2.0 reshape.26
  129.6 0.0 copy-start.2
  129.6 40.6 %collective-permute-done.7 = f32[128,1152]{0,1:T(8,128)} collective-permute-done((f32[128,1152]{0,1:T(8,128)}, f32[128,1152]{0,1:T(8,128)}, u32[]{:S(2)}, u32[]{:S(2)}) %collective-permute-start.7) | collective-permute-done | bytes 589856 | tf_op jit(solution)/shard_map/ppermute | solution.py:12
  170.2 1.4 multiply_reduce_fusion
  171.6 0.0 copy-done.2
  171.6 1.4 convolution_bitcast_fusion
  173.0 1.9 copy.42
  174.9 2.0 reshape.27
  176.9 3.8 pad_maximum_fusion
  180.7 0.0 all-reduce.3.cloned.1.call-update
  180.7 1.2 dynamic-slice
  181.9 0.5 add_add_fusion
  182.5 2226.1 %all-reduce.3.cloned.1.call-done = f32[256,2592]{1,0:T(8,128)} async-done(((f32[256,2592]{1,0:T(8,128)}), f32[256,2592]{1,0:T(8,128)}) %all-reduce.3.cloned.1.call-update) | async-done | bytes 2654224
  2408.6 2.1 fusion.30
  (2 shorter events, 0.0 us)
Async XLA Ops:
  7.2 1.1 copy-start
  7.2 15.1 copy-start.1
  7.2 15.1 copy-start.3
  7.2 2401.4 %all-reduce.3.cloned.1.call-start = ((), (), s32[]{:S(2)}) async-start(), calls=%async_computation | async-start | bytes 5505024
  18.5 26.6 %collective-permute-start = (bf16[128,1152]{0,1:T(8,128)(2,1)S(1)}, bf16[128,1152]{0,1:T(8,128)(2,1)S(1)}, u32[]{:S(2)}, u32[]{:S(2)}) collective-permute-start(bf16[128,1152]{0,1:T(8,128)(2,1)S(1)} %get-tuple-element.5), channel_id=1, source_target_pairs={{1020,0},{0,4},{4,8},{8,12},{12,16},{16,20},{20,24},{24,28},{28,32... | collective-permute-start | bytes 884744 | tf_op jit(solution)/shard_map/ppermute | solution.py:12
  46.4 29.5 %collective-permute-start.4 = (f32[128,1152]{0,1:T(8,128)}, f32[128,1152]{0,1:T(8,128)}, u32[]{:S(2)}, u32[]{:S(2)}) collective-permute-start(f32[128,1152]{0,1:T(8,128)} %fusion.23), channel_id=1, source_target_pairs={{1020,0},{0,4},{4,8},{8,12},{12,16},{16,20},{20,24},{24,28},{28,32... | collective-permute-start | bytes 1769480 | tf_op jit(solution)/shard_map/ppermute | solution.py:12
  48.4 24.3 %collective-permute-start.1 = (bf16[128,1152]{0,1:T(8,128)(2,1)S(1)}, bf16[128,1152]{0,1:T(8,128)(2,1)}, u32[]{:S(2)}, u32[]{:S(2)}) collective-permute-start(bf16[128,1152]{0,1:T(8,128)(2,1)S(1)} %collective-permute-done), channel_id=1, source_target_pairs={{1020,0},{0,4},{4,8},{8,12},{12,16},{16,20},{20,24},{24,28},{28,32... | collective-permute-start | bytes 884744 | tf_op jit(solution)/shard_map/ppermute | solution.py:12
  72.7 14.1 collective-permute-start.2
  77.2 22.2 collective-permute-start.5
  86.8 18.4 collective-permute-start.3
  99.5 17.4 collective-permute-start.6
  117.8 52.4 %collective-permute-start.7 = (f32[128,1152]{0,1:T(8,128)}, f32[128,1152]{0,1:T(8,128)}, u32[]{:S(2)}, u32[]{:S(2)}) collective-permute-start(f32[128,1152]{0,1:T(8,128)} %add.140), channel_id=1, source_target_pairs={{16,0},{20,4},{24,8},{28,12},{32,16},{36,20},{40,24},{44,28},{48,3... | collective-permute-start | bytes 1769480 | tf_op jit(solution)/shard_map/ppermute | solution.py:12
  129.6 42.0 %copy-start.2 = (bf16[128,1152]{1,0:T(8,128)(2,1)S(1)}, bf16[128,1152]{1,0:T(8,128)(2,1)}, u32[]{:S(2)}) copy-start(bf16[128,1152]{1,0:T(8,128)(2,1)} %param.7) | copy-start | bytes 884740
Sparse Core Ops, SparseCore 0:
  180.8 2227.6 all-reduce.2
where the time goes:
time: 2440 us; the launch traced here: 2420 us
  waiting for transfers between devices  2330 us (95%)
    unnamed x2, waiting for transfers between devices  2230 us
    ppermute x8, waiting for transfers between devices, passed_along(): return lax.ppermute(block, axis, route)  104 us
  transfers between devices with their start and end apart: 9, of which 8 were waited for; matrix products, arithmetic and copies ran while one was open for 1% of the time, Pallas kernels for 0%

commit v1 on v0

v1 whole, which is shorter than its diff:
```python
import jax
import jax.numpy as jnp
from jax import lax
from jax.sharding import PartitionSpec as P

RING = 32


def across(left, right):
    return lax.dot_general(
        left, right, (((1,), (1,)), ((), ())), preferred_element_type=jnp.float32
    )


def down(left, right):
    return lax.dot_general(
        left, right, (((0,), (0,)), ((), ())), preferred_element_type=jnp.float32
    )


def times(left, right):
    return jnp.dot(left, right, preferred_element_type=jnp.float32)


def rounded(x):
    return lax.reduce_precision(x, 8, 7)


def shifted(block, distances):
    dp, tower = lax.axis_size("dp"), lax.axis_size("tower")
    route = [
        (i * tower + t, ((i + distances[t % 2]) % dp) * tower + t)
        for i in range(dp)
        for t in range(tower)
    ]
    return lax.ppermute(block, ("dp", "tower"), route)


def shards(image_feats, text_feats, image_proj, text_proj, logit_scale, logit_bias):
    bf16, f32 = jnp.bfloat16, jnp.float32
    rows = image_feats.shape[0]
    width = image_proj.shape[1]
    dp, tower = lax.axis_size("dp"), lax.axis_size("tower")
    planes = dp // RING
    scale, bias = logit_scale[0], logit_bias[0]
    to_core = [(t, t ^ 1) for t in range(tower)]
    to_chip = [(t, t ^ 2) for t in range(tower)]
    core0 = (lax.axis_index("tower") % 2 == 0).astype(f32)

    zi = times(image_feats, image_proj)
    zt = times(text_feats, text_proj)
    mine = jnp.concatenate((zi, zt), axis=0).astype(bf16)
    other = lax.ppermute(mine, "tower", to_core)
    half = jnp.concatenate((mine, other), axis=1)
    i0, t0 = half[:rows], half[rows:]
    t1 = shifted(t0, (1, 2))
    i1 = shifted(i0, (-1, -2))
    t2 = shifted(t1, (2, 2))
    i2 = shifted(i1, (-2, -2))

    parts = [across(i0, t0), across(i0, t1), across(i0, t2), across(t0, i1), across(t0, i2)]
    squares = [
        jnp.sum(jnp.square(b.astype(f32)), axis=-1)[None] for b in (i0, t0, i1, i2, t1, t2)
    ]
    squares = jnp.concatenate(squares, axis=0)
    coarse = rounded(squares)
    payload = jnp.concatenate(
        [rounded(p) for p in parts]
        + [coarse, rounded(squares - coarse), jnp.zeros((4, rows), f32)],
        axis=0,
    ).astype(bf16)
    peer = lax.ppermute(payload, "tower", to_chip).astype(f32)
    total = payload.astype(f32) + peer
    s0, s1, s2, r1, r2 = (total[j * rows : (j + 1) * rows] for j in range(5))
    sq = total[5 * rows : 5 * rows + 6] + total[5 * rows + 6 : 5 * rows + 12]
    inv = lax.rsqrt(sq + 1e-06)
    ni, nt = inv[0], inv[1]

    def pair(raw, row_inv, col_inv):
        return scale * (raw * row_inv[:, None] * col_inv[None, :])

    eye = jnp.eye(rows, dtype=f32)
    c0, c1, c2 = pair(s0, ni, nt), pair(s1, ni, inv[4]), pair(s2, ni, inv[5])
    e1, e2 = pair(r1, nt, inv[2]), pair(r2, nt, inv[3])
    loss0 = jnp.sum(jax.nn.softplus((1.0 - 2.0 * eye) * (c0 + bias)), axis=-1)
    loss = (
        core0 * loss0
        + jnp.sum(jax.nn.softplus(c1 + bias), axis=-1)
        + jnp.sum(jax.nn.softplus(c2 + bias), axis=-1)
    )
    g0 = jax.nn.sigmoid(c0 + bias) - eye
    g1, g2 = jax.nn.sigmoid(c1 + bias), jax.nn.sigmoid(c2 + bias)
    h1, h2 = jax.nn.sigmoid(e1 + bias), jax.nn.sigmoid(e2 + bias)
    along_i = jnp.sum(g1 * c1 + g2 * c2, axis=-1)
    along_t = jnp.sum(h1 * e1 + h2 * e2, axis=-1)
    du = times((g1 * inv[4]).astype(bf16), t1) + times((g2 * inv[5]).astype(bf16), t2)
    dv = times((h1 * inv[2]).astype(bf16), i1) + times((h2 * inv[3]).astype(bf16), i2)
    du0 = times((g0 * nt[None, :]).astype(bf16), t0[:, :width])
    dv0 = down((g0 * ni[:, None]).astype(bf16), i0[:, :width])
    lines = jnp.stack((along_i, along_t, loss), axis=0)
    lines = jnp.pad(lines, ((0, 5), (0, width - rows)))
    sums = jnp.concatenate((du[:, width:], dv[:, width:], lines), axis=0)
    got = lax.ppermute(sums, "tower", to_core)
    lines = lines[:3, :rows] + got[2 * rows : 2 * rows + 3, :rows]
    along_i = lines[0] + jnp.sum(g0 * c0, axis=1)
    along_t = lines[1] + jnp.sum(g0 * c0, axis=0)
    loss = lines[2]
    du = scale * (du[:, :width] + got[:rows] + du0)
    dv = scale * (dv[:, :width] + got[rows : 2 * rows] + dv0)
    dzi = ((du - zi * (ni * along_i)[:, None]) * ni[:, None]).astype(bf16)
    dzt = ((dv - zt * (nt * along_t)[:, None]) * nt[:, None]).astype(bf16)

    depth = image_feats.shape[1]
    grads = jnp.concatenate((down(image_feats, dzi), down(text_feats, dzt)), axis=1)
    grads = grads.astype(bf16).reshape(planes, depth // planes, 2 * width)
    groups = [[g * RING + z for g in range(planes)] for z in range(RING)]
    grads = lax.all_to_all(grads, "dp", 0, 0, axis_index_groups=groups, tiled=True)
    grads = jnp.sum(grads.astype(f32), axis=0).astype(bf16)
    gi = grads[:, :width].reshape(RING, -1)
    gt = grads[:, width:].reshape(RING, -1)
    share = gi.shape[1]
    lanes = 128
    filled = -(-2 * share // lanes)
    flat = jnp.concatenate((gi, gt), axis=1)
    flat = jnp.pad(flat, ((0, 0), (0, filled * lanes - 2 * share)))
    flat = flat.reshape(RING, filled, lanes)
    groups = [[g * RING + z for z in range(RING)] for g in range(planes)]
    flat = lax.all_to_all(flat, "dp", 0, 0, axis_index_groups=groups, tiled=True)
    flat = jnp.sum(flat.astype(f32), axis=0).reshape(1, -1)
    return (loss, flat[:, :share], flat[:, share : 2 * share])


def solution(mesh):
    in_specs = (P("dp", None), P("dp", None), P(None, "tower"), P(None, "tower"), P(), P())
    out_specs = (P("dp"), P("tower", "dp"), P("tower", "dp"))
    return jax.shard_map(shards, mesh=mesh, in_specs=in_specs, out_specs=out_specs, check_vma=False)
```

time: 2440 us -> 147 us (0.06)
  waiting for transfers between devices: 2330 us -> 25.3 us
  blocking collectives: 17.5 us -> 71.3 us
    unnamed x2 -> x0, waiting for transfers between devices: 2230 us -> none
    ppermute x8 -> x7, waiting for transfers between devices: 104 us -> 25.3 us  [the longest x4 17.8 us: shifted(): return lax.ppermute(block, ('dp', 'tower'), route)]
    all_to_all x0 -> x2, blocking collectives: none -> 71.3 us  [the longest x1 42.7 us: shards(): lax.all_to_all(flat, 'dp', 0, 0, axis_index_groups=groups, tiled=True)]
  transfers between devices with their start and end apart: 9 -> 7, of which waited for: 8 -> 6; matrix products, arithmetic and copies ran while one was open for 1% -> 1% of each run, Pallas kernels for 0% -> 0%
where the time goes in v1:
time: 147 us; the launch traced here: 146 us
  blocking collectives  71.3 us (49%)
  starting transfers between devices  33 us (22%)
  waiting for transfers between devices  25.3 us (17%)
  matrix products  7.39 us (5%)
  local copies, waits for them, and re-layouts  4.94 us (3%)
  between operations  2.23 us (2%)
  other arithmetic  1.83 us (1%)
    all_to_all x1, blocking collectives, shards(): lax.all_to_all(flat, 'dp', 0, 0, axis_index_groups=groups, tiled=True)  42.7 us
    all_to_all x1, blocking collectives, shards(): lax.all_to_all(grads, 'dp', 0, 0, axis_index_groups=groups, tiled=True)  28.6 us
    ppermute x4, starting transfers between devices, shifted(): return lax.ppermute(block, ('dp', 'tower'), route)  26.1 us
    ppermute x4, waiting for transfers between devices, shifted(): return lax.ppermute(block, ('dp', 'tower'), route)  17.8 us
    ppermute x1, waiting for transfers between devices, shards(): peer = lax.ppermute(payload, 'tower', to_chip).astype(f32)  4.43 us
    dot_general x6, matrix products, times(): return jnp.dot(left, right, preferred_element_type=jnp.float32)  3.94 us
    ppermute x1, starting transfers between devices, shards(): peer = lax.ppermute(payload, 'tower', to_chip).astype(f32)  3.01 us
  transfers between devices with their start and end apart: 7, of which 6 were waited for; matrix products, arithmetic and copies ran while one was open for 1% of the time, Pallas kernels for 0%

profile of v1, /device:TPU:6, one launch (start us, length us, event | category | flops | bytes accessed | tf_op | source)
XLA Modules:
  0.0 146.0 jit_solution(18196176023398466586)
XLA Ops:
  0.6 0.0 copy-start
  0.6 1.1 copy-done
  1.7 1.3 fusion.80
  3.0 1.5 %fusion.79 = (bf16[128,288]{0,1:T(8,128)(2,1)S(1)}, f32[128,288]{0,1:T(8,128)S(1)}) fusion(bf16[128,1152]{1,0:T(8,128)(2,1)} %param.7, bf16[1152,288]{0,1:T(8,128)(2,1)} %param.9), kind=kOutput, calls=%fused_computation.140 | convolution fusion | flops 84971520 | bytes 1179648 | tf_op jit(solution)/shard_map/dot_general | solution.py:22
  4.6 1.9 %collective-permute-start = (bf16[256,288]{0,1:T(8,128)(2,1)S(1)}, bf16[256,288]{0,1:T(8,128)(2,1)S(1)}, u32[]{:S(2)}, u32[]{:S(2)}) collective-permute-start(bf16[256,288]{0,1:T(8,128)(2,1)S(1)} %pad_maximum_fusion.2), channel_id=1, source_target_pairs={{0,1},{1,0},{2,3},{3,2},{4,5},{5,4},{6,7},{7,6},{8,9},{9,8},{10,11... | collective-permute-start | bytes 442376 | tf_op jit(solution)/shard_map/ppermute | solution.py:53
  6.5 1.3 collective-permute-done
  7.9 18.9 %collective-permute-start.3 = (bf16[128,576]{0,1:T(8,128)(2,1)S(1)}, bf16[128,576]{0,1:T(8,128)(2,1)S(1)}, u32[]{:S(2)}, u32[]{:S(2)}) collective-permute-start(bf16[128,576]{0,1:T(8,128)(2,1)S(1)} %get-tuple-element.18), channel_id=1, source_target_pairs={{0,1020},{1,1017},{2,1022},{3,1019},{4,0},{5,1021},{6,2},{7,1023},... | collective-permute-start | bytes 442376 | tf_op jit(solution)/shard_map/ppermute | solution.py:36
  26.9 0.2 fusion.2
  27.1 1.9 %collective-permute-start.1 = (bf16[128,576]{0,1:T(8,128)(2,1)S(1)}, bf16[128,576]{0,1:T(8,128)(2,1)S(1)}, u32[]{:S(2)}, u32[]{:S(2)}) collective-permute-start(bf16[128,576]{0,1:T(8,128)(2,1)S(1)} %get-tuple-element.19), channel_id=1, source_target_pairs={{0,4},{1,9},{2,6},{3,11},{4,8},{5,13},{6,10},{7,15},{8,12},{9,17},... | collective-permute-start | bytes 442376 | tf_op jit(solution)/shard_map/ppermute | solution.py:36
  29.0 0.1 multiply_reduce_fusion.4
  29.1 3.2 %collective-permute-done.3 = bf16[128,576]{0,1:T(8,128)(2,1)S(1)} collective-permute-done((bf16[128,576]{0,1:T(8,128)(2,1)S(1)}, bf16[128,576]{0,1:T(8,128)(2,1)S(1)}, u32[]{:S(2)}, u32[]{:S(2)}) %collective-permute-start.3) | collective-permute-done | bytes 147488 | tf_op jit(solution)/shard_map/ppermute | solution.py:36
  32.3 3.4 %collective-permute-start.4 = (bf16[128,576]{0,1:T(8,128)(2,1)S(1)}, bf16[128,576]{0,1:T(8,128)(2,1)S(1)}, u32[]{:S(2)}, u32[]{:S(2)}) collective-permute-start(bf16[128,576]{0,1:T(8,128)(2,1)S(1)} %collective-permute-done.3), channel_id=1, source_target_pairs={{0,1016},{1,1017},{2,1018},{3,1019},{4,1020},{5,1021},{6,1022},{7,... | collective-permute-start | bytes 442376 | tf_op jit(solution)/shard_map/ppermute | solution.py:36
  35.6 0.2 fusion.5
  35.9 3.3 %collective-permute-done.1 = bf16[128,576]{0,1:T(8,128)(2,1)S(1)} collective-permute-done((bf16[128,576]{0,1:T(8,128)(2,1)S(1)}, bf16[128,576]{0,1:T(8,128)(2,1)S(1)}, u32[]{:S(2)}, u32[]{:S(2)}) %collective-permute-start.1) | collective-permute-done | bytes 147488 | tf_op jit(solution)/shard_map/ppermute | solution.py:36
  39.2 0.2 fusion.3
  39.4 0.1 multiply_reduce_fusion.3
  39.5 1.9 %collective-permute-start.2 = (bf16[128,576]{0,1:T(8,128)(2,1)S(1)}, bf16[128,576]{0,1:T(8,128)(2,1)S(1)}, u32[]{:S(2)}, u32[]{:S(2)}) collective-permute-start(bf16[128,576]{0,1:T(8,128)(2,1)S(1)} %collective-permute-done.1), channel_id=1, source_target_pairs={{0,8},{1,9},{2,10},{3,11},{4,12},{5,13},{6,14},{7,15},{8,16},{9,17... | collective-permute-start | bytes 442376 | tf_op jit(solution)/shard_map/ppermute | solution.py:36
  41.5 0.1 multiply_reduce_fusion.1
  41.6 0.0 collective-permute-done.4
  41.6 0.1 multiply_reduce_fusion.2
  41.7 11.3 %collective-permute-done.2 = bf16[128,576]{0,1:T(8,128)(2,1)S(1)} collective-permute-done((bf16[128,576]{0,1:T(8,128)(2,1)S(1)}, bf16[128,576]{0,1:T(8,128)(2,1)S(1)}, u32[]{:S(2)}, u32[]{:S(2)}) %collective-permute-start.2) | collective-permute-done | bytes 147488 | tf_op jit(solution)/shard_map/ppermute | solution.py:36
  53.0 0.1 multiply_reduce_fusion
  53.1 0.2 fusion.6
  53.3 0.2 fusion.4
  53.6 0.2 concatenate.32
  53.8 3.0 %collective-permute-start.5 = (bf16[656,128]{1,0:T(8,128)(2,1)S(1)}, bf16[656,128]{1,0:T(8,128)(2,1)S(1)}, u32[]{:S(2)}, u32[]{:S(2)}) collective-permute-start(bf16[656,128]{1,0:T(8,128)(2,1)S(1)} %concatenate.32), channel_id=1, source_target_pairs={{0,2},{1,3},{2,0},{3,1},{4,6},{5,7},{6,4},{7,5},{8,10},{9,11},{10,... | collective-permute-start | bytes 503816 | tf_op jit(solution)/shard_map/ppermute | solution.py:72
  58.1 4.4 %collective-permute-done.5 = bf16[656,128]{1,0:T(8,128)(2,1)S(1)} collective-permute-done((bf16[656,128]{1,0:T(8,128)(2,1)S(1)}, bf16[656,128]{1,0:T(8,128)(2,1)S(1)}, u32[]{:S(2)}, u32[]{:S(2)}) %collective-permute-start.5) | collective-permute-done | bytes 167968 | tf_op jit(solution)/shard_map/ppermute | solution.py:72
  62.6 0.4 fusion.69
  63.0 0.1 copy.18
  63.1 0.3 fusion.43
  63.4 0.3 convolution_add_fusion
  63.7 0.0 copy-start.2
  63.7 0.3 fusion.42
  64.0 0.3 convolution_add_fusion.1
  64.3 0.0 copy-start.1
  64.3 0.7 copy-done.1
  65.1 1.9 %collective-permute-start.6 = (f32[264,288]{0,1:T(8,128)S(1)}, f32[264,288]{0,1:T(8,128)S(1)}, u32[]{:S(2)}, u32[]{:S(2)}) collective-permute-start(f32[264,288]{0,1:T(8,128)S(1)} %select_maximum_fusion), channel_id=1, source_target_pairs={{0,1},{1,0},{2,3},{3,2},{4,5},{5,4},{6,7},{7,6},{8,9},{9,8},{10,11... | collective-permute-start | bytes 912392 | tf_op jit(solution)/shard_map/ppermute | solution.py:103
  67.0 1.8 %collective-permute-done.6 = f32[264,288]{0,1:T(8,128)S(1)} collective-permute-done((f32[264,288]{0,1:T(8,128)S(1)}, f32[264,288]{0,1:T(8,128)S(1)}, u32[]{:S(2)}, u32[]{:S(2)}) %collective-permute-start.6) | collective-permute-done | bytes 304160 | tf_op jit(solution)/shard_map/ppermute | solution.py:103
  68.8 0.0 copy-start.3
  68.8 0.7 slice_reduce_fusion.1
  69.5 0.0 copy-done.2
  69.5 0.6 fusion.1
  70.0 0.4 copy.20
  70.5 0.0 copy-done.3
  70.5 1.7 %fusion = bf16[1152,288]{0,1:T(8,128)(2,1)S(1)} fusion(bf16[128,1152]{1,0:T(8,128)(2,1)} %param.6, f32[264,288]{0,1:T(8,128)} %copy-done.3, f32[128,576]{0,1:T(8,128)} %copy-done.1, f32[128,288]{0,1:T(8,128)S(1)} %get-tuple-element.37, f32[128]{0:T(128)S(1)} %get-tuple-element.31, f32[128]{0:T(128)S(1)} %get-tuple-element.24, f32[]{:T(128)} %bitcast.56, ...), kind=kOutput, calls=%fused_computation.2 | convolution fusion | flops 95158272 | bytes 1543680 | tf_op jit(solution)/shard_map/dot_general | solution.py:16
  72.2 0.4 copy.19
  72.6 0.5 pad_maximum_fusion
  73.1 28.6 %all_to_all.10 = bf16[8,144,576]{2,1,0:T(8,128)(2,1)S(1)} all-to-all(bf16[8,144,576]{2,1,0:T(8,128)(2,1)S(1)} %pad_maximum_fusion), channel_id=1, replica_groups={{0,128,256,384,512,640,768,896},{4,132,260,388,516,644,772,900},{8,136,..., dimensions={0} | all-to-all | bytes 2654208 | tf_op jit(solution)/shard_map/all_to_all | solution.py:117
  101.7 0.2 reduce_sum.151
  101.9 0.1 fusion.77
  102.0 0.2 reshape.74
  102.2 0.2 reshape.75
  102.3 0.1 fusion.9
  102.4 0.1 reshape.76
  102.6 42.7 %all_to_all.11 = bf16[32,21,128]{2,1,0:T(8,128)(2,1)S(1)} all-to-all(bf16[32,21,128]{2,1,0:T(8,128)(2,1)S(1)} %reshape.76), channel_id=1, replica_groups={{0,4,8,12,16,20,24,28,32,36,40,44,48,52,56,60,64,68,72,76,80,84,88,92,9..., dimensions={0} | all-to-all | bytes 344064 | tf_op jit(solution)/shard_map/all_to_all | solution.py:128
  145.3 0.7 fusion.78
  (18 shorter events, 0.3 us)
Async XLA Ops:
  0.6 1.1 copy-start
  4.6 3.3 %collective-permute-start = (bf16[256,288]{0,1:T(8,128)(2,1)S(1)}, bf16[256,288]{0,1:T(8,128)(2,1)S(1)}, u32[]{:S(2)}, u32[]{:S(2)}) collective-permute-start(bf16[256,288]{0,1:T(8,128)(2,1)S(1)} %pad_maximum_fusion.2), channel_id=1, source_target_pairs={{0,1},{1,0},{2,3},{3,2},{4,5},{5,4},{6,7},{7,6},{8,9},{9,8},{10,11... | collective-permute-start | bytes 442376 | tf_op jit(solution)/shard_map/ppermute | solution.py:53
  7.9 24.4 %collective-permute-start.3 = (bf16[128,576]{0,1:T(8,128)(2,1)S(1)}, bf16[128,576]{0,1:T(8,128)(2,1)S(1)}, u32[]{:S(2)}, u32[]{:S(2)}) collective-permute-start(bf16[128,576]{0,1:T(8,128)(2,1)S(1)} %get-tuple-element.18), channel_id=1, source_target_pairs={{0,1020},{1,1017},{2,1022},{3,1019},{4,0},{5,1021},{6,2},{7,1023},... | collective-permute-start | bytes 442376 | tf_op jit(solution)/shard_map/ppermute | solution.py:36
  27.1 12.1 %collective-permute-start.1 = (bf16[128,576]{0,1:T(8,128)(2,1)S(1)}, bf16[128,576]{0,1:T(8,128)(2,1)S(1)}, u32[]{:S(2)}, u32[]{:S(2)}) collective-permute-start(bf16[128,576]{0,1:T(8,128)(2,1)S(1)} %get-tuple-element.19), channel_id=1, source_target_pairs={{0,4},{1,9},{2,6},{3,11},{4,8},{5,13},{6,10},{7,15},{8,12},{9,17},... | collective-permute-start | bytes 442376 | tf_op jit(solution)/shard_map/ppermute | solution.py:36
  32.3 9.3 %collective-permute-start.4 = (bf16[128,576]{0,1:T(8,128)(2,1)S(1)}, bf16[128,576]{0,1:T(8,128)(2,1)S(1)}, u32[]{:S(2)}, u32[]{:S(2)}) collective-permute-start(bf16[128,576]{0,1:T(8,128)(2,1)S(1)} %collective-permute-done.3), channel_id=1, source_target_pairs={{0,1016},{1,1017},{2,1018},{3,1019},{4,1020},{5,1021},{6,1022},{7,... | collective-permute-start | bytes 442376 | tf_op jit(solution)/shard_map/ppermute | solution.py:36
  39.5 13.4 %collective-permute-start.2 = (bf16[128,576]{0,1:T(8,128)(2,1)S(1)}, bf16[128,576]{0,1:T(8,128)(2,1)S(1)}, u32[]{:S(2)}, u32[]{:S(2)}) collective-permute-start(bf16[128,576]{0,1:T(8,128)(2,1)S(1)} %collective-permute-done.1), channel_id=1, source_target_pairs={{0,8},{1,9},{2,10},{3,11},{4,12},{5,13},{6,14},{7,15},{8,16},{9,17... | collective-permute-start | bytes 442376 | tf_op jit(solution)/shard_map/ppermute | solution.py:36
  53.8 8.7 %collective-permute-start.5 = (bf16[656,128]{1,0:T(8,128)(2,1)S(1)}, bf16[656,128]{1,0:T(8,128)(2,1)S(1)}, u32[]{:S(2)}, u32[]{:S(2)}) collective-permute-start(bf16[656,128]{1,0:T(8,128)(2,1)S(1)} %concatenate.32), channel_id=1, source_target_pairs={{0,2},{1,3},{2,0},{3,1},{4,6},{5,7},{6,4},{7,5},{8,10},{9,11},{10,... | collective-permute-start | bytes 503816 | tf_op jit(solution)/shard_map/ppermute | solution.py:72
  63.7 5.8 %copy-start.2 = (bf16[128,1152]{1,0:T(8,128)(2,1)S(1)}, bf16[128,1152]{1,0:T(8,128)(2,1)}, u32[]{:S(2)}) copy-start(bf16[128,1152]{1,0:T(8,128)(2,1)} %param.7) | copy-start | bytes 884740
  64.3 0.7 copy-start.1
  65.1 3.7 %collective-permute-start.6 = (f32[264,288]{0,1:T(8,128)S(1)}, f32[264,288]{0,1:T(8,128)S(1)}, u32[]{:S(2)}, u32[]{:S(2)}) collective-permute-start(f32[264,288]{0,1:T(8,128)S(1)} %select_maximum_fusion), channel_id=1, source_target_pairs={{0,1},{1,0},{2,3},{3,2},{4,5},{5,4},{6,7},{7,6},{8,9},{9,8},{10,11... | collective-permute-start | bytes 912392 | tf_op jit(solution)/shard_map/ppermute | solution.py:103
  68.8 1.7 %copy-start.3 = (f32[264,288]{0,1:T(8,128)}, f32[264,288]{0,1:T(8,128)S(1)}, u32[]{:S(2)}) copy-start(f32[264,288]{0,1:T(8,128)S(1)} %collective-permute-done.6) | copy-start | bytes 912388

commit v2 on v1

--- a/solution.py
+++ b/solution.py
@@ -4,6 +4,7 @@
 from jax.sharding import PartitionSpec as P
 
 RING = 32
+LANES = 128
 
 
 def across(left, right):
@@ -20,6 +21,54 @@
 
 def times(left, right):
     return jnp.dot(left, right, preferred_element_type=jnp.float32)
+
+
+def two_terms(x):
+    high = rounded(x)
+    return high.astype(jnp.bfloat16), (x - high).astype(jnp.bfloat16)
+
+
+def fine(weights, block):
+    return times(jnp.concatenate(two_terms(weights), axis=1), jnp.concatenate((block, block), axis=0))
+
+
+def fine_down(feats, grad):
+    return down(jnp.concatenate((feats, feats), axis=0), jnp.concatenate(two_terms(grad), axis=0))
+
+
+def laned(x):
+    rows, cols = x.shape[1:]
+    whole = cols // LANES * LANES
+    blocks = [x[:, :, j : j + LANES] for j in range(0, whole, LANES)]
+    rest = x[:, :, whole:]
+    blocks.append(jnp.concatenate((rest[:, : rows // 2], rest[:, rows // 2 :]), axis=2))
+    return jnp.concatenate(blocks, axis=1)
+
+
+def unlaned(x, rows, cols):
+    whole = cols // LANES
+    blocks = [x[j * rows : (j + 1) * rows] for j in range(whole)]
+    rest = x[whole * rows :]
+    blocks.append(jnp.concatenate((rest[:, : LANES // 2], rest[:, LANES // 2 :]), axis=0))
+    return jnp.concatenate(blocks, axis=1)
+
+
+def swapped(x, groups, spare):
+    f16, f32 = jnp.float16, jnp.float32
+    top = jnp.max(jnp.abs(x))
+    power = jnp.floor(jnp.log2(jnp.where(top > 0, top, 1.0))) - 13.0
+    power = jnp.maximum(power, -120.0)
+    x = x * jnp.exp2(-power)
+    if spare:
+        last = lax.broadcasted_iota(jnp.int32, x.shape, 1) == x.shape[1] - 1
+        last &= lax.broadcasted_iota(jnp.int32, x.shape, 2) == LANES - 1
+        x = jnp.where(last, power, x)
+    else:
+        x = jnp.concatenate((x, jnp.full((x.shape[0], 8, LANES), power)), axis=1)
+    sent = x.astype(f16)
+    got = lax.all_to_all(sent, "dp", 0, 0, axis_index_groups=groups, tiled=True).astype(f32)
+    summed = jnp.sum(got * jnp.exp2(got[:, -1:, -1:]), axis=0)
+    return summed if spare else summed[:-8]
 
 
 def rounded(x):
@@ -93,10 +142,10 @@
     h1, h2 = jax.nn.sigmoid(e1 + bias), jax.nn.sigmoid(e2 + bias)
     along_i = jnp.sum(g1 * c1 + g2 * c2, axis=-1)
     along_t = jnp.sum(h1 * e1 + h2 * e2, axis=-1)
-    du = times((g1 * inv[4]).astype(bf16), t1) + times((g2 * inv[5]).astype(bf16), t2)
-    dv = times((h1 * inv[2]).astype(bf16), i1) + times((h2 * inv[3]).astype(bf16), i2)
-    du0 = times((g0 * nt[None, :]).astype(bf16), t0[:, :width])
-    dv0 = down((g0 * ni[:, None]).astype(bf16), i0[:, :width])
+    du = fine(g1 * inv[4], t1) + fine(g2 * inv[5], t2)
+    dv = fine(h1 * inv[2], i1) + fine(h2 * inv[3], i2)
+    du0 = fine(g0 * nt[None, :], t0[:, :width])
+    dv0 = fine((g0 * ni[:, None]).T, i0[:, :width])
     lines = jnp.stack((along_i, along_t, loss), axis=0)
     lines = jnp.pad(lines, ((0, 5), (0, width - rows)))
     sums = jnp.concatenate((du[:, width:], dv[:, width:], lines), axis=0)
@@ -107,26 +156,22 @@
     loss = lines[2]
     du = scale * (du[:, :width] + got[:rows] + du0)
     dv = scale * (dv[:, :width] + got[rows : 2 * rows] + dv0)
-    dzi = ((du - zi * (ni * along_i)[:, None]) * ni[:, None]).astype(bf16)
-    dzt = ((dv - zt * (nt * along_t)[:, None]) * nt[:, None]).astype(bf16)
+    dzi = (du - zi * (ni * along_i)[:, None]) * ni[:, None]
+    dzt = (dv - zt * (nt * along_t)[:, None]) * nt[:, None]
 
     depth = image_feats.shape[1]
-    grads = jnp.concatenate((down(image_feats, dzi), down(text_feats, dzt)), axis=1)
-    grads = grads.astype(bf16).reshape(planes, depth // planes, 2 * width)
+    share = depth * width // dp
+    grads = jnp.concatenate((fine_down(image_feats, dzi), fine_down(text_feats, dzt)), axis=1)
+    grads = grads.reshape(planes, depth // planes, 2 * width)
     groups = [[g * RING + z for g in range(planes)] for z in range(RING)]
-    grads = lax.all_to_all(grads, "dp", 0, 0, axis_index_groups=groups, tiled=True)
-    grads = jnp.sum(grads.astype(f32), axis=0).astype(bf16)
-    gi = grads[:, :width].reshape(RING, -1)
-    gt = grads[:, width:].reshape(RING, -1)
-    share = gi.shape[1]
-    lanes = 128
-    filled = -(-2 * share // lanes)
-    flat = jnp.concatenate((gi, gt), axis=1)
-    flat = jnp.pad(flat, ((0, 0), (0, filled * lanes - 2 * share)))
-    flat = flat.reshape(RING, filled, lanes)
+    grads = unlaned(swapped(laned(grads), groups, False), depth // planes, 2 * width)
+    flat = jnp.concatenate(
+        (grads[:, :width].reshape(RING, share), grads[:, width:].reshape(RING, share)), axis=1
+    )
+    filled = -(-2 * share // LANES)
+    flat = jnp.pad(flat, ((0, 0), (0, filled * LANES - 2 * share)))
     groups = [[g * RING + z for z in range(RING)] for g in range(planes)]
-    flat = lax.all_to_all(flat, "dp", 0, 0, axis_index_groups=groups, tiled=True)
-    flat = jnp.sum(flat.astype(f32), axis=0).reshape(1, -1)
+    flat = swapped(flat.reshape(RING, filled, LANES), groups, True).reshape(1, -1)
     return (loss, flat[:, :share], flat[:, share : 2 * share])
 
 

time: 147 us -> 159 us (1.082)
  blocking collectives: 71.3 us -> 47.2 us
  starting transfers between devices: 33 us -> 46.4 us
  waiting for transfers between devices: 25.3 us -> 35.2 us
  local copies, waits for them, and re-layouts: 4.94 us -> 12.5 us
  other arithmetic: 1.83 us -> 5.11 us
  between operations: 2.23 us -> 5.09 us
    all_to_all x2 -> x1, blocking collectives: 71.3 us -> 47.2 us  [swapped(): lax.all_to_all(sent, 'dp', 0, 0, axis_index_groups=groups, tiled=True)]
    all_to_all x0 -> x1, waiting for transfers between devices: none -> 18.3 us  [swapped(): lax.all_to_all(sent, 'dp', 0, 0, axis_index_groups=groups, tiled=True)]
    all_to_all x0 -> x1, starting transfers between devices: none -> 9.71 us  [swapped(): lax.all_to_all(sent, 'dp', 0, 0, axis_index_groups=groups, tiled=True)]
    ppermute x4, waiting for transfers between devices: 17.8 us -> 9.43 us  [shifted(): return lax.ppermute(block, ('dp', 'tower'), route)]
    unnamed x9 -> x11, local copies, waits for them, and re-layouts: 1.82 us -> 5.53 us
    concatenate x0 -> x2, local copies, waits for them, and re-layouts: none -> 3.69 us  [the longest x1 2.34 us: shards(): jnp.concatenate((fine_down(image_feats, dzi), fine_down(text_feats, dzt))...]
    ppermute x4, starting transfers between devices: 26.1 us -> 29.7 us  [shifted(): return lax.ppermute(block, ('dp', 'tower'), route)]
    dot_general x6 -> x8, matrix products: 3.94 us -> 4.16 us  [times(): return jnp.dot(left, right, preferred_element_type=jnp.float32)]
  transfers between devices with their start and end apart: 7 -> 8, of which waited for: 6 -> 6; matrix products, arithmetic and copies ran while one was open for 1% -> 1% of each run, Pallas kernels for 0% -> 0%
where the time goes in v2:
time: 159 us; the launch traced here: 158 us
  blocking collectives  47.2 us (30%)
  starting transfers between devices  46.4 us (29%)
  waiting for transfers between devices  35.2 us (22%)
  local copies, waits for them, and re-layouts  12.5 us (8%)
  matrix products  6.11 us (4%)
  other arithmetic  5.11 us (3%)
  between operations  5.09 us (3%)
    all_to_all x1, blocking collectives, swapped(): lax.all_to_all(sent, 'dp', 0, 0, axis_index_groups=groups, tiled=True)  47.2 us
    ppermute x4, starting transfers between devices, shifted(): return lax.ppermute(block, ('dp', 'tower'), route)  29.7 us
    all_to_all x1, waiting for transfers between devices, swapped(): lax.all_to_all(sent, 'dp', 0, 0, axis_index_groups=groups, tiled=True)  18.3 us
    all_to_all x1, starting transfers between devices, swapped(): lax.all_to_all(sent, 'dp', 0, 0, axis_index_groups=groups, tiled=True)  9.71 us
    ppermute x4, waiting for transfers between devices, shifted(): return lax.ppermute(block, ('dp', 'tower'), route)  9.43 us
    unnamed x11, local copies, waits for them, and re-layouts  5.53 us
    ppermute x1, waiting for transfers between devices, shards(): peer = lax.ppermute(payload, 'tower', to_chip).astype(f32)  4.44 us
    dot_general x8, matrix products, times(): return jnp.dot(left, right, preferred_element_type=jnp.float32)  4.16 us
  transfers between devices with their start and end apart: 8, of which 6 were waited for; matrix products, arithmetic and copies ran while one was open for 1% of the time, Pallas kernels for 0%

profile of v2, /device:TPU:6, one launch (start us, length us, event | category | flops | bytes accessed | tf_op | source)
XLA Modules:
  0.0 157.5 jit_solution(9735459347290702914)
XLA Ops:
  0.6 1.1 copy-done
  1.7 1.3 fusion.116
  3.0 1.5 fusion.117
  4.6 1.9 %collective-permute-start = (bf16[256,288]{0,1:T(8,128)(2,1)S(1)}, bf16[256,288]{0,1:T(8,128)(2,1)S(1)}, u32[]{:S(2)}, u32[]{:S(2)}) collective-permute-start(bf16[256,288]{0,1:T(8,128)(2,1)S(1)} %pad_maximum_fusion.7), channel_id=1, source_target_pairs={{0,1},{1,0},{2,3},{3,2},{4,5},{5,4},{6,7},{7,6},{8,9},{9,8},{10,11... | collective-permute-start | bytes 442376 | tf_op jit(solution)/shard_map/ppermute | solution.py:102
  6.5 1.3 collective-permute-done
  7.9 3.8 %collective-permute-start.1 = (bf16[128,576]{0,1:T(8,128)(2,1)S(1)}, bf16[128,576]{0,1:T(8,128)(2,1)S(1)}, u32[]{:S(2)}, u32[]{:S(2)}) collective-permute-start(bf16[128,576]{0,1:T(8,128)(2,1)S(1)} %get-tuple-element.48), channel_id=1, source_target_pairs={{0,4},{1,9},{2,6},{3,11},{4,8},{5,13},{6,10},{7,15},{8,12},{9,17},... | collective-permute-start | bytes 442376 | tf_op jit(solution)/shard_map/ppermute | solution.py:85
  11.7 0.2 fusion
  12.0 17.0 %collective-permute-start.3 = (bf16[128,576]{0,1:T(8,128)(2,1)S(1)}, bf16[128,576]{0,1:T(8,128)(2,1)S(1)}, u32[]{:S(2)}, u32[]{:S(2)}) collective-permute-start(bf16[128,576]{0,1:T(8,128)(2,1)S(1)} %get-tuple-element.47), channel_id=1, source_target_pairs={{0,1020},{1,1017},{2,1022},{3,1019},{4,0},{5,1021},{6,2},{7,1023},... | collective-permute-start | bytes 442376 | tf_op jit(solution)/shard_map/ppermute | solution.py:85
  29.1 3.5 %collective-permute-done.1 = bf16[128,576]{0,1:T(8,128)(2,1)S(1)} collective-permute-done((bf16[128,576]{0,1:T(8,128)(2,1)S(1)}, bf16[128,576]{0,1:T(8,128)(2,1)S(1)}, u32[]{:S(2)}, u32[]{:S(2)}) %collective-permute-start.1) | collective-permute-done | bytes 147488 | tf_op jit(solution)/shard_map/ppermute | solution.py:85
  32.6 1.9 %collective-permute-start.2 = (bf16[128,576]{0,1:T(8,128)(2,1)S(1)}, bf16[128,576]{0,1:T(8,128)(2,1)S(1)}, u32[]{:S(2)}, u32[]{:S(2)}) collective-permute-start(bf16[128,576]{0,1:T(8,128)(2,1)S(1)} %collective-permute-done.1), channel_id=1, source_target_pairs={{0,8},{1,9},{2,10},{3,11},{4,12},{5,13},{6,14},{7,15},{8,16},{9,17... | collective-permute-start | bytes 442376 | tf_op jit(solution)/shard_map/ppermute | solution.py:85
  34.5 0.2 fusion.1
  34.8 0.2 fusion.3
  35.0 6.9 %collective-permute-start.4 = (bf16[128,576]{0,1:T(8,128)(2,1)S(1)}, bf16[128,576]{0,1:T(8,128)(2,1)S(1)}, u32[]{:S(2)}, u32[]{:S(2)}) collective-permute-start(bf16[128,576]{0,1:T(8,128)(2,1)S(1)} %collective-permute-done.3), channel_id=1, source_target_pairs={{0,1016},{1,1017},{2,1018},{3,1019},{4,1020},{5,1021},{6,1022},{7,... | collective-permute-start | bytes 442376 | tf_op jit(solution)/shard_map/ppermute | solution.py:85
  41.9 0.1 multiply_reduce_fusion.5
  42.0 0.1 multiply_reduce_fusion.3
  42.1 5.9 %collective-permute-done.4 = bf16[128,576]{0,1:T(8,128)(2,1)S(1)} collective-permute-done((bf16[128,576]{0,1:T(8,128)(2,1)S(1)}, bf16[128,576]{0,1:T(8,128)(2,1)S(1)}, u32[]{:S(2)}, u32[]{:S(2)}) %collective-permute-start.4) | collective-permute-done | bytes 147488 | tf_op jit(solution)/shard_map/ppermute | solution.py:85
  48.1 0.1 multiply_reduce_fusion.4
  48.2 0.1 multiply_reduce_fusion.2
  48.3 0.2 fusion.2
  48.5 0.2 fusion.4
  48.8 0.2 concatenate.93
  49.0 3.0 %collective-permute-start.5 = (bf16[656,128]{1,0:T(8,128)(2,1)S(1)}, bf16[656,128]{1,0:T(8,128)(2,1)S(1)}, u32[]{:S(2)}, u32[]{:S(2)}) collective-permute-start(bf16[656,128]{1,0:T(8,128)(2,1)S(1)} %concatenate.93), channel_id=1, source_target_pairs={{0,2},{1,3},{2,0},{3,1},{4,6},{5,7},{6,4},{7,5},{8,10},{9,11},{10,... | collective-permute-start | bytes 503816 | tf_op jit(solution)/shard_map/ppermute | solution.py:121
  53.3 4.4 %collective-permute-done.5 = bf16[656,128]{1,0:T(8,128)(2,1)S(1)} collective-permute-done((bf16[656,128]{1,0:T(8,128)(2,1)S(1)}, bf16[656,128]{1,0:T(8,128)(2,1)S(1)}, u32[]{:S(2)}, u32[]{:S(2)}) %collective-permute-start.5) | collective-permute-done | bytes 167968 | tf_op jit(solution)/shard_map/ppermute | solution.py:121
  57.8 0.2 reduce-precision_convert_fusion.4
  58.0 0.4 reduce-precision_convert_fusion.6
  58.4 0.1 copy.32
  58.5 0.2 fusion.20
  58.8 0.2 convolution_add_fusion
  59.0 0.2 fusion.13
  59.3 0.2 convolution_add_fusion.1
  59.6 2.1 %collective-permute-start.6 = (f32[264,288]{0,1:T(8,128)S(1)}, f32[264,288]{0,1:T(8,128)S(1)}, u32[]{:S(2)}, u32[]{:S(2)}) collective-permute-start(f32[264,288]{0,1:T(8,128)S(1)} %select_maximum_fusion), channel_id=1, source_target_pairs={{0,1},{1,0},{2,3},{3,2},{4,5},{5,4},{6,7},{7,6},{8,9},{9,8},{10,11... | collective-permute-start | bytes 912392 | tf_op jit(solution)/shard_map/ppermute | solution.py:152
  61.6 0.1 reduce-precision_convert_fusion.2
  61.7 1.7 %collective-permute-done.6 = f32[264,288]{0,1:T(8,128)S(1)} collective-permute-done((f32[264,288]{0,1:T(8,128)S(1)}, f32[264,288]{0,1:T(8,128)S(1)}, u32[]{:S(2)}, u32[]{:S(2)}) %collective-permute-start.6) | collective-permute-done | bytes 304160 | tf_op jit(solution)/shard_map/ppermute | solution.py:152
  63.4 0.7 slice_reduce_fusion.1
  64.1 0.2 reduce-precision_convert_fusion
  64.3 0.4 fusion.9
  64.7 0.2 reduce-precision_convert_fusion.1
  64.9 0.4 fusion.5
  65.3 0.2 pad_maximum_fusion
  65.5 2.3 %copy.33 = f32[1152,576]{1,0:T(8,128)} copy(f32[1152,576]{0,1:T(8,128)S(1)} %pad_maximum_fusion) | data formatting | bytes 5308416 | tf_op jit(solution)/shard_map/concatenate | solution.py:164
  67.8 1.1 slice_dynamic-update-slice_fusion.3
  68.9 1.1 fusion.111
  70.0 1.1 slice_dynamic-update-slice_fusion.2
  71.1 1.1 slice_dynamic-update-slice_fusion.1
  72.2 1.1 slice_dynamic-update-slice_fusion
  73.4 0.1 maximum_dynamic-update-slice_fusion
  73.5 0.8 abs_reduce_fusion
  75.7 0.3 multiply_convert_fusion
  75.9 1.3 concatenate.114
  77.3 9.7 %all-to-all-start = ((f16[8,656,128]{2,1,0:T(8,128)(2,1)}), f16[8,656,128]{2,1,0:T(8,128)(2,1)S(1)}, u32[]{:S(2)}, u32[]{:S(2)}) async-start(f16[8,656,128]{2,1,0:T(8,128)(2,1)} %concatenate.114), calls=%async_computation | async-start | bytes 2686976 | tf_op jit(solution)/shard_map/all_to_all | solution.py:69
  87.0 18.3 %all-to-all-done = f16[8,656,128]{2,1,0:T(8,128)(2,1)S(1)} async-done(((f16[8,656,128]{2,1,0:T(8,128)(2,1)}), f16[8,656,128]{2,1,0:T(8,128)(2,1)S(1)}, u32[]{:S(2)}, u32[]{:S(2)}) %all-to-all-start) | async-done | bytes 1343520 | tf_op jit(solution)/shard_map/all_to_all | solution.py:69
  105.3 0.2 convert_element_type.120
  105.5 0.2 fusion.94
  105.7 0.4 multiply_reduce_fusion
  106.2 0.2 pad_maximum_fusion.4
  106.3 0.1 reshape.74
  106.5 0.1 reshape.73
  106.6 0.7 abs_reduce_fusion.1
  108.7 0.1 fusion.28
  108.9 0.1 select_convert_fusion
  109.0 47.2 %all_to_all.10 = f16[32,21,128]{2,1,0:T(8,128)(2,1)S(1)} all-to-all(f16[32,21,128]{2,1,0:T(8,128)(2,1)S(1)} %select_convert_fusion), channel_id=1, replica_groups={{0,4,8,12,16,20,24,28,32,36,40,44,48,52,56,60,64,68,72,76,80,84,88,92,9..., dimensions={0} | all-to-all | bytes 344064 | tf_op jit(solution)/shard_map/all_to_all | solution.py:69
  156.2 0.5 fusion.88
  156.7 0.1 multiply_reduce_fusion.1
  156.8 0.7 fusion.115
  (31 shorter events, 0.5 us)
Async XLA Ops:
  0.6 1.1 copy-start
  4.6 3.3 %collective-permute-start = (bf16[256,288]{0,1:T(8,128)(2,1)S(1)}, bf16[256,288]{0,1:T(8,128)(2,1)S(1)}, u32[]{:S(2)}, u32[]{:S(2)}) collective-permute-start(bf16[256,288]{0,1:T(8,128)(2,1)S(1)} %pad_maximum_fusion.7), channel_id=1, source_target_pairs={{0,1},{1,0},{2,3},{3,2},{4,5},{5,4},{6,7},{7,6},{8,9},{9,8},{10,11... | collective-permute-start | bytes 442376 | tf_op jit(solution)/shard_map/ppermute | solution.py:102
  7.9 24.7 %collective-permute-start.1 = (bf16[128,576]{0,1:T(8,128)(2,1)S(1)}, bf16[128,576]{0,1:T(8,128)(2,1)S(1)}, u32[]{:S(2)}, u32[]{:S(2)}) collective-permute-start(bf16[128,576]{0,1:T(8,128)(2,1)S(1)} %get-tuple-element.48), channel_id=1, source_target_pairs={{0,4},{1,9},{2,6},{3,11},{4,8},{5,13},{6,10},{7,15},{8,12},{9,17},... | collective-permute-start | bytes 442376 | tf_op jit(solution)/shard_map/ppermute | solution.py:85
  12.0 22.8 %collective-permute-start.3 = (bf16[128,576]{0,1:T(8,128)(2,1)S(1)}, bf16[128,576]{0,1:T(8,128)(2,1)S(1)}, u32[]{:S(2)}, u32[]{:S(2)}) collective-permute-start(bf16[128,576]{0,1:T(8,128)(2,1)S(1)} %get-tuple-element.47), channel_id=1, source_target_pairs={{0,1020},{1,1017},{2,1022},{3,1019},{4,0},{5,1021},{6,2},{7,1023},... | collective-permute-start | bytes 442376 | tf_op jit(solution)/shard_map/ppermute | solution.py:85
  32.6 15.6 %collective-permute-start.2 = (bf16[128,576]{0,1:T(8,128)(2,1)S(1)}, bf16[128,576]{0,1:T(8,128)(2,1)S(1)}, u32[]{:S(2)}, u32[]{:S(2)}) collective-permute-start(bf16[128,576]{0,1:T(8,128)(2,1)S(1)} %collective-permute-done.1), channel_id=1, source_target_pairs={{0,8},{1,9},{2,10},{3,11},{4,12},{5,13},{6,14},{7,15},{8,16},{9,17... | collective-permute-start | bytes 442376 | tf_op jit(solution)/shard_map/ppermute | solution.py:85
  35.0 13.1 %collective-permute-start.4 = (bf16[128,576]{0,1:T(8,128)(2,1)S(1)}, bf16[128,576]{0,1:T(8,128)(2,1)S(1)}, u32[]{:S(2)}, u32[]{:S(2)}) collective-permute-start(bf16[128,576]{0,1:T(8,128)(2,1)S(1)} %collective-permute-done.3), channel_id=1, source_target_pairs={{0,1016},{1,1017},{2,1018},{3,1019},{4,1020},{5,1021},{6,1022},{7,... | collective-permute-start | bytes 442376 | tf_op jit(solution)/shard_map/ppermute | solution.py:85
  49.0 8.7 %collective-permute-start.5 = (bf16[656,128]{1,0:T(8,128)(2,1)S(1)}, bf16[656,128]{1,0:T(8,128)(2,1)S(1)}, u32[]{:S(2)}, u32[]{:S(2)}) collective-permute-start(bf16[656,128]{1,0:T(8,128)(2,1)S(1)} %concatenate.93), channel_id=1, source_target_pairs={{0,2},{1,3},{2,0},{3,1},{4,6},{5,7},{6,4},{7,5},{8,10},{9,11},{10,... | collective-permute-start | bytes 503816 | tf_op jit(solution)/shard_map/ppermute | solution.py:121
  58.5 5.8 %copy-start.1 = (bf16[128,1152]{1,0:T(8,128)(2,1)S(1)}, bf16[128,1152]{1,0:T(8,128)(2,1)}, u32[]{:S(2)}) copy-start(bf16[128,1152]{1,0:T(8,128)(2,1)} %param.7) | copy-start | bytes 884740
  59.5 5.4 %copy-start.2 = (bf16[128,1152]{1,0:T(8,128)(2,1)S(1)}, bf16[128,1152]{1,0:T(8,128)(2,1)}, u32[]{:S(2)}) copy-start(bf16[128,1152]{1,0:T(8,128)(2,1)} %param.6) | copy-start | bytes 884740
  59.6 3.8 %collective-permute-start.6 = (f32[264,288]{0,1:T(8,128)S(1)}, f32[264,288]{0,1:T(8,128)S(1)}, u32[]{:S(2)}, u32[]{:S(2)}) collective-permute-start(f32[264,288]{0,1:T(8,128)S(1)} %select_maximum_fusion), channel_id=1, source_target_pairs={{0,1},{1,0},{2,3},{3,2},{4,5},{5,4},{6,7},{7,6},{8,9},{9,8},{10,11... | collective-permute-start | bytes 912392 | tf_op jit(solution)/shard_map/ppermute | solution.py:152
  77.3 28.0 %all-to-all-start = ((f16[8,656,128]{2,1,0:T(8,128)(2,1)}), f16[8,656,128]{2,1,0:T(8,128)(2,1)S(1)}, u32[]{:S(2)}, u32[]{:S(2)}) async-start(f16[8,656,128]{2,1,0:T(8,128)(2,1)} %concatenate.114), calls=%async_computation | async-start | bytes 2686976 | tf_op jit(solution)/shard_map/all_to_all | solution.py:69

commit v3 on v1

v3 whole, which is shorter than its diff:
```python
import functools

import jax
import jax.numpy as jnp
from jax import lax
from jax.experimental import pallas as pl
from jax.experimental.pallas import tpu as pltpu
from jax.sharding import PartitionSpec as P

RING = 32
LANES = 128
BF16, F32 = jnp.bfloat16, jnp.float32
VMEM = pltpu.CompilerParams(vmem_limit_bytes=32 * 1024 * 1024)


def dot(left, right, over_left, over_right):
    return lax.dot_general(
        left, right, (((over_left,), (over_right,)), ((), ())), preferred_element_type=F32
    )


def two_terms(x):
    high = x.astype(BF16)
    return jnp.concatenate((high, (x - high.astype(F32)).astype(BF16)), axis=1)


def fine(block, weights):
    both = dot(block, two_terms(weights), 1, 0)
    return both[:, :LANES] + both[:, LANES:]


def shifted(block, distances):
    dp, tower = lax.axis_size("dp"), lax.axis_size("tower")
    route = [
        (i * tower + t, ((i + distances[t % 2]) % dp) * tower + t)
        for i in range(dp)
        for t in range(tower)
    ]
    return lax.ppermute(block, ("dp", "tower"), route)


def score_kernel(i0, t0, t1, t2, i1, i2, out):
    pairs = ((t0, i0), (t1, i0), (t2, i0), (i1, t0), (i2, t0))
    for j, (other, own) in enumerate(pairs):
        out[j * LANES : (j + 1) * LANES] = dot(other[...], own[...], 0, 0).astype(BF16)
    squares = [
        jnp.sum(jnp.square(b[...].astype(F32)), axis=0, keepdims=True)
        for b in (i0, t0, t1, t2, i1, i2)
    ]
    squares = jnp.concatenate(squares + [jnp.zeros((2, LANES), F32)], axis=0)
    high = squares.astype(BF16).astype(F32)
    low = (squares - high).astype(BF16).astype(F32)
    out[5 * LANES :] = jnp.concatenate((high, low), axis=0).astype(BF16)


def weight_kernel(numbers, mine, peer, own, t1, t2, i1, i2, send, keep):
    scale, bias, core0 = numbers[0], numbers[1], numbers[2]
    width = own.shape[0] // 2
    rows = 5 * LANES

    def total(start, size):
        a = mine[start : start + size].astype(F32)
        return a + peer[start : start + size].astype(F32)

    squares = total(rows, 16)
    inv = lax.rsqrt(squares[:8] + squares[8:] + 1e-06)
    down = inv.T

    def weigh(j, across, along):
        c = scale * (total(j * LANES, LANES) * across * along)
        s = c + bias
        e = jnp.exp(-jnp.abs(s))
        return c, s, jnp.log1p(e), jnp.where(s >= 0, 1.0, e) / (1.0 + e)

    ni, nt = inv[0:1], inv[1:2]
    eye = (
        lax.broadcasted_iota(jnp.int32, (LANES, LANES), 0)
        == lax.broadcasted_iota(jnp.int32, (LANES, LANES), 1)
    ).astype(F32)
    c, s, tail, g = weigh(0, ni, down[:, 1:2])
    loss = core0 * jnp.sum(jnp.maximum((1.0 - 2.0 * eye) * s, 0.0) + tail, axis=0, keepdims=True)
    g = g - eye
    gc = g * c
    along_i0 = jnp.sum(gc, axis=0, keepdims=True)
    along_t0 = jnp.sum(gc.T, axis=0, keepdims=True)
    du0 = fine(own[width:], g * down[:, 1:2])
    dv0 = fine(own[:width], (g * ni).T)

    along_i, along_t = jnp.zeros_like(ni), jnp.zeros_like(ni)
    du = dv = None
    for j, block in ((1, t1), (2, t2)):
        col = down[:, j + 1 : j + 2]
        c, s, tail, g = weigh(j, ni, col)
        loss += jnp.sum(jnp.maximum(s, 0.0) + tail, axis=0, keepdims=True)
        along_i += jnp.sum(g * c, axis=0, keepdims=True)
        term = fine(block[...], g * col)
        du = term if du is None else du + term
    for j, block in ((3, i1), (4, i2)):
        col = down[:, j + 1 : j + 2]
        c, s, tail, g = weigh(j, nt, col)
        along_t += jnp.sum(g * c, axis=0, keepdims=True)
        term = fine(block[...], g * col)
        dv = term if dv is None else dv + term
    zero = jnp.zeros_like(ni)
    send[:width] = du[width:]
    send[width : 2 * width] = dv[width:]
    send[2 * width :] = jnp.concatenate((along_i, along_t, loss) + (zero,) * 5, axis=0)
    keep[:width] = du[:width] + du0
    keep[width : 2 * width] = dv[:width] + dv0
    keep[2 * width :] = jnp.concatenate(
        (along_i + along_i0, along_t + along_t0, loss, ni, nt) + (zero,) * 3, axis=0
    )


def gradient_kernel(planes, numbers, keep, got, z, xi, xt, out, loss):
    scale = numbers[0]
    width = z.shape[0] // 2
    lines, more = keep[2 * width :], got[2 * width :]
    loss[...] = jnp.broadcast_to(lines[2:3] + more[2:3], loss.shape)
    grads = []
    for side in range(2):
        part = slice(side * width, (side + 1) * width)
        d = scale * (keep[part] + got[part])
        along = lines[side : side + 1] + more[side : side + 1]
        n = lines[3 + side : 4 + side]
        grads.append(two_terms((d - z[part] * (n * along)) * n))
    block = xi.shape[0] // planes
    whole = width // LANES * LANES
    rest = width - whole
    depth = grads[0].shape[1]
    fold = -(-block // 32) * 16
    folded = []
    for place in range(4):
        pieces = []
        if place:
            pieces.append(jnp.zeros((place * rest, depth), BF16))
        pieces.append(grads[place % 2][whole:])
        if place < 3:
            pieces.append(jnp.zeros(((3 - place) * rest, depth), BF16))
        folded.append(jnp.concatenate(pieces, axis=0))
    for p in range(planes):
        last = None
        for side, x in enumerate((xi, xt)):
            feats = x[p * block : (p + 1) * block]
            feats = jnp.concatenate((feats, feats), axis=1)
            main = dot(feats, grads[side][:whole], 1, 1).astype(BF16)
            for j in range(whole // LANES):
                at = (side * (whole // LANES) + j) * block
                out[p, at : at + block] = main[:, j * LANES : (j + 1) * LANES]
            for half in range(2):
                rows = feats[:fold] if half == 0 else feats[block - fold :]
                term = dot(rows, folded[2 * half + side], 1, 1)
                last = term if last is None else last + term
        out[p, 2 * whole // LANES * block :] = last.astype(BF16)


def unfolded(x, block, width):
    count = width // LANES
    rest = width - count * LANES
    last = x[2 * count * block :]
    fold = last.shape[0]
    sides = []
    for side in range(2):
        pieces = [x[(side * count + j) * block : (side * count + j + 1) * block] for j in range(count)]
        top = last[:, side * rest : (side + 1) * rest]
        low = last[2 * fold - block :, (2 + side) * rest : (3 + side) * rest]
        pieces.append(jnp.concatenate((top, low), axis=0))
        sides.append(jnp.concatenate(pieces, axis=1))
    return sides


def summed_over_ring(x):
    dp = lax.axis_size("dp")
    groups = [[g * RING + z for z in range(RING)] for g in range(dp // RING)]
    top = jnp.max(jnp.abs(x))
    power = jnp.floor(jnp.log2(jnp.where(top > 0, top, 1.0))) - 13.0
    power = jnp.maximum(power, -120.0)
    last = lax.broadcasted_iota(jnp.int32, x.shape, 1) == x.shape[1] - 1
    last &= lax.broadcasted_iota(jnp.int32, x.shape, 2) == LANES - 1
    sent = jnp.where(last, power, x * jnp.exp2(-power)).astype(jnp.float16)
    got = lax.all_to_all(sent, "dp", 0, 0, axis_index_groups=groups, tiled=True).astype(F32)
    return jnp.sum(got * jnp.exp2(got[:, -1:, -1:]), axis=0)


def shards(image_feats, text_feats, image_proj, text_proj, logit_scale, logit_bias):
    rows, depth = image_feats.shape
    width = image_proj.shape[1]
    dp, tower = lax.axis_size("dp"), lax.axis_size("tower")
    planes = dp // RING
    to_core = [(t, t ^ 1) for t in range(tower)]
    to_chip = [(t, t ^ 2) for t in range(tower)]
    core0 = (lax.axis_index("tower") % 2 == 0).astype(F32)
    numbers = jnp.concatenate((logit_scale, logit_bias, core0[None]))
    scalars = pl.BlockSpec(memory_space=pltpu.SMEM)
    array = pl.BlockSpec(memory_space=pltpu.VMEM)

    zi = jnp.dot(image_feats, image_proj, preferred_element_type=F32)
    zt = jnp.dot(text_feats, text_proj, preferred_element_type=F32)
    z = jnp.concatenate((zi.T, zt.T), axis=0)
    own = z.astype(BF16)
    other = lax.ppermute(own, "tower", to_core)
    i0 = jnp.concatenate((own[:width], other[:width]), axis=0)
    t0 = jnp.concatenate((own[width:], other[width:]), axis=0)
    t1 = shifted(t0, (1, 2))
    i1 = shifted(i0, (-1, -2))
    t2 = shifted(t1, (2, 2))
    i2 = shifted(i1, (-2, -2))
    scores = pl.pallas_call(
        score_kernel,
        out_shape=jax.ShapeDtypeStruct((5 * rows + 16, rows), BF16),
        in_specs=[array] * 6,
        out_specs=array,
        compiler_params=VMEM,
        name="scores",
    )(i0, t0, t1, t2, i1, i2)
    peer = lax.ppermute(scores, "tower", to_chip)
    sums = jax.ShapeDtypeStruct((2 * width + 8, rows), F32)
    send, keep = pl.pallas_call(
        weight_kernel,
        out_shape=(sums, sums),
        in_specs=[scalars] + [array] * 7,
        out_specs=(array, array),
        compiler_params=VMEM,
        name="weights",
    )(numbers, scores, peer, own, t1, t2, i1, i2)
    got = lax.ppermute(send, "tower", to_core)
    block = depth // planes
    payload = 2 * (width // LANES) * block + -(-block // 32) * 16
    grads, loss = pl.pallas_call(
        functools.partial(gradient_kernel, planes),
        out_shape=(
            jax.ShapeDtypeStruct((planes, payload, LANES), BF16),
            jax.ShapeDtypeStruct((8, rows), F32),
        ),
        in_specs=[scalars] + [array] * 5,
        out_specs=(array, array),
        compiler_params=VMEM,
        name="gradients",
    )(numbers, keep, got, z, image_feats.T, text_feats.T)

    groups = [[g * RING + z for g in range(planes)] for z in range(RING)]
    grads = lax.all_to_all(grads, "dp", 0, 0, axis_index_groups=groups, tiled=True)
    gi, gt = unfolded(jnp.sum(grads.astype(F32), axis=0), block, width)
    share = depth * width // dp
    flat = jnp.concatenate((gi.reshape(RING, share), gt.reshape(RING, share)), axis=1)
    filled = -(-2 * share // LANES)
    flat = jnp.pad(flat, ((0, 0), (0, filled * LANES - 2 * share)))
    flat = summed_over_ring(flat.reshape(RING, filled, LANES)).reshape(1, -1)
    return (loss[0], flat[:, :share], flat[:, share : 2 * share])


def solution(mesh):
    in_specs = (P("dp", None), P("dp", None), P(None, "tower"), P(None, "tower"), P(), P())
    out_specs = (P("dp"), P("tower", "dp"), P("tower", "dp"))
    return jax.shard_map(shards, mesh=mesh, in_specs=in_specs, out_specs=out_specs, check_vma=False)
```

time: 147 us -> 147 us (level)
  blocking collectives: 71.3 us -> 0 us
  waiting for transfers between devices: 25.3 us -> 70.6 us
  starting transfers between devices: 33 us -> 58.5 us
  Pallas kernels: 0 us -> 5 us
  matrix products: 7.39 us -> 2.8 us
  local copies, waits for them, and re-layouts: 4.94 us -> 3.25 us
    all_to_all x2 -> x0, blocking collectives: 71.3 us -> none  [the longest x1 42.7 us: shards(): lax.all_to_all(flat, 'dp', 0, 0, axis_index_groups=groups, tiled=True)]
    all_to_all x0 -> x2, waiting for transfers between devices: none -> 53.9 us  [the longest x1 35.6 us: summed_over_ring(): lax.all_to_all(sent, 'dp', 0, 0, axis_index_groups=groups, tiled=True)]
    all_to_all x0 -> x2, starting transfers between devices: none -> 21.7 us  [the longest x1 11.8 us: summed_over_ring(): lax.all_to_all(sent, 'dp', 0, 0, axis_index_groups=groups, tiled=True)]
    ppermute x4, waiting for transfers between devices: 17.8 us -> 9.91 us  [shifted(): return lax.ppermute(block, ('dp', 'tower'), route)]
    pallas_call x0 -> x3, Pallas kernels: none -> 5 us  [the longest x1 3.01 us: shards(): pl.pallas_call(functools.partial(gradient_kernel, planes), out_shape=(jax...]
    dot_general x13 -> x2, matrix products: 7.39 us -> 2.8 us  [the longest x1 1.5 us: shards(): zt = jnp.dot(text_feats, text_proj, preferred_element_type=F32)]
    ppermute x4, starting transfers between devices: 26.1 us -> 30 us  [shifted(): return lax.ppermute(block, ('dp', 'tower'), route)]
  transfers between devices with their start and end apart: 7 -> 9, of which waited for: 6 -> 8; matrix products, arithmetic and copies ran while one was open for 1% -> 1% of each run, Pallas kernels for 0% -> 0%
where the time goes in v3:
time: 147 us; the launch traced here: 146 us
  waiting for transfers between devices  70.6 us (48%)
  starting transfers between devices  58.5 us (40%)
  Pallas kernels  5 us (3%)
  between operations  3.56 us (2%)
  local copies, waits for them, and re-layouts  3.25 us (2%)
  matrix products  2.8 us (2%)
  other arithmetic  2.64 us (2%)
    all_to_all x1, waiting for transfers between devices, summed_over_ring(): lax.all_to_all(sent, 'dp', 0, 0, axis_index_groups=groups, tiled=True)  35.6 us
    ppermute x4, starting transfers between devices, shifted(): return lax.ppermute(block, ('dp', 'tower'), route)  30 us
    all_to_all x1, waiting for transfers between devices, shards(): lax.all_to_all(grads, 'dp', 0, 0, axis_index_groups=groups, tiled=True)  18.3 us
    all_to_all x1, starting transfers between devices, summed_over_ring(): lax.all_to_all(sent, 'dp', 0, 0, axis_index_groups=groups, tiled=True)  11.8 us
    ppermute x4, waiting for transfers between devices, shifted(): return lax.ppermute(block, ('dp', 'tower'), route)  9.91 us
    all_to_all x1, starting transfers between devices, shards(): lax.all_to_all(grads, 'dp', 0, 0, axis_index_groups=groups, tiled=True)  9.91 us
    ppermute x1, waiting for transfers between devices, shards(): peer = lax.ppermute(scores, 'tower', to_chip)  4.39 us
    pallas_call x1, Pallas kernels, shards(): pl.pallas_call(functools.partial(gradient_kernel, planes), out_shape=(jax...  3.01 us
  transfers between devices with their start and end apart: 9, of which 8 were waited for; matrix products, arithmetic and copies ran while one was open for 1% of the time, Pallas kernels for 0%

profile of v3, /device:TPU:6, one launch (start us, length us, event | category | flops | bytes accessed | tf_op | source)
XLA Modules:
  0.0 146.3 jit_solution(2839644565790932979)
XLA Ops:
  0.6 0.0 copy-start
  0.6 1.1 copy-done
  1.7 1.3 fusion.10
  3.0 1.5 %fusion.11 = f32[288,128]{1,0:T(8,128)S(1)} fusion(bf16[1152,288]{0,1:T(8,128)(2,1)} %param.9, bf16[128,1152]{1,0:T(8,128)(2,1)} %param.7), kind=kOutput, calls=%fused_computation.28 | convolution fusion | flops 84934656 | bytes 1105920 | tf_op jit(solution)/shard_map/dot_general | solution.py:198
  4.6 1.9 %collective-permute-start = (bf16[576,128]{1,0:T(8,128)(2,1)S(1)}, bf16[576,128]{1,0:T(8,128)(2,1)S(1)}, u32[]{:S(2)}, u32[]{:S(2)}) collective-permute-start(bf16[576,128]{1,0:T(8,128)(2,1)S(1)} %fusion.3.own), channel_id=1, source_target_pairs={{0,1},{1,0},{2,3},{3,2},{4,5},{5,4},{6,7},{7,6},{8,9},{9,8},{10,11... | collective-permute-start | bytes 442376 | tf_op jit(solution)/shard_map/ppermute | solution.py:201
  6.5 1.3 collective-permute-done
  7.8 0.0 copy-start.1
  7.9 4.0 %collective-permute-start.1 = (bf16[576,128]{1,0:T(8,128)(2,1)S(1)}, bf16[576,128]{1,0:T(8,128)(2,1)S(1)}, u32[]{:S(2)}, u32[]{:S(2)}) collective-permute-start(bf16[576,128]{1,0:T(8,128)(2,1)S(1)} %pad_maximum_fusion.2.t0), channel_id=1, source_target_pairs={{0,4},{1,9},{2,6},{3,11},{4,8},{5,13},{6,10},{7,15},{8,12},{9,17},... | collective-permute-start | bytes 442376 | tf_op jit(solution)/shard_map/ppermute | solution.py:39
  11.9 0.0 copy-start.2
  11.9 17.2 %collective-permute-start.3 = (bf16[576,128]{1,0:T(8,128)(2,1)S(1)}, bf16[576,128]{1,0:T(8,128)(2,1)S(1)}, u32[]{:S(2)}, u32[]{:S(2)}) collective-permute-start(bf16[576,128]{1,0:T(8,128)(2,1)S(1)} %pad_maximum_fusion.1.i0), channel_id=1, source_target_pairs={{0,1020},{1,1017},{2,1022},{3,1019},{4,0},{5,1021},{6,2},{7,1023},... | collective-permute-start | bytes 442376 | tf_op jit(solution)/shard_map/ppermute | solution.py:39
  29.1 3.6 %collective-permute-done.1.t1 = bf16[576,128]{1,0:T(8,128)(2,1)S(1)} collective-permute-done((bf16[576,128]{1,0:T(8,128)(2,1)S(1)}, bf16[576,128]{1,0:T(8,128)(2,1)S(1)}, u32[]{:S(2)}, u32[]{:S(2)}) %collective-permute-start.1) | collective-permute-done | bytes 147488 | tf_op jit(solution)/shard_map/ppermute | solution.py:39
  32.7 1.9 %collective-permute-start.2 = (bf16[576,128]{1,0:T(8,128)(2,1)S(1)}, bf16[576,128]{1,0:T(8,128)(2,1)S(1)}, u32[]{:S(2)}, u32[]{:S(2)}) collective-permute-start(bf16[576,128]{1,0:T(8,128)(2,1)S(1)} %collective-permute-done.1.t1), channel_id=1, source_target_pairs={{0,8},{1,9},{2,10},{3,11},{4,12},{5,13},{6,14},{7,15},{8,16},{9,17... | collective-permute-start | bytes 442376 | tf_op jit(solution)/shard_map/ppermute | solution.py:39
  34.6 0.0 collective-permute-done.3.i1
  34.6 6.9 %collective-permute-start.4 = (bf16[576,128]{1,0:T(8,128)(2,1)S(1)}, bf16[576,128]{1,0:T(8,128)(2,1)S(1)}, u32[]{:S(2)}, u32[]{:S(2)}) collective-permute-start(bf16[576,128]{1,0:T(8,128)(2,1)S(1)} %collective-permute-done.3.i1), channel_id=1, source_target_pairs={{0,1016},{1,1017},{2,1018},{3,1019},{4,1020},{5,1021},{6,1022},{7,... | collective-permute-start | bytes 442376 | tf_op jit(solution)/shard_map/ppermute | solution.py:39
  41.5 2.3 %collective-permute-done.2.t2 = bf16[576,128]{1,0:T(8,128)(2,1)S(1)} collective-permute-done((bf16[576,128]{1,0:T(8,128)(2,1)S(1)}, bf16[576,128]{1,0:T(8,128)(2,1)S(1)}, u32[]{:S(2)}, u32[]{:S(2)}) %collective-permute-start.2) | collective-permute-done | bytes 147488 | tf_op jit(solution)/shard_map/ppermute | solution.py:39
  43.8 4.0 %collective-permute-done.4.i2 = bf16[576,128]{1,0:T(8,128)(2,1)S(1)} collective-permute-done((bf16[576,128]{1,0:T(8,128)(2,1)S(1)}, bf16[576,128]{1,0:T(8,128)(2,1)S(1)}, u32[]{:S(2)}, u32[]{:S(2)}) %collective-permute-start.4) | collective-permute-done | bytes 147488 | tf_op jit(solution)/shard_map/ppermute | solution.py:39
  47.8 0.5 scores.1.mine
  48.4 3.0 %collective-permute-start.5 = (bf16[656,128]{1,0:T(8,128)(2,1)S(1)}, bf16[656,128]{1,0:T(8,128)(2,1)S(1)}, u32[]{:S(2)}, u32[]{:S(2)}) collective-permute-start(bf16[656,128]{1,0:T(8,128)(2,1)S(1)} %scores.1.mine), channel_id=1, source_target_pairs={{0,2},{1,3},{2,0},{3,1},{4,6},{5,7},{6,4},{7,5},{8,10},{9,11},{10,... | collective-permute-start | bytes 503816 | tf_op jit(solution)/shard_map/ppermute | solution.py:216
  52.7 0.1 pad_maximum_fusion.3.numbers
  52.8 4.4 %collective-permute-done.5.peer = bf16[656,128]{1,0:T(8,128)(2,1)S(1)} collective-permute-done((bf16[656,128]{1,0:T(8,128)(2,1)S(1)}, bf16[656,128]{1,0:T(8,128)(2,1)S(1)}, u32[]{:S(2)}, u32[]{:S(2)}) %collective-permute-start.5) | collective-permute-done | bytes 167968 | tf_op jit(solution)/shard_map/ppermute | solution.py:216
  57.1 1.4 weights.1
  58.6 1.9 %collective-permute-start.6 = (f32[584,128]{1,0:T(8,128)S(1)}, f32[584,128]{1,0:T(8,128)S(1)}, u32[]{:S(2)}, u32[]{:S(2)}) collective-permute-start(f32[584,128]{1,0:T(8,128)S(1)} %get-tuple-element.8), channel_id=1, source_target_pairs={{0,1},{1,0},{2,3},{3,2},{4,5},{5,4},{6,7},{7,6},{8,9},{9,8},{10,11... | collective-permute-start | bytes 897032 | tf_op jit(solution)/shard_map/ppermute | solution.py:226
  60.5 0.0 copy-done.1
  60.5 0.2 copy.30
  60.7 0.0 copy-done.2
  60.8 0.2 copy.31
  61.0 1.1 collective-permute-done.6.got
  62.1 3.0 %gradients.1 = (bf16[8,656,128]{2,1,0:T(8,128)(2,1)}, f32[8,128]{1,0:T(8,128)S(1)}) custom-call(f32[3]{0:T(128)S(1)} %pad_maximum_fusion.3.numbers, f32[584,128]{1,0:T(8,128)S(1)} %get-tuple-element.7.keep, f32[584,128]{1,0:T(8,128)S(1)} %collective-permute-done.6.got, f32[576,128]{1,0:T(8,128)S(1)} %pad_maximum_fusion.z, bf16[1152,128]{1,0:T(8,128)(2,1)S(1)} %bitcast.14, ...), custom_call_target="tpu_custom_call" | custom-call | tf_op jit(solution)/shard_map/gradients/pallas_call | solution.py:229
  65.1 9.9 %all-to-all-start = ((bf16[8,656,128]{2,1,0:T(8,128)(2,1)}), bf16[8,656,128]{2,1,0:T(8,128)(2,1)S(1)}, u32[]{:S(2)}, u32[]{:S(2)}) async-start(bf16[8,656,128]{2,1,0:T(8,128)(2,1)} %get-tuple-element.10), calls=%async_computation | async-start | bytes 2686976 | tf_op jit(solution)/shard_map/all_to_all | solution.py:242
  75.0 18.3 %all-to-all-done = bf16[8,656,128]{2,1,0:T(8,128)(2,1)S(1)} async-done(((bf16[8,656,128]{2,1,0:T(8,128)(2,1)}), bf16[8,656,128]{2,1,0:T(8,128)(2,1)S(1)}, u32[]{:S(2)}, u32[]{:S(2)}) %all-to-all-start) | async-done | bytes 1343520 | tf_op jit(solution)/shard_map/all_to_all | solution.py:242
  93.3 0.2 convert_reduce_fusion
  93.5 0.1 fusion.5
  93.6 0.1 fusion.6
  93.7 0.1 reshape.18
  93.9 0.1 reshape.19
  94.0 0.7 abs_reduce_fusion
  96.1 0.1 fusion
  96.2 0.1 mul.21
  96.3 0.8 select_convert_fusion
  97.1 11.8 %all-to-all-start.1 = ((f16[32,21,128]{2,1,0:T(8,128)(2,1)}), f16[32,21,128]{2,1,0:T(8,128)(2,1)S(1)}, u32[]{:S(2)}, u32[]{:S(2)}) async-start(f16[32,21,128]{2,1,0:T(8,128)(2,1)} %select_convert_fusion), calls=%async_computation.1 | async-start | bytes 393216 | tf_op jit(solution)/shard_map/all_to_all | solution.py:181
  108.8 0.5 slice_bitcast_fusion
  109.3 35.6 %all-to-all-done.1 = f16[32,21,128]{2,1,0:T(8,128)(2,1)S(1)} async-done(((f16[32,21,128]{2,1,0:T(8,128)(2,1)}), f16[32,21,128]{2,1,0:T(8,128)(2,1)S(1)}, u32[]{:S(2)}, u32[]{:S(2)}) %all-to-all-start.1) | async-done | bytes 172064 | tf_op jit(solution)/shard_map/all_to_all | solution.py:181
  145.0 0.5 fusion.2
  145.5 0.1 multiply_reduce_fusion
  145.6 0.7 fusion.9
  (12 shorter events, 0.2 us)
Async XLA Ops:
  0.6 1.1 copy-start
  4.6 3.3 %collective-permute-start = (bf16[576,128]{1,0:T(8,128)(2,1)S(1)}, bf16[576,128]{1,0:T(8,128)(2,1)S(1)}, u32[]{:S(2)}, u32[]{:S(2)}) collective-permute-start(bf16[576,128]{1,0:T(8,128)(2,1)S(1)} %fusion.3.own), channel_id=1, source_target_pairs={{0,1},{1,0},{2,3},{3,2},{4,5},{5,4},{6,7},{7,6},{8,9},{9,8},{10,11... | collective-permute-start | bytes 442376 | tf_op jit(solution)/shard_map/ppermute | solution.py:201
  7.8 52.7 %copy-start.1 = (bf16[128,1152]{1,0:T(8,128)(2,1)S(1)}, bf16[128,1152]{1,0:T(8,128)(2,1)}, u32[]{:S(2)}) copy-start(bf16[128,1152]{1,0:T(8,128)(2,1)} %param.6) | copy-start | bytes 884740
  7.9 24.8 %collective-permute-start.1 = (bf16[576,128]{1,0:T(8,128)(2,1)S(1)}, bf16[576,128]{1,0:T(8,128)(2,1)S(1)}, u32[]{:S(2)}, u32[]{:S(2)}) collective-permute-start(bf16[576,128]{1,0:T(8,128)(2,1)S(1)} %pad_maximum_fusion.2.t0), channel_id=1, source_target_pairs={{0,4},{1,9},{2,6},{3,11},{4,8},{5,13},{6,10},{7,15},{8,12},{9,17},... | collective-permute-start | bytes 442376 | tf_op jit(solution)/shard_map/ppermute | solution.py:39
  11.9 48.9 %copy-start.2 = (bf16[128,1152]{1,0:T(8,128)(2,1)S(1)}, bf16[128,1152]{1,0:T(8,128)(2,1)}, u32[]{:S(2)}) copy-start(bf16[128,1152]{1,0:T(8,128)(2,1)} %param.7) | copy-start | bytes 884740
  11.9 22.7 %collective-permute-start.3 = (bf16[576,128]{1,0:T(8,128)(2,1)S(1)}, bf16[576,128]{1,0:T(8,128)(2,1)S(1)}, u32[]{:S(2)}, u32[]{:S(2)}) collective-permute-start(bf16[576,128]{1,0:T(8,128)(2,1)S(1)} %pad_maximum_fusion.1.i0), channel_id=1, source_target_pairs={{0,1020},{1,1017},{2,1022},{3,1019},{4,0},{5,1021},{6,2},{7,1023},... | collective-permute-start | bytes 442376 | tf_op jit(solution)/shard_map/ppermute | solution.py:39
  32.7 11.1 %collective-permute-start.2 = (bf16[576,128]{1,0:T(8,128)(2,1)S(1)}, bf16[576,128]{1,0:T(8,128)(2,1)S(1)}, u32[]{:S(2)}, u32[]{:S(2)}) collective-permute-start(bf16[576,128]{1,0:T(8,128)(2,1)S(1)} %collective-permute-done.1.t1), channel_id=1, source_target_pairs={{0,8},{1,9},{2,10},{3,11},{4,12},{5,13},{6,14},{7,15},{8,16},{9,17... | collective-permute-start | bytes 442376 | tf_op jit(solution)/shard_map/ppermute | solution.py:39
  34.6 13.2 %collective-permute-start.4 = (bf16[576,128]{1,0:T(8,128)(2,1)S(1)}, bf16[576,128]{1,0:T(8,128)(2,1)S(1)}, u32[]{:S(2)}, u32[]{:S(2)}) collective-permute-start(bf16[576,128]{1,0:T(8,128)(2,1)S(1)} %collective-permute-done.3.i1), channel_id=1, source_target_pairs={{0,1016},{1,1017},{2,1018},{3,1019},{4,1020},{5,1021},{6,1022},{7,... | collective-permute-start | bytes 442376 | tf_op jit(solution)/shard_map/ppermute | solution.py:39
  48.4 8.8 %collective-permute-start.5 = (bf16[656,128]{1,0:T(8,128)(2,1)S(1)}, bf16[656,128]{1,0:T(8,128)(2,1)S(1)}, u32[]{:S(2)}, u32[]{:S(2)}) collective-permute-start(bf16[656,128]{1,0:T(8,128)(2,1)S(1)} %scores.1.mine), channel_id=1, source_target_pairs={{0,2},{1,3},{2,0},{3,1},{4,6},{5,7},{6,4},{7,5},{8,10},{9,11},{10,... | collective-permute-start | bytes 503816 | tf_op jit(solution)/shard_map/ppermute | solution.py:216
  58.6 3.5 %collective-permute-start.6 = (f32[584,128]{1,0:T(8,128)S(1)}, f32[584,128]{1,0:T(8,128)S(1)}, u32[]{:S(2)}, u32[]{:S(2)}) collective-permute-start(f32[584,128]{1,0:T(8,128)S(1)} %get-tuple-element.8), channel_id=1, source_target_pairs={{0,1},{1,0},{2,3},{3,2},{4,5},{5,4},{6,7},{7,6},{8,9},{9,8},{10,11... | collective-permute-start | bytes 897032 | tf_op jit(solution)/shard_map/ppermute | solution.py:226
  65.1 28.2 %all-to-all-start = ((bf16[8,656,128]{2,1,0:T(8,128)(2,1)}), bf16[8,656,128]{2,1,0:T(8,128)(2,1)S(1)}, u32[]{:S(2)}, u32[]{:S(2)}) async-start(bf16[8,656,128]{2,1,0:T(8,128)(2,1)} %get-tuple-element.10), calls=%async_computation | async-start | bytes 2686976 | tf_op jit(solution)/shard_map/all_to_all | solution.py:242
  97.1 47.9 %all-to-all-start.1 = ((f16[32,21,128]{2,1,0:T(8,128)(2,1)}), f16[32,21,128]{2,1,0:T(8,128)(2,1)S(1)}, u32[]{:S(2)}, u32[]{:S(2)}) async-start(f16[32,21,128]{2,1,0:T(8,128)(2,1)} %select_convert_fusion), calls=%async_computation.1 | async-start | bytes 393216 | tf_op jit(solution)/shard_map/all_to_all | solution.py:181

commit v4 on v3

--- a/solution.py
+++ b/solution.py
@@ -112,7 +112,7 @@
     )
 
 
-def gradient_kernel(planes, numbers, keep, got, z, xi, xt, out, loss):
+def gradient_kernel(parts, numbers, keep, got, z, xi, xt, out, loss):
     scale = numbers[0]
     width = z.shape[0] // 2
     lines, more = keep[2 * width :], got[2 * width :]
@@ -124,7 +124,7 @@
         along = lines[side : side + 1] + more[side : side + 1]
         n = lines[3 + side : 4 + side]
         grads.append(two_terms((d - z[part] * (n * along)) * n))
-    block = xi.shape[0] // planes
+    block = xi.shape[0] // parts
     whole = width // LANES * LANES
     rest = width - whole
     depth = grads[0].shape[1]
@@ -138,7 +138,7 @@
         if place < 3:
             pieces.append(jnp.zeros(((3 - place) * rest, depth), BF16))
         folded.append(jnp.concatenate(pieces, axis=0))
-    for p in range(planes):
+    for p in range(parts):
         last = None
         for side, x in enumerate((xi, xt)):
             feats = x[p * block : (p + 1) * block]
@@ -154,32 +154,43 @@
         out[p, 2 * whole // LANES * block :] = last.astype(BF16)
 
 
-def unfolded(x, block, width):
+def ring_kernel(got, out):
+    total = jnp.sum(got[...].astype(F32), axis=0)
+    top = jnp.max(jnp.max(jnp.abs(total), axis=0, keepdims=True), axis=1, keepdims=True)
+    power = jnp.floor(jnp.log2(jnp.where(top > 0, top, 1.0))) - 13.0
+    power = jnp.broadcast_to(jnp.maximum(power, -120.0), (1, LANES))
+    total = total * jnp.exp2(-power)
+    places = out.shape[0]
+    count = total.shape[0] // places
+    for j in range(count):
+        out[:, j] = total[j * places : (j + 1) * places]
+    out[:, count] = jnp.broadcast_to(power, (places, LANES))
+
+
+def row_sets(feats, planes):
+    x = feats.T.reshape(planes, RING // 2, -1, feats.shape[0])
+    nine = x.shape[2]
+    five = nine // 2 + 1
+    halves = [x[:, :, nine - five :] if q else x[:, :, :five] for q in range(2)]
+    x = jnp.stack(halves, axis=1).transpose(0, 1, 3, 2, 4)
+    return x.reshape(-1, feats.shape[0])
+
+
+def shares(total, width, share):
     count = width // LANES
     rest = width - count * LANES
-    last = x[2 * count * block :]
-    fold = last.shape[0]
-    sides = []
+    five = 5
+    fold = total[2 * count * five : 2 * count * five + five // 2 + 1]
+    half = lax.axis_index("dp") % 2
+    out = []
     for side in range(2):
-        pieces = [x[(side * count + j) * block : (side * count + j + 1) * block] for j in range(count)]
-        top = last[:, side * rest : (side + 1) * rest]
-        low = last[2 * fold - block :, (2 + side) * rest : (3 + side) * rest]
+        pieces = [total[(side * count + j) * five : (side * count + j + 1) * five] for j in range(count)]
+        top = fold[:, side * rest : (side + 1) * rest]
+        low = fold[1:, (2 + side) * rest : (3 + side) * rest]
         pieces.append(jnp.concatenate((top, low), axis=0))
-        sides.append(jnp.concatenate(pieces, axis=1))
-    return sides
-
-
-def summed_over_ring(x):
-    dp = lax.axis_size("dp")
-    groups = [[g * RING + z for z in range(RING)] for g in range(dp // RING)]
-    top = jnp.max(jnp.abs(x))
-    power = jnp.floor(jnp.log2(jnp.where(top > 0, top, 1.0))) - 13.0
-    power = jnp.maximum(power, -120.0)
-    last = lax.broadcasted_iota(jnp.int32, x.shape, 1) == x.shape[1] - 1
-    last &= lax.broadcasted_iota(jnp.int32, x.shape, 2) == LANES - 1
-    sent = jnp.where(last, power, x * jnp.exp2(-power)).astype(jnp.float16)
-    got = lax.all_to_all(sent, "dp", 0, 0, axis_index_groups=groups, tiled=True).astype(F32)
-    return jnp.sum(got * jnp.exp2(got[:, -1:, -1:]), axis=0)
+        flat = jnp.concatenate(pieces, axis=1).reshape(1, -1)
+        out.append(jnp.where(half == 0, flat[:, :share], flat[:, flat.shape[1] - share :]))
+    return out
 
 
 def shards(image_feats, text_feats, image_proj, text_proj, logit_scale, logit_bias):
@@ -205,6 +216,8 @@
     i1 = shifted(i0, (-1, -2))
     t2 = shifted(t1, (2, 2))
     i2 = shifted(i1, (-2, -2))
+    xi, xt = row_sets(image_feats, planes), row_sets(text_feats, planes)
+    i1, xi, xt = lax.optimization_barrier((i1, xi, xt))
     scores = pl.pallas_call(
         score_kernel,
         out_shape=jax.ShapeDtypeStruct((5 * rows + 16, rows), BF16),
@@ -224,29 +237,42 @@
         name="weights",
     )(numbers, scores, peer, own, t1, t2, i1, i2)
     got = lax.ppermute(send, "tower", to_core)
-    block = depth // planes
+    parts = 2 * planes
+    block = xi.shape[0] // parts
     payload = 2 * (width // LANES) * block + -(-block // 32) * 16
     grads, loss = pl.pallas_call(
-        functools.partial(gradient_kernel, planes),
+        functools.partial(gradient_kernel, parts),
         out_shape=(
-            jax.ShapeDtypeStruct((planes, payload, LANES), BF16),
+            jax.ShapeDtypeStruct((parts, payload, LANES), BF16),
             jax.ShapeDtypeStruct((8, rows), F32),
         ),
         in_specs=[scalars] + [array] * 5,
         out_specs=(array, array),
         compiler_params=VMEM,
         name="gradients",
-    )(numbers, keep, got, z, image_feats.T, text_feats.T)
-
-    groups = [[g * RING + z for g in range(planes)] for z in range(RING)]
+    )(numbers, keep, got, z, xi, xt)
+
+    places = RING // 2
+    groups = [
+        [g * RING + 2 * m + q for g in range(planes) for q in range(2)] for m in range(places)
+    ]
     grads = lax.all_to_all(grads, "dp", 0, 0, axis_index_groups=groups, tiled=True)
-    gi, gt = unfolded(jnp.sum(grads.astype(F32), axis=0), block, width)
-    share = depth * width // dp
-    flat = jnp.concatenate((gi.reshape(RING, share), gt.reshape(RING, share)), axis=1)
-    filled = -(-2 * share // LANES)
-    flat = jnp.pad(flat, ((0, 0), (0, filled * LANES - 2 * share)))
-    flat = summed_over_ring(flat.reshape(RING, filled, LANES)).reshape(1, -1)
-    return (loss[0], flat[:, :share], flat[:, share : 2 * share])
+    sent = pl.pallas_call(
+        ring_kernel,
+        out_shape=jax.ShapeDtypeStruct((places, payload // places + 1, LANES), F32),
+        in_specs=[array],
+        out_specs=array,
+        compiler_params=VMEM,
+        name="ring",
+    )(grads)
+    groups = [
+        [g * RING + 2 * m + q for m in range(places)] for g in range(planes) for q in range(2)
+    ]
+    sent = sent.astype(jnp.float16)
+    back = lax.all_to_all(sent, "dp", 0, 0, axis_index_groups=groups, tiled=True).astype(F32)
+    total = jnp.sum(back * jnp.exp2(back[:, -1:]), axis=0)
+    image_grad, text_grad = shares(total, width, depth * width // dp)
+    return (loss[0], image_grad, text_grad)
 
 
 def solution(mesh):

time: 147 us -> 134 us (0.912)
  blocking collectives: 0 us -> 30.3 us
  waiting for transfers between devices: 70.6 us -> 49 us
  starting transfers between devices: 58.5 us -> 38.9 us
    all_to_all x0 -> x1, blocking collectives: none -> 30.3 us  [shards(): lax.all_to_all(grads, 'dp', 0, 0, axis_index_groups=groups, tiled=True)]
    all_to_all x2 -> x1, waiting for transfers between devices: 53.9 us -> 24.8 us  [shards(): lax.all_to_all(sent, 'dp', 0, 0, axis_index_groups=groups, tiled=True)]
    all_to_all x2 -> x1, starting transfers between devices: 21.7 us -> 5.83 us  [shards(): lax.all_to_all(sent, 'dp', 0, 0, axis_index_groups=groups, tiled=True)]
    ppermute x4, waiting for transfers between devices: 9.91 us -> 17.8 us  [shifted(): return lax.ppermute(block, ('dp', 'tower'), route)]
    ppermute x4, starting transfers between devices: 30 us -> 26.1 us  [shifted(): return lax.ppermute(block, ('dp', 'tower'), route)]
    pallas_call x1 -> x2, Pallas kernels: 3.01 us -> 3.24 us  [the longest x1 2.76 us: shards(): pl.pallas_call(functools.partial(gradient_kernel, parts), out_shape=(jax....]
  transfers between devices with their start and end apart: 9 -> 8, of which waited for: 8 -> 7; matrix products, arithmetic and copies ran while one was open for 1% -> 1% of each run, Pallas kernels for 0% -> 0%
where the time goes in v4:
time: 134 us; the launch traced here: 133 us
  waiting for transfers between devices  49 us (37%)
  starting transfers between devices  38.9 us (29%)
  blocking collectives  30.3 us (23%)
  Pallas kernels  5.24 us (4%)
  local copies, waits for them, and re-layouts  2.95 us (2%)
  matrix products  2.8 us (2%)
  between operations  2.23 us (2%)
  other arithmetic  1.81 us (1%)
    all_to_all x1, blocking collectives, shards(): lax.all_to_all(grads, 'dp', 0, 0, axis_index_groups=groups, tiled=True)  30.3 us
    ppermute x4, starting transfers between devices, shifted(): return lax.ppermute(block, ('dp', 'tower'), route)  26.1 us
    all_to_all x1, waiting for transfers between devices, shards(): lax.all_to_all(sent, 'dp', 0, 0, axis_index_groups=groups, tiled=True)  24.8 us
    ppermute x4, waiting for transfers between devices, shifted(): return lax.ppermute(block, ('dp', 'tower'), route)  17.8 us
    all_to_all x1, starting transfers between devices, shards(): lax.all_to_all(sent, 'dp', 0, 0, axis_index_groups=groups, tiled=True)  5.83 us
    ppermute x1, waiting for transfers between devices, shards(): peer = lax.ppermute(scores, 'tower', to_chip)  4.35 us
    ppermute x1, starting transfers between devices, shards(): peer = lax.ppermute(scores, 'tower', to_chip)  3.02 us
    pallas_call x1, Pallas kernels, shards(): pl.pallas_call(functools.partial(gradient_kernel, parts), out_shape=(jax....  2.76 us
  transfers between devices with their start and end apart: 8, of which 7 were waited for; matrix products, arithmetic and copies ran while one was open for 1% of the time, Pallas kernels for 0%

profile of v4, /device:TPU:6, one launch (start us, length us, event | category | flops | bytes accessed | tf_op | source)
XLA Modules:
  0.0 133.2 jit_solution(7242653899206678158)
XLA Ops:
  0.6 0.0 copy-start
  0.6 0.0 copy-start.1
  0.7 1.1 copy-done
  1.7 1.3 fusion.7
  3.0 1.5 %fusion.8 = f32[288,128]{1,0:T(8,128)S(1)} fusion(bf16[1152,288]{0,1:T(8,128)(2,1)} %param.9, bf16[128,1152]{1,0:T(8,128)(2,1)} %param.7), kind=kOutput, calls=%fused_computation.25 | convolution fusion | flops 84934656 | bytes 1105920 | tf_op jit(solution)/shard_map/dot_general | solution.py:209
  4.5 0.0 copy-start.2
  4.6 2.1 %collective-permute-start = (bf16[576,128]{1,0:T(8,128)(2,1)S(1)}, bf16[576,128]{1,0:T(8,128)(2,1)S(1)}, u32[]{:S(2)}, u32[]{:S(2)}) collective-permute-start(bf16[576,128]{1,0:T(8,128)(2,1)S(1)} %fusion.1.own), channel_id=1, source_target_pairs={{0,1},{1,0},{2,3},{3,2},{4,5},{5,4},{6,7},{7,6},{8,9},{9,8},{10,11... | collective-permute-start | bytes 442376 | tf_op jit(solution)/shard_map/ppermute | solution.py:212
  6.6 0.0 copy-done.1
  6.6 0.2 copy.15
  6.9 0.1 reshape.26
  7.0 0.1 slice_bitcast_fusion.1
  7.1 0.0 copy-done.2
  7.1 0.2 copy.13
  7.3 0.1 reshape.24
  7.5 0.5 collective-permute-done
  8.0 18.9 %collective-permute-start.3 = (bf16[576,128]{1,0:T(8,128)(2,1)S(1)}, bf16[576,128]{1,0:T(8,128)(2,1)S(1)}, u32[]{:S(2)}, u32[]{:S(2)}) collective-permute-start(bf16[576,128]{1,0:T(8,128)(2,1)S(1)} %pad_maximum_fusion.1.i0), channel_id=1, source_target_pairs={{0,1020},{1,1017},{2,1022},{3,1019},{4,0},{5,1021},{6,2},{7,1023},... | collective-permute-start | bytes 442376 | tf_op jit(solution)/shard_map/ppermute | solution.py:39
  27.0 1.9 %collective-permute-start.1 = (bf16[576,128]{1,0:T(8,128)(2,1)S(1)}, bf16[576,128]{1,0:T(8,128)(2,1)S(1)}, u32[]{:S(2)}, u32[]{:S(2)}) collective-permute-start(bf16[576,128]{1,0:T(8,128)(2,1)S(1)} %pad_maximum_fusion.2.t0), channel_id=1, source_target_pairs={{0,4},{1,9},{2,6},{3,11},{4,8},{5,13},{6,10},{7,15},{8,12},{9,17},... | collective-permute-start | bytes 442376 | tf_op jit(solution)/shard_map/ppermute | solution.py:39
  28.9 0.1 slice_bitcast_fusion.3
  29.0 3.3 %collective-permute-done.3.i1 = bf16[576,128]{1,0:T(8,128)(2,1)S(1)} collective-permute-done((bf16[576,128]{1,0:T(8,128)(2,1)S(1)}, bf16[576,128]{1,0:T(8,128)(2,1)S(1)}, u32[]{:S(2)}, u32[]{:S(2)}) %collective-permute-start.3) | collective-permute-done | bytes 147488 | tf_op jit(solution)/shard_map/ppermute | solution.py:39
  32.4 3.3 %collective-permute-start.4 = (bf16[576,128]{1,0:T(8,128)(2,1)S(1)}, bf16[576,128]{1,0:T(8,128)(2,1)S(1)}, u32[]{:S(2)}, u32[]{:S(2)}) collective-permute-start(bf16[576,128]{1,0:T(8,128)(2,1)S(1)} %collective-permute-done.3.i1), channel_id=1, source_target_pairs={{0,1016},{1,1017},{2,1018},{3,1019},{4,1020},{5,1021},{6,1022},{7,... | collective-permute-start | bytes 442376 | tf_op jit(solution)/shard_map/ppermute | solution.py:39
  35.7 3.3 %collective-permute-done.1.t1 = bf16[576,128]{1,0:T(8,128)(2,1)S(1)} collective-permute-done((bf16[576,128]{1,0:T(8,128)(2,1)S(1)}, bf16[576,128]{1,0:T(8,128)(2,1)S(1)}, u32[]{:S(2)}, u32[]{:S(2)}) %collective-permute-start.1) | collective-permute-done | bytes 147488 | tf_op jit(solution)/shard_map/ppermute | solution.py:39
  39.1 1.9 %collective-permute-start.2 = (bf16[576,128]{1,0:T(8,128)(2,1)S(1)}, bf16[576,128]{1,0:T(8,128)(2,1)S(1)}, u32[]{:S(2)}, u32[]{:S(2)}) collective-permute-start(bf16[576,128]{1,0:T(8,128)(2,1)S(1)} %collective-permute-done.1.t1), channel_id=1, source_target_pairs={{0,8},{1,9},{2,10},{3,11},{4,12},{5,13},{6,14},{7,15},{8,16},{9,17... | collective-permute-start | bytes 442376 | tf_op jit(solution)/shard_map/ppermute | solution.py:39
  41.0 0.1 maximum_bitcast_fusion.1
  41.2 0.1 maximum_bitcast_fusion
  41.4 0.0 collective-permute-done.4.i2
  41.4 11.1 %collective-permute-done.2.t2 = bf16[576,128]{1,0:T(8,128)(2,1)S(1)} collective-permute-done((bf16[576,128]{1,0:T(8,128)(2,1)S(1)}, bf16[576,128]{1,0:T(8,128)(2,1)S(1)}, u32[]{:S(2)}, u32[]{:S(2)}) %collective-permute-start.2) | collective-permute-done | bytes 147488 | tf_op jit(solution)/shard_map/ppermute | solution.py:39
  52.5 0.5 scores.1.mine
  53.0 3.0 %collective-permute-start.5 = (bf16[656,128]{1,0:T(8,128)(2,1)S(1)}, bf16[656,128]{1,0:T(8,128)(2,1)S(1)}, u32[]{:S(2)}, u32[]{:S(2)}) collective-permute-start(bf16[656,128]{1,0:T(8,128)(2,1)S(1)} %scores.1.mine), channel_id=1, source_target_pairs={{0,2},{1,3},{2,0},{3,1},{4,6},{5,7},{6,4},{7,5},{8,10},{9,11},{10,... | collective-permute-start | bytes 503816 | tf_op jit(solution)/shard_map/ppermute | solution.py:229
  57.4 0.1 pad_maximum_fusion.3.numbers
  57.5 4.4 %collective-permute-done.5.peer = bf16[656,128]{1,0:T(8,128)(2,1)S(1)} collective-permute-done((bf16[656,128]{1,0:T(8,128)(2,1)S(1)}, bf16[656,128]{1,0:T(8,128)(2,1)S(1)}, u32[]{:S(2)}, u32[]{:S(2)}) %collective-permute-start.5) | collective-permute-done | bytes 167968 | tf_op jit(solution)/shard_map/ppermute | solution.py:229
  61.8 1.5 %weights.1 = (f32[584,128]{1,0:T(8,128)S(1)}, f32[584,128]{1,0:T(8,128)S(1)}) custom-call(f32[3]{0:T(128)S(1)} %pad_maximum_fusion.3.numbers, bf16[656,128]{1,0:T(8,128)(2,1)S(1)} %scores.1.mine, bf16[656,128]{1,0:T(8,128)(2,1)S(1)} %collective-permute-done.5.peer, bf16[576,128]{1,0:T(8,128)(2,1)S(1)} %fusion.1.own, ...), custom_call_target="tpu_custom_call" | custom-call | tf_op jit(solution)/shard_map/weights/pallas_call | solution.py:231
  63.3 1.9 %collective-permute-start.6 = (f32[584,128]{1,0:T(8,128)S(1)}, f32[584,128]{1,0:T(8,128)S(1)}, u32[]{:S(2)}, u32[]{:S(2)}) collective-permute-start(f32[584,128]{1,0:T(8,128)S(1)} %get-tuple-element.12), channel_id=1, source_target_pairs={{0,1},{1,0},{2,3},{3,2},{4,5},{5,4},{6,7},{7,6},{8,9},{9,8},{10,11... | collective-permute-start | bytes 897032 | tf_op jit(solution)/shard_map/ppermute | solution.py:239
  65.2 1.5 %collective-permute-done.6.got = f32[584,128]{1,0:T(8,128)S(1)} collective-permute-done((f32[584,128]{1,0:T(8,128)S(1)}, f32[584,128]{1,0:T(8,128)S(1)}, u32[]{:S(2)}, u32[]{:S(2)}) %collective-permute-start.6) | collective-permute-done | bytes 299040 | tf_op jit(solution)/shard_map/ppermute | solution.py:239
  66.8 2.8 %gradients.1 = (bf16[16,368,128]{2,1,0:T(8,128)(2,1)S(1)}, f32[8,128]{1,0:T(8,128)S(1)}) custom-call(f32[3]{0:T(128)S(1)} %pad_maximum_fusion.3.numbers, f32[584,128]{1,0:T(8,128)S(1)} %get-tuple-element.11.keep, f32[584,128]{1,0:T(8,128)S(1)} %collective-permute-done.6.got, f32[576,128]{1,0:T(8,128)S(1)} %pad_maximum_fusion.z, ...), custom_call_target="tpu_custom_call" | custom-call | tf_op jit(solution)/shard_map/gradients/pallas_call | solution.py:243
  69.5 30.3 %all_to_all.10.got = bf16[16,368,128]{2,1,0:T(8,128)(2,1)S(1)} all-to-all(bf16[16,368,128]{2,1,0:T(8,128)(2,1)S(1)} %get-tuple-element.16), channel_id=1, replica_groups={{0,4,128,132,256,260,384,388,512,516,640,644,768,772,896,900},{8,12,136..., dimensions={0} | all-to-all | bytes 3014656 | tf_op jit(solution)/shard_map/all_to_all | solution.py:259
  99.8 0.5 ring.1
  100.3 0.7 convert_element_type.11
  100.9 5.8 %all-to-all-start.1 = ((f16[16,24,128]{2,1,0:T(8,128)(2,1)}), f16[16,24,128]{2,1,0:T(8,128)(2,1)S(1)}, u32[]{:S(2)}, u32[]{:S(2)}) async-start(f16[16,24,128]{2,1,0:T(8,128)(2,1)} %convert_element_type.11), calls=%async_computation.1 | async-start | bytes 196608 | tf_op jit(solution)/shard_map/all_to_all | solution.py:272
  106.8 0.5 slice_bitcast_fusion.4
  107.3 24.8 %all-to-all-done.1 = f16[16,24,128]{2,1,0:T(8,128)(2,1)S(1)} async-done(((f16[16,24,128]{2,1,0:T(8,128)(2,1)}), f16[16,24,128]{2,1,0:T(8,128)(2,1)S(1)}, u32[]{:S(2)}, u32[]{:S(2)}) %all-to-all-start.1) | async-done | bytes 98336 | tf_op jit(solution)/shard_map/all_to_all | solution.py:272
  132.2 0.1 fusion.6
  132.3 0.1 fusion.5
  132.4 0.1 reshape.29
  132.5 0.1 reshape.28
  132.5 0.7 broadcast_select_fusion
  (14 shorter events, 0.3 us)
Async XLA Ops:
  0.6 1.1 copy-start
  0.6 6.0 %copy-start.1 = (bf16[128,1152]{1,0:T(8,128)(2,1)S(1)}, bf16[128,1152]{1,0:T(8,128)(2,1)}, u32[]{:S(2)}) copy-start(bf16[128,1152]{1,0:T(8,128)(2,1)} %param.7) | copy-start | bytes 884740
  4.5 2.6 %copy-start.2 = (bf16[128,1152]{1,0:T(8,128)(2,1)S(1)}, bf16[128,1152]{1,0:T(8,128)(2,1)}, u32[]{:S(2)}) copy-start(bf16[128,1152]{1,0:T(8,128)(2,1)} %param.6) | copy-start | bytes 884740
  4.6 3.4 %collective-permute-start = (bf16[576,128]{1,0:T(8,128)(2,1)S(1)}, bf16[576,128]{1,0:T(8,128)(2,1)S(1)}, u32[]{:S(2)}, u32[]{:S(2)}) collective-permute-start(bf16[576,128]{1,0:T(8,128)(2,1)S(1)} %fusion.1.own), channel_id=1, source_target_pairs={{0,1},{1,0},{2,3},{3,2},{4,5},{5,4},{6,7},{7,6},{8,9},{9,8},{10,11... | collective-permute-start | bytes 442376 | tf_op jit(solution)/shard_map/ppermute | solution.py:212
  8.0 24.4 %collective-permute-start.3 = (bf16[576,128]{1,0:T(8,128)(2,1)S(1)}, bf16[576,128]{1,0:T(8,128)(2,1)S(1)}, u32[]{:S(2)}, u32[]{:S(2)}) collective-permute-start(bf16[576,128]{1,0:T(8,128)(2,1)S(1)} %pad_maximum_fusion.1.i0), channel_id=1, source_target_pairs={{0,1020},{1,1017},{2,1022},{3,1019},{4,0},{5,1021},{6,2},{7,1023},... | collective-permute-start | bytes 442376 | tf_op jit(solution)/shard_map/ppermute | solution.py:39
  27.0 12.1 %collective-permute-start.1 = (bf16[576,128]{1,0:T(8,128)(2,1)S(1)}, bf16[576,128]{1,0:T(8,128)(2,1)S(1)}, u32[]{:S(2)}, u32[]{:S(2)}) collective-permute-start(bf16[576,128]{1,0:T(8,128)(2,1)S(1)} %pad_maximum_fusion.2.t0), channel_id=1, source_target_pairs={{0,4},{1,9},{2,6},{3,11},{4,8},{5,13},{6,10},{7,15},{8,12},{9,17},... | collective-permute-start | bytes 442376 | tf_op jit(solution)/shard_map/ppermute | solution.py:39
  32.4 9.0 %collective-permute-start.4 = (bf16[576,128]{1,0:T(8,128)(2,1)S(1)}, bf16[576,128]{1,0:T(8,128)(2,1)S(1)}, u32[]{:S(2)}, u32[]{:S(2)}) collective-permute-start(bf16[576,128]{1,0:T(8,128)(2,1)S(1)} %collective-permute-done.3.i1), channel_id=1, source_target_pairs={{0,1016},{1,1017},{2,1018},{3,1019},{4,1020},{5,1021},{6,1022},{7,... | collective-permute-start | bytes 442376 | tf_op jit(solution)/shard_map/ppermute | solution.py:39
  39.1 13.4 %collective-permute-start.2 = (bf16[576,128]{1,0:T(8,128)(2,1)S(1)}, bf16[576,128]{1,0:T(8,128)(2,1)S(1)}, u32[]{:S(2)}, u32[]{:S(2)}) collective-permute-start(bf16[576,128]{1,0:T(8,128)(2,1)S(1)} %collective-permute-done.1.t1), channel_id=1, source_target_pairs={{0,8},{1,9},{2,10},{3,11},{4,12},{5,13},{6,14},{7,15},{8,16},{9,17... | collective-permute-start | bytes 442376 | tf_op jit(solution)/shard_map/ppermute | solution.py:39
  53.0 8.8 %collective-permute-start.5 = (bf16[656,128]{1,0:T(8,128)(2,1)S(1)}, bf16[656,128]{1,0:T(8,128)(2,1)S(1)}, u32[]{:S(2)}, u32[]{:S(2)}) collective-permute-start(bf16[656,128]{1,0:T(8,128)(2,1)S(1)} %scores.1.mine), channel_id=1, source_target_pairs={{0,2},{1,3},{2,0},{3,1},{4,6},{5,7},{6,4},{7,5},{8,10},{9,11},{10,... | collective-permute-start | bytes 503816 | tf_op jit(solution)/shard_map/ppermute | solution.py:229
  63.3 3.5 %collective-permute-start.6 = (f32[584,128]{1,0:T(8,128)S(1)}, f32[584,128]{1,0:T(8,128)S(1)}, u32[]{:S(2)}, u32[]{:S(2)}) collective-permute-start(f32[584,128]{1,0:T(8,128)S(1)} %get-tuple-element.12), channel_id=1, source_target_pairs={{0,1},{1,0},{2,3},{3,2},{4,5},{5,4},{6,7},{7,6},{8,9},{9,8},{10,11... | collective-permute-start | bytes 897032 | tf_op jit(solution)/shard_map/ppermute | solution.py:239
  100.9 31.2 %all-to-all-start.1 = ((f16[16,24,128]{2,1,0:T(8,128)(2,1)}), f16[16,24,128]{2,1,0:T(8,128)(2,1)S(1)}, u32[]{:S(2)}, u32[]{:S(2)}) async-start(f16[16,24,128]{2,1,0:T(8,128)(2,1)} %convert_element_type.11), calls=%async_computation.1 | async-start | bytes 196608 | tf_op jit(solution)/shard_map/all_to_all | solution.py:272

commit v5 on v4

--- a/solution.py
+++ b/solution.py
@@ -37,6 +37,24 @@
         for t in range(tower)
     ]
     return lax.ppermute(block, ("dp", "tower"), route)
+
+
+def project_kernel(xi, wi, xt, wt, z, own, xi_here, wi_here, xt_here, wt_here, arrived):
+    moves = [
+        pltpu.make_async_copy(there, here, arrived.at[j])
+        for j, (there, here) in enumerate(
+            ((xi, xi_here), (wi, wi_here), (xt, xt_here), (wt, wt_here))
+        )
+    ]
+    for move in moves:
+        move.start()
+    width = wi_here.shape[0]
+    for side, (x, w) in enumerate(((xi_here, wi_here), (xt_here, wt_here))):
+        moves[2 * side].wait()
+        moves[2 * side + 1].wait()
+        part = dot(w[...], x[...], 1, 1)
+        z[side * width : (side + 1) * width] = part
+        own[side * width : (side + 1) * width] = part.astype(BF16)
 
 
 def score_kernel(i0, t0, t1, t2, i1, i2, out):
@@ -127,31 +145,25 @@
     block = xi.shape[0] // parts
     whole = width // LANES * LANES
     rest = width - whole
-    depth = grads[0].shape[1]
     fold = -(-block // 32) * 16
-    folded = []
-    for place in range(4):
-        pieces = []
-        if place:
-            pieces.append(jnp.zeros((place * rest, depth), BF16))
-        pieces.append(grads[place % 2][whole:])
-        if place < 3:
-            pieces.append(jnp.zeros(((3 - place) * rest, depth), BF16))
-        folded.append(jnp.concatenate(pieces, axis=0))
+    tail = None
+    for side, x in enumerate((xi, xt)):
+        feats = jnp.concatenate((x[...], x[...]), axis=1)
+        main = dot(feats, grads[side][:whole], 1, 1).astype(BF16)
+        for j in range(whole // LANES):
+            at = (side * (whole // LANES) + j) * block
+            for p in range(parts):
+                out[p, at : at + block] = main[p * block : (p + 1) * block, j * LANES : (j + 1) * LANES]
+        piece = grads[side][whole:]
+        gap = jnp.zeros_like(piece)
+        pieces = [gap] * (2 * LANES // rest)
+        pieces[side] = pieces[LANES // rest + LANES // rest // 2 + side] = piece
+        term = dot(feats, jnp.concatenate(pieces, axis=0), 1, 1)
+        tail = term if tail is None else tail + term
     for p in range(parts):
-        last = None
-        for side, x in enumerate((xi, xt)):
-            feats = x[p * block : (p + 1) * block]
-            feats = jnp.concatenate((feats, feats), axis=1)
-            main = dot(feats, grads[side][:whole], 1, 1).astype(BF16)
-            for j in range(whole // LANES):
-                at = (side * (whole // LANES) + j) * block
-                out[p, at : at + block] = main[:, j * LANES : (j + 1) * LANES]
-            for half in range(2):
-                rows = feats[:fold] if half == 0 else feats[block - fold :]
-                term = dot(rows, folded[2 * half + side], 1, 1)
-                last = term if last is None else last + term
-        out[p, 2 * whole // LANES * block :] = last.astype(BF16)
+        upper = tail[p * block : p * block + fold, :LANES]
+        lower = tail[(p + 1) * block - fold : (p + 1) * block, LANES:]
+        out[p, 2 * whole // LANES * block :] = (upper + lower).astype(BF16)
 
 
 def ring_kernel(got, out):
@@ -205,17 +217,26 @@
     scalars = pl.BlockSpec(memory_space=pltpu.SMEM)
     array = pl.BlockSpec(memory_space=pltpu.VMEM)
 
-    zi = jnp.dot(image_feats, image_proj, preferred_element_type=F32)
-    zt = jnp.dot(text_feats, text_proj, preferred_element_type=F32)
-    z = jnp.concatenate((zi.T, zt.T), axis=0)
-    own = z.astype(BF16)
+    here = [pltpu.VMEM((rows, depth), BF16), pltpu.VMEM((width, depth), BF16)] * 2
+    z, own = pl.pallas_call(
+        project_kernel,
+        out_shape=(
+            jax.ShapeDtypeStruct((2 * width, rows), F32),
+            jax.ShapeDtypeStruct((2 * width, rows), BF16),
+        ),
+        in_specs=[pl.BlockSpec(memory_space=pl.ANY)] * 4,
+        out_specs=(array, array),
+        scratch_shapes=here + [pltpu.SemaphoreType.DMA((4,))],
+        compiler_params=pltpu.CompilerParams(vmem_limit_bytes=60 * 1024 * 1024),
+        name="project",
+    )(image_feats, image_proj.T, text_feats, text_proj.T)
     other = lax.ppermute(own, "tower", to_core)
     i0 = jnp.concatenate((own[:width], other[:width]), axis=0)
     t0 = jnp.concatenate((own[width:], other[width:]), axis=0)
+    t2 = shifted(t0, (4, 3))
+    i2 = shifted(i0, (-4, -3))
     t1 = shifted(t0, (1, 2))
     i1 = shifted(i0, (-1, -2))
-    t2 = shifted(t1, (2, 2))
-    i2 = shifted(i1, (-2, -2))
     xi, xt = row_sets(image_feats, planes), row_sets(text_feats, planes)
     i1, xi, xt = lax.optimization_barrier((i1, xi, xt))
     scores = pl.pallas_call(

time: 134 us -> 133 us (level)
  starting transfers between devices: 38.9 us -> 45.8 us
  blocking collectives: 30.3 us -> 27.5 us
  matrix products: 2.8 us -> 0 us
  waiting for transfers between devices: 49 us -> 46.2 us
  Pallas kernels: 5.24 us -> 6.84 us
    ppermute x4, starting transfers between devices: 26.1 us -> 30.6 us  [shifted(): return lax.ppermute(block, ('dp', 'tower'), route)]
    pallas_call x0 -> x1, Pallas kernels: none -> 2.94 us  [shards(): pl.pallas_call(project_kernel, out_shape=(jax.ShapeDtypeStruct((2 * width...]
    dot_general x2 -> x0, matrix products: 2.8 us -> none  [the longest x1 1.5 us: shards(): zt = jnp.dot(text_feats, text_proj, preferred_element_type=F32)]
    all_to_all x1, blocking collectives: 30.3 us -> 27.5 us  [shards(): lax.all_to_all(grads, 'dp', 0, 0, axis_index_groups=groups, tiled=True)]
    ppermute x4, waiting for transfers between devices: 17.8 us -> 15.2 us  [shifted(): return lax.ppermute(block, ('dp', 'tower'), route)]
    all_to_all x1, starting transfers between devices: 5.83 us -> 8.21 us  [shards(): lax.all_to_all(sent, 'dp', 0, 0, axis_index_groups=groups, tiled=True)]
where the time goes in v5:
time: 133 us
  waiting for transfers between devices  46.2 us (35%)
  starting transfers between devices  45.8 us (34%)
  blocking collectives  27.5 us (21%)
  Pallas kernels  6.84 us (5%)
  between operations  2.2 us (2%)
  local copies, waits for them, and re-layouts  2.17 us (2%)
  other arithmetic  1.78 us (1%)
    ppermute x4, starting transfers between devices, shifted(): return lax.ppermute(block, ('dp', 'tower'), route)  30.6 us
    all_to_all x1, blocking collectives, shards(): lax.all_to_all(grads, 'dp', 0, 0, axis_index_groups=groups, tiled=True)  27.5 us
    all_to_all x1, waiting for transfers between devices, shards(): lax.all_to_all(sent, 'dp', 0, 0, axis_index_groups=groups, tiled=True)  24.1 us
    ppermute x4, waiting for transfers between devices, shifted(): return lax.ppermute(block, ('dp', 'tower'), route)  15.2 us
    all_to_all x1, starting transfers between devices, shards(): lax.all_to_all(sent, 'dp', 0, 0, axis_index_groups=groups, tiled=True)  8.21 us
    ppermute x1, waiting for transfers between devices, shards(): peer = lax.ppermute(scores, 'tower', to_chip)  5.15 us
    ppermute x1, starting transfers between devices, shards(): peer = lax.ppermute(scores, 'tower', to_chip)  3.01 us
    pallas_call x1, Pallas kernels, shards(): pl.pallas_call(project_kernel, out_shape=(jax.ShapeDtypeStruct((2 * width...  2.94 us
  transfers between devices with their start and end apart: 8, of which 7 were waited for; matrix products, arithmetic and copies ran while one was open for 1% of the time, Pallas kernels for 0%

profile of v5, /device:TPU:6, one launch (start us, length us, event | category | flops | bytes accessed | tf_op | source)
XLA Modules:
  0.0 132.5 jit_solution(13113289209134339260)
XLA Ops:
  0.6 0.0 copy-start.2
  0.6 2.9 %project.1 = (f32[576,128]{1,0:T(8,128)}, bf16[576,128]{1,0:T(8,128)(2,1)}) custom-call(bf16[128,1152]{1,0:T(8,128)(2,1)} %xi.1, bf16[288,1152]{1,0:T(8,128)(2,1)} %bitcast.26, bf16[128,1152]{1,0:T(8,128)(2,1)} %xt.1, bf16[288,1152]{1,0:T(8,128)(2,1)} %bitcast.27), custom_call_target="tpu_custom_call" | custom-call | tf_op jit(solution)/shard_map/project/pallas_call | solution.py:221
  3.6 0.0 copy-start.3
  3.6 2.1 %collective-permute-start = (bf16[576,128]{1,0:T(8,128)(2,1)}, bf16[576,128]{1,0:T(8,128)(2,1)S(1)}, u32[]{:S(2)}, u32[]{:S(2)}) collective-permute-start(bf16[576,128]{1,0:T(8,128)(2,1)} %get-tuple-element.12.own), channel_id=1, source_target_pairs={{0,1},{1,0},{2,3},{3,2},{4,5},{5,4},{6,7},{7,6},{8,9},{9,8},{10,11... | collective-permute-start | bytes 442376 | tf_op jit(solution)/shard_map/ppermute | solution.py:233
  5.7 0.0 copy-done.2
  5.7 0.2 copy.15
  5.9 0.1 reshape.26
  6.0 0.0 copy-start
  6.0 0.1 slice_bitcast_fusion.1
  6.1 0.0 copy-done.3
  6.2 0.2 copy.13
  6.4 0.1 reshape.24
  6.5 0.1 slice_bitcast_fusion.3
  6.6 0.3 copy-done
  6.9 0.3 collective-permute-done
  7.2 20.3 %collective-permute-start.4 = (bf16[576,128]{1,0:T(8,128)(2,1)S(1)}, bf16[576,128]{1,0:T(8,128)(2,1)S(1)}, u32[]{:S(2)}, u32[]{:S(2)}) collective-permute-start(bf16[576,128]{1,0:T(8,128)(2,1)S(1)} %pad_maximum_fusion.i0), channel_id=1, source_target_pairs={{0,1008},{1,1013},{2,1010},{3,1015},{4,1012},{5,1017},{6,1014},{7,... | collective-permute-start | bytes 442376 | tf_op jit(solution)/shard_map/ppermute | solution.py:39
  27.5 4.1 %collective-permute-start.3 = (bf16[576,128]{1,0:T(8,128)(2,1)S(1)}, bf16[576,128]{1,0:T(8,128)(2,1)S(1)}, u32[]{:S(2)}, u32[]{:S(2)}) collective-permute-start(bf16[576,128]{1,0:T(8,128)(2,1)S(1)} %pad_maximum_fusion.i0), channel_id=1, source_target_pairs={{0,1020},{1,1017},{2,1022},{3,1019},{4,0},{5,1021},{6,2},{7,1023},... | collective-permute-start | bytes 442376 | tf_op jit(solution)/shard_map/ppermute | solution.py:39
  31.7 4.3 %collective-permute-start.2 = (bf16[576,128]{1,0:T(8,128)(2,1)S(1)}, bf16[576,128]{1,0:T(8,128)(2,1)S(1)}, u32[]{:S(2)}, u32[]{:S(2)}) collective-permute-start(bf16[576,128]{1,0:T(8,128)(2,1)S(1)} %pad_maximum_fusion.1.t0), channel_id=1, source_target_pairs={{0,16},{1,13},{2,18},{3,15},{4,20},{5,17},{6,22},{7,19},{8,24},{9,... | collective-permute-start | bytes 442376 | tf_op jit(solution)/shard_map/ppermute | solution.py:39
  36.0 1.9 %collective-permute-start.1 = (bf16[576,128]{1,0:T(8,128)(2,1)S(1)}, bf16[576,128]{1,0:T(8,128)(2,1)S(1)}, u32[]{:S(2)}, u32[]{:S(2)}) collective-permute-start(bf16[576,128]{1,0:T(8,128)(2,1)S(1)} %pad_maximum_fusion.1.t0), channel_id=1, source_target_pairs={{0,4},{1,9},{2,6},{3,11},{4,8},{5,13},{6,10},{7,15},{8,12},{9,17},... | collective-permute-start | bytes 442376 | tf_op jit(solution)/shard_map/ppermute | solution.py:39
  37.9 0.1 maximum_bitcast_fusion.1
  38.1 0.1 maximum_bitcast_fusion
  38.2 0.0 copy-start.1
  38.3 4.9 %collective-permute-done.3.i1 = bf16[576,128]{1,0:T(8,128)(2,1)S(1)} collective-permute-done((bf16[576,128]{1,0:T(8,128)(2,1)S(1)}, bf16[576,128]{1,0:T(8,128)(2,1)S(1)}, u32[]{:S(2)}, u32[]{:S(2)}) %collective-permute-start.3) | collective-permute-done | bytes 147488 | tf_op jit(solution)/shard_map/ppermute | solution.py:39
  43.2 0.0 collective-permute-done.4.i2
  43.2 6.7 %collective-permute-done.2.t2 = bf16[576,128]{1,0:T(8,128)(2,1)S(1)} collective-permute-done((bf16[576,128]{1,0:T(8,128)(2,1)S(1)}, bf16[576,128]{1,0:T(8,128)(2,1)S(1)}, u32[]{:S(2)}, u32[]{:S(2)}) %collective-permute-start.2) | collective-permute-done | bytes 147488 | tf_op jit(solution)/shard_map/ppermute | solution.py:39
  50.0 3.5 %collective-permute-done.1.t1 = bf16[576,128]{1,0:T(8,128)(2,1)S(1)} collective-permute-done((bf16[576,128]{1,0:T(8,128)(2,1)S(1)}, bf16[576,128]{1,0:T(8,128)(2,1)S(1)}, u32[]{:S(2)}, u32[]{:S(2)}) %collective-permute-start.1) | collective-permute-done | bytes 147488 | tf_op jit(solution)/shard_map/ppermute | solution.py:39
  53.5 0.5 scores.1.mine
  54.0 3.0 %collective-permute-start.5 = (bf16[656,128]{1,0:T(8,128)(2,1)S(1)}, bf16[656,128]{1,0:T(8,128)(2,1)S(1)}, u32[]{:S(2)}, u32[]{:S(2)}) collective-permute-start(bf16[656,128]{1,0:T(8,128)(2,1)S(1)} %scores.1.mine), channel_id=1, source_target_pairs={{0,2},{1,3},{2,0},{3,1},{4,6},{5,7},{6,4},{7,5},{8,10},{9,11},{10,... | collective-permute-start | bytes 503816 | tf_op jit(solution)/shard_map/ppermute | solution.py:250
  58.4 0.1 pad_maximum_fusion.2.numbers
  58.4 5.1 %collective-permute-done.5.peer = bf16[656,128]{1,0:T(8,128)(2,1)S(1)} collective-permute-done((bf16[656,128]{1,0:T(8,128)(2,1)S(1)}, bf16[656,128]{1,0:T(8,128)(2,1)S(1)}, u32[]{:S(2)}, u32[]{:S(2)}) %collective-permute-start.5) | collective-permute-done | bytes 167968 | tf_op jit(solution)/shard_map/ppermute | solution.py:250
  63.6 1.4 %weights.1 = (f32[584,128]{1,0:T(8,128)S(1)}, f32[584,128]{1,0:T(8,128)S(1)}) custom-call(f32[3]{0:T(128)S(1)} %pad_maximum_fusion.2.numbers, bf16[656,128]{1,0:T(8,128)(2,1)S(1)} %scores.1.mine, bf16[656,128]{1,0:T(8,128)(2,1)S(1)} %collective-permute-done.5.peer, bf16[576,128]{1,0:T(8,128)(2,1)S(1)} %copy-done, ...), custom_call_target="tpu_custom_call" | custom-call | tf_op jit(solution)/shard_map/weights/pallas_call | solution.py:252
  65.0 1.9 %collective-permute-start.6 = (f32[584,128]{1,0:T(8,128)S(1)}, f32[584,128]{1,0:T(8,128)S(1)}, u32[]{:S(2)}, u32[]{:S(2)}) collective-permute-start(f32[584,128]{1,0:T(8,128)S(1)} %get-tuple-element.15), channel_id=1, source_target_pairs={{0,1},{1,0},{2,3},{3,2},{4,5},{5,4},{6,7},{7,6},{8,9},{9,8},{10,11... | collective-permute-start | bytes 897032 | tf_op jit(solution)/shard_map/ppermute | solution.py:260
  67.0 1.6 %collective-permute-done.6.got = f32[584,128]{1,0:T(8,128)S(1)} collective-permute-done((f32[584,128]{1,0:T(8,128)S(1)}, f32[584,128]{1,0:T(8,128)S(1)}, u32[]{:S(2)}, u32[]{:S(2)}) %collective-permute-start.6) | collective-permute-done | bytes 299040 | tf_op jit(solution)/shard_map/ppermute | solution.py:260
  68.5 0.0 copy-done.1
  68.5 1.4 %gradients.1 = (bf16[16,368,128]{2,1,0:T(8,128)(2,1)S(1)}, f32[8,128]{1,0:T(8,128)S(1)}) custom-call(f32[3]{0:T(128)S(1)} %pad_maximum_fusion.2.numbers, f32[584,128]{1,0:T(8,128)S(1)} %get-tuple-element.14.keep, f32[584,128]{1,0:T(8,128)S(1)} %collective-permute-done.6.got, f32[576,128]{1,0:T(8,128)S(1)} %copy-done.1, bf16[1280,128]{1,0:T(8,128)(2,1)S(1)} %bitcast.23, ...), custom_call_target="tpu_custom_call" | custom-call | tf_op jit(solution)/shard_map/gradients/pallas_call | solution.py:264
  70.0 27.5 %all_to_all.10.got = bf16[16,368,128]{2,1,0:T(8,128)(2,1)S(1)} all-to-all(bf16[16,368,128]{2,1,0:T(8,128)(2,1)S(1)} %get-tuple-element.20), channel_id=1, replica_groups={{0,4,128,132,256,260,384,388,512,516,640,644,768,772,896,900},{8,12,136..., dimensions={0} | all-to-all | bytes 3014656 | tf_op jit(solution)/shard_map/all_to_all | solution.py:280
  97.5 0.5 ring.1
  98.0 0.7 convert_element_type.7
  98.6 8.2 %all-to-all-start.1 = ((f16[16,24,128]{2,1,0:T(8,128)(2,1)}), f16[16,24,128]{2,1,0:T(8,128)(2,1)S(1)}, u32[]{:S(2)}, u32[]{:S(2)}) async-start(f16[16,24,128]{2,1,0:T(8,128)(2,1)} %convert_element_type.7), calls=%async_computation.1 | async-start | bytes 196608 | tf_op jit(solution)/shard_map/all_to_all | solution.py:293
  106.8 0.5 slice_bitcast_fusion.4
  107.4 24.1 %all-to-all-done.1 = f16[16,24,128]{2,1,0:T(8,128)(2,1)S(1)} async-done(((f16[16,24,128]{2,1,0:T(8,128)(2,1)}), f16[16,24,128]{2,1,0:T(8,128)(2,1)S(1)}, u32[]{:S(2)}, u32[]{:S(2)}) %all-to-all-start.1) | async-done | bytes 98336 | tf_op jit(solution)/shard_map/all_to_all | solution.py:293
  131.5 0.1 fusion.5
  131.6 0.1 fusion.4
  131.7 0.1 reshape.29
  131.8 0.1 reshape.28
  131.8 0.7 broadcast_select_fusion
  (12 shorter events, 0.2 us)
Async XLA Ops:
  0.6 5.0 %copy-start.2 = (bf16[128,1152]{1,0:T(8,128)(2,1)S(1)}, bf16[128,1152]{1,0:T(8,128)(2,1)}, u32[]{:S(2)}) copy-start(bf16[128,1152]{1,0:T(8,128)(2,1)} %xt.1) | copy-start | bytes 884740
  3.6 2.6 %copy-start.3 = (bf16[128,1152]{1,0:T(8,128)(2,1)S(1)}, bf16[128,1152]{1,0:T(8,128)(2,1)}, u32[]{:S(2)}) copy-start(bf16[128,1152]{1,0:T(8,128)(2,1)} %xi.1) | copy-start | bytes 884740
  3.6 3.6 %collective-permute-start = (bf16[576,128]{1,0:T(8,128)(2,1)}, bf16[576,128]{1,0:T(8,128)(2,1)S(1)}, u32[]{:S(2)}, u32[]{:S(2)}) collective-permute-start(bf16[576,128]{1,0:T(8,128)(2,1)} %get-tuple-element.12.own), channel_id=1, source_target_pairs={{0,1},{1,0},{2,3},{3,2},{4,5},{5,4},{6,7},{7,6},{8,9},{9,8},{10,11... | collective-permute-start | bytes 442376 | tf_op jit(solution)/shard_map/ppermute | solution.py:233
  6.0 0.9 copy-start
  7.2 36.0 %collective-permute-start.4 = (bf16[576,128]{1,0:T(8,128)(2,1)S(1)}, bf16[576,128]{1,0:T(8,128)(2,1)S(1)}, u32[]{:S(2)}, u32[]{:S(2)}) collective-permute-start(bf16[576,128]{1,0:T(8,128)(2,1)S(1)} %pad_maximum_fusion.i0), channel_id=1, source_target_pairs={{0,1008},{1,1013},{2,1010},{3,1015},{4,1012},{5,1017},{6,1014},{7,... | collective-permute-start | bytes 442376 | tf_op jit(solution)/shard_map/ppermute | solution.py:39
  27.5 15.7 %collective-permute-start.3 = (bf16[576,128]{1,0:T(8,128)(2,1)S(1)}, bf16[576,128]{1,0:T(8,128)(2,1)S(1)}, u32[]{:S(2)}, u32[]{:S(2)}) collective-permute-start(bf16[576,128]{1,0:T(8,128)(2,1)S(1)} %pad_maximum_fusion.i0), channel_id=1, source_target_pairs={{0,1020},{1,1017},{2,1022},{3,1019},{4,0},{5,1021},{6,2},{7,1023},... | collective-permute-start | bytes 442376 | tf_op jit(solution)/shard_map/ppermute | solution.py:39
  31.7 18.3 %collective-permute-start.2 = (bf16[576,128]{1,0:T(8,128)(2,1)S(1)}, bf16[576,128]{1,0:T(8,128)(2,1)S(1)}, u32[]{:S(2)}, u32[]{:S(2)}) collective-permute-start(bf16[576,128]{1,0:T(8,128)(2,1)S(1)} %pad_maximum_fusion.1.t0), channel_id=1, source_target_pairs={{0,16},{1,13},{2,18},{3,15},{4,20},{5,17},{6,22},{7,19},{8,24},{9,... | collective-permute-start | bytes 442376 | tf_op jit(solution)/shard_map/ppermute | solution.py:39
  36.0 17.5 %collective-permute-start.1 = (bf16[576,128]{1,0:T(8,128)(2,1)S(1)}, bf16[576,128]{1,0:T(8,128)(2,1)S(1)}, u32[]{:S(2)}, u32[]{:S(2)}) collective-permute-start(bf16[576,128]{1,0:T(8,128)(2,1)S(1)} %pad_maximum_fusion.1.t0), channel_id=1, source_target_pairs={{0,4},{1,9},{2,6},{3,11},{4,8},{5,13},{6,10},{7,15},{8,12},{9,17},... | collective-permute-start | bytes 442376 | tf_op jit(solution)/shard_map/ppermute | solution.py:39
  38.2 30.3 %copy-start.1 = (f32[576,128]{1,0:T(8,128)S(1)}, f32[576,128]{1,0:T(8,128)}, u32[]{:S(2)}) copy-start(f32[576,128]{1,0:T(8,128)} %get-tuple-element.16.z) | copy-start | bytes 884740
  54.0 9.6 %collective-permute-start.5 = (bf16[656,128]{1,0:T(8,128)(2,1)S(1)}, bf16[656,128]{1,0:T(8,128)(2,1)S(1)}, u32[]{:S(2)}, u32[]{:S(2)}) collective-permute-start(bf16[656,128]{1,0:T(8,128)(2,1)S(1)} %scores.1.mine), channel_id=1, source_target_pairs={{0,2},{1,3},{2,0},{3,1},{4,6},{5,7},{6,4},{7,5},{8,10},{9,11},{10,... | collective-permute-start | bytes 503816 | tf_op jit(solution)/shard_map/ppermute | solution.py:250
  65.0 3.5 %collective-permute-start.6 = (f32[584,128]{1,0:T(8,128)S(1)}, f32[584,128]{1,0:T(8,128)S(1)}, u32[]{:S(2)}, u32[]{:S(2)}) collective-permute-start(f32[584,128]{1,0:T(8,128)S(1)} %get-tuple-element.15), channel_id=1, source_target_pairs={{0,1},{1,0},{2,3},{3,2},{4,5},{5,4},{6,7},{7,6},{8,9},{9,8},{10,11... | collective-permute-start | bytes 897032 | tf_op jit(solution)/shard_map/ppermute | solution.py:260
  98.6 32.8 %all-to-all-start.1 = ((f16[16,24,128]{2,1,0:T(8,128)(2,1)}), f16[16,24,128]{2,1,0:T(8,128)(2,1)S(1)}, u32[]{:S(2)}, u32[]{:S(2)}) async-start(f16[16,24,128]{2,1,0:T(8,128)(2,1)} %convert_element_type.7), calls=%async_computation.1 | async-start | bytes 196608 | tf_op jit(solution)/shard_map/all_to_all | solution.py:293

commit v6 on v5

--- a/solution.py
+++ b/solution.py
@@ -57,91 +57,68 @@
         own[side * width : (side + 1) * width] = part.astype(BF16)
 
 
-def score_kernel(i0, t0, t1, t2, i1, i2, out):
-    pairs = ((t0, i0), (t1, i0), (t2, i0), (i1, t0), (i2, t0))
-    for j, (other, own) in enumerate(pairs):
-        out[j * LANES : (j + 1) * LANES] = dot(other[...], own[...], 0, 0).astype(BF16)
-    squares = [
-        jnp.sum(jnp.square(b[...].astype(F32)), axis=0, keepdims=True)
-        for b in (i0, t0, t1, t2, i1, i2)
-    ]
+def score_kernel(own, o0, o1, o2, far, out):
+    size = own.shape[0]
+    blocks = [own[...], o0[...], o1[...], o2[...], far[:size], far[size:]]
+    for j, other in enumerate(blocks[1:]):
+        out[j * LANES : (j + 1) * LANES] = dot(other, blocks[0], 0, 0).astype(BF16)
+    squares = [jnp.sum(jnp.square(b.astype(F32)), axis=0, keepdims=True) for b in blocks]
     squares = jnp.concatenate(squares + [jnp.zeros((2, LANES), F32)], axis=0)
     high = squares.astype(BF16).astype(F32)
     low = (squares - high).astype(BF16).astype(F32)
     out[5 * LANES :] = jnp.concatenate((high, low), axis=0).astype(BF16)
 
 
-def weight_kernel(numbers, mine, peer, own, t1, t2, i1, i2, send, keep):
-    scale, bias, core0 = numbers[0], numbers[1], numbers[2]
-    width = own.shape[0] // 2
-    rows = 5 * LANES
-
-    def total(start, size):
-        a = mine[start : start + size].astype(F32)
-        return a + peer[start : start + size].astype(F32)
-
-    squares = total(rows, 16)
+def weight_kernel(numbers, mine, peer, o0, o1, o2, far, send, keep):
+    scale, bias = numbers[0], numbers[1]
+    size = o0.shape[0]
+    width = size // 2
+
+    def total(start, rows):
+        a = mine[start : start + rows].astype(F32)
+        return a + peer[start : start + rows].astype(F32)
+
+    squares = total(5 * LANES, 16)
     inv = lax.rsqrt(squares[:8] + squares[8:] + 1e-06)
     down = inv.T
-
-    def weigh(j, across, along):
-        c = scale * (total(j * LANES, LANES) * across * along)
-        s = c + bias
-        e = jnp.exp(-jnp.abs(s))
-        return c, s, jnp.log1p(e), jnp.where(s >= 0, 1.0, e) / (1.0 + e)
-
-    ni, nt = inv[0:1], inv[1:2]
     eye = (
         lax.broadcasted_iota(jnp.int32, (LANES, LANES), 0)
         == lax.broadcasted_iota(jnp.int32, (LANES, LANES), 1)
     ).astype(F32)
-    c, s, tail, g = weigh(0, ni, down[:, 1:2])
-    loss = core0 * jnp.sum(jnp.maximum((1.0 - 2.0 * eye) * s, 0.0) + tail, axis=0, keepdims=True)
-    g = g - eye
-    gc = g * c
-    along_i0 = jnp.sum(gc, axis=0, keepdims=True)
-    along_t0 = jnp.sum(gc.T, axis=0, keepdims=True)
-    du0 = fine(own[width:], g * down[:, 1:2])
-    dv0 = fine(own[:width], (g * ni).T)
-
-    along_i, along_t = jnp.zeros_like(ni), jnp.zeros_like(ni)
-    du = dv = None
-    for j, block in ((1, t1), (2, t2)):
+    n = inv[0:1]
+    loss = along = jnp.zeros_like(n)
+    d = None
+    for j, other in enumerate((o0[...], o1[...], o2[...], far[:size], far[size:])):
         col = down[:, j + 1 : j + 2]
-        c, s, tail, g = weigh(j, ni, col)
-        loss += jnp.sum(jnp.maximum(s, 0.0) + tail, axis=0, keepdims=True)
-        along_i += jnp.sum(g * c, axis=0, keepdims=True)
-        term = fine(block[...], g * col)
-        du = term if du is None else du + term
-    for j, block in ((3, i1), (4, i2)):
-        col = down[:, j + 1 : j + 2]
-        c, s, tail, g = weigh(j, nt, col)
-        along_t += jnp.sum(g * c, axis=0, keepdims=True)
-        term = fine(block[...], g * col)
-        dv = term if dv is None else dv + term
-    zero = jnp.zeros_like(ni)
-    send[:width] = du[width:]
-    send[width : 2 * width] = dv[width:]
-    send[2 * width :] = jnp.concatenate((along_i, along_t, loss) + (zero,) * 5, axis=0)
-    keep[:width] = du[:width] + du0
-    keep[width : 2 * width] = dv[:width] + dv0
-    keep[2 * width :] = jnp.concatenate(
-        (along_i + along_i0, along_t + along_t0, loss, ni, nt) + (zero,) * 3, axis=0
-    )
+        c = scale * (total(j * LANES, LANES) * n * col)
+        s = c + bias
+        e = jnp.exp(-jnp.abs(s))
+        g = jnp.where(s >= 0, 1.0, e) / (1.0 + e)
+        signed = s
+        if j == 0:
+            signed, g = (1.0 - 2.0 * eye) * s, g - eye
+        loss += jnp.sum(jnp.maximum(signed, 0.0) + jnp.log1p(e), axis=0, keepdims=True)
+        along += jnp.sum(g * c, axis=0, keepdims=True)
+        term = fine(other, g * col)
+        d = term if d is None else d + term
+    lines = jnp.concatenate((along, loss, n, jnp.zeros((5, LANES), F32)), axis=0)
+    keep[:width], send[:width] = d[:width], d[width:]
+    keep[width:], send[width:] = lines, lines
 
 
 def gradient_kernel(parts, numbers, keep, got, z, xi, xt, out, loss):
-    scale = numbers[0]
+    scale, first = numbers[0], numbers[2] > 0
     width = z.shape[0] // 2
-    lines, more = keep[2 * width :], got[2 * width :]
-    loss[...] = jnp.broadcast_to(lines[2:3] + more[2:3], loss.shape)
     grads = []
     for side in range(2):
-        part = slice(side * width, (side + 1) * width)
-        d = scale * (keep[part] + got[part])
-        along = lines[side : side + 1] + more[side : side + 1]
-        n = lines[3 + side : 4 + side]
-        grads.append(two_terms((d - z[part] * (n * along)) * n))
+        own, other = (keep, got) if side == 0 else (got, keep)
+        lines = jnp.where(first, own[width:], other[width:])
+        along, n = lines[0:1], lines[2:3]
+        if side == 0:
+            loss[...] = jnp.broadcast_to(lines[1:2], loss.shape)
+        d = scale * jnp.where(first, own[:width], other[:width])
+        part = z[side * width : (side + 1) * width]
+        grads.append(two_terms((d - part * (n * along)) * n))
     block = xi.shape[0] // parts
     whole = width // LANES * LANES
     rest = width - whole
@@ -212,7 +189,8 @@
     planes = dp // RING
     to_core = [(t, t ^ 1) for t in range(tower)]
     to_chip = [(t, t ^ 2) for t in range(tower)]
-    core0 = (lax.axis_index("tower") % 2 == 0).astype(F32)
+    first = lax.axis_index("tower") % 2 == 0
+    core0 = first.astype(F32)
     numbers = jnp.concatenate((logit_scale, logit_bias, core0[None]))
     scalars = pl.BlockSpec(memory_space=pltpu.SMEM)
     array = pl.BlockSpec(memory_space=pltpu.VMEM)
@@ -233,30 +211,30 @@
     other = lax.ppermute(own, "tower", to_core)
     i0 = jnp.concatenate((own[:width], other[:width]), axis=0)
     t0 = jnp.concatenate((own[width:], other[width:]), axis=0)
-    t2 = shifted(t0, (4, 3))
-    i2 = shifted(i0, (-4, -3))
-    t1 = shifted(t0, (1, 2))
-    i1 = shifted(i0, (-1, -2))
+    mine, o0 = jnp.where(first, i0, t0), jnp.where(first, t0, i0)
+    o1 = shifted(o0, (1, -1))
+    o2 = shifted(o0, (2, -2))
+    far = shifted(jnp.concatenate((o1, o2), axis=0), (2, -2))
     xi, xt = row_sets(image_feats, planes), row_sets(text_feats, planes)
-    i1, xi, xt = lax.optimization_barrier((i1, xi, xt))
+    mine, xi, xt = lax.optimization_barrier((mine, xi, xt))
     scores = pl.pallas_call(
         score_kernel,
         out_shape=jax.ShapeDtypeStruct((5 * rows + 16, rows), BF16),
-        in_specs=[array] * 6,
+        in_specs=[array] * 5,
         out_specs=array,
         compiler_params=VMEM,
         name="scores",
-    )(i0, t0, t1, t2, i1, i2)
+    )(mine, o0, o1, o2, far)
     peer = lax.ppermute(scores, "tower", to_chip)
-    sums = jax.ShapeDtypeStruct((2 * width + 8, rows), F32)
+    sums = jax.ShapeDtypeStruct((width + 8, rows), F32)
     send, keep = pl.pallas_call(
         weight_kernel,
         out_shape=(sums, sums),
-        in_specs=[scalars] + [array] * 7,
+        in_specs=[scalars] + [array] * 6,
         out_specs=(array, array),
         compiler_params=VMEM,
         name="weights",
-    )(numbers, scores, peer, own, t1, t2, i1, i2)
+    )(numbers, scores, peer, o0, o1, o2, far)
     got = lax.ppermute(send, "tower", to_core)
     parts = 2 * planes
     block = xi.shape[0] // parts

time: 133 us -> 130 us (0.977)
  starting transfers between devices: 45.8 us -> 29.9 us
  waiting for transfers between devices: 46.2 us -> 58.2 us
    ppermute x4 -> x3, starting transfers between devices: 30.6 us -> 11.1 us  [shifted(): return lax.ppermute(block, ('dp', 'tower'), route)]
    ppermute x4 -> x3, waiting for transfers between devices: 15.2 us -> 26.5 us  [shifted(): return lax.ppermute(block, ('dp', 'tower'), route)]
    all_to_all x1, starting transfers between devices: 8.21 us -> 11.9 us  [shards(): lax.all_to_all(sent, 'dp', 0, 0, axis_index_groups=groups, tiled=True)]
  transfers between devices with their start and end apart: 8 -> 7, of which waited for: 7 -> 7; matrix products, arithmetic and copies ran while one was open for 1% -> 1% of each run, Pallas kernels for 0% -> 0%
where the time goes in v6:
time: 130 us; the launch traced here: 129 us
  waiting for transfers between devices  58.2 us (45%)
  starting transfers between devices  29.9 us (23%)
  blocking collectives  28.7 us (22%)
  Pallas kernels  6.73 us (5%)
  between operations  2.21 us (2%)
  local copies, waits for them, and re-layouts  1.87 us (1%)
  other arithmetic  1.84 us (1%)
    all_to_all x1, blocking collectives, shards(): lax.all_to_all(grads, 'dp', 0, 0, axis_index_groups=groups, tiled=True)  28.7 us
    ppermute x3, waiting for transfers between devices, shifted(): return lax.ppermute(block, ('dp', 'tower'), route)  26.5 us
    all_to_all x1, waiting for transfers between devices, shards(): lax.all_to_all(sent, 'dp', 0, 0, axis_index_groups=groups, tiled=True)  24.9 us
    all_to_all x1, starting transfers between devices, shards(): lax.all_to_all(sent, 'dp', 0, 0, axis_index_groups=groups, tiled=True)  11.9 us
    ppermute x3, starting transfers between devices, shifted(): return lax.ppermute(block, ('dp', 'tower'), route)  11.1 us
    ppermute x1, waiting for transfers between devices, shards(): peer = lax.ppermute(scores, 'tower', to_chip)  4.35 us
    ppermute x1, starting transfers between devices, shards(): peer = lax.ppermute(scores, 'tower', to_chip)  3.02 us
    pallas_call x1, Pallas kernels, shards(): pl.pallas_call(project_kernel, out_shape=(jax.ShapeDtypeStruct((2 * width...  2.94 us
  transfers between devices with their start and end apart: 7, of which 7 were waited for; matrix products, arithmetic and copies ran while one was open for 1% of the time, Pallas kernels for 0%

profile of v6, /device:TPU:6, one launch (start us, length us, event | category | flops | bytes accessed | tf_op | source)
XLA Modules:
  0.0 129.5 jit_solution(6662213671900593140)
XLA Ops:
  0.6 0.0 copy-start.1
  0.6 2.9 %project.1 = (f32[576,128]{1,0:T(8,128)}, bf16[576,128]{1,0:T(8,128)(2,1)}) custom-call(bf16[128,1152]{1,0:T(8,128)(2,1)} %xi.1, bf16[288,1152]{1,0:T(8,128)(2,1)} %bitcast.26, bf16[128,1152]{1,0:T(8,128)(2,1)} %xt.1, bf16[288,1152]{1,0:T(8,128)(2,1)} %bitcast.27), custom_call_target="tpu_custom_call" | custom-call | tf_op jit(solution)/shard_map/project/pallas_call | solution.py:199
  3.6 0.0 copy-start.3
  3.6 2.1 %collective-permute-start = (bf16[576,128]{1,0:T(8,128)(2,1)}, bf16[576,128]{1,0:T(8,128)(2,1)S(1)}, u32[]{:S(2)}, u32[]{:S(2)}) collective-permute-start(bf16[576,128]{1,0:T(8,128)(2,1)} %get-tuple-element.12), channel_id=1, source_target_pairs={{0,1},{1,0},{2,3},{3,2},{4,5},{5,4},{6,7},{7,6},{8,9},{9,8},{10,11... | collective-permute-start | bytes 442376 | tf_op jit(solution)/shard_map/ppermute | solution.py:211
  5.7 0.0 copy-done.1
  5.7 0.2 copy.15
  5.9 0.1 reshape.26
  6.0 0.0 copy-done.3
  6.1 1.1 collective-permute-done
  7.2 0.1 broadcast_select_fusion
  7.3 0.0 copy-start.2
  7.3 5.3 %collective-permute-start.2 = (bf16[576,128]{1,0:T(8,128)(2,1)S(1)}, bf16[576,128]{1,0:T(8,128)(2,1)S(1)}, u32[]{:S(2)}, u32[]{:S(2)}) collective-permute-start(bf16[576,128]{1,0:T(8,128)(2,1)S(1)} %get-tuple-element.25.o0), channel_id=1, source_target_pairs={{0,8},{1,1017},{2,10},{3,1019},{4,12},{5,1021},{6,14},{7,1023},{8,... | collective-permute-start | bytes 442376 | tf_op jit(solution)/shard_map/ppermute | solution.py:39
  12.6 3.8 %collective-permute-start.1 = (bf16[576,128]{1,0:T(8,128)(2,1)S(1)}, bf16[576,128]{1,0:T(8,128)(2,1)S(1)}, u32[]{:S(2)}, u32[]{:S(2)}) collective-permute-start(bf16[576,128]{1,0:T(8,128)(2,1)S(1)} %get-tuple-element.25.o0), channel_id=1, source_target_pairs={{0,4},{1,1021},{2,6},{3,1023},{4,8},{5,1},{6,10},{7,3},{8,12},{9,5... | collective-permute-start | bytes 442376 | tf_op jit(solution)/shard_map/ppermute | solution.py:39
  16.5 0.1 slice_bitcast_fusion.1
  16.6 0.1 maximum_bitcast_fusion.1
  16.8 0.0 copy-done.2
  16.8 0.2 copy.13
  17.0 0.1 reshape.24
  17.1 12.9 %collective-permute-done.2.o2 = bf16[576,128]{1,0:T(8,128)(2,1)S(1)} collective-permute-done((bf16[576,128]{1,0:T(8,128)(2,1)S(1)}, bf16[576,128]{1,0:T(8,128)(2,1)S(1)}, u32[]{:S(2)}, u32[]{:S(2)}) %collective-permute-start.2) | collective-permute-done | bytes 147488 | tf_op jit(solution)/shard_map/ppermute | solution.py:39
  30.0 2.6 %collective-permute-done.1.o1 = bf16[576,128]{1,0:T(8,128)(2,1)S(1)} collective-permute-done((bf16[576,128]{1,0:T(8,128)(2,1)S(1)}, bf16[576,128]{1,0:T(8,128)(2,1)S(1)}, u32[]{:S(2)}, u32[]{:S(2)}) %collective-permute-start.1) | collective-permute-done | bytes 147488 | tf_op jit(solution)/shard_map/ppermute | solution.py:39
  32.7 1.9 %collective-permute-start.3 = (bf16[1152,128]{1,0:T(8,128)(2,1)S(1)}, bf16[1152,128]{1,0:T(8,128)(2,1)S(1)}, u32[]{:S(2)}, u32[]{:S(2)}) collective-permute-start(bf16[1152,128]{1,0:T(8,128)(2,1)S(1)} %pad_maximum_fusion), channel_id=1, source_target_pairs={{0,8},{1,1017},{2,10},{3,1019},{4,12},{5,1021},{6,14},{7,1023},{8,... | collective-permute-start | bytes 884744 | tf_op jit(solution)/shard_map/ppermute | solution.py:39
  34.6 0.1 slice_bitcast_fusion.3
  34.7 0.1 maximum_bitcast_fusion
  34.8 0.0 copy-start
  34.9 11.0 %collective-permute-done.3.far = bf16[1152,128]{1,0:T(8,128)(2,1)S(1)} collective-permute-done((bf16[1152,128]{1,0:T(8,128)(2,1)S(1)}, bf16[1152,128]{1,0:T(8,128)(2,1)S(1)}, u32[]{:S(2)}, u32[]{:S(2)}) %collective-permute-start.3) | collective-permute-done | bytes 294944 | tf_op jit(solution)/shard_map/ppermute | solution.py:39
  45.9 0.4 scores.1.mine
  46.3 3.0 %collective-permute-start.4 = (bf16[656,128]{1,0:T(8,128)(2,1)S(1)}, bf16[656,128]{1,0:T(8,128)(2,1)S(1)}, u32[]{:S(2)}, u32[]{:S(2)}) collective-permute-start(bf16[656,128]{1,0:T(8,128)(2,1)S(1)} %scores.1.mine), channel_id=1, source_target_pairs={{0,2},{1,3},{2,0},{3,1},{4,6},{5,7},{6,4},{7,5},{8,10},{9,11},{10,... | collective-permute-start | bytes 503816 | tf_op jit(solution)/shard_map/ppermute | solution.py:228
  50.6 0.1 pad_maximum_fusion.3.numbers
  50.7 4.4 %collective-permute-done.4.peer = bf16[656,128]{1,0:T(8,128)(2,1)S(1)} collective-permute-done((bf16[656,128]{1,0:T(8,128)(2,1)S(1)}, bf16[656,128]{1,0:T(8,128)(2,1)S(1)}, u32[]{:S(2)}, u32[]{:S(2)}) %collective-permute-start.4) | collective-permute-done | bytes 167968 | tf_op jit(solution)/shard_map/ppermute | solution.py:228
  55.1 1.4 %weights.1 = (f32[296,128]{1,0:T(8,128)S(1)}, f32[296,128]{1,0:T(8,128)S(1)}) custom-call(f32[3]{0:T(128)S(1)} %pad_maximum_fusion.3.numbers, bf16[656,128]{1,0:T(8,128)(2,1)S(1)} %scores.1.mine, bf16[656,128]{1,0:T(8,128)(2,1)S(1)} %collective-permute-done.4.peer, bf16[576,128]{1,0:T(8,128)(2,1)S(1)} %get-tuple-element.25.o0, ...), custom_call_target="tpu_custom_call" | custom-call | tf_op jit(solution)/shard_map/weights/pallas_call | solution.py:230
  56.5 1.9 %collective-permute-start.5 = (f32[296,128]{1,0:T(8,128)S(1)}, f32[296,128]{1,0:T(8,128)S(1)}, u32[]{:S(2)}, u32[]{:S(2)}) collective-permute-start(f32[296,128]{1,0:T(8,128)S(1)} %get-tuple-element.15), channel_id=1, source_target_pairs={{0,1},{1,0},{2,3},{3,2},{4,5},{5,4},{6,7},{7,6},{8,9},{9,8},{10,11... | collective-permute-start | bytes 454664 | tf_op jit(solution)/shard_map/ppermute | solution.py:238
  58.4 1.3 %collective-permute-done.5.got = f32[296,128]{1,0:T(8,128)S(1)} collective-permute-done((f32[296,128]{1,0:T(8,128)S(1)}, f32[296,128]{1,0:T(8,128)S(1)}, u32[]{:S(2)}, u32[]{:S(2)}) %collective-permute-start.5) | collective-permute-done | bytes 151584 | tf_op jit(solution)/shard_map/ppermute | solution.py:238
  59.8 0.0 copy-done
  59.8 1.4 %gradients.1 = (bf16[16,368,128]{2,1,0:T(8,128)(2,1)S(1)}, f32[8,128]{1,0:T(8,128)S(1)}) custom-call(f32[3]{0:T(128)S(1)} %pad_maximum_fusion.3.numbers, f32[296,128]{1,0:T(8,128)S(1)} %get-tuple-element.14.keep, f32[296,128]{1,0:T(8,128)S(1)} %collective-permute-done.5.got, f32[576,128]{1,0:T(8,128)S(1)} %copy-done, bf16[1280,128]{1,0:T(8,128)(2,1)S(1)} %bitcast.23, ...), custom_call_target="tpu_custom_call" | custom-call | tf_op jit(solution)/shard_map/gradients/pallas_call | solution.py:242
  61.2 28.7 %all_to_all.10.got = bf16[16,368,128]{2,1,0:T(8,128)(2,1)S(1)} all-to-all(bf16[16,368,128]{2,1,0:T(8,128)(2,1)S(1)} %get-tuple-element.20), channel_id=1, replica_groups={{0,4,128,132,256,260,384,388,512,516,640,644,768,772,896,900},{8,12,136..., dimensions={0} | all-to-all | bytes 3014656 | tf_op jit(solution)/shard_map/all_to_all | solution.py:258
  90.0 0.5 ring.1
  90.5 0.7 convert_element_type.7
  91.1 11.9 %all-to-all-start.1 = ((f16[16,24,128]{2,1,0:T(8,128)(2,1)}), f16[16,24,128]{2,1,0:T(8,128)(2,1)S(1)}, u32[]{:S(2)}, u32[]{:S(2)}) async-start(f16[16,24,128]{2,1,0:T(8,128)(2,1)} %convert_element_type.7), calls=%async_computation.1 | async-start | bytes 196608 | tf_op jit(solution)/shard_map/all_to_all | solution.py:271
  103.0 0.5 slice_bitcast_fusion.4
  103.5 24.9 %all-to-all-done.1 = f16[16,24,128]{2,1,0:T(8,128)(2,1)S(1)} async-done(((f16[16,24,128]{2,1,0:T(8,128)(2,1)}), f16[16,24,128]{2,1,0:T(8,128)(2,1)S(1)}, u32[]{:S(2)}, u32[]{:S(2)}) %all-to-all-start.1) | async-done | bytes 98336 | tf_op jit(solution)/shard_map/all_to_all | solution.py:271
  128.5 0.1 fusion.5
  128.5 0.1 fusion.4
  128.6 0.1 reshape.29
  128.7 0.1 reshape.28
  128.8 0.7 broadcast_select_fusion.2
  (11 shorter events, 0.2 us)
Async XLA Ops:
  0.6 5.0 %copy-start.1 = (bf16[128,1152]{1,0:T(8,128)(2,1)S(1)}, bf16[128,1152]{1,0:T(8,128)(2,1)}, u32[]{:S(2)}) copy-start(bf16[128,1152]{1,0:T(8,128)(2,1)} %xt.1) | copy-start | bytes 884740
  3.6 2.4 %copy-start.3 = (bf16[576,128]{1,0:T(8,128)(2,1)S(1)}, bf16[576,128]{1,0:T(8,128)(2,1)}, u32[]{:S(2)}) copy-start(bf16[576,128]{1,0:T(8,128)(2,1)} %get-tuple-element.12) | copy-start | bytes 442372
  3.6 3.6 %collective-permute-start = (bf16[576,128]{1,0:T(8,128)(2,1)}, bf16[576,128]{1,0:T(8,128)(2,1)S(1)}, u32[]{:S(2)}, u32[]{:S(2)}) collective-permute-start(bf16[576,128]{1,0:T(8,128)(2,1)} %get-tuple-element.12), channel_id=1, source_target_pairs={{0,1},{1,0},{2,3},{3,2},{4,5},{5,4},{6,7},{7,6},{8,9},{9,8},{10,11... | collective-permute-start | bytes 442376 | tf_op jit(solution)/shard_map/ppermute | solution.py:211
  7.3 9.5 %copy-start.2 = (bf16[128,1152]{1,0:T(8,128)(2,1)S(1)}, bf16[128,1152]{1,0:T(8,128)(2,1)}, u32[]{:S(2)}) copy-start(bf16[128,1152]{1,0:T(8,128)(2,1)} %xi.1) | copy-start | bytes 884740
  7.3 22.7 %collective-permute-start.2 = (bf16[576,128]{1,0:T(8,128)(2,1)S(1)}, bf16[576,128]{1,0:T(8,128)(2,1)S(1)}, u32[]{:S(2)}, u32[]{:S(2)}) collective-permute-start(bf16[576,128]{1,0:T(8,128)(2,1)S(1)} %get-tuple-element.25.o0), channel_id=1, source_target_pairs={{0,8},{1,1017},{2,10},{3,1019},{4,12},{5,1021},{6,14},{7,1023},{8,... | collective-permute-start | bytes 442376 | tf_op jit(solution)/shard_map/ppermute | solution.py:39
  12.6 20.0 %collective-permute-start.1 = (bf16[576,128]{1,0:T(8,128)(2,1)S(1)}, bf16[576,128]{1,0:T(8,128)(2,1)S(1)}, u32[]{:S(2)}, u32[]{:S(2)}) collective-permute-start(bf16[576,128]{1,0:T(8,128)(2,1)S(1)} %get-tuple-element.25.o0), channel_id=1, source_target_pairs={{0,4},{1,1021},{2,6},{3,1023},{4,8},{5,1},{6,10},{7,3},{8,12},{9,5... | collective-permute-start | bytes 442376 | tf_op jit(solution)/shard_map/ppermute | solution.py:39
  32.7 13.2 %collective-permute-start.3 = (bf16[1152,128]{1,0:T(8,128)(2,1)S(1)}, bf16[1152,128]{1,0:T(8,128)(2,1)S(1)}, u32[]{:S(2)}, u32[]{:S(2)}) collective-permute-start(bf16[1152,128]{1,0:T(8,128)(2,1)S(1)} %pad_maximum_fusion), channel_id=1, source_target_pairs={{0,8},{1,1017},{2,10},{3,1019},{4,12},{5,1021},{6,14},{7,1023},{8,... | collective-permute-start | bytes 884744 | tf_op jit(solution)/shard_map/ppermute | solution.py:39
  34.8 24.9 %copy-start = (f32[576,128]{1,0:T(8,128)S(1)}, f32[576,128]{1,0:T(8,128)}, u32[]{:S(2)}) copy-start(f32[576,128]{1,0:T(8,128)} %get-tuple-element.16.z) | copy-start | bytes 884740
  46.3 8.8 %collective-permute-start.4 = (bf16[656,128]{1,0:T(8,128)(2,1)S(1)}, bf16[656,128]{1,0:T(8,128)(2,1)S(1)}, u32[]{:S(2)}, u32[]{:S(2)}) collective-permute-start(bf16[656,128]{1,0:T(8,128)(2,1)S(1)} %scores.1.mine), channel_id=1, source_target_pairs={{0,2},{1,3},{2,0},{3,1},{4,6},{5,7},{6,4},{7,5},{8,10},{9,11},{10,... | collective-permute-start | bytes 503816 | tf_op jit(solution)/shard_map/ppermute | solution.py:228
  56.5 3.3 %collective-permute-start.5 = (f32[296,128]{1,0:T(8,128)S(1)}, f32[296,128]{1,0:T(8,128)S(1)}, u32[]{:S(2)}, u32[]{:S(2)}) collective-permute-start(f32[296,128]{1,0:T(8,128)S(1)} %get-tuple-element.15), channel_id=1, source_target_pairs={{0,1},{1,0},{2,3},{3,2},{4,5},{5,4},{6,7},{7,6},{8,9},{9,8},{10,11... | collective-permute-start | bytes 454664 | tf_op jit(solution)/shard_map/ppermute | solution.py:238
  91.1 37.3 %all-to-all-start.1 = ((f16[16,24,128]{2,1,0:T(8,128)(2,1)}), f16[16,24,128]{2,1,0:T(8,128)(2,1)S(1)}, u32[]{:S(2)}, u32[]{:S(2)}) async-start(f16[16,24,128]{2,1,0:T(8,128)(2,1)} %convert_element_type.7), calls=%async_computation.1 | async-start | bytes 196608 | tf_op jit(solution)/shard_map/all_to_all | solution.py:271

commit v7 on v6

--- a/solution.py
+++ b/solution.py
@@ -106,10 +106,9 @@
     keep[width:], send[width:] = lines, lines
 
 
-def gradient_kernel(parts, numbers, keep, got, z, xi, xt, out, loss):
+def slope_kernel(numbers, keep, got, z, slopes, send, loss):
     scale, first = numbers[0], numbers[2] > 0
     width = z.shape[0] // 2
-    grads = []
     for side in range(2):
         own, other = (keep, got) if side == 0 else (got, keep)
         lines = jnp.where(first, own[width:], other[width:])
@@ -117,21 +116,30 @@
         if side == 0:
             loss[...] = jnp.broadcast_to(lines[1:2], loss.shape)
         d = scale * jnp.where(first, own[:width], other[:width])
-        part = z[side * width : (side + 1) * width]
-        grads.append(two_terms((d - part * (n * along)) * n))
+        part = slice(side * width, (side + 1) * width)
+        terms = two_terms((d - z[part] * (n * along)) * n)
+        slopes[part] = terms
+        send[part] = terms[:, :LANES]
+
+
+def gradient_kernel(parts, slopes, theirs, xi, xt, beside, out):
+    width, count = slopes.shape[0] // 2, xi.shape[0]
     block = xi.shape[0] // parts
     whole = width // LANES * LANES
     rest = width - whole
     fold = -(-block // 32) * 16
     tail = None
     for side, x in enumerate((xi, xt)):
-        feats = jnp.concatenate((x[...], x[...]), axis=1)
-        main = dot(feats, grads[side][:whole], 1, 1).astype(BF16)
+        there = slice(side * count, (side + 1) * count)
+        feats = jnp.concatenate((x[...], x[...], beside[there]), axis=1)
+        part = slice(side * width, (side + 1) * width)
+        grads = jnp.concatenate((slopes[part], theirs[part]), axis=1)
+        main = dot(feats, grads[:whole], 1, 1).astype(BF16)
         for j in range(whole // LANES):
             at = (side * (whole // LANES) + j) * block
             for p in range(parts):
                 out[p, at : at + block] = main[p * block : (p + 1) * block, j * LANES : (j + 1) * LANES]
-        piece = grads[side][whole:]
+        piece = grads[whole:]
         gap = jnp.zeros_like(piece)
         pieces = [gap] * (2 * LANES // rest)
         pieces[side] = pieces[LANES // rest + LANES // rest // 2 + side] = piece
@@ -156,13 +164,27 @@
     out[:, count] = jnp.broadcast_to(power, (places, LANES))
 
 
-def row_sets(feats, planes):
-    x = feats.T.reshape(planes, RING // 2, -1, feats.shape[0])
-    nine = x.shape[2]
-    five = nine // 2 + 1
-    halves = [x[:, :, nine - five :] if q else x[:, :, :five] for q in range(2)]
-    x = jnp.stack(halves, axis=1).transpose(0, 1, 3, 2, 4)
-    return x.reshape(-1, feats.shape[0])
+def order_kernel(column, xi, xt, own_i, own_t, away, turned):
+    places = RING // 2
+    depth, size = turned.shape[0], own_i.shape[0]
+    five = 5
+    nine = 2 * five - 1
+    planes = size // (2 * five * places)
+    block = depth // (2 * planes)
+    for side, x in enumerate((xi, xt)):
+        turned[...] = x[...].astype(F32).T
+        for beside in range(2):
+            first = (column[0] + beside) % 2 * block
+            for p in range(planes):
+                for q in range(2):
+                    for r in range(five):
+                        start = first + 2 * p * block + (five - 1) * q + r
+                        rows = turned[pl.ds(start, places, stride=nine)].astype(BF16)
+                        at = ((2 * p + q) * five + r) * places
+                        if beside:
+                            away[side * size + at : side * size + at + places] = rows
+                        else:
+                            (own_t if side else own_i)[at : at + places] = rows
 
 
 def shares(total, width, share):
@@ -215,8 +237,21 @@
     o1 = shifted(o0, (1, -1))
     o2 = shifted(o0, (2, -2))
     far = shifted(jnp.concatenate((o1, o2), axis=0), (2, -2))
-    xi, xt = row_sets(image_feats, planes), row_sets(text_feats, planes)
-    mine, xi, xt = lax.optimization_barrier((mine, xi, xt))
+    column = (lax.axis_index("dp") // RING % 2).astype(jnp.int32)[None]
+    beside = [(i, i ^ RING) for i in range(dp)]
+    image_feats, text_feats, column, _ = lax.optimization_barrier((image_feats, text_feats, column, o0))
+    size = planes * 5 * (RING // 2)
+    xi, xt, away = pl.pallas_call(
+        order_kernel,
+        out_shape=tuple(jax.ShapeDtypeStruct((n, rows), BF16) for n in (size, size, 2 * size)),
+        in_specs=[scalars, array, array],
+        out_specs=(array,) * 3,
+        scratch_shapes=[pltpu.VMEM((depth, rows), F32)],
+        compiler_params=VMEM,
+        name="order",
+    )(column, image_feats, text_feats)
+    x_beside = lax.ppermute(away, "dp", beside)
+    mine, xi, xt, x_beside = lax.optimization_barrier((mine, xi, xt, x_beside))
     scores = pl.pallas_call(
         score_kernel,
         out_shape=jax.ShapeDtypeStruct((5 * rows + 16, rows), BF16),
@@ -236,24 +271,36 @@
         name="weights",
     )(numbers, scores, peer, o0, o1, o2, far)
     got = lax.ppermute(send, "tower", to_core)
-    parts = 2 * planes
+    slopes, send, loss = pl.pallas_call(
+        slope_kernel,
+        out_shape=(
+            jax.ShapeDtypeStruct((2 * width, 2 * rows), BF16),
+            jax.ShapeDtypeStruct((2 * width, rows), BF16),
+            jax.ShapeDtypeStruct((8, rows), F32),
+        ),
+        in_specs=[scalars] + [array] * 3,
+        out_specs=(array,) * 3,
+        compiler_params=VMEM,
+        name="slopes",
+    )(numbers, keep, got, z)
+    theirs = lax.ppermute(send, "dp", beside)
+    parts = planes
     block = xi.shape[0] // parts
     payload = 2 * (width // LANES) * block + -(-block // 32) * 16
-    grads, loss = pl.pallas_call(
+    grads = pl.pallas_call(
         functools.partial(gradient_kernel, parts),
-        out_shape=(
-            jax.ShapeDtypeStruct((parts, payload, LANES), BF16),
-            jax.ShapeDtypeStruct((8, rows), F32),
-        ),
-        in_specs=[scalars] + [array] * 5,
-        out_specs=(array, array),
+        out_shape=jax.ShapeDtypeStruct((parts, payload, LANES), BF16),
+        in_specs=[array] * 5,
+        out_specs=array,
         compiler_params=VMEM,
         name="gradients",
-    )(numbers, keep, got, z, xi, xt)
+    )(slopes, theirs, xi, xt, x_beside)
 
     places = RING // 2
     groups = [
-        [g * RING + 2 * m + q for g in range(planes) for q in range(2)] for m in range(places)
+        [(2 * y + x) * RING + 2 * m + q for y in range(planes // 2) for q in range(2)]
+        for x in range(2)
+        for m in range(places)
     ]
     grads = lax.all_to_all(grads, "dp", 0, 0, axis_index_groups=groups, tiled=True)
     sent = pl.pallas_call(

time: 130 us -> 127 us (0.977)
  blocking collectives: 28.7 us -> 15.1 us
  starting transfers between devices: 29.9 us -> 40.2 us
    all_to_all x1, blocking collectives: 28.7 us -> 15.1 us  [shards(): lax.all_to_all(grads, 'dp', 0, 0, axis_index_groups=groups, tiled=True)]
    ppermute x0 -> x2, starting transfers between devices: none -> 10.3 us  [the longest x1 7.58 us: shards(): theirs = lax.ppermute(send, 'dp', beside)]
    ppermute x0 -> x2, waiting for transfers between devices: none -> 4.14 us  [the longest x1 4.14 us: shards(): theirs = lax.ppermute(send, 'dp', beside)]
    ppermute x3, waiting for transfers between devices: 26.5 us -> 24.3 us  [shifted(): return lax.ppermute(block, ('dp', 'tower'), route)]
    all_to_all x1, waiting for transfers between devices: 24.9 us -> 23.5 us  [shards(): lax.all_to_all(sent, 'dp', 0, 0, axis_index_groups=groups, tiled=True)]
  transfers between devices with their start and end apart: 7 -> 9, of which waited for: 7 -> 8; matrix products, arithmetic and copies ran while one was open for 1% -> 1% of each run, Pallas kernels for 0% -> 0%
where the time goes in v7:
time: 127 us
  waiting for transfers between devices  58.7 us (46%)
  starting transfers between devices  40.2 us (32%)
  blocking collectives  15.1 us (12%)
  Pallas kernels  6.93 us (5%)
  between operations  2.19 us (2%)
  local copies, waits for them, and re-layouts  1.79 us (1%)
  other arithmetic  1.6 us (1%)
    ppermute x3, waiting for transfers between devices, shifted(): return lax.ppermute(block, ('dp', 'tower'), route)  24.3 us
    all_to_all x1, waiting for transfers between devices, shards(): lax.all_to_all(sent, 'dp', 0, 0, axis_index_groups=groups, tiled=True)  23.5 us
    all_to_all x1, blocking collectives, shards(): lax.all_to_all(grads, 'dp', 0, 0, axis_index_groups=groups, tiled=True)  15.1 us
    all_to_all x1, starting transfers between devices, shards(): lax.all_to_all(sent, 'dp', 0, 0, axis_index_groups=groups, tiled=True)  12 us
    ppermute x3, starting transfers between devices, shifted(): return lax.ppermute(block, ('dp', 'tower'), route)  11.1 us
    ppermute x1, starting transfers between devices, shards(): theirs = lax.ppermute(send, 'dp', beside)  7.58 us
    ppermute x1, waiting for transfers between devices, shards(): peer = lax.ppermute(scores, 'tower', to_chip)  4.78 us
    ppermute x1, waiting for transfers between devices, shards(): theirs = lax.ppermute(send, 'dp', beside)  4.14 us
  transfers between devices with their start and end apart: 9, of which 8 were waited for; matrix products, arithmetic and copies ran while one was open for 1% of the time, Pallas kernels for 0%

profile of v7, /device:TPU:6, one launch (start us, length us, event | category | flops | bytes accessed | tf_op | source)
XLA Modules:
  0.0 126.6 jit_solution(12248682020681744375)
XLA Ops:
  0.6 2.9 %project.1 = (f32[576,128]{1,0:T(8,128)}, bf16[576,128]{1,0:T(8,128)(2,1)}) custom-call(bf16[128,1152]{1,0:T(8,128)(2,1)} %xi.2, bf16[288,1152]{1,0:T(8,128)(2,1)} %bitcast.7, bf16[128,1152]{1,0:T(8,128)(2,1)} %xt.2, bf16[288,1152]{1,0:T(8,128)(2,1)} %bitcast.8), custom_call_target="tpu_custom_call" | custom-call | tf_op jit(solution)/shard_map/project/pallas_call | solution.py:221
  3.5 1.9 %collective-permute-start = (bf16[576,128]{1,0:T(8,128)(2,1)}, bf16[576,128]{1,0:T(8,128)(2,1)S(1)}, u32[]{:S(2)}, u32[]{:S(2)}) collective-permute-start(bf16[576,128]{1,0:T(8,128)(2,1)} %get-tuple-element.20), channel_id=1, source_target_pairs={{0,1},{1,0},{2,3},{3,2},{4,5},{5,4},{6,7},{7,6},{8,9},{9,8},{10,11... | collective-permute-start | bytes 442376 | tf_op jit(solution)/shard_map/ppermute | solution.py:233
  5.5 0.9 fusion.1
  6.4 0.6 collective-permute-done
  7.0 0.0 copy-start
  7.0 0.0 copy-start.1
  7.1 0.1 broadcast_select_fusion
  7.1 5.3 %collective-permute-start.3 = (bf16[576,128]{1,0:T(8,128)(2,1)S(1)}, bf16[576,128]{1,0:T(8,128)(2,1)S(1)}, u32[]{:S(2)}, u32[]{:S(2)}) collective-permute-start(bf16[576,128]{1,0:T(8,128)(2,1)S(1)} %get-tuple-element.37.o0), channel_id=1, source_target_pairs={{0,8},{1,1017},{2,10},{3,1019},{4,12},{5,1021},{6,14},{7,1023},{8,... | collective-permute-start | bytes 442376 | tf_op jit(solution)/shard_map/ppermute | solution.py:39
  12.4 3.8 %collective-permute-start.2 = (bf16[576,128]{1,0:T(8,128)(2,1)S(1)}, bf16[576,128]{1,0:T(8,128)(2,1)S(1)}, u32[]{:S(2)}, u32[]{:S(2)}) collective-permute-start(bf16[576,128]{1,0:T(8,128)(2,1)S(1)} %get-tuple-element.37.o0), channel_id=1, source_target_pairs={{0,4},{1,1021},{2,6},{3,1023},{4,8},{5,1},{6,10},{7,3},{8,12},{9,5... | collective-permute-start | bytes 442376 | tf_op jit(solution)/shard_map/ppermute | solution.py:39
  16.3 0.0 copy-done
  16.3 0.0 copy-done.1
  16.3 0.3 order.1
  16.7 2.7 %collective-permute-start.1 = (bf16[1280,128]{1,0:T(8,128)(2,1)S(1)}, bf16[1280,128]{1,0:T(8,128)(2,1)S(1)}, u32[]{:S(2)}, u32[]{:S(2)}) collective-permute-start(bf16[1280,128]{1,0:T(8,128)(2,1)S(1)} %get-tuple-element.26), channel_id=1, source_target_pairs={{0,128},{4,132},{8,136},{12,140},{16,144},{20,148},{24,152},{28,15... | collective-permute-start | bytes 983048 | tf_op jit(solution)/shard_map/ppermute | solution.py:253
  19.4 10.5 %collective-permute-done.3.o2 = bf16[576,128]{1,0:T(8,128)(2,1)S(1)} collective-permute-done((bf16[576,128]{1,0:T(8,128)(2,1)S(1)}, bf16[576,128]{1,0:T(8,128)(2,1)S(1)}, u32[]{:S(2)}, u32[]{:S(2)}) %collective-permute-start.3) | collective-permute-done | bytes 147488 | tf_op jit(solution)/shard_map/ppermute | solution.py:39
  29.9 2.6 %collective-permute-done.2.o1 = bf16[576,128]{1,0:T(8,128)(2,1)S(1)} collective-permute-done((bf16[576,128]{1,0:T(8,128)(2,1)S(1)}, bf16[576,128]{1,0:T(8,128)(2,1)S(1)}, u32[]{:S(2)}, u32[]{:S(2)}) %collective-permute-start.2) | collective-permute-done | bytes 147488 | tf_op jit(solution)/shard_map/ppermute | solution.py:39
  32.5 1.9 %collective-permute-start.4 = (bf16[1152,128]{1,0:T(8,128)(2,1)S(1)}, bf16[1152,128]{1,0:T(8,128)(2,1)S(1)}, u32[]{:S(2)}, u32[]{:S(2)}) collective-permute-start(bf16[1152,128]{1,0:T(8,128)(2,1)S(1)} %pad_maximum_fusion), channel_id=1, source_target_pairs={{0,8},{1,1017},{2,10},{3,1019},{4,12},{5,1021},{6,14},{7,1023},{8,... | collective-permute-start | bytes 884744 | tf_op jit(solution)/shard_map/ppermute | solution.py:39
  34.4 0.0 collective-permute-done.1.beside
  34.4 11.3 %collective-permute-done.4.far = bf16[1152,128]{1,0:T(8,128)(2,1)S(1)} collective-permute-done((bf16[1152,128]{1,0:T(8,128)(2,1)S(1)}, bf16[1152,128]{1,0:T(8,128)(2,1)S(1)}, u32[]{:S(2)}, u32[]{:S(2)}) %collective-permute-start.4) | collective-permute-done | bytes 294944 | tf_op jit(solution)/shard_map/ppermute | solution.py:39
  45.7 0.4 scores.1.mine
  46.1 3.0 %collective-permute-start.5 = (bf16[656,128]{1,0:T(8,128)(2,1)S(1)}, bf16[656,128]{1,0:T(8,128)(2,1)S(1)}, u32[]{:S(2)}, u32[]{:S(2)}) collective-permute-start(bf16[656,128]{1,0:T(8,128)(2,1)S(1)} %scores.1.mine), channel_id=1, source_target_pairs={{0,2},{1,3},{2,0},{3,1},{4,6},{5,7},{6,4},{7,5},{8,10},{9,11},{10,... | collective-permute-start | bytes 503816 | tf_op jit(solution)/shard_map/ppermute | solution.py:263
  50.5 0.1 pad_maximum_fusion.3.numbers
  50.5 0.0 copy-start.2
  50.5 4.8 %collective-permute-done.5.peer = bf16[656,128]{1,0:T(8,128)(2,1)S(1)} collective-permute-done((bf16[656,128]{1,0:T(8,128)(2,1)S(1)}, bf16[656,128]{1,0:T(8,128)(2,1)S(1)}, u32[]{:S(2)}, u32[]{:S(2)}) %collective-permute-start.5) | collective-permute-done | bytes 167968 | tf_op jit(solution)/shard_map/ppermute | solution.py:263
  55.3 1.4 %weights.1 = (f32[296,128]{1,0:T(8,128)S(1)}, f32[296,128]{1,0:T(8,128)S(1)}) custom-call(f32[3]{0:T(128)S(1)} %pad_maximum_fusion.3.numbers, bf16[656,128]{1,0:T(8,128)(2,1)S(1)} %scores.1.mine, bf16[656,128]{1,0:T(8,128)(2,1)S(1)} %collective-permute-done.5.peer, bf16[576,128]{1,0:T(8,128)(2,1)S(1)} %get-tuple-element.37.o0, ...), custom_call_target="tpu_custom_call" | custom-call | tf_op jit(solution)/shard_map/weights/pallas_call | solution.py:265
  56.8 1.9 %collective-permute-start.6 = (f32[296,128]{1,0:T(8,128)S(1)}, f32[296,128]{1,0:T(8,128)S(1)}, u32[]{:S(2)}, u32[]{:S(2)}) collective-permute-start(f32[296,128]{1,0:T(8,128)S(1)} %get-tuple-element.29), channel_id=1, source_target_pairs={{0,1},{1,0},{2,3},{3,2},{4,5},{5,4},{6,7},{7,6},{8,9},{9,8},{10,11... | collective-permute-start | bytes 454664 | tf_op jit(solution)/shard_map/ppermute | solution.py:273
  58.7 1.3 %collective-permute-done.6.got = f32[296,128]{1,0:T(8,128)S(1)} collective-permute-done((f32[296,128]{1,0:T(8,128)S(1)}, f32[296,128]{1,0:T(8,128)S(1)}, u32[]{:S(2)}, u32[]{:S(2)}) %collective-permute-start.6) | collective-permute-done | bytes 151584 | tf_op jit(solution)/shard_map/ppermute | solution.py:273
  60.0 0.0 copy-done.2
  60.0 0.6 slopes.1
  60.7 7.6 %collective-permute-start.7 = (bf16[576,128]{1,0:T(8,128)(2,1)S(1)}, bf16[576,128]{1,0:T(8,128)(2,1)S(1)}, u32[]{:S(2)}, u32[]{:S(2)}) collective-permute-start(bf16[576,128]{1,0:T(8,128)(2,1)S(1)} %get-tuple-element.33), channel_id=1, source_target_pairs={{0,128},{4,132},{8,136},{12,140},{16,144},{20,148},{24,152},{28,15... | collective-permute-start | bytes 442376 | tf_op jit(solution)/shard_map/ppermute | solution.py:286
  68.3 4.1 %collective-permute-done.7.theirs = bf16[576,128]{1,0:T(8,128)(2,1)S(1)} collective-permute-done((bf16[576,128]{1,0:T(8,128)(2,1)S(1)}, bf16[576,128]{1,0:T(8,128)(2,1)S(1)}, u32[]{:S(2)}, u32[]{:S(2)}) %collective-permute-start.7) | collective-permute-done | bytes 147488 | tf_op jit(solution)/shard_map/ppermute | solution.py:286
  72.4 0.8 gradients.1
  73.3 15.1 %all_to_all.10.got = bf16[8,368,128]{2,1,0:T(8,128)(2,1)S(1)} all-to-all(bf16[8,368,128]{2,1,0:T(8,128)(2,1)S(1)} %gradients.1), channel_id=1, replica_groups={{0,4,256,260,512,516,768,772},{8,12,264,268,520,524,776,780},{16,20,272..., dimensions={0} | all-to-all | bytes 1507328 | tf_op jit(solution)/shard_map/all_to_all | solution.py:305
  88.4 0.3 ring.1
  88.7 0.7 convert_element_type.7
  89.4 12.0 %all-to-all-start.1 = ((f16[16,24,128]{2,1,0:T(8,128)(2,1)}), f16[16,24,128]{2,1,0:T(8,128)(2,1)S(1)}, u32[]{:S(2)}, u32[]{:S(2)}) async-start(f16[16,24,128]{2,1,0:T(8,128)(2,1)} %convert_element_type.7), calls=%async_computation.1 | async-start | bytes 196608 | tf_op jit(solution)/shard_map/all_to_all | solution.py:318
  101.4 0.5 slice_bitcast_fusion
  102.0 23.5 %all-to-all-done.1 = f16[16,24,128]{2,1,0:T(8,128)(2,1)S(1)} async-done(((f16[16,24,128]{2,1,0:T(8,128)(2,1)}), f16[16,24,128]{2,1,0:T(8,128)(2,1)S(1)}, u32[]{:S(2)}, u32[]{:S(2)}) %all-to-all-start.1) | async-done | bytes 98336 | tf_op jit(solution)/shard_map/all_to_all | solution.py:318
  125.6 0.1 fusion.5
  125.6 0.1 fusion.4
  125.7 0.1 reshape.13
  125.8 0.1 reshape.12
  125.9 0.7 broadcast_select_fusion.2
  (8 shorter events, 0.1 us)
Async XLA Ops:
  3.5 3.5 %collective-permute-start = (bf16[576,128]{1,0:T(8,128)(2,1)}, bf16[576,128]{1,0:T(8,128)(2,1)S(1)}, u32[]{:S(2)}, u32[]{:S(2)}) collective-permute-start(bf16[576,128]{1,0:T(8,128)(2,1)} %get-tuple-element.20), channel_id=1, source_target_pairs={{0,1},{1,0},{2,3},{3,2},{4,5},{5,4},{6,7},{7,6},{8,9},{9,8},{10,11... | collective-permute-start | bytes 442376 | tf_op jit(solution)/shard_map/ppermute | solution.py:233
  7.0 9.3 %copy-start = (bf16[128,1152]{1,0:T(8,128)(2,1)S(1)}, bf16[128,1152]{1,0:T(8,128)(2,1)}, u32[]{:S(2)}) copy-start(bf16[128,1152]{1,0:T(8,128)(2,1)} %xi.2) | copy-start | bytes 884740
  7.0 9.3 %copy-start.1 = (bf16[128,1152]{1,0:T(8,128)(2,1)S(1)}, bf16[128,1152]{1,0:T(8,128)(2,1)}, u32[]{:S(2)}) copy-start(bf16[128,1152]{1,0:T(8,128)(2,1)} %xt.2) | copy-start | bytes 884740
  7.1 22.7 %collective-permute-start.3 = (bf16[576,128]{1,0:T(8,128)(2,1)S(1)}, bf16[576,128]{1,0:T(8,128)(2,1)S(1)}, u32[]{:S(2)}, u32[]{:S(2)}) collective-permute-start(bf16[576,128]{1,0:T(8,128)(2,1)S(1)} %get-tuple-element.37.o0), channel_id=1, source_target_pairs={{0,8},{1,1017},{2,10},{3,1019},{4,12},{5,1021},{6,14},{7,1023},{8,... | collective-permute-start | bytes 442376 | tf_op jit(solution)/shard_map/ppermute | solution.py:39
  12.4 20.0 %collective-permute-start.2 = (bf16[576,128]{1,0:T(8,128)(2,1)S(1)}, bf16[576,128]{1,0:T(8,128)(2,1)S(1)}, u32[]{:S(2)}, u32[]{:S(2)}) collective-permute-start(bf16[576,128]{1,0:T(8,128)(2,1)S(1)} %get-tuple-element.37.o0), channel_id=1, source_target_pairs={{0,4},{1,1021},{2,6},{3,1023},{4,8},{5,1},{6,10},{7,3},{8,12},{9,5... | collective-permute-start | bytes 442376 | tf_op jit(solution)/shard_map/ppermute | solution.py:39
  16.7 17.8 %collective-permute-start.1 = (bf16[1280,128]{1,0:T(8,128)(2,1)S(1)}, bf16[1280,128]{1,0:T(8,128)(2,1)S(1)}, u32[]{:S(2)}, u32[]{:S(2)}) collective-permute-start(bf16[1280,128]{1,0:T(8,128)(2,1)S(1)} %get-tuple-element.26), channel_id=1, source_target_pairs={{0,128},{4,132},{8,136},{12,140},{16,144},{20,148},{24,152},{28,15... | collective-permute-start | bytes 983048 | tf_op jit(solution)/shard_map/ppermute | solution.py:253
  32.5 13.2 %collective-permute-start.4 = (bf16[1152,128]{1,0:T(8,128)(2,1)S(1)}, bf16[1152,128]{1,0:T(8,128)(2,1)S(1)}, u32[]{:S(2)}, u32[]{:S(2)}) collective-permute-start(bf16[1152,128]{1,0:T(8,128)(2,1)S(1)} %pad_maximum_fusion), channel_id=1, source_target_pairs={{0,8},{1,1017},{2,10},{3,1019},{4,12},{5,1021},{6,14},{7,1023},{8,... | collective-permute-start | bytes 884744 | tf_op jit(solution)/shard_map/ppermute | solution.py:39
  46.1 9.2 %collective-permute-start.5 = (bf16[656,128]{1,0:T(8,128)(2,1)S(1)}, bf16[656,128]{1,0:T(8,128)(2,1)S(1)}, u32[]{:S(2)}, u32[]{:S(2)}) collective-permute-start(bf16[656,128]{1,0:T(8,128)(2,1)S(1)} %scores.1.mine), channel_id=1, source_target_pairs={{0,2},{1,3},{2,0},{3,1},{4,6},{5,7},{6,4},{7,5},{8,10},{9,11},{10,... | collective-permute-start | bytes 503816 | tf_op jit(solution)/shard_map/ppermute | solution.py:263
  50.5 9.5 %copy-start.2 = (f32[576,128]{1,0:T(8,128)S(1)}, f32[576,128]{1,0:T(8,128)}, u32[]{:S(2)}) copy-start(f32[576,128]{1,0:T(8,128)} %get-tuple-element.30.z) | copy-start | bytes 884740
  56.8 3.3 %collective-permute-start.6 = (f32[296,128]{1,0:T(8,128)S(1)}, f32[296,128]{1,0:T(8,128)S(1)}, u32[]{:S(2)}, u32[]{:S(2)}) collective-permute-start(f32[296,128]{1,0:T(8,128)S(1)} %get-tuple-element.29), channel_id=1, source_target_pairs={{0,1},{1,0},{2,3},{3,2},{4,5},{5,4},{6,7},{7,6},{8,9},{9,8},{10,11... | collective-permute-start | bytes 454664 | tf_op jit(solution)/shard_map/ppermute | solution.py:273
  60.7 11.7 %collective-permute-start.7 = (bf16[576,128]{1,0:T(8,128)(2,1)S(1)}, bf16[576,128]{1,0:T(8,128)(2,1)S(1)}, u32[]{:S(2)}, u32[]{:S(2)}) collective-permute-start(bf16[576,128]{1,0:T(8,128)(2,1)S(1)} %get-tuple-element.33), channel_id=1, source_target_pairs={{0,128},{4,132},{8,136},{12,140},{16,144},{20,148},{24,152},{28,15... | collective-permute-start | bytes 442376 | tf_op jit(solution)/shard_map/ppermute | solution.py:286
  89.4 36.1 %all-to-all-start.1 = ((f16[16,24,128]{2,1,0:T(8,128)(2,1)}), f16[16,24,128]{2,1,0:T(8,128)(2,1)S(1)}, u32[]{:S(2)}, u32[]{:S(2)}) async-start(f16[16,24,128]{2,1,0:T(8,128)(2,1)} %convert_element_type.7), calls=%async_computation.1 | async-start | bytes 196608 | tf_op jit(solution)/shard_map/all_to_all | solution.py:318

commit v8 on v7

--- a/solution.py
+++ b/solution.py
@@ -57,9 +57,8 @@
         own[side * width : (side + 1) * width] = part.astype(BF16)
 
 
-def score_kernel(own, o0, o1, o2, far, out):
-    size = own.shape[0]
-    blocks = [own[...], o0[...], o1[...], o2[...], far[:size], far[size:]]
+def score_kernel(own, o0, o1, o2, o3, o4, out):
+    blocks = [b[...] for b in (own, o0, o1, o2, o3, o4)]
     for j, other in enumerate(blocks[1:]):
         out[j * LANES : (j + 1) * LANES] = dot(other, blocks[0], 0, 0).astype(BF16)
     squares = [jnp.sum(jnp.square(b.astype(F32)), axis=0, keepdims=True) for b in blocks]
@@ -69,10 +68,9 @@
     out[5 * LANES :] = jnp.concatenate((high, low), axis=0).astype(BF16)
 
 
-def weight_kernel(numbers, mine, peer, o0, o1, o2, far, send, keep):
+def weight_kernel(numbers, mine, peer, o0, o1, o2, o3, o4, send, keep):
     scale, bias = numbers[0], numbers[1]
-    size = o0.shape[0]
-    width = size // 2
+    width = o0.shape[0] // 2
 
     def total(start, rows):
         a = mine[start : start + rows].astype(F32)
@@ -88,7 +86,7 @@
     n = inv[0:1]
     loss = along = jnp.zeros_like(n)
     d = None
-    for j, other in enumerate((o0[...], o1[...], o2[...], far[:size], far[size:])):
+    for j, other in enumerate((o0, o1, o2, o3, o4)):
         col = down[:, j + 1 : j + 2]
         c = scale * (total(j * LANES, LANES) * n * col)
         s = c + bias
@@ -99,7 +97,7 @@
             signed, g = (1.0 - 2.0 * eye) * s, g - eye
         loss += jnp.sum(jnp.maximum(signed, 0.0) + jnp.log1p(e), axis=0, keepdims=True)
         along += jnp.sum(g * c, axis=0, keepdims=True)
-        term = fine(other, g * col)
+        term = fine(other[...], g * col)
         d = term if d is None else d + term
     lines = jnp.concatenate((along, loss, n, jnp.zeros((5, LANES), F32)), axis=0)
     keep[:width], send[:width] = d[:width], d[width:]
@@ -234,12 +232,13 @@
     i0 = jnp.concatenate((own[:width], other[:width]), axis=0)
     t0 = jnp.concatenate((own[width:], other[width:]), axis=0)
     mine, o0 = jnp.where(first, i0, t0), jnp.where(first, t0, i0)
+    o2 = shifted(o0, (2, -2))
     o1 = shifted(o0, (1, -1))
-    o2 = shifted(o0, (2, -2))
-    far = shifted(jnp.concatenate((o1, o2), axis=0), (2, -2))
+    o4 = shifted(o2, (2, -2))
+    o3 = shifted(o1, (2, -2))
     column = (lax.axis_index("dp") // RING % 2).astype(jnp.int32)[None]
     beside = [(i, i ^ RING) for i in range(dp)]
-    image_feats, text_feats, column, _ = lax.optimization_barrier((image_feats, text_feats, column, o0))
+    image_feats, text_feats, column = lax.optimization_barrier((image_feats, text_feats, column, o0))[:3]
     size = planes * 5 * (RING // 2)
     xi, xt, away = pl.pallas_call(
         order_kernel,
@@ -251,25 +250,25 @@
         name="order",
     )(column, image_feats, text_feats)
     x_beside = lax.ppermute(away, "dp", beside)
-    mine, xi, xt, x_beside = lax.optimization_barrier((mine, xi, xt, x_beside))
+
     scores = pl.pallas_call(
         score_kernel,
         out_shape=jax.ShapeDtypeStruct((5 * rows + 16, rows), BF16),
-        in_specs=[array] * 5,
+        in_specs=[array] * 6,
         out_specs=array,
         compiler_params=VMEM,
         name="scores",
-    )(mine, o0, o1, o2, far)
+    )(mine, o0, o1, o2, o3, o4)
     peer = lax.ppermute(scores, "tower", to_chip)
     sums = jax.ShapeDtypeStruct((width + 8, rows), F32)
     send, keep = pl.pallas_call(
         weight_kernel,
         out_shape=(sums, sums),
-        in_specs=[scalars] + [array] * 6,
+        in_specs=[scalars] + [array] * 7,
         out_specs=(array, array),
         compiler_params=VMEM,
         name="weights",
-    )(numbers, scores, peer, o0, o1, o2, far)
+    )(numbers, scores, lax.optimization_barrier((peer, x_beside))[0], o0, o1, o2, o3, o4)
     got = lax.ppermute(send, "tower", to_core)
     slopes, send, loss = pl.pallas_call(
         slope_kernel,

time: 127 us -> 126 us (level)
  waiting for transfers between devices: 58.7 us -> 55.1 us
  starting transfers between devices: 40.2 us -> 42.7 us
    ppermute x3 -> x4, waiting for transfers between devices: 24.3 us -> 21.1 us  [shifted(): return lax.ppermute(block, ('dp', 'tower'), route)]
    ppermute x3 -> x4, starting transfers between devices: 11.1 us -> 13 us  [shifted(): return lax.ppermute(block, ('dp', 'tower'), route)]
  transfers between devices with their start and end apart: 9 -> 10, of which waited for: 8 -> 9; matrix products, arithmetic and copies ran while one was open for 1% -> 1% of each run, Pallas kernels for 0% -> 1%
where the time goes in v8:
time: 126 us; the launch traced here: 125 us
  waiting for transfers between devices  55.1 us (44%)
  starting transfers between devices  42.7 us (34%)
  blocking collectives  15.1 us (12%)
  Pallas kernels  6.91 us (5%)
  between operations  2.19 us (2%)
  local copies, waits for them, and re-layouts  1.79 us (1%)
  other arithmetic  1.58 us (1%)
    all_to_all x1, waiting for transfers between devices, shards(): lax.all_to_all(sent, 'dp', 0, 0, axis_index_groups=groups, tiled=True)  23.5 us
    ppermute x4, waiting for transfers between devices, shifted(): return lax.ppermute(block, ('dp', 'tower'), route)  21.1 us
    all_to_all x1, blocking collectives, shards(): lax.all_to_all(grads, 'dp', 0, 0, axis_index_groups=groups, tiled=True)  15.1 us
    ppermute x4, starting transfers between devices, shifted(): return lax.ppermute(block, ('dp', 'tower'), route)  13 us
    all_to_all x1, starting transfers between devices, shards(): lax.all_to_all(sent, 'dp', 0, 0, axis_index_groups=groups, tiled=True)  12.6 us
    ppermute x1, starting transfers between devices, shards(): theirs = lax.ppermute(send, 'dp', beside)  6.33 us
    ppermute x1, waiting for transfers between devices, shards(): peer = lax.ppermute(scores, 'tower', to_chip)  4.77 us
    ppermute x1, waiting for transfers between devices, shards(): theirs = lax.ppermute(send, 'dp', beside)  4.14 us
  transfers between devices with their start and end apart: 10, of which 9 were waited for; matrix products, arithmetic and copies ran while one was open for 1% of the time, Pallas kernels for 1%

profile of v8, /device:TPU:6, one launch (start us, length us, event | category | flops | bytes accessed | tf_op | source)
XLA Modules:
  0.0 125.4 jit_solution(16636362580511973929)
XLA Ops:
  0.6 2.9 %project.1 = (f32[576,128]{1,0:T(8,128)}, bf16[576,128]{1,0:T(8,128)(2,1)}) custom-call(bf16[128,1152]{1,0:T(8,128)(2,1)} %xi.2, bf16[288,1152]{1,0:T(8,128)(2,1)} %bitcast.7, bf16[128,1152]{1,0:T(8,128)(2,1)} %xt.2, bf16[288,1152]{1,0:T(8,128)(2,1)} %bitcast.8), custom_call_target="tpu_custom_call" | custom-call | tf_op jit(solution)/shard_map/project/pallas_call | solution.py:219
  3.5 1.9 %collective-permute-start = (bf16[576,128]{1,0:T(8,128)(2,1)}, bf16[576,128]{1,0:T(8,128)(2,1)S(1)}, u32[]{:S(2)}, u32[]{:S(2)}) collective-permute-start(bf16[576,128]{1,0:T(8,128)(2,1)} %get-tuple-element.17), channel_id=1, source_target_pairs={{0,1},{1,0},{2,3},{3,2},{4,5},{5,4},{6,7},{7,6},{8,9},{9,8},{10,11... | collective-permute-start | bytes 442376 | tf_op jit(solution)/shard_map/ppermute | solution.py:231
  5.5 0.9 fusion.1
  6.4 0.6 collective-permute-done
  7.0 0.0 copy-start
  7.0 0.0 copy-start.1
  7.0 0.1 broadcast_select_fusion
  7.1 4.0 %collective-permute-start.1 = (bf16[576,128]{1,0:T(8,128)(2,1)S(1)}, bf16[576,128]{1,0:T(8,128)(2,1)S(1)}, u32[]{:S(2)}, u32[]{:S(2)}) collective-permute-start(bf16[576,128]{1,0:T(8,128)(2,1)S(1)} %get-tuple-element.31.o0), channel_id=1, source_target_pairs={{0,4},{1,1021},{2,6},{3,1023},{4,8},{5,1},{6,10},{7,3},{8,12},{9,5... | collective-permute-start | bytes 442376 | tf_op jit(solution)/shard_map/ppermute | solution.py:39
  11.1 5.2 %collective-permute-start.2 = (bf16[576,128]{1,0:T(8,128)(2,1)S(1)}, bf16[576,128]{1,0:T(8,128)(2,1)S(1)}, u32[]{:S(2)}, u32[]{:S(2)}) collective-permute-start(bf16[576,128]{1,0:T(8,128)(2,1)S(1)} %get-tuple-element.31.o0), channel_id=1, source_target_pairs={{0,8},{1,1017},{2,10},{3,1019},{4,12},{5,1021},{6,14},{7,1023},{8,... | collective-permute-start | bytes 442376 | tf_op jit(solution)/shard_map/ppermute | solution.py:39
  16.3 0.0 copy-done
  16.3 0.0 copy-done.1
  16.3 0.3 order.1
  16.6 2.7 %collective-permute-start.6 = (bf16[1280,128]{1,0:T(8,128)(2,1)S(1)}, bf16[1280,128]{1,0:T(8,128)(2,1)S(1)}, u32[]{:S(2)}, u32[]{:S(2)}) collective-permute-start(bf16[1280,128]{1,0:T(8,128)(2,1)S(1)} %get-tuple-element.21), channel_id=1, source_target_pairs={{0,128},{4,132},{8,136},{12,140},{16,144},{20,148},{24,152},{28,15... | collective-permute-start | bytes 983048 | tf_op jit(solution)/shard_map/ppermute | solution.py:252
  19.4 9.9 %collective-permute-done.1.o1 = bf16[576,128]{1,0:T(8,128)(2,1)S(1)} collective-permute-done((bf16[576,128]{1,0:T(8,128)(2,1)S(1)}, bf16[576,128]{1,0:T(8,128)(2,1)S(1)}, u32[]{:S(2)}, u32[]{:S(2)}) %collective-permute-start.1) | collective-permute-done | bytes 147488 | tf_op jit(solution)/shard_map/ppermute | solution.py:39
  29.3 1.9 %collective-permute-start.3 = (bf16[576,128]{1,0:T(8,128)(2,1)S(1)}, bf16[576,128]{1,0:T(8,128)(2,1)S(1)}, u32[]{:S(2)}, u32[]{:S(2)}) collective-permute-start(bf16[576,128]{1,0:T(8,128)(2,1)S(1)} %collective-permute-done.1.o1), channel_id=1, source_target_pairs={{0,8},{1,1017},{2,10},{3,1019},{4,12},{5,1021},{6,14},{7,1023},{8,... | collective-permute-start | bytes 442376 | tf_op jit(solution)/shard_map/ppermute | solution.py:39
  31.2 3.0 %collective-permute-done.2.o2 = bf16[576,128]{1,0:T(8,128)(2,1)S(1)} collective-permute-done((bf16[576,128]{1,0:T(8,128)(2,1)S(1)}, bf16[576,128]{1,0:T(8,128)(2,1)S(1)}, u32[]{:S(2)}, u32[]{:S(2)}) %collective-permute-start.2) | collective-permute-done | bytes 147488 | tf_op jit(solution)/shard_map/ppermute | solution.py:39
  34.2 1.9 %collective-permute-start.4 = (bf16[576,128]{1,0:T(8,128)(2,1)S(1)}, bf16[576,128]{1,0:T(8,128)(2,1)S(1)}, u32[]{:S(2)}, u32[]{:S(2)}) collective-permute-start(bf16[576,128]{1,0:T(8,128)(2,1)S(1)} %collective-permute-done.2.o2), channel_id=1, source_target_pairs={{0,8},{1,1017},{2,10},{3,1019},{4,12},{5,1021},{6,14},{7,1023},{8,... | collective-permute-start | bytes 442376 | tf_op jit(solution)/shard_map/ppermute | solution.py:39
  36.1 4.6 %collective-permute-done.3.o3 = bf16[576,128]{1,0:T(8,128)(2,1)S(1)} collective-permute-done((bf16[576,128]{1,0:T(8,128)(2,1)S(1)}, bf16[576,128]{1,0:T(8,128)(2,1)S(1)}, u32[]{:S(2)}, u32[]{:S(2)}) %collective-permute-start.3) | collective-permute-done | bytes 147488 | tf_op jit(solution)/shard_map/ppermute | solution.py:39
  40.7 3.6 %collective-permute-done.4.o4 = bf16[576,128]{1,0:T(8,128)(2,1)S(1)} collective-permute-done((bf16[576,128]{1,0:T(8,128)(2,1)S(1)}, bf16[576,128]{1,0:T(8,128)(2,1)S(1)}, u32[]{:S(2)}, u32[]{:S(2)}) %collective-permute-start.4) | collective-permute-done | bytes 147488 | tf_op jit(solution)/shard_map/ppermute | solution.py:39
  44.3 0.4 scores.1.mine
  44.7 3.3 %collective-permute-start.5 = (bf16[656,128]{1,0:T(8,128)(2,1)S(1)}, bf16[656,128]{1,0:T(8,128)(2,1)S(1)}, u32[]{:S(2)}, u32[]{:S(2)}) collective-permute-start(bf16[656,128]{1,0:T(8,128)(2,1)S(1)} %scores.1.mine), channel_id=1, source_target_pairs={{0,2},{1,3},{2,0},{3,1},{4,6},{5,7},{6,4},{7,5},{8,10},{9,11},{10,... | collective-permute-start | bytes 503816 | tf_op jit(solution)/shard_map/ppermute | solution.py:262
  49.3 0.1 pad_maximum_fusion.2.numbers
  49.4 0.0 copy-start.2
  49.4 0.0 collective-permute-done.6.beside
  49.4 4.8 %collective-permute-done.5.peer = bf16[656,128]{1,0:T(8,128)(2,1)S(1)} collective-permute-done((bf16[656,128]{1,0:T(8,128)(2,1)S(1)}, bf16[656,128]{1,0:T(8,128)(2,1)S(1)}, u32[]{:S(2)}, u32[]{:S(2)}) %collective-permute-start.5) | collective-permute-done | bytes 167968 | tf_op jit(solution)/shard_map/ppermute | solution.py:262
  54.2 1.4 %weights.1 = (f32[296,128]{1,0:T(8,128)S(1)}, f32[296,128]{1,0:T(8,128)S(1)}) custom-call(f32[3]{0:T(128)S(1)} %pad_maximum_fusion.2.numbers, bf16[656,128]{1,0:T(8,128)(2,1)S(1)} %scores.1.mine, bf16[656,128]{1,0:T(8,128)(2,1)S(1)} %collective-permute-done.5.peer, bf16[576,128]{1,0:T(8,128)(2,1)S(1)} %get-tuple-element.31.o0, ...), custom_call_target="tpu_custom_call" | custom-call | tf_op jit(solution)/shard_map/weights/pallas_call | solution.py:264
  55.6 2.8 %collective-permute-start.7 = (f32[296,128]{1,0:T(8,128)S(1)}, f32[296,128]{1,0:T(8,128)S(1)}, u32[]{:S(2)}, u32[]{:S(2)}) collective-permute-start(f32[296,128]{1,0:T(8,128)S(1)} %get-tuple-element.24), channel_id=1, source_target_pairs={{0,1},{1,0},{2,3},{3,2},{4,5},{5,4},{6,7},{7,6},{8,9},{9,8},{10,11... | collective-permute-start | bytes 454664 | tf_op jit(solution)/shard_map/ppermute | solution.py:272
  58.5 1.0 collective-permute-done.7.got
  59.5 0.0 copy-done.2
  59.5 0.6 slopes.1
  60.1 6.3 %collective-permute-start.8 = (bf16[576,128]{1,0:T(8,128)(2,1)S(1)}, bf16[576,128]{1,0:T(8,128)(2,1)S(1)}, u32[]{:S(2)}, u32[]{:S(2)}) collective-permute-start(bf16[576,128]{1,0:T(8,128)(2,1)S(1)} %get-tuple-element.28), channel_id=1, source_target_pairs={{0,128},{4,132},{8,136},{12,140},{16,144},{20,148},{24,152},{28,15... | collective-permute-start | bytes 442376 | tf_op jit(solution)/shard_map/ppermute | solution.py:285
  66.5 4.1 %collective-permute-done.8.theirs = bf16[576,128]{1,0:T(8,128)(2,1)S(1)} collective-permute-done((bf16[576,128]{1,0:T(8,128)(2,1)S(1)}, bf16[576,128]{1,0:T(8,128)(2,1)S(1)}, u32[]{:S(2)}, u32[]{:S(2)}) %collective-permute-start.8) | collective-permute-done | bytes 147488 | tf_op jit(solution)/shard_map/ppermute | solution.py:285
  70.6 0.9 gradients.1
  71.5 15.1 %all_to_all.10.got = bf16[8,368,128]{2,1,0:T(8,128)(2,1)S(1)} all-to-all(bf16[8,368,128]{2,1,0:T(8,128)(2,1)S(1)} %gradients.1), channel_id=1, replica_groups={{0,4,256,260,512,516,768,772},{8,12,264,268,520,524,776,780},{16,20,272..., dimensions={0} | all-to-all | bytes 1507328 | tf_op jit(solution)/shard_map/all_to_all | solution.py:304
  86.6 0.3 ring.1
  86.9 0.7 convert_element_type.7
  87.6 12.6 %all-to-all-start.1 = ((f16[16,24,128]{2,1,0:T(8,128)(2,1)}), f16[16,24,128]{2,1,0:T(8,128)(2,1)S(1)}, u32[]{:S(2)}, u32[]{:S(2)}) async-start(f16[16,24,128]{2,1,0:T(8,128)(2,1)} %convert_element_type.7), calls=%async_computation.1 | async-start | bytes 196608 | tf_op jit(solution)/shard_map/all_to_all | solution.py:317
  100.2 0.5 slice_bitcast_fusion
  100.7 23.5 %all-to-all-done.1 = f16[16,24,128]{2,1,0:T(8,128)(2,1)S(1)} async-done(((f16[16,24,128]{2,1,0:T(8,128)(2,1)}), f16[16,24,128]{2,1,0:T(8,128)(2,1)S(1)}, u32[]{:S(2)}, u32[]{:S(2)}) %all-to-all-start.1) | async-done | bytes 98336 | tf_op jit(solution)/shard_map/all_to_all | solution.py:317
  124.4 0.1 fusion.4
  124.4 0.1 fusion.5
  124.5 0.1 reshape.12
  124.6 0.1 reshape.13
  124.7 0.7 broadcast_select_fusion.2
  (7 shorter events, 0.1 us)
Async XLA Ops:
  3.5 3.5 %collective-permute-start = (bf16[576,128]{1,0:T(8,128)(2,1)}, bf16[576,128]{1,0:T(8,128)(2,1)S(1)}, u32[]{:S(2)}, u32[]{:S(2)}) collective-permute-start(bf16[576,128]{1,0:T(8,128)(2,1)} %get-tuple-element.17), channel_id=1, source_target_pairs={{0,1},{1,0},{2,3},{3,2},{4,5},{5,4},{6,7},{7,6},{8,9},{9,8},{10,11... | collective-permute-start | bytes 442376 | tf_op jit(solution)/shard_map/ppermute | solution.py:231
  7.0 9.3 %copy-start = (bf16[128,1152]{1,0:T(8,128)(2,1)S(1)}, bf16[128,1152]{1,0:T(8,128)(2,1)}, u32[]{:S(2)}) copy-start(bf16[128,1152]{1,0:T(8,128)(2,1)} %xi.2) | copy-start | bytes 884740
  7.0 9.3 %copy-start.1 = (bf16[128,1152]{1,0:T(8,128)(2,1)S(1)}, bf16[128,1152]{1,0:T(8,128)(2,1)}, u32[]{:S(2)}) copy-start(bf16[128,1152]{1,0:T(8,128)(2,1)} %xt.2) | copy-start | bytes 884740
  7.1 22.2 %collective-permute-start.1 = (bf16[576,128]{1,0:T(8,128)(2,1)S(1)}, bf16[576,128]{1,0:T(8,128)(2,1)S(1)}, u32[]{:S(2)}, u32[]{:S(2)}) collective-permute-start(bf16[576,128]{1,0:T(8,128)(2,1)S(1)} %get-tuple-element.31.o0), channel_id=1, source_target_pairs={{0,4},{1,1021},{2,6},{3,1023},{4,8},{5,1},{6,10},{7,3},{8,12},{9,5... | collective-permute-start | bytes 442376 | tf_op jit(solution)/shard_map/ppermute | solution.py:39
  11.1 23.1 %collective-permute-start.2 = (bf16[576,128]{1,0:T(8,128)(2,1)S(1)}, bf16[576,128]{1,0:T(8,128)(2,1)S(1)}, u32[]{:S(2)}, u32[]{:S(2)}) collective-permute-start(bf16[576,128]{1,0:T(8,128)(2,1)S(1)} %get-tuple-element.31.o0), channel_id=1, source_target_pairs={{0,8},{1,1017},{2,10},{3,1019},{4,12},{5,1021},{6,14},{7,1023},{8,... | collective-permute-start | bytes 442376 | tf_op jit(solution)/shard_map/ppermute | solution.py:39
  16.6 32.8 %collective-permute-start.6 = (bf16[1280,128]{1,0:T(8,128)(2,1)S(1)}, bf16[1280,128]{1,0:T(8,128)(2,1)S(1)}, u32[]{:S(2)}, u32[]{:S(2)}) collective-permute-start(bf16[1280,128]{1,0:T(8,128)(2,1)S(1)} %get-tuple-element.21), channel_id=1, source_target_pairs={{0,128},{4,132},{8,136},{12,140},{16,144},{20,148},{24,152},{28,15... | collective-permute-start | bytes 983048 | tf_op jit(solution)/shard_map/ppermute | solution.py:252
  29.3 11.4 %collective-permute-start.3 = (bf16[576,128]{1,0:T(8,128)(2,1)S(1)}, bf16[576,128]{1,0:T(8,128)(2,1)S(1)}, u32[]{:S(2)}, u32[]{:S(2)}) collective-permute-start(bf16[576,128]{1,0:T(8,128)(2,1)S(1)} %collective-permute-done.1.o1), channel_id=1, source_target_pairs={{0,8},{1,1017},{2,10},{3,1019},{4,12},{5,1021},{6,14},{7,1023},{8,... | collective-permute-start | bytes 442376 | tf_op jit(solution)/shard_map/ppermute | solution.py:39
  34.2 10.1 %collective-permute-start.4 = (bf16[576,128]{1,0:T(8,128)(2,1)S(1)}, bf16[576,128]{1,0:T(8,128)(2,1)S(1)}, u32[]{:S(2)}, u32[]{:S(2)}) collective-permute-start(bf16[576,128]{1,0:T(8,128)(2,1)S(1)} %collective-permute-done.2.o2), channel_id=1, source_target_pairs={{0,8},{1,1017},{2,10},{3,1019},{4,12},{5,1021},{6,14},{7,1023},{8,... | collective-permute-start | bytes 442376 | tf_op jit(solution)/shard_map/ppermute | solution.py:39
  44.7 9.5 %collective-permute-start.5 = (bf16[656,128]{1,0:T(8,128)(2,1)S(1)}, bf16[656,128]{1,0:T(8,128)(2,1)S(1)}, u32[]{:S(2)}, u32[]{:S(2)}) collective-permute-start(bf16[656,128]{1,0:T(8,128)(2,1)S(1)} %scores.1.mine), channel_id=1, source_target_pairs={{0,2},{1,3},{2,0},{3,1},{4,6},{5,7},{6,4},{7,5},{8,10},{9,11},{10,... | collective-permute-start | bytes 503816 | tf_op jit(solution)/shard_map/ppermute | solution.py:262
  49.4 10.0 %copy-start.2 = (f32[576,128]{1,0:T(8,128)S(1)}, f32[576,128]{1,0:T(8,128)}, u32[]{:S(2)}) copy-start(f32[576,128]{1,0:T(8,128)} %get-tuple-element.25.z) | copy-start | bytes 884740
  55.6 3.8 %collective-permute-start.7 = (f32[296,128]{1,0:T(8,128)S(1)}, f32[296,128]{1,0:T(8,128)S(1)}, u32[]{:S(2)}, u32[]{:S(2)}) collective-permute-start(f32[296,128]{1,0:T(8,128)S(1)} %get-tuple-element.24), channel_id=1, source_target_pairs={{0,1},{1,0},{2,3},{3,2},{4,5},{5,4},{6,7},{7,6},{8,9},{9,8},{10,11... | collective-permute-start | bytes 454664 | tf_op jit(solution)/shard_map/ppermute | solution.py:272
  60.1 10.5 %collective-permute-start.8 = (bf16[576,128]{1,0:T(8,128)(2,1)S(1)}, bf16[576,128]{1,0:T(8,128)(2,1)S(1)}, u32[]{:S(2)}, u32[]{:S(2)}) collective-permute-start(bf16[576,128]{1,0:T(8,128)(2,1)S(1)} %get-tuple-element.28), channel_id=1, source_target_pairs={{0,128},{4,132},{8,136},{12,140},{16,144},{20,148},{24,152},{28,15... | collective-permute-start | bytes 442376 | tf_op jit(solution)/shard_map/ppermute | solution.py:285
  87.6 36.7 %all-to-all-start.1 = ((f16[16,24,128]{2,1,0:T(8,128)(2,1)}), f16[16,24,128]{2,1,0:T(8,128)(2,1)S(1)}, u32[]{:S(2)}, u32[]{:S(2)}) async-start(f16[16,24,128]{2,1,0:T(8,128)(2,1)} %convert_element_type.7), calls=%async_computation.1 | async-start | bytes 196608 | tf_op jit(solution)/shard_map/all_to_all | solution.py:317

commit v9 on v8

--- a/solution.py
+++ b/solution.py
@@ -238,7 +238,7 @@
     o3 = shifted(o1, (2, -2))
     column = (lax.axis_index("dp") // RING % 2).astype(jnp.int32)[None]
     beside = [(i, i ^ RING) for i in range(dp)]
-    image_feats, text_feats, column = lax.optimization_barrier((image_feats, text_feats, column, o0))[:3]
+    image_feats, text_feats, column = lax.optimization_barrier((image_feats, text_feats, column, o1))[:3]
     size = planes * 5 * (RING // 2)
     xi, xt, away = pl.pallas_call(
         order_kernel,
@@ -250,7 +250,6 @@
         name="order",
     )(column, image_feats, text_feats)
     x_beside = lax.ppermute(away, "dp", beside)
-
     scores = pl.pallas_call(
         score_kernel,
         out_shape=jax.ShapeDtypeStruct((5 * rows + 16, rows), BF16),
@@ -268,8 +267,9 @@
         out_specs=(array, array),
         compiler_params=VMEM,
         name="weights",
-    )(numbers, scores, lax.optimization_barrier((peer, x_beside))[0], o0, o1, o2, o3, o4)
+    )(numbers, scores, peer, o0, o1, o2, o3, o4)
     got = lax.ppermute(send, "tower", to_core)
+    got, x_beside = lax.optimization_barrier((got, x_beside))
     slopes, send, loss = pl.pallas_call(
         slope_kernel,
         out_shape=(

time: 126 us -> 127 us (level)
  starting transfers between devices: 42.7 us -> 45 us
  waiting for transfers between devices: 55.1 us -> 53 us
    ppermute x4, waiting for transfers between devices: 21.1 us -> 17.5 us  [shifted(): return lax.ppermute(block, ('dp', 'tower'), route)]
    ppermute x1, starting transfers between devices: 2.73 us -> 5.55 us  [shards(): x_beside = lax.ppermute(away, 'dp', beside)]
    ppermute x1, waiting for transfers between devices: 4.77 us -> 6.22 us  [shards(): peer = lax.ppermute(scores, 'tower', to_chip)]
  transfers between devices with their start and end apart: 10 -> 10, of which waited for: 9 -> 8; matrix products, arithmetic and copies ran while one was open for 1% -> 1% of each run, Pallas kernels for 1% -> 2%
where the time goes in v9:
time: 127 us; the launch traced here: 126 us
  waiting for transfers between devices  53 us (42%)
  starting transfers between devices  45 us (35%)
  blocking collectives  15.9 us (13%)
  Pallas kernels  6.92 us (5%)
  between operations  2.2 us (2%)
  local copies, waits for them, and re-layouts  1.79 us (1%)
  other arithmetic  1.58 us (1%)
    all_to_all x1, waiting for transfers between devices, shards(): lax.all_to_all(sent, 'dp', 0, 0, axis_index_groups=groups, tiled=True)  23.5 us
    ppermute x4, waiting for transfers between devices, shifted(): return lax.ppermute(block, ('dp', 'tower'), route)  17.5 us
    all_to_all x1, blocking collectives, shards(): lax.all_to_all(grads, 'dp', 0, 0, axis_index_groups=groups, tiled=True)  15.9 us
    ppermute x4, starting transfers between devices, shifted(): return lax.ppermute(block, ('dp', 'tower'), route)  13 us
    all_to_all x1, starting transfers between devices, shards(): lax.all_to_all(sent, 'dp', 0, 0, axis_index_groups=groups, tiled=True)  12.4 us
    ppermute x1, waiting for transfers between devices, shards(): peer = lax.ppermute(scores, 'tower', to_chip)  6.22 us
    ppermute x1, starting transfers between devices, shards(): theirs = lax.ppermute(send, 'dp', beside)  5.98 us
    ppermute x1, starting transfers between devices, shards(): x_beside = lax.ppermute(away, 'dp', beside)  5.55 us
  transfers between devices with their start and end apart: 10, of which 8 were waited for; matrix products, arithmetic and copies ran while one was open for 1% of the time, Pallas kernels for 2%

profile of v9, /device:TPU:6, one launch (start us, length us, event | category | flops | bytes accessed | tf_op | source)
XLA Modules:
  0.0 126.4 jit_solution(379300015764488713)
XLA Ops:
  0.6 2.9 %project.1 = (f32[576,128]{1,0:T(8,128)}, bf16[576,128]{1,0:T(8,128)(2,1)}) custom-call(bf16[128,1152]{1,0:T(8,128)(2,1)} %xi.2, bf16[288,1152]{1,0:T(8,128)(2,1)} %bitcast.7, bf16[128,1152]{1,0:T(8,128)(2,1)} %xt.2, bf16[288,1152]{1,0:T(8,128)(2,1)} %bitcast.8), custom_call_target="tpu_custom_call" | custom-call | tf_op jit(solution)/shard_map/project/pallas_call | solution.py:219
  3.5 1.9 %collective-permute-start = (bf16[576,128]{1,0:T(8,128)(2,1)}, bf16[576,128]{1,0:T(8,128)(2,1)S(1)}, u32[]{:S(2)}, u32[]{:S(2)}) collective-permute-start(bf16[576,128]{1,0:T(8,128)(2,1)} %get-tuple-element.18), channel_id=1, source_target_pairs={{0,1},{1,0},{2,3},{3,2},{4,5},{5,4},{6,7},{7,6},{8,9},{9,8},{10,11... | collective-permute-start | bytes 442376 | tf_op jit(solution)/shard_map/ppermute | solution.py:231
  5.5 0.9 fusion.1
  6.4 0.6 collective-permute-done
  7.0 0.0 copy-start
  7.0 0.0 copy-start.1
  7.0 0.1 broadcast_select_fusion
  7.1 5.3 %collective-permute-start.2 = (bf16[576,128]{1,0:T(8,128)(2,1)S(1)}, bf16[576,128]{1,0:T(8,128)(2,1)S(1)}, u32[]{:S(2)}, u32[]{:S(2)}) collective-permute-start(bf16[576,128]{1,0:T(8,128)(2,1)S(1)} %get-tuple-element.33.o0), channel_id=1, source_target_pairs={{0,8},{1,1017},{2,10},{3,1019},{4,12},{5,1021},{6,14},{7,1023},{8,... | collective-permute-start | bytes 442376 | tf_op jit(solution)/shard_map/ppermute | solution.py:39
  12.4 3.8 %collective-permute-start.1 = (bf16[576,128]{1,0:T(8,128)(2,1)S(1)}, bf16[576,128]{1,0:T(8,128)(2,1)S(1)}, u32[]{:S(2)}, u32[]{:S(2)}) collective-permute-start(bf16[576,128]{1,0:T(8,128)(2,1)S(1)} %get-tuple-element.33.o0), channel_id=1, source_target_pairs={{0,4},{1,1021},{2,6},{3,1023},{4,8},{5,1},{6,10},{7,3},{8,12},{9,5... | collective-permute-start | bytes 442376 | tf_op jit(solution)/shard_map/ppermute | solution.py:39
  16.3 13.6 %collective-permute-done.2.o2 = bf16[576,128]{1,0:T(8,128)(2,1)S(1)} collective-permute-done((bf16[576,128]{1,0:T(8,128)(2,1)S(1)}, bf16[576,128]{1,0:T(8,128)(2,1)S(1)}, u32[]{:S(2)}, u32[]{:S(2)}) %collective-permute-start.2) | collective-permute-done | bytes 147488 | tf_op jit(solution)/shard_map/ppermute | solution.py:39
  29.8 1.9 %collective-permute-start.4 = (bf16[576,128]{1,0:T(8,128)(2,1)S(1)}, bf16[576,128]{1,0:T(8,128)(2,1)S(1)}, u32[]{:S(2)}, u32[]{:S(2)}) collective-permute-start(bf16[576,128]{1,0:T(8,128)(2,1)S(1)} %collective-permute-done.2.o2), channel_id=1, source_target_pairs={{0,8},{1,1017},{2,10},{3,1019},{4,12},{5,1021},{6,14},{7,1023},{8,... | collective-permute-start | bytes 442376 | tf_op jit(solution)/shard_map/ppermute | solution.py:39
  31.8 0.7 collective-permute-done.1.o1
  32.5 1.9 %collective-permute-start.3 = (bf16[576,128]{1,0:T(8,128)(2,1)S(1)}, bf16[576,128]{1,0:T(8,128)(2,1)S(1)}, u32[]{:S(2)}, u32[]{:S(2)}) collective-permute-start(bf16[576,128]{1,0:T(8,128)(2,1)S(1)} %collective-permute-done.1.o1), channel_id=1, source_target_pairs={{0,8},{1,1017},{2,10},{3,1019},{4,12},{5,1021},{6,14},{7,1023},{8,... | collective-permute-start | bytes 442376 | tf_op jit(solution)/shard_map/ppermute | solution.py:39
  34.4 0.0 copy-done
  34.4 0.0 copy-done.1
  34.4 0.3 order.1
  34.8 5.6 %collective-permute-start.7 = (bf16[1280,128]{1,0:T(8,128)(2,1)S(1)}, bf16[1280,128]{1,0:T(8,128)(2,1)S(1)}, u32[]{:S(2)}, u32[]{:S(2)}) collective-permute-start(bf16[1280,128]{1,0:T(8,128)(2,1)S(1)} %get-tuple-element.24), channel_id=1, source_target_pairs={{0,128},{4,132},{8,136},{12,140},{16,144},{20,148},{24,152},{28,15... | collective-permute-start | bytes 983048 | tf_op jit(solution)/shard_map/ppermute | solution.py:252
  40.3 0.0 collective-permute-done.4.o4
  40.3 3.2 %collective-permute-done.3.o3 = bf16[576,128]{1,0:T(8,128)(2,1)S(1)} collective-permute-done((bf16[576,128]{1,0:T(8,128)(2,1)S(1)}, bf16[576,128]{1,0:T(8,128)(2,1)S(1)}, u32[]{:S(2)}, u32[]{:S(2)}) %collective-permute-start.3) | collective-permute-done | bytes 147488 | tf_op jit(solution)/shard_map/ppermute | solution.py:39
  43.6 0.4 scores.1.mine
  44.0 3.0 %collective-permute-start.5 = (bf16[656,128]{1,0:T(8,128)(2,1)S(1)}, bf16[656,128]{1,0:T(8,128)(2,1)S(1)}, u32[]{:S(2)}, u32[]{:S(2)}) collective-permute-start(bf16[656,128]{1,0:T(8,128)(2,1)S(1)} %scores.1.mine), channel_id=1, source_target_pairs={{0,2},{1,3},{2,0},{3,1},{4,6},{5,7},{6,4},{7,5},{8,10},{9,11},{10,... | collective-permute-start | bytes 503816 | tf_op jit(solution)/shard_map/ppermute | solution.py:261
  48.3 0.1 pad_maximum_fusion.2.numbers
  48.4 0.0 copy-start.2
  48.4 6.2 %collective-permute-done.5.peer = bf16[656,128]{1,0:T(8,128)(2,1)S(1)} collective-permute-done((bf16[656,128]{1,0:T(8,128)(2,1)S(1)}, bf16[656,128]{1,0:T(8,128)(2,1)S(1)}, u32[]{:S(2)}, u32[]{:S(2)}) %collective-permute-start.5) | collective-permute-done | bytes 167968 | tf_op jit(solution)/shard_map/ppermute | solution.py:261
  54.6 1.4 %weights.1 = (f32[296,128]{1,0:T(8,128)S(1)}, f32[296,128]{1,0:T(8,128)S(1)}) custom-call(f32[3]{0:T(128)S(1)} %pad_maximum_fusion.2.numbers, bf16[656,128]{1,0:T(8,128)(2,1)S(1)} %scores.1.mine, bf16[656,128]{1,0:T(8,128)(2,1)S(1)} %collective-permute-done.5.peer, bf16[576,128]{1,0:T(8,128)(2,1)S(1)} %get-tuple-element.33.o0, ...), custom_call_target="tpu_custom_call" | custom-call | tf_op jit(solution)/shard_map/weights/pallas_call | solution.py:263
  56.1 3.2 %collective-permute-start.6 = (f32[296,128]{1,0:T(8,128)S(1)}, f32[296,128]{1,0:T(8,128)S(1)}, u32[]{:S(2)}, u32[]{:S(2)}) collective-permute-start(f32[296,128]{1,0:T(8,128)S(1)} %get-tuple-element.20), channel_id=1, source_target_pairs={{0,1},{1,0},{2,3},{3,2},{4,5},{5,4},{6,7},{7,6},{8,9},{9,8},{10,11... | collective-permute-start | bytes 454664 | tf_op jit(solution)/shard_map/ppermute | solution.py:271
  59.2 0.0 collective-permute-done.7.beside
  59.3 1.0 collective-permute-done.6.got
  60.2 0.0 copy-done.2
  60.2 0.6 slopes.1
  60.9 6.0 %collective-permute-start.8 = (bf16[576,128]{1,0:T(8,128)(2,1)S(1)}, bf16[576,128]{1,0:T(8,128)(2,1)S(1)}, u32[]{:S(2)}, u32[]{:S(2)}) collective-permute-start(bf16[576,128]{1,0:T(8,128)(2,1)S(1)} %get-tuple-element.29), channel_id=1, source_target_pairs={{0,128},{4,132},{8,136},{12,140},{16,144},{20,148},{24,152},{28,15... | collective-permute-start | bytes 442376 | tf_op jit(solution)/shard_map/ppermute | solution.py:285
  66.9 4.1 %collective-permute-done.8.theirs = bf16[576,128]{1,0:T(8,128)(2,1)S(1)} collective-permute-done((bf16[576,128]{1,0:T(8,128)(2,1)S(1)}, bf16[576,128]{1,0:T(8,128)(2,1)S(1)}, u32[]{:S(2)}, u32[]{:S(2)}) %collective-permute-start.8) | collective-permute-done | bytes 147488 | tf_op jit(solution)/shard_map/ppermute | solution.py:285
  71.0 0.9 gradients.1
  71.9 15.9 %all_to_all.10.got = bf16[8,368,128]{2,1,0:T(8,128)(2,1)S(1)} all-to-all(bf16[8,368,128]{2,1,0:T(8,128)(2,1)S(1)} %gradients.1), channel_id=1, replica_groups={{0,4,256,260,512,516,768,772},{8,12,264,268,520,524,776,780},{16,20,272..., dimensions={0} | all-to-all | bytes 1507328 | tf_op jit(solution)/shard_map/all_to_all | solution.py:304
  87.8 0.3 ring.1
  88.1 0.7 convert_element_type.7
  88.8 12.4 %all-to-all-start.1 = ((f16[16,24,128]{2,1,0:T(8,128)(2,1)}), f16[16,24,128]{2,1,0:T(8,128)(2,1)S(1)}, u32[]{:S(2)}, u32[]{:S(2)}) async-start(f16[16,24,128]{2,1,0:T(8,128)(2,1)} %convert_element_type.7), calls=%async_computation.1 | async-start | bytes 196608 | tf_op jit(solution)/shard_map/all_to_all | solution.py:317
  101.2 0.5 slice_bitcast_fusion
  101.7 23.5 %all-to-all-done.1 = f16[16,24,128]{2,1,0:T(8,128)(2,1)S(1)} async-done(((f16[16,24,128]{2,1,0:T(8,128)(2,1)}), f16[16,24,128]{2,1,0:T(8,128)(2,1)S(1)}, u32[]{:S(2)}, u32[]{:S(2)}) %all-to-all-start.1) | async-done | bytes 98336 | tf_op jit(solution)/shard_map/all_to_all | solution.py:317
  125.3 0.1 fusion.5
  125.4 0.1 fusion.4
  125.5 0.1 reshape.13
  125.6 0.1 reshape.12
  125.7 0.7 broadcast_select_fusion.2
  (7 shorter events, 0.1 us)
Async XLA Ops:
  3.5 3.5 %collective-permute-start = (bf16[576,128]{1,0:T(8,128)(2,1)}, bf16[576,128]{1,0:T(8,128)(2,1)S(1)}, u32[]{:S(2)}, u32[]{:S(2)}) collective-permute-start(bf16[576,128]{1,0:T(8,128)(2,1)} %get-tuple-element.18), channel_id=1, source_target_pairs={{0,1},{1,0},{2,3},{3,2},{4,5},{5,4},{6,7},{7,6},{8,9},{9,8},{10,11... | collective-permute-start | bytes 442376 | tf_op jit(solution)/shard_map/ppermute | solution.py:231
  7.0 27.4 %copy-start = (bf16[128,1152]{1,0:T(8,128)(2,1)S(1)}, bf16[128,1152]{1,0:T(8,128)(2,1)}, u32[]{:S(2)}) copy-start(bf16[128,1152]{1,0:T(8,128)(2,1)} %xi.2) | copy-start | bytes 884740
  7.0 27.4 %copy-start.1 = (bf16[128,1152]{1,0:T(8,128)(2,1)S(1)}, bf16[128,1152]{1,0:T(8,128)(2,1)}, u32[]{:S(2)}) copy-start(bf16[128,1152]{1,0:T(8,128)(2,1)} %xt.2) | copy-start | bytes 884740
  7.1 22.7 %collective-permute-start.2 = (bf16[576,128]{1,0:T(8,128)(2,1)S(1)}, bf16[576,128]{1,0:T(8,128)(2,1)S(1)}, u32[]{:S(2)}, u32[]{:S(2)}) collective-permute-start(bf16[576,128]{1,0:T(8,128)(2,1)S(1)} %get-tuple-element.33.o0), channel_id=1, source_target_pairs={{0,8},{1,1017},{2,10},{3,1019},{4,12},{5,1021},{6,14},{7,1023},{8,... | collective-permute-start | bytes 442376 | tf_op jit(solution)/shard_map/ppermute | solution.py:39
  12.4 20.0 %collective-permute-start.1 = (bf16[576,128]{1,0:T(8,128)(2,1)S(1)}, bf16[576,128]{1,0:T(8,128)(2,1)S(1)}, u32[]{:S(2)}, u32[]{:S(2)}) collective-permute-start(bf16[576,128]{1,0:T(8,128)(2,1)S(1)} %get-tuple-element.33.o0), channel_id=1, source_target_pairs={{0,4},{1,1021},{2,6},{3,1023},{4,8},{5,1},{6,10},{7,3},{8,12},{9,5... | collective-permute-start | bytes 442376 | tf_op jit(solution)/shard_map/ppermute | solution.py:39
  29.8 10.5 %collective-permute-start.4 = (bf16[576,128]{1,0:T(8,128)(2,1)S(1)}, bf16[576,128]{1,0:T(8,128)(2,1)S(1)}, u32[]{:S(2)}, u32[]{:S(2)}) collective-permute-start(bf16[576,128]{1,0:T(8,128)(2,1)S(1)} %collective-permute-done.2.o2), channel_id=1, source_target_pairs={{0,8},{1,1017},{2,10},{3,1019},{4,12},{5,1021},{6,14},{7,1023},{8,... | collective-permute-start | bytes 442376 | tf_op jit(solution)/shard_map/ppermute | solution.py:39
  32.5 11.1 %collective-permute-start.3 = (bf16[576,128]{1,0:T(8,128)(2,1)S(1)}, bf16[576,128]{1,0:T(8,128)(2,1)S(1)}, u32[]{:S(2)}, u32[]{:S(2)}) collective-permute-start(bf16[576,128]{1,0:T(8,128)(2,1)S(1)} %collective-permute-done.1.o1), channel_id=1, source_target_pairs={{0,8},{1,1017},{2,10},{3,1019},{4,12},{5,1021},{6,14},{7,1023},{8,... | collective-permute-start | bytes 442376 | tf_op jit(solution)/shard_map/ppermute | solution.py:39
  34.8 24.5 %collective-permute-start.7 = (bf16[1280,128]{1,0:T(8,128)(2,1)S(1)}, bf16[1280,128]{1,0:T(8,128)(2,1)S(1)}, u32[]{:S(2)}, u32[]{:S(2)}) collective-permute-start(bf16[1280,128]{1,0:T(8,128)(2,1)S(1)} %get-tuple-element.24), channel_id=1, source_target_pairs={{0,128},{4,132},{8,136},{12,140},{16,144},{20,148},{24,152},{28,15... | collective-permute-start | bytes 983048 | tf_op jit(solution)/shard_map/ppermute | solution.py:252
  44.0 10.6 %collective-permute-start.5 = (bf16[656,128]{1,0:T(8,128)(2,1)S(1)}, bf16[656,128]{1,0:T(8,128)(2,1)S(1)}, u32[]{:S(2)}, u32[]{:S(2)}) collective-permute-start(bf16[656,128]{1,0:T(8,128)(2,1)S(1)} %scores.1.mine), channel_id=1, source_target_pairs={{0,2},{1,3},{2,0},{3,1},{4,6},{5,7},{6,4},{7,5},{8,10},{9,11},{10,... | collective-permute-start | bytes 503816 | tf_op jit(solution)/shard_map/ppermute | solution.py:261
  48.4 11.8 %copy-start.2 = (f32[576,128]{1,0:T(8,128)S(1)}, f32[576,128]{1,0:T(8,128)}, u32[]{:S(2)}) copy-start(f32[576,128]{1,0:T(8,128)} %get-tuple-element.26.z) | copy-start | bytes 884740
  56.1 4.2 %collective-permute-start.6 = (f32[296,128]{1,0:T(8,128)S(1)}, f32[296,128]{1,0:T(8,128)S(1)}, u32[]{:S(2)}, u32[]{:S(2)}) collective-permute-start(f32[296,128]{1,0:T(8,128)S(1)} %get-tuple-element.20), channel_id=1, source_target_pairs={{0,1},{1,0},{2,3},{3,2},{4,5},{5,4},{6,7},{7,6},{8,9},{9,8},{10,11... | collective-permute-start | bytes 454664 | tf_op jit(solution)/shard_map/ppermute | solution.py:271
  60.9 10.1 %collective-permute-start.8 = (bf16[576,128]{1,0:T(8,128)(2,1)S(1)}, bf16[576,128]{1,0:T(8,128)(2,1)S(1)}, u32[]{:S(2)}, u32[]{:S(2)}) collective-permute-start(bf16[576,128]{1,0:T(8,128)(2,1)S(1)} %get-tuple-element.29), channel_id=1, source_target_pairs={{0,128},{4,132},{8,136},{12,140},{16,144},{20,148},{24,152},{28,15... | collective-permute-start | bytes 442376 | tf_op jit(solution)/shard_map/ppermute | solution.py:285
  88.8 36.5 %all-to-all-start.1 = ((f16[16,24,128]{2,1,0:T(8,128)(2,1)}), f16[16,24,128]{2,1,0:T(8,128)(2,1)S(1)}, u32[]{:S(2)}, u32[]{:S(2)}) async-start(f16[16,24,128]{2,1,0:T(8,128)(2,1)} %convert_element_type.7), calls=%async_computation.1 | async-start | bytes 196608 | tf_op jit(solution)/shard_map/all_to_all | solution.py:317

commit v10 on v8

--- a/solution.py
+++ b/solution.py
@@ -158,7 +158,9 @@
     places = out.shape[0]
     count = total.shape[0] // places
     for j in range(count):
-        out[:, j] = total[j * places : (j + 1) * places]
+        middle = j * places + places // 2
+        out[: places // 2, j] = total[middle : (j + 1) * places]
+        out[places // 2 :, j] = total[j * places : middle]
     out[:, count] = jnp.broadcast_to(power, (places, LANES))
 
 
@@ -311,7 +313,9 @@
         name="ring",
     )(grads)
     groups = [
-        [g * RING + 2 * m + q for m in range(places)] for g in range(planes) for q in range(2)
+        [g * RING + (2 * m + places) % RING + q for m in range(places)]
+        for g in range(planes)
+        for q in range(2)
     ]
     sent = sent.astype(jnp.float16)
     back = lax.all_to_all(sent, "dp", 0, 0, axis_index_groups=groups, tiled=True).astype(F32)

time: 126 us -> 119 us (0.944)
  waiting for transfers between devices: 55.1 us -> 39.3 us
  starting transfers between devices: 42.7 us -> 51.7 us
    all_to_all x1, waiting for transfers between devices: 23.5 us -> 7.7 us  [shards(): lax.all_to_all(sent, 'dp', 0, 0, axis_index_groups=groups, tiled=True)]
    all_to_all x1, starting transfers between devices: 12.6 us -> 21.6 us  [shards(): lax.all_to_all(sent, 'dp', 0, 0, axis_index_groups=groups, tiled=True)]
where the time goes in v10:
time: 119 us
  starting transfers between devices  51.7 us (43%)
  waiting for transfers between devices  39.3 us (33%)
  blocking collectives  15.1 us (13%)
  Pallas kernels  6.91 us (6%)
  between operations  2.17 us (2%)
  local copies, waits for them, and re-layouts  1.79 us (2%)
  other arithmetic  1.58 us (1%)
    all_to_all x1, starting transfers between devices, shards(): lax.all_to_all(sent, 'dp', 0, 0, axis_index_groups=groups, tiled=True)  21.6 us
    ppermute x4, waiting for transfers between devices, shifted(): return lax.ppermute(block, ('dp', 'tower'), route)  21.1 us
    all_to_all x1, blocking collectives, shards(): lax.all_to_all(grads, 'dp', 0, 0, axis_index_groups=groups, tiled=True)  15.1 us
    ppermute x4, starting transfers between devices, shifted(): return lax.ppermute(block, ('dp', 'tower'), route)  13 us
    all_to_all x1, waiting for transfers between devices, shards(): lax.all_to_all(sent, 'dp', 0, 0, axis_index_groups=groups, tiled=True)  7.7 us
    ppermute x1, starting transfers between devices, shards(): theirs = lax.ppermute(send, 'dp', beside)  6.33 us
    ppermute x1, waiting for transfers between devices, shards(): peer = lax.ppermute(scores, 'tower', to_chip)  4.77 us
    ppermute x1, waiting for transfers between devices, shards(): theirs = lax.ppermute(send, 'dp', beside)  4.14 us
  transfers between devices with their start and end apart: 10, of which 9 were waited for; matrix products, arithmetic and copies ran while one was open for 1% of the time, Pallas kernels for 1%

profile of v10, /device:TPU:6, one launch (start us, length us, event | category | flops | bytes accessed | tf_op | source)
XLA Modules:
  0.0 118.6 jit_solution(4802233756600357327)
XLA Ops:
  0.6 2.9 %project.1 = (f32[576,128]{1,0:T(8,128)}, bf16[576,128]{1,0:T(8,128)(2,1)}) custom-call(bf16[128,1152]{1,0:T(8,128)(2,1)} %xi.2, bf16[288,1152]{1,0:T(8,128)(2,1)} %bitcast.7, bf16[128,1152]{1,0:T(8,128)(2,1)} %xt.2, bf16[288,1152]{1,0:T(8,128)(2,1)} %bitcast.8), custom_call_target="tpu_custom_call" | custom-call | tf_op jit(solution)/shard_map/project/pallas_call | solution.py:221
  3.5 1.9 %collective-permute-start = (bf16[576,128]{1,0:T(8,128)(2,1)}, bf16[576,128]{1,0:T(8,128)(2,1)S(1)}, u32[]{:S(2)}, u32[]{:S(2)}) collective-permute-start(bf16[576,128]{1,0:T(8,128)(2,1)} %get-tuple-element.17), channel_id=1, source_target_pairs={{0,1},{1,0},{2,3},{3,2},{4,5},{5,4},{6,7},{7,6},{8,9},{9,8},{10,11... | collective-permute-start | bytes 442376 | tf_op jit(solution)/shard_map/ppermute | solution.py:233
  5.5 0.9 fusion.1
  6.4 0.6 collective-permute-done
  7.0 0.0 copy-start
  7.0 0.0 copy-start.1
  7.0 0.1 broadcast_select_fusion
  7.1 4.0 %collective-permute-start.1 = (bf16[576,128]{1,0:T(8,128)(2,1)S(1)}, bf16[576,128]{1,0:T(8,128)(2,1)S(1)}, u32[]{:S(2)}, u32[]{:S(2)}) collective-permute-start(bf16[576,128]{1,0:T(8,128)(2,1)S(1)} %get-tuple-element.31.o0), channel_id=1, source_target_pairs={{0,4},{1,1021},{2,6},{3,1023},{4,8},{5,1},{6,10},{7,3},{8,12},{9,5... | collective-permute-start | bytes 442376 | tf_op jit(solution)/shard_map/ppermute | solution.py:39
  11.1 5.2 %collective-permute-start.2 = (bf16[576,128]{1,0:T(8,128)(2,1)S(1)}, bf16[576,128]{1,0:T(8,128)(2,1)S(1)}, u32[]{:S(2)}, u32[]{:S(2)}) collective-permute-start(bf16[576,128]{1,0:T(8,128)(2,1)S(1)} %get-tuple-element.31.o0), channel_id=1, source_target_pairs={{0,8},{1,1017},{2,10},{3,1019},{4,12},{5,1021},{6,14},{7,1023},{8,... | collective-permute-start | bytes 442376 | tf_op jit(solution)/shard_map/ppermute | solution.py:39
  16.3 0.0 copy-done
  16.3 0.0 copy-done.1
  16.3 0.3 order.1
  16.6 2.7 %collective-permute-start.6 = (bf16[1280,128]{1,0:T(8,128)(2,1)S(1)}, bf16[1280,128]{1,0:T(8,128)(2,1)S(1)}, u32[]{:S(2)}, u32[]{:S(2)}) collective-permute-start(bf16[1280,128]{1,0:T(8,128)(2,1)S(1)} %get-tuple-element.21), channel_id=1, source_target_pairs={{0,128},{4,132},{8,136},{12,140},{16,144},{20,148},{24,152},{28,15... | collective-permute-start | bytes 983048 | tf_op jit(solution)/shard_map/ppermute | solution.py:254
  19.4 9.9 %collective-permute-done.1.o1 = bf16[576,128]{1,0:T(8,128)(2,1)S(1)} collective-permute-done((bf16[576,128]{1,0:T(8,128)(2,1)S(1)}, bf16[576,128]{1,0:T(8,128)(2,1)S(1)}, u32[]{:S(2)}, u32[]{:S(2)}) %collective-permute-start.1) | collective-permute-done | bytes 147488 | tf_op jit(solution)/shard_map/ppermute | solution.py:39
  29.3 1.9 %collective-permute-start.3 = (bf16[576,128]{1,0:T(8,128)(2,1)S(1)}, bf16[576,128]{1,0:T(8,128)(2,1)S(1)}, u32[]{:S(2)}, u32[]{:S(2)}) collective-permute-start(bf16[576,128]{1,0:T(8,128)(2,1)S(1)} %collective-permute-done.1.o1), channel_id=1, source_target_pairs={{0,8},{1,1017},{2,10},{3,1019},{4,12},{5,1021},{6,14},{7,1023},{8,... | collective-permute-start | bytes 442376 | tf_op jit(solution)/shard_map/ppermute | solution.py:39
  31.2 3.0 %collective-permute-done.2.o2 = bf16[576,128]{1,0:T(8,128)(2,1)S(1)} collective-permute-done((bf16[576,128]{1,0:T(8,128)(2,1)S(1)}, bf16[576,128]{1,0:T(8,128)(2,1)S(1)}, u32[]{:S(2)}, u32[]{:S(2)}) %collective-permute-start.2) | collective-permute-done | bytes 147488 | tf_op jit(solution)/shard_map/ppermute | solution.py:39
  34.2 1.9 %collective-permute-start.4 = (bf16[576,128]{1,0:T(8,128)(2,1)S(1)}, bf16[576,128]{1,0:T(8,128)(2,1)S(1)}, u32[]{:S(2)}, u32[]{:S(2)}) collective-permute-start(bf16[576,128]{1,0:T(8,128)(2,1)S(1)} %collective-permute-done.2.o2), channel_id=1, source_target_pairs={{0,8},{1,1017},{2,10},{3,1019},{4,12},{5,1021},{6,14},{7,1023},{8,... | collective-permute-start | bytes 442376 | tf_op jit(solution)/shard_map/ppermute | solution.py:39
  36.1 4.6 %collective-permute-done.3.o3 = bf16[576,128]{1,0:T(8,128)(2,1)S(1)} collective-permute-done((bf16[576,128]{1,0:T(8,128)(2,1)S(1)}, bf16[576,128]{1,0:T(8,128)(2,1)S(1)}, u32[]{:S(2)}, u32[]{:S(2)}) %collective-permute-start.3) | collective-permute-done | bytes 147488 | tf_op jit(solution)/shard_map/ppermute | solution.py:39
  40.7 3.6 %collective-permute-done.4.o4 = bf16[576,128]{1,0:T(8,128)(2,1)S(1)} collective-permute-done((bf16[576,128]{1,0:T(8,128)(2,1)S(1)}, bf16[576,128]{1,0:T(8,128)(2,1)S(1)}, u32[]{:S(2)}, u32[]{:S(2)}) %collective-permute-start.4) | collective-permute-done | bytes 147488 | tf_op jit(solution)/shard_map/ppermute | solution.py:39
  44.3 0.4 scores.1.mine
  44.7 3.3 %collective-permute-start.5 = (bf16[656,128]{1,0:T(8,128)(2,1)S(1)}, bf16[656,128]{1,0:T(8,128)(2,1)S(1)}, u32[]{:S(2)}, u32[]{:S(2)}) collective-permute-start(bf16[656,128]{1,0:T(8,128)(2,1)S(1)} %scores.1.mine), channel_id=1, source_target_pairs={{0,2},{1,3},{2,0},{3,1},{4,6},{5,7},{6,4},{7,5},{8,10},{9,11},{10,... | collective-permute-start | bytes 503816 | tf_op jit(solution)/shard_map/ppermute | solution.py:264
  49.3 0.1 pad_maximum_fusion.2.numbers
  49.4 0.0 copy-start.2
  49.4 0.0 collective-permute-done.6.beside
  49.4 4.8 %collective-permute-done.5.peer = bf16[656,128]{1,0:T(8,128)(2,1)S(1)} collective-permute-done((bf16[656,128]{1,0:T(8,128)(2,1)S(1)}, bf16[656,128]{1,0:T(8,128)(2,1)S(1)}, u32[]{:S(2)}, u32[]{:S(2)}) %collective-permute-start.5) | collective-permute-done | bytes 167968 | tf_op jit(solution)/shard_map/ppermute | solution.py:264
  54.2 1.4 %weights.1 = (f32[296,128]{1,0:T(8,128)S(1)}, f32[296,128]{1,0:T(8,128)S(1)}) custom-call(f32[3]{0:T(128)S(1)} %pad_maximum_fusion.2.numbers, bf16[656,128]{1,0:T(8,128)(2,1)S(1)} %scores.1.mine, bf16[656,128]{1,0:T(8,128)(2,1)S(1)} %collective-permute-done.5.peer, bf16[576,128]{1,0:T(8,128)(2,1)S(1)} %get-tuple-element.31.o0, ...), custom_call_target="tpu_custom_call" | custom-call | tf_op jit(solution)/shard_map/weights/pallas_call | solution.py:266
  55.6 2.8 %collective-permute-start.7 = (f32[296,128]{1,0:T(8,128)S(1)}, f32[296,128]{1,0:T(8,128)S(1)}, u32[]{:S(2)}, u32[]{:S(2)}) collective-permute-start(f32[296,128]{1,0:T(8,128)S(1)} %get-tuple-element.24), channel_id=1, source_target_pairs={{0,1},{1,0},{2,3},{3,2},{4,5},{5,4},{6,7},{7,6},{8,9},{9,8},{10,11... | collective-permute-start | bytes 454664 | tf_op jit(solution)/shard_map/ppermute | solution.py:274
  58.5 1.0 collective-permute-done.7.got
  59.5 0.0 copy-done.2
  59.5 0.6 slopes.1
  60.1 6.3 %collective-permute-start.8 = (bf16[576,128]{1,0:T(8,128)(2,1)S(1)}, bf16[576,128]{1,0:T(8,128)(2,1)S(1)}, u32[]{:S(2)}, u32[]{:S(2)}) collective-permute-start(bf16[576,128]{1,0:T(8,128)(2,1)S(1)} %get-tuple-element.28), channel_id=1, source_target_pairs={{0,128},{4,132},{8,136},{12,140},{16,144},{20,148},{24,152},{28,15... | collective-permute-start | bytes 442376 | tf_op jit(solution)/shard_map/ppermute | solution.py:287
  66.5 4.1 %collective-permute-done.8.theirs = bf16[576,128]{1,0:T(8,128)(2,1)S(1)} collective-permute-done((bf16[576,128]{1,0:T(8,128)(2,1)S(1)}, bf16[576,128]{1,0:T(8,128)(2,1)S(1)}, u32[]{:S(2)}, u32[]{:S(2)}) %collective-permute-start.8) | collective-permute-done | bytes 147488 | tf_op jit(solution)/shard_map/ppermute | solution.py:287
  70.6 0.9 gradients.1
  71.5 15.1 %all_to_all.10.got = bf16[8,368,128]{2,1,0:T(8,128)(2,1)S(1)} all-to-all(bf16[8,368,128]{2,1,0:T(8,128)(2,1)S(1)} %gradients.1), channel_id=1, replica_groups={{0,4,256,260,512,516,768,772},{8,12,264,268,520,524,776,780},{16,20,272..., dimensions={0} | all-to-all | bytes 1507328 | tf_op jit(solution)/shard_map/all_to_all | solution.py:306
  86.6 0.3 ring.1
  86.9 0.7 convert_element_type.7
  87.6 21.6 %all-to-all-start.1 = ((f16[16,24,128]{2,1,0:T(8,128)(2,1)}), f16[16,24,128]{2,1,0:T(8,128)(2,1)S(1)}, u32[]{:S(2)}, u32[]{:S(2)}) async-start(f16[16,24,128]{2,1,0:T(8,128)(2,1)} %convert_element_type.7), calls=%async_computation.1 | async-start | bytes 196608 | tf_op jit(solution)/shard_map/all_to_all | solution.py:321
  109.2 0.5 slice_bitcast_fusion
  109.7 7.7 %all-to-all-done.1 = f16[16,24,128]{2,1,0:T(8,128)(2,1)S(1)} async-done(((f16[16,24,128]{2,1,0:T(8,128)(2,1)}), f16[16,24,128]{2,1,0:T(8,128)(2,1)S(1)}, u32[]{:S(2)}, u32[]{:S(2)}) %all-to-all-start.1) | async-done | bytes 98336 | tf_op jit(solution)/shard_map/all_to_all | solution.py:321
  117.5 0.1 fusion.4
  117.6 0.1 fusion.5
  117.7 0.1 reshape.12
  117.8 0.1 reshape.13
  117.9 0.7 broadcast_select_fusion.2
  (7 shorter events, 0.1 us)
Async XLA Ops:
  3.5 3.5 %collective-permute-start = (bf16[576,128]{1,0:T(8,128)(2,1)}, bf16[576,128]{1,0:T(8,128)(2,1)S(1)}, u32[]{:S(2)}, u32[]{:S(2)}) collective-permute-start(bf16[576,128]{1,0:T(8,128)(2,1)} %get-tuple-element.17), channel_id=1, source_target_pairs={{0,1},{1,0},{2,3},{3,2},{4,5},{5,4},{6,7},{7,6},{8,9},{9,8},{10,11... | collective-permute-start | bytes 442376 | tf_op jit(solution)/shard_map/ppermute | solution.py:233
  7.0 9.3 %copy-start = (bf16[128,1152]{1,0:T(8,128)(2,1)S(1)}, bf16[128,1152]{1,0:T(8,128)(2,1)}, u32[]{:S(2)}) copy-start(bf16[128,1152]{1,0:T(8,128)(2,1)} %xi.2) | copy-start | bytes 884740
  7.0 9.3 %copy-start.1 = (bf16[128,1152]{1,0:T(8,128)(2,1)S(1)}, bf16[128,1152]{1,0:T(8,128)(2,1)}, u32[]{:S(2)}) copy-start(bf16[128,1152]{1,0:T(8,128)(2,1)} %xt.2) | copy-start | bytes 884740
  7.1 22.2 %collective-permute-start.1 = (bf16[576,128]{1,0:T(8,128)(2,1)S(1)}, bf16[576,128]{1,0:T(8,128)(2,1)S(1)}, u32[]{:S(2)}, u32[]{:S(2)}) collective-permute-start(bf16[576,128]{1,0:T(8,128)(2,1)S(1)} %get-tuple-element.31.o0), channel_id=1, source_target_pairs={{0,4},{1,1021},{2,6},{3,1023},{4,8},{5,1},{6,10},{7,3},{8,12},{9,5... | collective-permute-start | bytes 442376 | tf_op jit(solution)/shard_map/ppermute | solution.py:39
  11.1 23.1 %collective-permute-start.2 = (bf16[576,128]{1,0:T(8,128)(2,1)S(1)}, bf16[576,128]{1,0:T(8,128)(2,1)S(1)}, u32[]{:S(2)}, u32[]{:S(2)}) collective-permute-start(bf16[576,128]{1,0:T(8,128)(2,1)S(1)} %get-tuple-element.31.o0), channel_id=1, source_target_pairs={{0,8},{1,1017},{2,10},{3,1019},{4,12},{5,1021},{6,14},{7,1023},{8,... | collective-permute-start | bytes 442376 | tf_op jit(solution)/shard_map/ppermute | solution.py:39
  16.6 32.8 %collective-permute-start.6 = (bf16[1280,128]{1,0:T(8,128)(2,1)S(1)}, bf16[1280,128]{1,0:T(8,128)(2,1)S(1)}, u32[]{:S(2)}, u32[]{:S(2)}) collective-permute-start(bf16[1280,128]{1,0:T(8,128)(2,1)S(1)} %get-tuple-element.21), channel_id=1, source_target_pairs={{0,128},{4,132},{8,136},{12,140},{16,144},{20,148},{24,152},{28,15... | collective-permute-start | bytes 983048 | tf_op jit(solution)/shard_map/ppermute | solution.py:254
  29.3 11.4 %collective-permute-start.3 = (bf16[576,128]{1,0:T(8,128)(2,1)S(1)}, bf16[576,128]{1,0:T(8,128)(2,1)S(1)}, u32[]{:S(2)}, u32[]{:S(2)}) collective-permute-start(bf16[576,128]{1,0:T(8,128)(2,1)S(1)} %collective-permute-done.1.o1), channel_id=1, source_target_pairs={{0,8},{1,1017},{2,10},{3,1019},{4,12},{5,1021},{6,14},{7,1023},{8,... | collective-permute-start | bytes 442376 | tf_op jit(solution)/shard_map/ppermute | solution.py:39
  34.2 10.1 %collective-permute-start.4 = (bf16[576,128]{1,0:T(8,128)(2,1)S(1)}, bf16[576,128]{1,0:T(8,128)(2,1)S(1)}, u32[]{:S(2)}, u32[]{:S(2)}) collective-permute-start(bf16[576,128]{1,0:T(8,128)(2,1)S(1)} %collective-permute-done.2.o2), channel_id=1, source_target_pairs={{0,8},{1,1017},{2,10},{3,1019},{4,12},{5,1021},{6,14},{7,1023},{8,... | collective-permute-start | bytes 442376 | tf_op jit(solution)/shard_map/ppermute | solution.py:39
  44.7 9.5 %collective-permute-start.5 = (bf16[656,128]{1,0:T(8,128)(2,1)S(1)}, bf16[656,128]{1,0:T(8,128)(2,1)S(1)}, u32[]{:S(2)}, u32[]{:S(2)}) collective-permute-start(bf16[656,128]{1,0:T(8,128)(2,1)S(1)} %scores.1.mine), channel_id=1, source_target_pairs={{0,2},{1,3},{2,0},{3,1},{4,6},{5,7},{6,4},{7,5},{8,10},{9,11},{10,... | collective-permute-start | bytes 503816 | tf_op jit(solution)/shard_map/ppermute | solution.py:264
  49.4 10.0 %copy-start.2 = (f32[576,128]{1,0:T(8,128)S(1)}, f32[576,128]{1,0:T(8,128)}, u32[]{:S(2)}) copy-start(f32[576,128]{1,0:T(8,128)} %get-tuple-element.25.z) | copy-start | bytes 884740
  55.6 3.8 %collective-permute-start.7 = (f32[296,128]{1,0:T(8,128)S(1)}, f32[296,128]{1,0:T(8,128)S(1)}, u32[]{:S(2)}, u32[]{:S(2)}) collective-permute-start(f32[296,128]{1,0:T(8,128)S(1)} %get-tuple-element.24), channel_id=1, source_target_pairs={{0,1},{1,0},{2,3},{3,2},{4,5},{5,4},{6,7},{7,6},{8,9},{9,8},{10,11... | collective-permute-start | bytes 454664 | tf_op jit(solution)/shard_map/ppermute | solution.py:274
  60.1 10.5 %collective-permute-start.8 = (bf16[576,128]{1,0:T(8,128)(2,1)S(1)}, bf16[576,128]{1,0:T(8,128)(2,1)S(1)}, u32[]{:S(2)}, u32[]{:S(2)}) collective-permute-start(bf16[576,128]{1,0:T(8,128)(2,1)S(1)} %get-tuple-element.28), channel_id=1, source_target_pairs={{0,128},{4,132},{8,136},{12,140},{16,144},{20,148},{24,152},{28,15... | collective-permute-start | bytes 442376 | tf_op jit(solution)/shard_map/ppermute | solution.py:287
  87.6 29.9 %all-to-all-start.1 = ((f16[16,24,128]{2,1,0:T(8,128)(2,1)}), f16[16,24,128]{2,1,0:T(8,128)(2,1)S(1)}, u32[]{:S(2)}, u32[]{:S(2)}) async-start(f16[16,24,128]{2,1,0:T(8,128)(2,1)} %convert_element_type.7), calls=%async_computation.1 | async-start | bytes 196608 | tf_op jit(solution)/shard_map/all_to_all | solution.py:321

commit v11 on v10

--- a/solution.py
+++ b/solution.py
@@ -57,49 +57,65 @@
         own[side * width : (side + 1) * width] = part.astype(BF16)
 
 
-def score_kernel(own, o0, o1, o2, o3, o4, out):
-    blocks = [b[...] for b in (own, o0, o1, o2, o3, o4)]
+def score_kernel(count, own, *refs):
+    blocks, out = [b[...] for b in (own,) + refs[:count]], refs[count]
     for j, other in enumerate(blocks[1:]):
         out[j * LANES : (j + 1) * LANES] = dot(other, blocks[0], 0, 0).astype(BF16)
     squares = [jnp.sum(jnp.square(b.astype(F32)), axis=0, keepdims=True) for b in blocks]
-    squares = jnp.concatenate(squares + [jnp.zeros((2, LANES), F32)], axis=0)
+    squares = jnp.concatenate(squares + [jnp.zeros((7 - count, LANES), F32)], axis=0)
     high = squares.astype(BF16).astype(F32)
     low = (squares - high).astype(BF16).astype(F32)
-    out[5 * LANES :] = jnp.concatenate((high, low), axis=0).astype(BF16)
-
-
-def weight_kernel(numbers, mine, peer, o0, o1, o2, o3, o4, send, keep):
+    out[count * LANES :] = jnp.concatenate((high, low), axis=0).astype(BF16)
+
+
+def weigh(numbers, mine, peer, others, paired, d, along, loss):
     scale, bias = numbers[0], numbers[1]
-    width = o0.shape[0] // 2
 
     def total(start, rows):
         a = mine[start : start + rows].astype(F32)
         return a + peer[start : start + rows].astype(F32)
 
-    squares = total(5 * LANES, 16)
+    squares = total(len(others) * LANES, 16)
     inv = lax.rsqrt(squares[:8] + squares[8:] + 1e-06)
     down = inv.T
-    eye = (
-        lax.broadcasted_iota(jnp.int32, (LANES, LANES), 0)
-        == lax.broadcasted_iota(jnp.int32, (LANES, LANES), 1)
-    ).astype(F32)
     n = inv[0:1]
-    loss = along = jnp.zeros_like(n)
-    d = None
-    for j, other in enumerate((o0, o1, o2, o3, o4)):
+    for j, other in enumerate(others):
         col = down[:, j + 1 : j + 2]
         c = scale * (total(j * LANES, LANES) * n * col)
         s = c + bias
         e = jnp.exp(-jnp.abs(s))
         g = jnp.where(s >= 0, 1.0, e) / (1.0 + e)
         signed = s
-        if j == 0:
+        if paired and j == 0:
+            eye = (
+                lax.broadcasted_iota(jnp.int32, (LANES, LANES), 0)
+                == lax.broadcasted_iota(jnp.int32, (LANES, LANES), 1)
+            ).astype(F32)
             signed, g = (1.0 - 2.0 * eye) * s, g - eye
-        loss += jnp.sum(jnp.maximum(signed, 0.0) + jnp.log1p(e), axis=0, keepdims=True)
-        along += jnp.sum(g * c, axis=0, keepdims=True)
-        term = fine(other[...], g * col)
-        d = term if d is None else d + term
-    lines = jnp.concatenate((along, loss, n, jnp.zeros((5, LANES), F32)), axis=0)
+        terms = (
+            fine(other[...], g * col),
+            jnp.sum(g * c, axis=0, keepdims=True),
+            jnp.sum(jnp.maximum(signed, 0.0) + jnp.log1p(e), axis=0, keepdims=True),
+        )
+        if d is None:
+            d, along, loss = terms
+        else:
+            d, along, loss = d + terms[0], along + terms[1], loss + terms[2]
+    return d, along, loss, n
+
+
+def near_kernel(numbers, mine, peer, o0, o1, o2, d_out, lines):
+    d, along, loss, n = weigh(numbers, mine, peer, (o0, o1, o2), True, None, None, None)
+    d_out[...] = d
+    lines[...] = jnp.concatenate((along, loss, n, jnp.zeros((5, LANES), F32)), axis=0)
+
+
+def far_kernel(numbers, mine, peer, d_in, near, o3, o4, send, keep):
+    width = d_in.shape[0] // 2
+    d, along, loss, _ = weigh(
+        numbers, mine, peer, (o3, o4), False, d_in[...], near[0:1], near[1:2]
+    )
+    lines = jnp.concatenate((along, loss, near[2:8]), axis=0)
     keep[:width], send[:width] = d[:width], d[width:]
     keep[width:], send[width:] = lines, lines
 
@@ -253,24 +269,42 @@
     )(column, image_feats, text_feats)
     x_beside = lax.ppermute(away, "dp", beside)
 
-    scores = pl.pallas_call(
-        score_kernel,
-        out_shape=jax.ShapeDtypeStruct((5 * rows + 16, rows), BF16),
-        in_specs=[array] * 6,
-        out_specs=array,
-        compiler_params=VMEM,
-        name="scores",
-    )(mine, o0, o1, o2, o3, o4)
-    peer = lax.ppermute(scores, "tower", to_chip)
+    def scores(*blocks):
+        count = len(blocks) - 1
+        return pl.pallas_call(
+            functools.partial(score_kernel, count),
+            out_shape=jax.ShapeDtypeStruct((count * rows + 16, rows), BF16),
+            in_specs=[array] * (count + 1),
+            out_specs=array,
+            compiler_params=VMEM,
+            name="scores",
+        )(*blocks)
+
+    near = scores(mine, o0, o1, o2)
+    near_peer = lax.ppermute(near, "tower", to_chip)
+    far = scores(mine, o3, o4)
+    far_peer = lax.ppermute(far, "tower", to_chip)
+    d, lines = pl.pallas_call(
+        near_kernel,
+        out_shape=(
+            jax.ShapeDtypeStruct((2 * width, rows), F32),
+            jax.ShapeDtypeStruct((8, rows), F32),
+        ),
+        in_specs=[scalars] + [array] * 5,
+        out_specs=(array, array),
+        compiler_params=VMEM,
+        name="near",
+    )(numbers, near, near_peer, o0, o1, o2)
+    far_peer, x_beside = lax.optimization_barrier((far_peer, x_beside))
     sums = jax.ShapeDtypeStruct((width + 8, rows), F32)
     send, keep = pl.pallas_call(
-        weight_kernel,
+        far_kernel,
         out_shape=(sums, sums),
-        in_specs=[scalars] + [array] * 7,
+        in_specs=[scalars] + [array] * 6,
         out_specs=(array, array),
         compiler_params=VMEM,
-        name="weights",
-    )(numbers, scores, lax.optimization_barrier((peer, x_beside))[0], o0, o1, o2, o3, o4)
+        name="far",
+    )(numbers, far, far_peer, d, lines, o3, o4)
     got = lax.ppermute(send, "tower", to_core)
     slopes, send, loss = pl.pallas_call(
         slope_kernel,

time: 119 us -> 119 us (level)
  waiting for transfers between devices: 39.3 us -> 31.6 us
  starting transfers between devices: 51.7 us -> 56 us
  blocking collectives: 15.1 us -> 16.7 us
    ppermute x4, waiting for transfers between devices: 21.1 us -> 15.6 us  [shifted(): return lax.ppermute(block, ('dp', 'tower'), route)]
    ppermute x1 -> x2, starting transfers between devices: 3.31 us -> 6.84 us  [the longest x1 3.72 us: shards(): far_peer = lax.ppermute(far, 'tower', to_chip)]
    ppermute x1 -> x2, waiting for transfers between devices: 4.77 us -> 2.68 us  [the longest x1 2.68 us: shards(): far_peer = lax.ppermute(far, 'tower', to_chip)]
    all_to_all x1, blocking collectives: 15.1 us -> 16.7 us  [shards(): lax.all_to_all(grads, 'dp', 0, 0, axis_index_groups=groups, tiled=True)]
    pallas_call x2 -> x4, Pallas kernels: 1.86 us -> 2.92 us  [the longest x1 1.21 us: shards(): pl.pallas_call(near_kernel, out_shape=(jax.ShapeDtypeStruct((2 * width, r...]
  transfers between devices with their start and end apart: 10 -> 11, of which waited for: 9 -> 9; matrix products, arithmetic and copies ran while one was open for 1% -> 1% of each run, Pallas kernels for 1% -> 2%
where the time goes in v11:
time: 119 us; the launch traced here: 118 us
  starting transfers between devices  56 us (47%)
  waiting for transfers between devices  31.6 us (27%)
  blocking collectives  16.7 us (14%)
  Pallas kernels  7.97 us (7%)
  between operations  2.2 us (2%)
  local copies, waits for them, and re-layouts  1.79 us (2%)
  other arithmetic  1.58 us (1%)
    all_to_all x1, starting transfers between devices, shards(): lax.all_to_all(sent, 'dp', 0, 0, axis_index_groups=groups, tiled=True)  21.6 us
    all_to_all x1, blocking collectives, shards(): lax.all_to_all(grads, 'dp', 0, 0, axis_index_groups=groups, tiled=True)  16.7 us
    ppermute x4, waiting for transfers between devices, shifted(): return lax.ppermute(block, ('dp', 'tower'), route)  15.6 us
    ppermute x4, starting transfers between devices, shifted(): return lax.ppermute(block, ('dp', 'tower'), route)  13 us
    all_to_all x1, waiting for transfers between devices, shards(): lax.all_to_all(sent, 'dp', 0, 0, axis_index_groups=groups, tiled=True)  7.33 us
    ppermute x1, starting transfers between devices, shards(): theirs = lax.ppermute(send, 'dp', beside)  6.42 us
    ppermute x1, waiting for transfers between devices, shards(): theirs = lax.ppermute(send, 'dp', beside)  4.35 us
    ppermute x1, starting transfers between devices, shards(): far_peer = lax.ppermute(far, 'tower', to_chip)  3.72 us
  transfers between devices with their start and end apart: 11, of which 9 were waited for; matrix products, arithmetic and copies ran while one was open for 1% of the time, Pallas kernels for 2%

profile of v11, /device:TPU:6, one launch (start us, length us, event | category | flops | bytes accessed | tf_op | source)
XLA Modules:
  0.0 117.9 jit_solution(991377204197765717)
XLA Ops:
  0.6 2.9 %project.1 = (f32[576,128]{1,0:T(8,128)}, bf16[576,128]{1,0:T(8,128)(2,1)}) custom-call(bf16[128,1152]{1,0:T(8,128)(2,1)} %xi.2, bf16[288,1152]{1,0:T(8,128)(2,1)} %bitcast.7, bf16[128,1152]{1,0:T(8,128)(2,1)} %xt.2, bf16[288,1152]{1,0:T(8,128)(2,1)} %bitcast.8), custom_call_target="tpu_custom_call" | custom-call | tf_op jit(solution)/shard_map/project/pallas_call | solution.py:237
  3.5 1.9 %collective-permute-start = (bf16[576,128]{1,0:T(8,128)(2,1)}, bf16[576,128]{1,0:T(8,128)(2,1)S(1)}, u32[]{:S(2)}, u32[]{:S(2)}) collective-permute-start(bf16[576,128]{1,0:T(8,128)(2,1)} %get-tuple-element.20), channel_id=1, source_target_pairs={{0,1},{1,0},{2,3},{3,2},{4,5},{5,4},{6,7},{7,6},{8,9},{9,8},{10,11... | collective-permute-start | bytes 442376 | tf_op jit(solution)/shard_map/ppermute | solution.py:249
  5.5 0.9 fusion.1
  6.4 0.6 collective-permute-done
  7.0 0.0 copy-start
  7.0 0.0 copy-start.1
  7.1 0.1 broadcast_select_fusion
  7.1 5.3 %collective-permute-start.3 = (bf16[576,128]{1,0:T(8,128)(2,1)S(1)}, bf16[576,128]{1,0:T(8,128)(2,1)S(1)}, u32[]{:S(2)}, u32[]{:S(2)}) collective-permute-start(bf16[576,128]{1,0:T(8,128)(2,1)S(1)} %get-tuple-element.37.refs_0_.o0), channel_id=1, source_target_pairs={{0,8},{1,1017},{2,10},{3,1019},{4,12},{5,1021},{6,14},{7,1023},{8,... | collective-permute-start | bytes 442376 | tf_op jit(solution)/shard_map/ppermute | solution.py:39
  12.4 3.8 %collective-permute-start.1 = (bf16[576,128]{1,0:T(8,128)(2,1)S(1)}, bf16[576,128]{1,0:T(8,128)(2,1)S(1)}, u32[]{:S(2)}, u32[]{:S(2)}) collective-permute-start(bf16[576,128]{1,0:T(8,128)(2,1)S(1)} %get-tuple-element.37.refs_0_.o0), channel_id=1, source_target_pairs={{0,4},{1,1021},{2,6},{3,1023},{4,8},{5,1},{6,10},{7,3},{8,12},{9,5... | collective-permute-start | bytes 442376 | tf_op jit(solution)/shard_map/ppermute | solution.py:39
  16.3 0.0 copy-done
  16.3 0.0 copy-done.1
  16.3 0.3 order.1
  16.7 2.7 %collective-permute-start.6 = (bf16[1280,128]{1,0:T(8,128)(2,1)S(1)}, bf16[1280,128]{1,0:T(8,128)(2,1)S(1)}, u32[]{:S(2)}, u32[]{:S(2)}) collective-permute-start(bf16[1280,128]{1,0:T(8,128)(2,1)S(1)} %get-tuple-element.24), channel_id=1, source_target_pairs={{0,128},{4,132},{8,136},{12,140},{16,144},{20,148},{24,152},{28,15... | collective-permute-start | bytes 983048 | tf_op jit(solution)/shard_map/ppermute | solution.py:270
  19.4 10.5 %collective-permute-done.3.refs_2_.o2 = bf16[576,128]{1,0:T(8,128)(2,1)S(1)} collective-permute-done((bf16[576,128]{1,0:T(8,128)(2,1)S(1)}, bf16[576,128]{1,0:T(8,128)(2,1)S(1)}, u32[]{:S(2)}, u32[]{:S(2)}) %collective-permute-start.3) | collective-permute-done | bytes 147488 | tf_op jit(solution)/shard_map/ppermute | solution.py:39
  29.9 1.9 %collective-permute-start.4 = (bf16[576,128]{1,0:T(8,128)(2,1)S(1)}, bf16[576,128]{1,0:T(8,128)(2,1)S(1)}, u32[]{:S(2)}, u32[]{:S(2)}) collective-permute-start(bf16[576,128]{1,0:T(8,128)(2,1)S(1)} %collective-permute-done.3.refs_2_.o2), channel_id=1, source_target_pairs={{0,8},{1,1017},{2,10},{3,1019},{4,12},{5,1021},{6,14},{7,1023},{8,... | collective-permute-start | bytes 442376 | tf_op jit(solution)/shard_map/ppermute | solution.py:39
  31.8 0.7 collective-permute-done.1.refs_1_.o1
  32.5 1.9 %collective-permute-start.2 = (bf16[576,128]{1,0:T(8,128)(2,1)S(1)}, bf16[576,128]{1,0:T(8,128)(2,1)S(1)}, u32[]{:S(2)}, u32[]{:S(2)}) collective-permute-start(bf16[576,128]{1,0:T(8,128)(2,1)S(1)} %collective-permute-done.1.refs_1_.o1), channel_id=1, source_target_pairs={{0,8},{1,1017},{2,10},{3,1019},{4,12},{5,1021},{6,14},{7,1023},{8,... | collective-permute-start | bytes 442376 | tf_op jit(solution)/shard_map/ppermute | solution.py:39
  35.7 0.3 scores.3.mine
  36.0 3.1 %collective-permute-start.7 = (bf16[400,128]{1,0:T(8,128)(2,1)S(1)}, bf16[400,128]{1,0:T(8,128)(2,1)S(1)}, u32[]{:S(2)}, u32[]{:S(2)}) collective-permute-start(bf16[400,128]{1,0:T(8,128)(2,1)S(1)} %scores.3.mine), channel_id=1, source_target_pairs={{0,2},{1,3},{2,0},{3,1},{4,6},{5,7},{6,4},{7,5},{8,10},{9,11},{10,... | collective-permute-start | bytes 307208 | tf_op jit(solution)/shard_map/ppermute | solution.py:284
  39.2 0.8 collective-permute-done.4.refs_1_.o4
  40.0 3.6 %collective-permute-done.2.refs_0_.o3 = bf16[576,128]{1,0:T(8,128)(2,1)S(1)} collective-permute-done((bf16[576,128]{1,0:T(8,128)(2,1)S(1)}, bf16[576,128]{1,0:T(8,128)(2,1)S(1)}, u32[]{:S(2)}, u32[]{:S(2)}) %collective-permute-start.2) | collective-permute-done | bytes 147488 | tf_op jit(solution)/shard_map/ppermute | solution.py:39
  43.6 0.3 scores.2.mine
  43.9 3.7 %collective-permute-start.5 = (bf16[272,128]{1,0:T(8,128)(2,1)S(1)}, bf16[272,128]{1,0:T(8,128)(2,1)S(1)}, u32[]{:S(2)}, u32[]{:S(2)}) collective-permute-start(bf16[272,128]{1,0:T(8,128)(2,1)S(1)} %scores.2.mine), channel_id=1, source_target_pairs={{0,2},{1,3},{2,0},{3,1},{4,6},{5,7},{6,4},{7,5},{8,10},{9,11},{10,... | collective-permute-start | bytes 208904 | tf_op jit(solution)/shard_map/ppermute | solution.py:286
  47.7 0.1 pad_maximum_fusion.2.numbers
  47.7 0.0 collective-permute-done.7.peer
  47.7 1.2 %near.1 = (f32[576,128]{1,0:T(8,128)S(1)}, f32[8,128]{1,0:T(8,128)S(1)}) custom-call(f32[3]{0:T(128)S(1)} %pad_maximum_fusion.2.numbers, bf16[400,128]{1,0:T(8,128)(2,1)S(1)} %scores.3.mine, bf16[400,128]{1,0:T(8,128)(2,1)S(1)} %collective-permute-done.7.peer, bf16[576,128]{1,0:T(8,128)(2,1)S(1)} %get-tuple-element.37.refs_0_.o0, ...), custom_call_target="tpu_custom_call" | custom-call | tf_op jit(solution)/shard_map/near/pallas_call | solution.py:287
  49.0 0.0 collective-permute-done.6.beside
  49.0 2.7 %collective-permute-done.5.peer = bf16[272,128]{1,0:T(8,128)(2,1)S(1)} collective-permute-done((bf16[272,128]{1,0:T(8,128)(2,1)S(1)}, bf16[272,128]{1,0:T(8,128)(2,1)S(1)}, u32[]{:S(2)}, u32[]{:S(2)}) %collective-permute-start.5) | collective-permute-done | bytes 69664 | tf_op jit(solution)/shard_map/ppermute | solution.py:286
  51.6 0.0 copy-start.2
  51.6 1.1 far.1
  52.8 3.5 %collective-permute-start.8 = (f32[296,128]{1,0:T(8,128)S(1)}, f32[296,128]{1,0:T(8,128)S(1)}, u32[]{:S(2)}, u32[]{:S(2)}) collective-permute-start(f32[296,128]{1,0:T(8,128)S(1)} %get-tuple-element.29), channel_id=1, source_target_pairs={{0,1},{1,0},{2,3},{3,2},{4,5},{5,4},{6,7},{7,6},{8,9},{9,8},{10,11... | collective-permute-start | bytes 454664 | tf_op jit(solution)/shard_map/ppermute | solution.py:308
  56.2 1.0 collective-permute-done.8.got
  57.2 0.0 copy-done.2
  57.2 0.6 slopes.1
  57.9 6.4 %collective-permute-start.9 = (bf16[576,128]{1,0:T(8,128)(2,1)S(1)}, bf16[576,128]{1,0:T(8,128)(2,1)S(1)}, u32[]{:S(2)}, u32[]{:S(2)}) collective-permute-start(bf16[576,128]{1,0:T(8,128)(2,1)S(1)} %get-tuple-element.33), channel_id=1, source_target_pairs={{0,128},{4,132},{8,136},{12,140},{16,144},{20,148},{24,152},{28,15... | collective-permute-start | bytes 442376 | tf_op jit(solution)/shard_map/ppermute | solution.py:321
  64.3 4.3 %collective-permute-done.9.theirs = bf16[576,128]{1,0:T(8,128)(2,1)S(1)} collective-permute-done((bf16[576,128]{1,0:T(8,128)(2,1)S(1)}, bf16[576,128]{1,0:T(8,128)(2,1)S(1)}, u32[]{:S(2)}, u32[]{:S(2)}) %collective-permute-start.9) | collective-permute-done | bytes 147488 | tf_op jit(solution)/shard_map/ppermute | solution.py:321
  68.6 0.9 gradients.1
  69.5 16.7 %all_to_all.10.got = bf16[8,368,128]{2,1,0:T(8,128)(2,1)S(1)} all-to-all(bf16[8,368,128]{2,1,0:T(8,128)(2,1)S(1)} %gradients.1), channel_id=1, replica_groups={{0,4,256,260,512,516,768,772},{8,12,264,268,520,524,776,780},{16,20,272..., dimensions={0} | all-to-all | bytes 1507328 | tf_op jit(solution)/shard_map/all_to_all | solution.py:340
  86.2 0.3 ring.1
  86.6 0.7 convert_element_type.7
  87.2 21.6 %all-to-all-start.1 = ((f16[16,24,128]{2,1,0:T(8,128)(2,1)}), f16[16,24,128]{2,1,0:T(8,128)(2,1)S(1)}, u32[]{:S(2)}, u32[]{:S(2)}) async-start(f16[16,24,128]{2,1,0:T(8,128)(2,1)} %convert_element_type.7), calls=%async_computation.1 | async-start | bytes 196608 | tf_op jit(solution)/shard_map/all_to_all | solution.py:355
  108.9 0.5 slice_bitcast_fusion
  109.4 7.3 %all-to-all-done.1 = f16[16,24,128]{2,1,0:T(8,128)(2,1)S(1)} async-done(((f16[16,24,128]{2,1,0:T(8,128)(2,1)}), f16[16,24,128]{2,1,0:T(8,128)(2,1)S(1)}, u32[]{:S(2)}, u32[]{:S(2)}) %all-to-all-start.1) | async-done | bytes 98336 | tf_op jit(solution)/shard_map/all_to_all | solution.py:355
  116.8 0.1 fusion.5
  116.9 0.1 fusion.4
  117.0 0.1 reshape.13
  117.1 0.1 reshape.12
  117.2 0.7 broadcast_select_fusion.2
  (7 shorter events, 0.1 us)
Async XLA Ops:
  3.5 3.5 %collective-permute-start = (bf16[576,128]{1,0:T(8,128)(2,1)}, bf16[576,128]{1,0:T(8,128)(2,1)S(1)}, u32[]{:S(2)}, u32[]{:S(2)}) collective-permute-start(bf16[576,128]{1,0:T(8,128)(2,1)} %get-tuple-element.20), channel_id=1, source_target_pairs={{0,1},{1,0},{2,3},{3,2},{4,5},{5,4},{6,7},{7,6},{8,9},{9,8},{10,11... | collective-permute-start | bytes 442376 | tf_op jit(solution)/shard_map/ppermute | solution.py:249
  7.0 9.3 %copy-start = (bf16[128,1152]{1,0:T(8,128)(2,1)S(1)}, bf16[128,1152]{1,0:T(8,128)(2,1)}, u32[]{:S(2)}) copy-start(bf16[128,1152]{1,0:T(8,128)(2,1)} %xi.2) | copy-start | bytes 884740
  7.0 9.3 %copy-start.1 = (bf16[128,1152]{1,0:T(8,128)(2,1)S(1)}, bf16[128,1152]{1,0:T(8,128)(2,1)}, u32[]{:S(2)}) copy-start(bf16[128,1152]{1,0:T(8,128)(2,1)} %xt.2) | copy-start | bytes 884740
  7.1 22.7 %collective-permute-start.3 = (bf16[576,128]{1,0:T(8,128)(2,1)S(1)}, bf16[576,128]{1,0:T(8,128)(2,1)S(1)}, u32[]{:S(2)}, u32[]{:S(2)}) collective-permute-start(bf16[576,128]{1,0:T(8,128)(2,1)S(1)} %get-tuple-element.37.refs_0_.o0), channel_id=1, source_target_pairs={{0,8},{1,1017},{2,10},{3,1019},{4,12},{5,1021},{6,14},{7,1023},{8,... | collective-permute-start | bytes 442376 | tf_op jit(solution)/shard_map/ppermute | solution.py:39
  12.4 20.0 %collective-permute-start.1 = (bf16[576,128]{1,0:T(8,128)(2,1)S(1)}, bf16[576,128]{1,0:T(8,128)(2,1)S(1)}, u32[]{:S(2)}, u32[]{:S(2)}) collective-permute-start(bf16[576,128]{1,0:T(8,128)(2,1)S(1)} %get-tuple-element.37.refs_0_.o0), channel_id=1, source_target_pairs={{0,4},{1,1021},{2,6},{3,1023},{4,8},{5,1},{6,10},{7,3},{8,12},{9,5... | collective-permute-start | bytes 442376 | tf_op jit(solution)/shard_map/ppermute | solution.py:39
  16.7 32.3 %collective-permute-start.6 = (bf16[1280,128]{1,0:T(8,128)(2,1)S(1)}, bf16[1280,128]{1,0:T(8,128)(2,1)S(1)}, u32[]{:S(2)}, u32[]{:S(2)}) collective-permute-start(bf16[1280,128]{1,0:T(8,128)(2,1)S(1)} %get-tuple-element.24), channel_id=1, source_target_pairs={{0,128},{4,132},{8,136},{12,140},{16,144},{20,148},{24,152},{28,15... | collective-permute-start | bytes 983048 | tf_op jit(solution)/shard_map/ppermute | solution.py:270
  29.9 10.1 %collective-permute-start.4 = (bf16[576,128]{1,0:T(8,128)(2,1)S(1)}, bf16[576,128]{1,0:T(8,128)(2,1)S(1)}, u32[]{:S(2)}, u32[]{:S(2)}) collective-permute-start(bf16[576,128]{1,0:T(8,128)(2,1)S(1)} %collective-permute-done.3.refs_2_.o2), channel_id=1, source_target_pairs={{0,8},{1,1017},{2,10},{3,1019},{4,12},{5,1021},{6,14},{7,1023},{8,... | collective-permute-start | bytes 442376 | tf_op jit(solution)/shard_map/ppermute | solution.py:39
  32.5 11.2 %collective-permute-start.2 = (bf16[576,128]{1,0:T(8,128)(2,1)S(1)}, bf16[576,128]{1,0:T(8,128)(2,1)S(1)}, u32[]{:S(2)}, u32[]{:S(2)}) collective-permute-start(bf16[576,128]{1,0:T(8,128)(2,1)S(1)} %collective-permute-done.1.refs_1_.o1), channel_id=1, source_target_pairs={{0,8},{1,1017},{2,10},{3,1019},{4,12},{5,1021},{6,14},{7,1023},{8,... | collective-permute-start | bytes 442376 | tf_op jit(solution)/shard_map/ppermute | solution.py:39
  36.0 11.7 %collective-permute-start.7 = (bf16[400,128]{1,0:T(8,128)(2,1)S(1)}, bf16[400,128]{1,0:T(8,128)(2,1)S(1)}, u32[]{:S(2)}, u32[]{:S(2)}) collective-permute-start(bf16[400,128]{1,0:T(8,128)(2,1)S(1)} %scores.3.mine), channel_id=1, source_target_pairs={{0,2},{1,3},{2,0},{3,1},{4,6},{5,7},{6,4},{7,5},{8,10},{9,11},{10,... | collective-permute-start | bytes 307208 | tf_op jit(solution)/shard_map/ppermute | solution.py:284
  43.9 7.7 %collective-permute-start.5 = (bf16[272,128]{1,0:T(8,128)(2,1)S(1)}, bf16[272,128]{1,0:T(8,128)(2,1)S(1)}, u32[]{:S(2)}, u32[]{:S(2)}) collective-permute-start(bf16[272,128]{1,0:T(8,128)(2,1)S(1)} %scores.2.mine), channel_id=1, source_target_pairs={{0,2},{1,3},{2,0},{3,1},{4,6},{5,7},{6,4},{7,5},{8,10},{9,11},{10,... | collective-permute-start | bytes 208904 | tf_op jit(solution)/shard_map/ppermute | solution.py:286
  51.6 5.6 %copy-start.2 = (f32[576,128]{1,0:T(8,128)S(1)}, f32[576,128]{1,0:T(8,128)}, u32[]{:S(2)}) copy-start(f32[576,128]{1,0:T(8,128)} %get-tuple-element.30.z) | copy-start | bytes 884740
  52.8 4.5 %collective-permute-start.8 = (f32[296,128]{1,0:T(8,128)S(1)}, f32[296,128]{1,0:T(8,128)S(1)}, u32[]{:S(2)}, u32[]{:S(2)}) collective-permute-start(f32[296,128]{1,0:T(8,128)S(1)} %get-tuple-element.29), channel_id=1, source_target_pairs={{0,1},{1,0},{2,3},{3,2},{4,5},{5,4},{6,7},{7,6},{8,9},{9,8},{10,11... | collective-permute-start | bytes 454664 | tf_op jit(solution)/shard_map/ppermute | solution.py:308
  57.9 10.8 %collective-permute-start.9 = (bf16[576,128]{1,0:T(8,128)(2,1)S(1)}, bf16[576,128]{1,0:T(8,128)(2,1)S(1)}, u32[]{:S(2)}, u32[]{:S(2)}) collective-permute-start(bf16[576,128]{1,0:T(8,128)(2,1)S(1)} %get-tuple-element.33), channel_id=1, source_target_pairs={{0,128},{4,132},{8,136},{12,140},{16,144},{20,148},{24,152},{28,15... | collective-permute-start | bytes 442376 | tf_op jit(solution)/shard_map/ppermute | solution.py:321
  87.2 29.5 %all-to-all-start.1 = ((f16[16,24,128]{2,1,0:T(8,128)(2,1)}), f16[16,24,128]{2,1,0:T(8,128)(2,1)S(1)}, u32[]{:S(2)}, u32[]{:S(2)}) async-start(f16[16,24,128]{2,1,0:T(8,128)(2,1)} %convert_element_type.7), calls=%async_computation.1 | async-start | bytes 196608 | tf_op jit(solution)/shard_map/all_to_all | solution.py:355

commit v12 on v11

--- a/solution.py
+++ b/solution.py
@@ -282,6 +282,7 @@
 
     near = scores(mine, o0, o1, o2)
     near_peer = lax.ppermute(near, "tower", to_chip)
+    near_peer, x_beside = lax.optimization_barrier((near_peer, x_beside))
     far = scores(mine, o3, o4)
     far_peer = lax.ppermute(far, "tower", to_chip)
     d, lines = pl.pallas_call(
@@ -295,7 +296,6 @@
         compiler_params=VMEM,
         name="near",
     )(numbers, near, near_peer, o0, o1, o2)
-    far_peer, x_beside = lax.optimization_barrier((far_peer, x_beside))
     sums = jax.ShapeDtypeStruct((width + 8, rows), F32)
     send, keep = pl.pallas_call(
         far_kernel,

time: 119 us -> 118 us (level)
  blocking collectives: 16.7 us -> 15.1 us
  waiting for transfers between devices: 31.6 us -> 32.8 us
    all_to_all x1, blocking collectives: 16.7 us -> 15.1 us  [shards(): lax.all_to_all(grads, 'dp', 0, 0, axis_index_groups=groups, tiled=True)]
  transfers between devices with their start and end apart: 11 -> 11, of which waited for: 9 -> 8; matrix products, arithmetic and copies ran while one was open for 1% -> 1% of each run, Pallas kernels for 2% -> 2%
where the time goes in v12:
time: 118 us; the launch traced here: 117 us
  starting transfers between devices  55.6 us (47%)
  waiting for transfers between devices  32.8 us (28%)
  blocking collectives  15.1 us (13%)
  Pallas kernels  7.99 us (7%)
  between operations  2.21 us (2%)
  local copies, waits for them, and re-layouts  1.79 us (2%)
  other arithmetic  1.58 us (1%)
    all_to_all x1, starting transfers between devices, shards(): lax.all_to_all(sent, 'dp', 0, 0, axis_index_groups=groups, tiled=True)  21.6 us
    ppermute x4, waiting for transfers between devices, shifted(): return lax.ppermute(block, ('dp', 'tower'), route)  16.3 us
    all_to_all x1, blocking collectives, shards(): lax.all_to_all(grads, 'dp', 0, 0, axis_index_groups=groups, tiled=True)  15.1 us
    ppermute x4, starting transfers between devices, shifted(): return lax.ppermute(block, ('dp', 'tower'), route)  13 us
    all_to_all x1, waiting for transfers between devices, shards(): lax.all_to_all(sent, 'dp', 0, 0, axis_index_groups=groups, tiled=True)  7.7 us
    ppermute x1, starting transfers between devices, shards(): theirs = lax.ppermute(send, 'dp', beside)  6.79 us
    ppermute x1, waiting for transfers between devices, shards(): theirs = lax.ppermute(send, 'dp', beside)  4.14 us
    ppermute x1, starting transfers between devices, shards(): far_peer = lax.ppermute(far, 'tower', to_chip)  3.31 us
  transfers between devices with their start and end apart: 11, of which 8 were waited for; matrix products, arithmetic and copies ran while one was open for 1% of the time, Pallas kernels for 2%

profile of v12, /device:TPU:6, one launch (start us, length us, event | category | flops | bytes accessed | tf_op | source)
XLA Modules:
  0.0 117.1 jit_solution(3622881830502738341)
XLA Ops:
  0.6 2.9 %project.1 = (f32[576,128]{1,0:T(8,128)}, bf16[576,128]{1,0:T(8,128)(2,1)}) custom-call(bf16[128,1152]{1,0:T(8,128)(2,1)} %xi.2, bf16[288,1152]{1,0:T(8,128)(2,1)} %bitcast.7, bf16[128,1152]{1,0:T(8,128)(2,1)} %xt.2, bf16[288,1152]{1,0:T(8,128)(2,1)} %bitcast.8), custom_call_target="tpu_custom_call" | custom-call | tf_op jit(solution)/shard_map/project/pallas_call | solution.py:237
  3.5 1.9 %collective-permute-start = (bf16[576,128]{1,0:T(8,128)(2,1)}, bf16[576,128]{1,0:T(8,128)(2,1)S(1)}, u32[]{:S(2)}, u32[]{:S(2)}) collective-permute-start(bf16[576,128]{1,0:T(8,128)(2,1)} %get-tuple-element.20), channel_id=1, source_target_pairs={{0,1},{1,0},{2,3},{3,2},{4,5},{5,4},{6,7},{7,6},{8,9},{9,8},{10,11... | collective-permute-start | bytes 442376 | tf_op jit(solution)/shard_map/ppermute | solution.py:249
  5.5 0.9 fusion.1
  6.4 0.6 collective-permute-done
  7.0 0.0 copy-start
  7.0 0.0 copy-start.1
  7.1 0.1 broadcast_select_fusion
  7.1 4.0 %collective-permute-start.1 = (bf16[576,128]{1,0:T(8,128)(2,1)S(1)}, bf16[576,128]{1,0:T(8,128)(2,1)S(1)}, u32[]{:S(2)}, u32[]{:S(2)}) collective-permute-start(bf16[576,128]{1,0:T(8,128)(2,1)S(1)} %get-tuple-element.37.refs_0_.o0), channel_id=1, source_target_pairs={{0,4},{1,1021},{2,6},{3,1023},{4,8},{5,1},{6,10},{7,3},{8,12},{9,5... | collective-permute-start | bytes 442376 | tf_op jit(solution)/shard_map/ppermute | solution.py:39
  11.1 5.2 %collective-permute-start.3 = (bf16[576,128]{1,0:T(8,128)(2,1)S(1)}, bf16[576,128]{1,0:T(8,128)(2,1)S(1)}, u32[]{:S(2)}, u32[]{:S(2)}) collective-permute-start(bf16[576,128]{1,0:T(8,128)(2,1)S(1)} %get-tuple-element.37.refs_0_.o0), channel_id=1, source_target_pairs={{0,8},{1,1017},{2,10},{3,1019},{4,12},{5,1021},{6,14},{7,1023},{8,... | collective-permute-start | bytes 442376 | tf_op jit(solution)/shard_map/ppermute | solution.py:39
  16.3 0.0 copy-done
  16.3 0.0 copy-done.1
  16.3 0.3 order.1
  16.7 2.7 %collective-permute-start.7 = (bf16[1280,128]{1,0:T(8,128)(2,1)S(1)}, bf16[1280,128]{1,0:T(8,128)(2,1)S(1)}, u32[]{:S(2)}, u32[]{:S(2)}) collective-permute-start(bf16[1280,128]{1,0:T(8,128)(2,1)S(1)} %get-tuple-element.24), channel_id=1, source_target_pairs={{0,128},{4,132},{8,136},{12,140},{16,144},{20,148},{24,152},{28,15... | collective-permute-start | bytes 983048 | tf_op jit(solution)/shard_map/ppermute | solution.py:270
  19.4 9.9 %collective-permute-done.1.refs_1_.o1 = bf16[576,128]{1,0:T(8,128)(2,1)S(1)} collective-permute-done((bf16[576,128]{1,0:T(8,128)(2,1)S(1)}, bf16[576,128]{1,0:T(8,128)(2,1)S(1)}, u32[]{:S(2)}, u32[]{:S(2)}) %collective-permute-start.1) | collective-permute-done | bytes 147488 | tf_op jit(solution)/shard_map/ppermute | solution.py:39
  29.3 1.9 %collective-permute-start.2 = (bf16[576,128]{1,0:T(8,128)(2,1)S(1)}, bf16[576,128]{1,0:T(8,128)(2,1)S(1)}, u32[]{:S(2)}, u32[]{:S(2)}) collective-permute-start(bf16[576,128]{1,0:T(8,128)(2,1)S(1)} %collective-permute-done.1.refs_1_.o1), channel_id=1, source_target_pairs={{0,8},{1,1017},{2,10},{3,1019},{4,12},{5,1021},{6,14},{7,1023},{8,... | collective-permute-start | bytes 442376 | tf_op jit(solution)/shard_map/ppermute | solution.py:39
  31.2 3.0 %collective-permute-done.3.refs_2_.o2 = bf16[576,128]{1,0:T(8,128)(2,1)S(1)} collective-permute-done((bf16[576,128]{1,0:T(8,128)(2,1)S(1)}, bf16[576,128]{1,0:T(8,128)(2,1)S(1)}, u32[]{:S(2)}, u32[]{:S(2)}) %collective-permute-start.3) | collective-permute-done | bytes 147488 | tf_op jit(solution)/shard_map/ppermute | solution.py:39
  34.2 1.9 %collective-permute-start.4 = (bf16[576,128]{1,0:T(8,128)(2,1)S(1)}, bf16[576,128]{1,0:T(8,128)(2,1)S(1)}, u32[]{:S(2)}, u32[]{:S(2)}) collective-permute-start(bf16[576,128]{1,0:T(8,128)(2,1)S(1)} %collective-permute-done.3.refs_2_.o2), channel_id=1, source_target_pairs={{0,8},{1,1017},{2,10},{3,1019},{4,12},{5,1021},{6,14},{7,1023},{8,... | collective-permute-start | bytes 442376 | tf_op jit(solution)/shard_map/ppermute | solution.py:39
  37.4 0.3 scores.3.mine
  37.7 3.1 %collective-permute-start.6 = (bf16[400,128]{1,0:T(8,128)(2,1)S(1)}, bf16[400,128]{1,0:T(8,128)(2,1)S(1)}, u32[]{:S(2)}, u32[]{:S(2)}) collective-permute-start(bf16[400,128]{1,0:T(8,128)(2,1)S(1)} %scores.3.mine), channel_id=1, source_target_pairs={{0,2},{1,3},{2,0},{3,1},{4,6},{5,7},{6,4},{7,5},{8,10},{9,11},{10,... | collective-permute-start | bytes 307208 | tf_op jit(solution)/shard_map/ppermute | solution.py:284
  40.9 0.0 collective-permute-done.2.refs_0_.o3
  40.9 3.4 %collective-permute-done.4.refs_1_.o4 = bf16[576,128]{1,0:T(8,128)(2,1)S(1)} collective-permute-done((bf16[576,128]{1,0:T(8,128)(2,1)S(1)}, bf16[576,128]{1,0:T(8,128)(2,1)S(1)}, u32[]{:S(2)}, u32[]{:S(2)}) %collective-permute-start.4) | collective-permute-done | bytes 147488 | tf_op jit(solution)/shard_map/ppermute | solution.py:39
  44.3 0.3 scores.2.mine
  44.6 3.3 %collective-permute-start.5 = (bf16[272,128]{1,0:T(8,128)(2,1)S(1)}, bf16[272,128]{1,0:T(8,128)(2,1)S(1)}, u32[]{:S(2)}, u32[]{:S(2)}) collective-permute-start(bf16[272,128]{1,0:T(8,128)(2,1)S(1)} %scores.2.mine), channel_id=1, source_target_pairs={{0,2},{1,3},{2,0},{3,1},{4,6},{5,7},{6,4},{7,5},{8,10},{9,11},{10,... | collective-permute-start | bytes 208904 | tf_op jit(solution)/shard_map/ppermute | solution.py:287
  47.9 0.1 pad_maximum_fusion.2.numbers
  48.0 0.0 collective-permute-done.6.peer
  48.0 0.0 collective-permute-done.7.beside
  48.0 1.2 %near.1 = (f32[576,128]{1,0:T(8,128)S(1)}, f32[8,128]{1,0:T(8,128)S(1)}) custom-call(f32[3]{0:T(128)S(1)} %pad_maximum_fusion.2.numbers, bf16[400,128]{1,0:T(8,128)(2,1)S(1)} %scores.3.mine, bf16[400,128]{1,0:T(8,128)(2,1)S(1)} %collective-permute-done.6.peer, bf16[576,128]{1,0:T(8,128)(2,1)S(1)} %get-tuple-element.37.refs_0_.o0, ...), custom_call_target="tpu_custom_call" | custom-call | tf_op jit(solution)/shard_map/near/pallas_call | solution.py:288
  49.2 3.1 %collective-permute-done.5.peer = bf16[272,128]{1,0:T(8,128)(2,1)S(1)} collective-permute-done((bf16[272,128]{1,0:T(8,128)(2,1)S(1)}, bf16[272,128]{1,0:T(8,128)(2,1)S(1)}, u32[]{:S(2)}, u32[]{:S(2)}) %collective-permute-start.5) | collective-permute-done | bytes 69664 | tf_op jit(solution)/shard_map/ppermute | solution.py:287
  52.3 0.0 copy-start.2
  52.3 1.1 far.1
  53.4 3.1 %collective-permute-start.8 = (f32[296,128]{1,0:T(8,128)S(1)}, f32[296,128]{1,0:T(8,128)S(1)}, u32[]{:S(2)}, u32[]{:S(2)}) collective-permute-start(f32[296,128]{1,0:T(8,128)S(1)} %get-tuple-element.29), channel_id=1, source_target_pairs={{0,1},{1,0},{2,3},{3,2},{4,5},{5,4},{6,7},{7,6},{8,9},{9,8},{10,11... | collective-permute-start | bytes 454664 | tf_op jit(solution)/shard_map/ppermute | solution.py:308
  56.5 1.0 collective-permute-done.8.got
  57.5 0.0 copy-done.2
  57.5 0.6 slopes.1
  58.2 6.8 %collective-permute-start.9 = (bf16[576,128]{1,0:T(8,128)(2,1)S(1)}, bf16[576,128]{1,0:T(8,128)(2,1)S(1)}, u32[]{:S(2)}, u32[]{:S(2)}) collective-permute-start(bf16[576,128]{1,0:T(8,128)(2,1)S(1)} %get-tuple-element.33), channel_id=1, source_target_pairs={{0,128},{4,132},{8,136},{12,140},{16,144},{20,148},{24,152},{28,15... | collective-permute-start | bytes 442376 | tf_op jit(solution)/shard_map/ppermute | solution.py:321
  65.0 4.1 %collective-permute-done.9.theirs = bf16[576,128]{1,0:T(8,128)(2,1)S(1)} collective-permute-done((bf16[576,128]{1,0:T(8,128)(2,1)S(1)}, bf16[576,128]{1,0:T(8,128)(2,1)S(1)}, u32[]{:S(2)}, u32[]{:S(2)}) %collective-permute-start.9) | collective-permute-done | bytes 147488 | tf_op jit(solution)/shard_map/ppermute | solution.py:321
  69.1 0.8 gradients.1
  70.0 15.1 %all_to_all.10.got = bf16[8,368,128]{2,1,0:T(8,128)(2,1)S(1)} all-to-all(bf16[8,368,128]{2,1,0:T(8,128)(2,1)S(1)} %gradients.1), channel_id=1, replica_groups={{0,4,256,260,512,516,768,772},{8,12,264,268,520,524,776,780},{16,20,272..., dimensions={0} | all-to-all | bytes 1507328 | tf_op jit(solution)/shard_map/all_to_all | solution.py:340
  85.1 0.3 ring.1
  85.4 0.7 convert_element_type.7
  86.1 21.6 %all-to-all-start.1 = ((f16[16,24,128]{2,1,0:T(8,128)(2,1)}), f16[16,24,128]{2,1,0:T(8,128)(2,1)S(1)}, u32[]{:S(2)}, u32[]{:S(2)}) async-start(f16[16,24,128]{2,1,0:T(8,128)(2,1)} %convert_element_type.7), calls=%async_computation.1 | async-start | bytes 196608 | tf_op jit(solution)/shard_map/all_to_all | solution.py:355
  107.7 0.5 slice_bitcast_fusion
  108.2 7.7 %all-to-all-done.1 = f16[16,24,128]{2,1,0:T(8,128)(2,1)S(1)} async-done(((f16[16,24,128]{2,1,0:T(8,128)(2,1)}), f16[16,24,128]{2,1,0:T(8,128)(2,1)S(1)}, u32[]{:S(2)}, u32[]{:S(2)}) %all-to-all-start.1) | async-done | bytes 98336 | tf_op jit(solution)/shard_map/all_to_all | solution.py:355
  116.0 0.1 fusion.4
  116.1 0.1 fusion.5
  116.2 0.1 reshape.12
  116.3 0.1 reshape.13
  116.4 0.7 broadcast_select_fusion.2
  (7 shorter events, 0.1 us)
Async XLA Ops:
  3.5 3.5 %collective-permute-start = (bf16[576,128]{1,0:T(8,128)(2,1)}, bf16[576,128]{1,0:T(8,128)(2,1)S(1)}, u32[]{:S(2)}, u32[]{:S(2)}) collective-permute-start(bf16[576,128]{1,0:T(8,128)(2,1)} %get-tuple-element.20), channel_id=1, source_target_pairs={{0,1},{1,0},{2,3},{3,2},{4,5},{5,4},{6,7},{7,6},{8,9},{9,8},{10,11... | collective-permute-start | bytes 442376 | tf_op jit(solution)/shard_map/ppermute | solution.py:249
  7.0 9.3 %copy-start = (bf16[128,1152]{1,0:T(8,128)(2,1)S(1)}, bf16[128,1152]{1,0:T(8,128)(2,1)}, u32[]{:S(2)}) copy-start(bf16[128,1152]{1,0:T(8,128)(2,1)} %xi.2) | copy-start | bytes 884740
  7.0 9.3 %copy-start.1 = (bf16[128,1152]{1,0:T(8,128)(2,1)S(1)}, bf16[128,1152]{1,0:T(8,128)(2,1)}, u32[]{:S(2)}) copy-start(bf16[128,1152]{1,0:T(8,128)(2,1)} %xt.2) | copy-start | bytes 884740
  7.1 22.2 %collective-permute-start.1 = (bf16[576,128]{1,0:T(8,128)(2,1)S(1)}, bf16[576,128]{1,0:T(8,128)(2,1)S(1)}, u32[]{:S(2)}, u32[]{:S(2)}) collective-permute-start(bf16[576,128]{1,0:T(8,128)(2,1)S(1)} %get-tuple-element.37.refs_0_.o0), channel_id=1, source_target_pairs={{0,4},{1,1021},{2,6},{3,1023},{4,8},{5,1},{6,10},{7,3},{8,12},{9,5... | collective-permute-start | bytes 442376 | tf_op jit(solution)/shard_map/ppermute | solution.py:39
  11.1 23.1 %collective-permute-start.3 = (bf16[576,128]{1,0:T(8,128)(2,1)S(1)}, bf16[576,128]{1,0:T(8,128)(2,1)S(1)}, u32[]{:S(2)}, u32[]{:S(2)}) collective-permute-start(bf16[576,128]{1,0:T(8,128)(2,1)S(1)} %get-tuple-element.37.refs_0_.o0), channel_id=1, source_target_pairs={{0,8},{1,1017},{2,10},{3,1019},{4,12},{5,1021},{6,14},{7,1023},{8,... | collective-permute-start | bytes 442376 | tf_op jit(solution)/shard_map/ppermute | solution.py:39
  16.7 31.3 %collective-permute-start.7 = (bf16[1280,128]{1,0:T(8,128)(2,1)S(1)}, bf16[1280,128]{1,0:T(8,128)(2,1)S(1)}, u32[]{:S(2)}, u32[]{:S(2)}) collective-permute-start(bf16[1280,128]{1,0:T(8,128)(2,1)S(1)} %get-tuple-element.24), channel_id=1, source_target_pairs={{0,128},{4,132},{8,136},{12,140},{16,144},{20,148},{24,152},{28,15... | collective-permute-start | bytes 983048 | tf_op jit(solution)/shard_map/ppermute | solution.py:270
  29.3 11.6 %collective-permute-start.2 = (bf16[576,128]{1,0:T(8,128)(2,1)S(1)}, bf16[576,128]{1,0:T(8,128)(2,1)S(1)}, u32[]{:S(2)}, u32[]{:S(2)}) collective-permute-start(bf16[576,128]{1,0:T(8,128)(2,1)S(1)} %collective-permute-done.1.refs_1_.o1), channel_id=1, source_target_pairs={{0,8},{1,1017},{2,10},{3,1019},{4,12},{5,1021},{6,14},{7,1023},{8,... | collective-permute-start | bytes 442376 | tf_op jit(solution)/shard_map/ppermute | solution.py:39
  34.2 10.1 %collective-permute-start.4 = (bf16[576,128]{1,0:T(8,128)(2,1)S(1)}, bf16[576,128]{1,0:T(8,128)(2,1)S(1)}, u32[]{:S(2)}, u32[]{:S(2)}) collective-permute-start(bf16[576,128]{1,0:T(8,128)(2,1)S(1)} %collective-permute-done.3.refs_2_.o2), channel_id=1, source_target_pairs={{0,8},{1,1017},{2,10},{3,1019},{4,12},{5,1021},{6,14},{7,1023},{8,... | collective-permute-start | bytes 442376 | tf_op jit(solution)/shard_map/ppermute | solution.py:39
  37.7 10.3 %collective-permute-start.6 = (bf16[400,128]{1,0:T(8,128)(2,1)S(1)}, bf16[400,128]{1,0:T(8,128)(2,1)S(1)}, u32[]{:S(2)}, u32[]{:S(2)}) collective-permute-start(bf16[400,128]{1,0:T(8,128)(2,1)S(1)} %scores.3.mine), channel_id=1, source_target_pairs={{0,2},{1,3},{2,0},{3,1},{4,6},{5,7},{6,4},{7,5},{8,10},{9,11},{10,... | collective-permute-start | bytes 307208 | tf_op jit(solution)/shard_map/ppermute | solution.py:284
  44.6 7.7 %collective-permute-start.5 = (bf16[272,128]{1,0:T(8,128)(2,1)S(1)}, bf16[272,128]{1,0:T(8,128)(2,1)S(1)}, u32[]{:S(2)}, u32[]{:S(2)}) collective-permute-start(bf16[272,128]{1,0:T(8,128)(2,1)S(1)} %scores.2.mine), channel_id=1, source_target_pairs={{0,2},{1,3},{2,0},{3,1},{4,6},{5,7},{6,4},{7,5},{8,10},{9,11},{10,... | collective-permute-start | bytes 208904 | tf_op jit(solution)/shard_map/ppermute | solution.py:287
  52.3 5.2 %copy-start.2 = (f32[576,128]{1,0:T(8,128)S(1)}, f32[576,128]{1,0:T(8,128)}, u32[]{:S(2)}) copy-start(f32[576,128]{1,0:T(8,128)} %get-tuple-element.30.z) | copy-start | bytes 884740
  53.4 4.1 %collective-permute-start.8 = (f32[296,128]{1,0:T(8,128)S(1)}, f32[296,128]{1,0:T(8,128)S(1)}, u32[]{:S(2)}, u32[]{:S(2)}) collective-permute-start(f32[296,128]{1,0:T(8,128)S(1)} %get-tuple-element.29), channel_id=1, source_target_pairs={{0,1},{1,0},{2,3},{3,2},{4,5},{5,4},{6,7},{7,6},{8,9},{9,8},{10,11... | collective-permute-start | bytes 454664 | tf_op jit(solution)/shard_map/ppermute | solution.py:308
  58.2 10.9 %collective-permute-start.9 = (bf16[576,128]{1,0:T(8,128)(2,1)S(1)}, bf16[576,128]{1,0:T(8,128)(2,1)S(1)}, u32[]{:S(2)}, u32[]{:S(2)}) collective-permute-start(bf16[576,128]{1,0:T(8,128)(2,1)S(1)} %get-tuple-element.33), channel_id=1, source_target_pairs={{0,128},{4,132},{8,136},{12,140},{16,144},{20,148},{24,152},{28,15... | collective-permute-start | bytes 442376 | tf_op jit(solution)/shard_map/ppermute | solution.py:321
  86.1 29.9 %all-to-all-start.1 = ((f16[16,24,128]{2,1,0:T(8,128)(2,1)}), f16[16,24,128]{2,1,0:T(8,128)(2,1)S(1)}, u32[]{:S(2)}, u32[]{:S(2)}) async-start(f16[16,24,128]{2,1,0:T(8,128)(2,1)} %convert_element_type.7), calls=%async_computation.1 | async-start | bytes 196608 | tf_op jit(solution)/shard_map/all_to_all | solution.py:355

commit v13 on v12

--- a/solution.py
+++ b/solution.py
@@ -165,7 +165,12 @@
         out[p, 2 * whole // LANES * block :] = (upper + lower).astype(BF16)
 
 
-def ring_kernel(got, out):
+def ring_order(places):
+    near = [m // 2 if m % 2 == 0 else places - 1 - m // 2 for m in range(places)]
+    return [places // 2] + [m for m in near if m != places // 2]
+
+
+def ring_kernel(got, out, laid):
     total = jnp.sum(got[...].astype(F32), axis=0)
     top = jnp.max(jnp.max(jnp.abs(total), axis=0, keepdims=True), axis=1, keepdims=True)
     power = jnp.floor(jnp.log2(jnp.where(top > 0, top, 1.0))) - 13.0
@@ -174,10 +179,10 @@
     places = out.shape[0]
     count = total.shape[0] // places
     for j in range(count):
-        middle = j * places + places // 2
-        out[: places // 2, j] = total[middle : (j + 1) * places]
-        out[places // 2 :, j] = total[j * places : middle]
-    out[:, count] = jnp.broadcast_to(power, (places, LANES))
+        laid[:, j] = total[j * places : (j + 1) * places]
+    laid[:, count] = jnp.broadcast_to(power, (places, LANES))
+    for at, place in enumerate(ring_order(places)):
+        out[at] = laid[place]
 
 
 def order_kernel(column, xi, xt, own_i, own_t, away, turned):
@@ -343,13 +348,12 @@
         out_shape=jax.ShapeDtypeStruct((places, payload // places + 1, LANES), F32),
         in_specs=[array],
         out_specs=array,
+        scratch_shapes=[pltpu.VMEM((places, payload // places + 1, LANES), F32)],
         compiler_params=VMEM,
         name="ring",
     )(grads)
     groups = [
-        [g * RING + (2 * m + places) % RING + q for m in range(places)]
-        for g in range(planes)
-        for q in range(2)
+        [g * RING + 2 * m + q for m in ring_order(places)] for g in range(planes) for q in range(2)
     ]
     sent = sent.astype(jnp.float16)
     back = lax.all_to_all(sent, "dp", 0, 0, axis_index_groups=groups, tiled=True).astype(F32)

time: 118 us -> 117 us (level)
  no operation moved by 1% of the time
where the time goes in v13:
time: 117 us; the launch traced here: 116 us
  starting transfers between devices  55.6 us (48%)
  waiting for transfers between devices  31.9 us (27%)
  blocking collectives  15.1 us (13%)
  Pallas kernels  8 us (7%)
  between operations  2.2 us (2%)
  local copies, waits for them, and re-layouts  1.79 us (2%)
  other arithmetic  1.58 us (1%)
    all_to_all x1, starting transfers between devices, shards(): lax.all_to_all(sent, 'dp', 0, 0, axis_index_groups=groups, tiled=True)  21.6 us
    ppermute x4, waiting for transfers between devices, shifted(): return lax.ppermute(block, ('dp', 'tower'), route)  16.3 us
    all_to_all x1, blocking collectives, shards(): lax.all_to_all(grads, 'dp', 0, 0, axis_index_groups=groups, tiled=True)  15.1 us
    ppermute x4, starting transfers between devices, shifted(): return lax.ppermute(block, ('dp', 'tower'), route)  13 us
    ppermute x1, starting transfers between devices, shards(): theirs = lax.ppermute(send, 'dp', beside)  6.79 us
    all_to_all x1, waiting for transfers between devices, shards(): lax.all_to_all(sent, 'dp', 0, 0, axis_index_groups=groups, tiled=True)  6.77 us
    ppermute x1, waiting for transfers between devices, shards(): theirs = lax.ppermute(send, 'dp', beside)  4.14 us
    ppermute x1, starting transfers between devices, shards(): far_peer = lax.ppermute(far, 'tower', to_chip)  3.31 us
  transfers between devices with their start and end apart: 11, of which 8 were waited for; matrix products, arithmetic and copies ran while one was open for 1% of the time, Pallas kernels for 2%

profile of v13, /device:TPU:6, one launch (start us, length us, event | category | flops | bytes accessed | tf_op | source)
XLA Modules:
  0.0 116.2 jit_solution(3931112067372149633)
XLA Ops:
  0.6 2.9 %project.1 = (f32[576,128]{1,0:T(8,128)}, bf16[576,128]{1,0:T(8,128)(2,1)}) custom-call(bf16[128,1152]{1,0:T(8,128)(2,1)} %xi.2, bf16[288,1152]{1,0:T(8,128)(2,1)} %bitcast.7, bf16[128,1152]{1,0:T(8,128)(2,1)} %xt.2, bf16[288,1152]{1,0:T(8,128)(2,1)} %bitcast.8), custom_call_target="tpu_custom_call" | custom-call | tf_op jit(solution)/shard_map/project/pallas_call | solution.py:242
  3.5 1.9 %collective-permute-start = (bf16[576,128]{1,0:T(8,128)(2,1)}, bf16[576,128]{1,0:T(8,128)(2,1)S(1)}, u32[]{:S(2)}, u32[]{:S(2)}) collective-permute-start(bf16[576,128]{1,0:T(8,128)(2,1)} %get-tuple-element.20), channel_id=1, source_target_pairs={{0,1},{1,0},{2,3},{3,2},{4,5},{5,4},{6,7},{7,6},{8,9},{9,8},{10,11... | collective-permute-start | bytes 442376 | tf_op jit(solution)/shard_map/ppermute | solution.py:254
  5.5 0.9 fusion.1
  6.4 0.6 collective-permute-done
  7.0 0.0 copy-start
  7.0 0.0 copy-start.1
  7.1 0.1 broadcast_select_fusion
  7.1 4.0 %collective-permute-start.1 = (bf16[576,128]{1,0:T(8,128)(2,1)S(1)}, bf16[576,128]{1,0:T(8,128)(2,1)S(1)}, u32[]{:S(2)}, u32[]{:S(2)}) collective-permute-start(bf16[576,128]{1,0:T(8,128)(2,1)S(1)} %get-tuple-element.37.refs_0_.o0), channel_id=1, source_target_pairs={{0,4},{1,1021},{2,6},{3,1023},{4,8},{5,1},{6,10},{7,3},{8,12},{9,5... | collective-permute-start | bytes 442376 | tf_op jit(solution)/shard_map/ppermute | solution.py:39
  11.1 5.2 %collective-permute-start.3 = (bf16[576,128]{1,0:T(8,128)(2,1)S(1)}, bf16[576,128]{1,0:T(8,128)(2,1)S(1)}, u32[]{:S(2)}, u32[]{:S(2)}) collective-permute-start(bf16[576,128]{1,0:T(8,128)(2,1)S(1)} %get-tuple-element.37.refs_0_.o0), channel_id=1, source_target_pairs={{0,8},{1,1017},{2,10},{3,1019},{4,12},{5,1021},{6,14},{7,1023},{8,... | collective-permute-start | bytes 442376 | tf_op jit(solution)/shard_map/ppermute | solution.py:39
  16.3 0.0 copy-done
  16.3 0.0 copy-done.1
  16.3 0.3 order.1
  16.7 2.7 %collective-permute-start.7 = (bf16[1280,128]{1,0:T(8,128)(2,1)S(1)}, bf16[1280,128]{1,0:T(8,128)(2,1)S(1)}, u32[]{:S(2)}, u32[]{:S(2)}) collective-permute-start(bf16[1280,128]{1,0:T(8,128)(2,1)S(1)} %get-tuple-element.24), channel_id=1, source_target_pairs={{0,128},{4,132},{8,136},{12,140},{16,144},{20,148},{24,152},{28,15... | collective-permute-start | bytes 983048 | tf_op jit(solution)/shard_map/ppermute | solution.py:275
  19.4 9.9 %collective-permute-done.1.refs_1_.o1 = bf16[576,128]{1,0:T(8,128)(2,1)S(1)} collective-permute-done((bf16[576,128]{1,0:T(8,128)(2,1)S(1)}, bf16[576,128]{1,0:T(8,128)(2,1)S(1)}, u32[]{:S(2)}, u32[]{:S(2)}) %collective-permute-start.1) | collective-permute-done | bytes 147488 | tf_op jit(solution)/shard_map/ppermute | solution.py:39
  29.3 1.9 %collective-permute-start.2 = (bf16[576,128]{1,0:T(8,128)(2,1)S(1)}, bf16[576,128]{1,0:T(8,128)(2,1)S(1)}, u32[]{:S(2)}, u32[]{:S(2)}) collective-permute-start(bf16[576,128]{1,0:T(8,128)(2,1)S(1)} %collective-permute-done.1.refs_1_.o1), channel_id=1, source_target_pairs={{0,8},{1,1017},{2,10},{3,1019},{4,12},{5,1021},{6,14},{7,1023},{8,... | collective-permute-start | bytes 442376 | tf_op jit(solution)/shard_map/ppermute | solution.py:39
  31.2 3.0 %collective-permute-done.3.refs_2_.o2 = bf16[576,128]{1,0:T(8,128)(2,1)S(1)} collective-permute-done((bf16[576,128]{1,0:T(8,128)(2,1)S(1)}, bf16[576,128]{1,0:T(8,128)(2,1)S(1)}, u32[]{:S(2)}, u32[]{:S(2)}) %collective-permute-start.3) | collective-permute-done | bytes 147488 | tf_op jit(solution)/shard_map/ppermute | solution.py:39
  34.2 1.9 %collective-permute-start.4 = (bf16[576,128]{1,0:T(8,128)(2,1)S(1)}, bf16[576,128]{1,0:T(8,128)(2,1)S(1)}, u32[]{:S(2)}, u32[]{:S(2)}) collective-permute-start(bf16[576,128]{1,0:T(8,128)(2,1)S(1)} %collective-permute-done.3.refs_2_.o2), channel_id=1, source_target_pairs={{0,8},{1,1017},{2,10},{3,1019},{4,12},{5,1021},{6,14},{7,1023},{8,... | collective-permute-start | bytes 442376 | tf_op jit(solution)/shard_map/ppermute | solution.py:39
  37.4 0.3 scores.3.mine
  37.7 3.1 %collective-permute-start.6 = (bf16[400,128]{1,0:T(8,128)(2,1)S(1)}, bf16[400,128]{1,0:T(8,128)(2,1)S(1)}, u32[]{:S(2)}, u32[]{:S(2)}) collective-permute-start(bf16[400,128]{1,0:T(8,128)(2,1)S(1)} %scores.3.mine), channel_id=1, source_target_pairs={{0,2},{1,3},{2,0},{3,1},{4,6},{5,7},{6,4},{7,5},{8,10},{9,11},{10,... | collective-permute-start | bytes 307208 | tf_op jit(solution)/shard_map/ppermute | solution.py:289
  40.9 0.0 collective-permute-done.2.refs_0_.o3
  40.9 3.4 %collective-permute-done.4.refs_1_.o4 = bf16[576,128]{1,0:T(8,128)(2,1)S(1)} collective-permute-done((bf16[576,128]{1,0:T(8,128)(2,1)S(1)}, bf16[576,128]{1,0:T(8,128)(2,1)S(1)}, u32[]{:S(2)}, u32[]{:S(2)}) %collective-permute-start.4) | collective-permute-done | bytes 147488 | tf_op jit(solution)/shard_map/ppermute | solution.py:39
  44.3 0.3 scores.2.mine
  44.6 3.3 %collective-permute-start.5 = (bf16[272,128]{1,0:T(8,128)(2,1)S(1)}, bf16[272,128]{1,0:T(8,128)(2,1)S(1)}, u32[]{:S(2)}, u32[]{:S(2)}) collective-permute-start(bf16[272,128]{1,0:T(8,128)(2,1)S(1)} %scores.2.mine), channel_id=1, source_target_pairs={{0,2},{1,3},{2,0},{3,1},{4,6},{5,7},{6,4},{7,5},{8,10},{9,11},{10,... | collective-permute-start | bytes 208904 | tf_op jit(solution)/shard_map/ppermute | solution.py:292
  47.9 0.1 pad_maximum_fusion.2.numbers
  48.0 0.0 collective-permute-done.6.peer
  48.0 0.0 collective-permute-done.7.beside
  48.0 1.2 %near.1 = (f32[576,128]{1,0:T(8,128)S(1)}, f32[8,128]{1,0:T(8,128)S(1)}) custom-call(f32[3]{0:T(128)S(1)} %pad_maximum_fusion.2.numbers, bf16[400,128]{1,0:T(8,128)(2,1)S(1)} %scores.3.mine, bf16[400,128]{1,0:T(8,128)(2,1)S(1)} %collective-permute-done.6.peer, bf16[576,128]{1,0:T(8,128)(2,1)S(1)} %get-tuple-element.37.refs_0_.o0, ...), custom_call_target="tpu_custom_call" | custom-call | tf_op jit(solution)/shard_map/near/pallas_call | solution.py:293
  49.2 3.1 %collective-permute-done.5.peer = bf16[272,128]{1,0:T(8,128)(2,1)S(1)} collective-permute-done((bf16[272,128]{1,0:T(8,128)(2,1)S(1)}, bf16[272,128]{1,0:T(8,128)(2,1)S(1)}, u32[]{:S(2)}, u32[]{:S(2)}) %collective-permute-start.5) | collective-permute-done | bytes 69664 | tf_op jit(solution)/shard_map/ppermute | solution.py:292
  52.3 0.0 copy-start.2
  52.3 1.1 far.1
  53.4 3.1 %collective-permute-start.8 = (f32[296,128]{1,0:T(8,128)S(1)}, f32[296,128]{1,0:T(8,128)S(1)}, u32[]{:S(2)}, u32[]{:S(2)}) collective-permute-start(f32[296,128]{1,0:T(8,128)S(1)} %get-tuple-element.29), channel_id=1, source_target_pairs={{0,1},{1,0},{2,3},{3,2},{4,5},{5,4},{6,7},{7,6},{8,9},{9,8},{10,11... | collective-permute-start | bytes 454664 | tf_op jit(solution)/shard_map/ppermute | solution.py:313
  56.5 1.0 collective-permute-done.8.got
  57.5 0.0 copy-done.2
  57.5 0.6 slopes.1
  58.2 6.8 %collective-permute-start.9 = (bf16[576,128]{1,0:T(8,128)(2,1)S(1)}, bf16[576,128]{1,0:T(8,128)(2,1)S(1)}, u32[]{:S(2)}, u32[]{:S(2)}) collective-permute-start(bf16[576,128]{1,0:T(8,128)(2,1)S(1)} %get-tuple-element.33), channel_id=1, source_target_pairs={{0,128},{4,132},{8,136},{12,140},{16,144},{20,148},{24,152},{28,15... | collective-permute-start | bytes 442376 | tf_op jit(solution)/shard_map/ppermute | solution.py:326
  65.0 4.1 %collective-permute-done.9.theirs = bf16[576,128]{1,0:T(8,128)(2,1)S(1)} collective-permute-done((bf16[576,128]{1,0:T(8,128)(2,1)S(1)}, bf16[576,128]{1,0:T(8,128)(2,1)S(1)}, u32[]{:S(2)}, u32[]{:S(2)}) %collective-permute-start.9) | collective-permute-done | bytes 147488 | tf_op jit(solution)/shard_map/ppermute | solution.py:326
  69.1 0.8 gradients.1
  70.0 15.1 %all_to_all.10.got = bf16[8,368,128]{2,1,0:T(8,128)(2,1)S(1)} all-to-all(bf16[8,368,128]{2,1,0:T(8,128)(2,1)S(1)} %gradients.1), channel_id=1, replica_groups={{0,4,256,260,512,516,768,772},{8,12,264,268,520,524,776,780},{16,20,272..., dimensions={0} | all-to-all | bytes 1507328 | tf_op jit(solution)/shard_map/all_to_all | solution.py:345
  85.1 0.4 ring.1
  85.4 0.7 convert_element_type.7
  86.1 21.6 %all-to-all-start.1 = ((f16[16,24,128]{2,1,0:T(8,128)(2,1)}), f16[16,24,128]{2,1,0:T(8,128)(2,1)S(1)}, u32[]{:S(2)}, u32[]{:S(2)}) async-start(f16[16,24,128]{2,1,0:T(8,128)(2,1)} %convert_element_type.7), calls=%async_computation.1 | async-start | bytes 196608 | tf_op jit(solution)/shard_map/all_to_all | solution.py:359
  107.7 0.5 slice_bitcast_fusion
  108.3 6.8 %all-to-all-done.1 = f16[16,24,128]{2,1,0:T(8,128)(2,1)S(1)} async-done(((f16[16,24,128]{2,1,0:T(8,128)(2,1)}), f16[16,24,128]{2,1,0:T(8,128)(2,1)S(1)}, u32[]{:S(2)}, u32[]{:S(2)}) %all-to-all-start.1) | async-done | bytes 98336 | tf_op jit(solution)/shard_map/all_to_all | solution.py:359
  115.1 0.1 fusion.4
  115.2 0.1 fusion.5
  115.3 0.1 reshape.12
  115.4 0.1 reshape.13
  115.5 0.7 broadcast_select_fusion.2
  (7 shorter events, 0.1 us)
Async XLA Ops:
  3.5 3.5 %collective-permute-start = (bf16[576,128]{1,0:T(8,128)(2,1)}, bf16[576,128]{1,0:T(8,128)(2,1)S(1)}, u32[]{:S(2)}, u32[]{:S(2)}) collective-permute-start(bf16[576,128]{1,0:T(8,128)(2,1)} %get-tuple-element.20), channel_id=1, source_target_pairs={{0,1},{1,0},{2,3},{3,2},{4,5},{5,4},{6,7},{7,6},{8,9},{9,8},{10,11... | collective-permute-start | bytes 442376 | tf_op jit(solution)/shard_map/ppermute | solution.py:254
  7.0 9.3 %copy-start = (bf16[128,1152]{1,0:T(8,128)(2,1)S(1)}, bf16[128,1152]{1,0:T(8,128)(2,1)}, u32[]{:S(2)}) copy-start(bf16[128,1152]{1,0:T(8,128)(2,1)} %xi.2) | copy-start | bytes 884740
  7.0 9.3 %copy-start.1 = (bf16[128,1152]{1,0:T(8,128)(2,1)S(1)}, bf16[128,1152]{1,0:T(8,128)(2,1)}, u32[]{:S(2)}) copy-start(bf16[128,1152]{1,0:T(8,128)(2,1)} %xt.2) | copy-start | bytes 884740
  7.1 22.2 %collective-permute-start.1 = (bf16[576,128]{1,0:T(8,128)(2,1)S(1)}, bf16[576,128]{1,0:T(8,128)(2,1)S(1)}, u32[]{:S(2)}, u32[]{:S(2)}) collective-permute-start(bf16[576,128]{1,0:T(8,128)(2,1)S(1)} %get-tuple-element.37.refs_0_.o0), channel_id=1, source_target_pairs={{0,4},{1,1021},{2,6},{3,1023},{4,8},{5,1},{6,10},{7,3},{8,12},{9,5... | collective-permute-start | bytes 442376 | tf_op jit(solution)/shard_map/ppermute | solution.py:39
  11.1 23.1 %collective-permute-start.3 = (bf16[576,128]{1,0:T(8,128)(2,1)S(1)}, bf16[576,128]{1,0:T(8,128)(2,1)S(1)}, u32[]{:S(2)}, u32[]{:S(2)}) collective-permute-start(bf16[576,128]{1,0:T(8,128)(2,1)S(1)} %get-tuple-element.37.refs_0_.o0), channel_id=1, source_target_pairs={{0,8},{1,1017},{2,10},{3,1019},{4,12},{5,1021},{6,14},{7,1023},{8,... | collective-permute-start | bytes 442376 | tf_op jit(solution)/shard_map/ppermute | solution.py:39
  16.7 31.3 %collective-permute-start.7 = (bf16[1280,128]{1,0:T(8,128)(2,1)S(1)}, bf16[1280,128]{1,0:T(8,128)(2,1)S(1)}, u32[]{:S(2)}, u32[]{:S(2)}) collective-permute-start(bf16[1280,128]{1,0:T(8,128)(2,1)S(1)} %get-tuple-element.24), channel_id=1, source_target_pairs={{0,128},{4,132},{8,136},{12,140},{16,144},{20,148},{24,152},{28,15... | collective-permute-start | bytes 983048 | tf_op jit(solution)/shard_map/ppermute | solution.py:275
  29.3 11.6 %collective-permute-start.2 = (bf16[576,128]{1,0:T(8,128)(2,1)S(1)}, bf16[576,128]{1,0:T(8,128)(2,1)S(1)}, u32[]{:S(2)}, u32[]{:S(2)}) collective-permute-start(bf16[576,128]{1,0:T(8,128)(2,1)S(1)} %collective-permute-done.1.refs_1_.o1), channel_id=1, source_target_pairs={{0,8},{1,1017},{2,10},{3,1019},{4,12},{5,1021},{6,14},{7,1023},{8,... | collective-permute-start | bytes 442376 | tf_op jit(solution)/shard_map/ppermute | solution.py:39
  34.2 10.1 %collective-permute-start.4 = (bf16[576,128]{1,0:T(8,128)(2,1)S(1)}, bf16[576,128]{1,0:T(8,128)(2,1)S(1)}, u32[]{:S(2)}, u32[]{:S(2)}) collective-permute-start(bf16[576,128]{1,0:T(8,128)(2,1)S(1)} %collective-permute-done.3.refs_2_.o2), channel_id=1, source_target_pairs={{0,8},{1,1017},{2,10},{3,1019},{4,12},{5,1021},{6,14},{7,1023},{8,... | collective-permute-start | bytes 442376 | tf_op jit(solution)/shard_map/ppermute | solution.py:39
  37.7 10.3 %collective-permute-start.6 = (bf16[400,128]{1,0:T(8,128)(2,1)S(1)}, bf16[400,128]{1,0:T(8,128)(2,1)S(1)}, u32[]{:S(2)}, u32[]{:S(2)}) collective-permute-start(bf16[400,128]{1,0:T(8,128)(2,1)S(1)} %scores.3.mine), channel_id=1, source_target_pairs={{0,2},{1,3},{2,0},{3,1},{4,6},{5,7},{6,4},{7,5},{8,10},{9,11},{10,... | collective-permute-start | bytes 307208 | tf_op jit(solution)/shard_map/ppermute | solution.py:289
  44.6 7.7 %collective-permute-start.5 = (bf16[272,128]{1,0:T(8,128)(2,1)S(1)}, bf16[272,128]{1,0:T(8,128)(2,1)S(1)}, u32[]{:S(2)}, u32[]{:S(2)}) collective-permute-start(bf16[272,128]{1,0:T(8,128)(2,1)S(1)} %scores.2.mine), channel_id=1, source_target_pairs={{0,2},{1,3},{2,0},{3,1},{4,6},{5,7},{6,4},{7,5},{8,10},{9,11},{10,... | collective-permute-start | bytes 208904 | tf_op jit(solution)/shard_map/ppermute | solution.py:292
  52.3 5.2 %copy-start.2 = (f32[576,128]{1,0:T(8,128)S(1)}, f32[576,128]{1,0:T(8,128)}, u32[]{:S(2)}) copy-start(f32[576,128]{1,0:T(8,128)} %get-tuple-element.30.z) | copy-start | bytes 884740
  53.4 4.1 %collective-permute-start.8 = (f32[296,128]{1,0:T(8,128)S(1)}, f32[296,128]{1,0:T(8,128)S(1)}, u32[]{:S(2)}, u32[]{:S(2)}) collective-permute-start(f32[296,128]{1,0:T(8,128)S(1)} %get-tuple-element.29), channel_id=1, source_target_pairs={{0,1},{1,0},{2,3},{3,2},{4,5},{5,4},{6,7},{7,6},{8,9},{9,8},{10,11... | collective-permute-start | bytes 454664 | tf_op jit(solution)/shard_map/ppermute | solution.py:313
  58.2 10.9 %collective-permute-start.9 = (bf16[576,128]{1,0:T(8,128)(2,1)S(1)}, bf16[576,128]{1,0:T(8,128)(2,1)S(1)}, u32[]{:S(2)}, u32[]{:S(2)}) collective-permute-start(bf16[576,128]{1,0:T(8,128)(2,1)S(1)} %get-tuple-element.33), channel_id=1, source_target_pairs={{0,128},{4,132},{8,136},{12,140},{16,144},{20,148},{24,152},{28,15... | collective-permute-start | bytes 442376 | tf_op jit(solution)/shard_map/ppermute | solution.py:326
  86.1 28.9 %all-to-all-start.1 = ((f16[16,24,128]{2,1,0:T(8,128)(2,1)}), f16[16,24,128]{2,1,0:T(8,128)(2,1)S(1)}, u32[]{:S(2)}, u32[]{:S(2)}) async-start(f16[16,24,128]{2,1,0:T(8,128)(2,1)} %convert_element_type.7), calls=%async_computation.1 | async-start | bytes 196608 | tf_op jit(solution)/shard_map/all_to_all | solution.py:359

commit v14 on v13

--- a/solution.py
+++ b/solution.py
@@ -166,8 +166,9 @@
 
 
 def ring_order(places):
+    first = 3 * places // 8
     near = [m // 2 if m % 2 == 0 else places - 1 - m // 2 for m in range(places)]
-    return [places // 2] + [m for m in near if m != places // 2]
+    return [first] + [m for m in near if m != first]
 
 
 def ring_kernel(got, out, laid):

time: 117 us -> 119 us (1.017)
  waiting for transfers between devices: 31.9 us -> 36 us
  starting transfers between devices: 55.6 us -> 53.5 us
    all_to_all x1, waiting for transfers between devices: 6.77 us -> 10.9 us  [shards(): lax.all_to_all(sent, 'dp', 0, 0, axis_index_groups=groups, tiled=True)]
    all_to_all x1, starting transfers between devices: 21.6 us -> 19.6 us  [shards(): lax.all_to_all(sent, 'dp', 0, 0, axis_index_groups=groups, tiled=True)]
where the time goes in v14:
time: 119 us; the launch traced here: 118 us
  starting transfers between devices  53.5 us (45%)
  waiting for transfers between devices  36 us (30%)
  blocking collectives  15.1 us (13%)
  Pallas kernels  8 us (7%)
  between operations  2.2 us (2%)
  local copies, waits for them, and re-layouts  1.79 us (2%)
  other arithmetic  1.58 us (1%)
    all_to_all x1, starting transfers between devices, shards(): lax.all_to_all(sent, 'dp', 0, 0, axis_index_groups=groups, tiled=True)  19.6 us
    ppermute x4, waiting for transfers between devices, shifted(): return lax.ppermute(block, ('dp', 'tower'), route)  16.3 us
    all_to_all x1, blocking collectives, shards(): lax.all_to_all(grads, 'dp', 0, 0, axis_index_groups=groups, tiled=True)  15.1 us
    ppermute x4, starting transfers between devices, shifted(): return lax.ppermute(block, ('dp', 'tower'), route)  13 us
    all_to_all x1, waiting for transfers between devices, shards(): lax.all_to_all(sent, 'dp', 0, 0, axis_index_groups=groups, tiled=True)  10.9 us
    ppermute x1, starting transfers between devices, shards(): theirs = lax.ppermute(send, 'dp', beside)  6.79 us
    ppermute x1, waiting for transfers between devices, shards(): theirs = lax.ppermute(send, 'dp', beside)  4.14 us
    ppermute x1, starting transfers between devices, shards(): far_peer = lax.ppermute(far, 'tower', to_chip)  3.31 us
  transfers between devices with their start and end apart: 11, of which 8 were waited for; matrix products, arithmetic and copies ran while one was open for 1% of the time, Pallas kernels for 2%

profile of v14, /device:TPU:6, one launch (start us, length us, event | category | flops | bytes accessed | tf_op | source)
XLA Modules:
  0.0 118.2 jit_solution(8775302294841696487)
XLA Ops:
  0.6 2.9 %project.1 = (f32[576,128]{1,0:T(8,128)}, bf16[576,128]{1,0:T(8,128)(2,1)}) custom-call(bf16[128,1152]{1,0:T(8,128)(2,1)} %xi.2, bf16[288,1152]{1,0:T(8,128)(2,1)} %bitcast.7, bf16[128,1152]{1,0:T(8,128)(2,1)} %xt.2, bf16[288,1152]{1,0:T(8,128)(2,1)} %bitcast.8), custom_call_target="tpu_custom_call" | custom-call | tf_op jit(solution)/shard_map/project/pallas_call | solution.py:243
  3.5 1.9 %collective-permute-start = (bf16[576,128]{1,0:T(8,128)(2,1)}, bf16[576,128]{1,0:T(8,128)(2,1)S(1)}, u32[]{:S(2)}, u32[]{:S(2)}) collective-permute-start(bf16[576,128]{1,0:T(8,128)(2,1)} %get-tuple-element.20), channel_id=1, source_target_pairs={{0,1},{1,0},{2,3},{3,2},{4,5},{5,4},{6,7},{7,6},{8,9},{9,8},{10,11... | collective-permute-start | bytes 442376 | tf_op jit(solution)/shard_map/ppermute | solution.py:255
  5.5 0.9 fusion.1
  6.4 0.6 collective-permute-done
  7.0 0.0 copy-start
  7.0 0.0 copy-start.1
  7.1 0.1 broadcast_select_fusion
  7.1 4.0 %collective-permute-start.1 = (bf16[576,128]{1,0:T(8,128)(2,1)S(1)}, bf16[576,128]{1,0:T(8,128)(2,1)S(1)}, u32[]{:S(2)}, u32[]{:S(2)}) collective-permute-start(bf16[576,128]{1,0:T(8,128)(2,1)S(1)} %get-tuple-element.37.refs_0_.o0), channel_id=1, source_target_pairs={{0,4},{1,1021},{2,6},{3,1023},{4,8},{5,1},{6,10},{7,3},{8,12},{9,5... | collective-permute-start | bytes 442376 | tf_op jit(solution)/shard_map/ppermute | solution.py:39
  11.1 5.2 %collective-permute-start.3 = (bf16[576,128]{1,0:T(8,128)(2,1)S(1)}, bf16[576,128]{1,0:T(8,128)(2,1)S(1)}, u32[]{:S(2)}, u32[]{:S(2)}) collective-permute-start(bf16[576,128]{1,0:T(8,128)(2,1)S(1)} %get-tuple-element.37.refs_0_.o0), channel_id=1, source_target_pairs={{0,8},{1,1017},{2,10},{3,1019},{4,12},{5,1021},{6,14},{7,1023},{8,... | collective-permute-start | bytes 442376 | tf_op jit(solution)/shard_map/ppermute | solution.py:39
  16.3 0.0 copy-done
  16.3 0.0 copy-done.1
  16.3 0.3 order.1
  16.7 2.7 %collective-permute-start.7 = (bf16[1280,128]{1,0:T(8,128)(2,1)S(1)}, bf16[1280,128]{1,0:T(8,128)(2,1)S(1)}, u32[]{:S(2)}, u32[]{:S(2)}) collective-permute-start(bf16[1280,128]{1,0:T(8,128)(2,1)S(1)} %get-tuple-element.24), channel_id=1, source_target_pairs={{0,128},{4,132},{8,136},{12,140},{16,144},{20,148},{24,152},{28,15... | collective-permute-start | bytes 983048 | tf_op jit(solution)/shard_map/ppermute | solution.py:276
  19.4 9.9 %collective-permute-done.1.refs_1_.o1 = bf16[576,128]{1,0:T(8,128)(2,1)S(1)} collective-permute-done((bf16[576,128]{1,0:T(8,128)(2,1)S(1)}, bf16[576,128]{1,0:T(8,128)(2,1)S(1)}, u32[]{:S(2)}, u32[]{:S(2)}) %collective-permute-start.1) | collective-permute-done | bytes 147488 | tf_op jit(solution)/shard_map/ppermute | solution.py:39
  29.3 1.9 %collective-permute-start.2 = (bf16[576,128]{1,0:T(8,128)(2,1)S(1)}, bf16[576,128]{1,0:T(8,128)(2,1)S(1)}, u32[]{:S(2)}, u32[]{:S(2)}) collective-permute-start(bf16[576,128]{1,0:T(8,128)(2,1)S(1)} %collective-permute-done.1.refs_1_.o1), channel_id=1, source_target_pairs={{0,8},{1,1017},{2,10},{3,1019},{4,12},{5,1021},{6,14},{7,1023},{8,... | collective-permute-start | bytes 442376 | tf_op jit(solution)/shard_map/ppermute | solution.py:39
  31.2 3.0 %collective-permute-done.3.refs_2_.o2 = bf16[576,128]{1,0:T(8,128)(2,1)S(1)} collective-permute-done((bf16[576,128]{1,0:T(8,128)(2,1)S(1)}, bf16[576,128]{1,0:T(8,128)(2,1)S(1)}, u32[]{:S(2)}, u32[]{:S(2)}) %collective-permute-start.3) | collective-permute-done | bytes 147488 | tf_op jit(solution)/shard_map/ppermute | solution.py:39
  34.2 1.9 %collective-permute-start.4 = (bf16[576,128]{1,0:T(8,128)(2,1)S(1)}, bf16[576,128]{1,0:T(8,128)(2,1)S(1)}, u32[]{:S(2)}, u32[]{:S(2)}) collective-permute-start(bf16[576,128]{1,0:T(8,128)(2,1)S(1)} %collective-permute-done.3.refs_2_.o2), channel_id=1, source_target_pairs={{0,8},{1,1017},{2,10},{3,1019},{4,12},{5,1021},{6,14},{7,1023},{8,... | collective-permute-start | bytes 442376 | tf_op jit(solution)/shard_map/ppermute | solution.py:39
  37.4 0.3 scores.3.mine
  37.7 3.1 %collective-permute-start.6 = (bf16[400,128]{1,0:T(8,128)(2,1)S(1)}, bf16[400,128]{1,0:T(8,128)(2,1)S(1)}, u32[]{:S(2)}, u32[]{:S(2)}) collective-permute-start(bf16[400,128]{1,0:T(8,128)(2,1)S(1)} %scores.3.mine), channel_id=1, source_target_pairs={{0,2},{1,3},{2,0},{3,1},{4,6},{5,7},{6,4},{7,5},{8,10},{9,11},{10,... | collective-permute-start | bytes 307208 | tf_op jit(solution)/shard_map/ppermute | solution.py:290
  40.9 0.0 collective-permute-done.2.refs_0_.o3
  40.9 3.4 %collective-permute-done.4.refs_1_.o4 = bf16[576,128]{1,0:T(8,128)(2,1)S(1)} collective-permute-done((bf16[576,128]{1,0:T(8,128)(2,1)S(1)}, bf16[576,128]{1,0:T(8,128)(2,1)S(1)}, u32[]{:S(2)}, u32[]{:S(2)}) %collective-permute-start.4) | collective-permute-done | bytes 147488 | tf_op jit(solution)/shard_map/ppermute | solution.py:39
  44.3 0.3 scores.2.mine
  44.6 3.3 %collective-permute-start.5 = (bf16[272,128]{1,0:T(8,128)(2,1)S(1)}, bf16[272,128]{1,0:T(8,128)(2,1)S(1)}, u32[]{:S(2)}, u32[]{:S(2)}) collective-permute-start(bf16[272,128]{1,0:T(8,128)(2,1)S(1)} %scores.2.mine), channel_id=1, source_target_pairs={{0,2},{1,3},{2,0},{3,1},{4,6},{5,7},{6,4},{7,5},{8,10},{9,11},{10,... | collective-permute-start | bytes 208904 | tf_op jit(solution)/shard_map/ppermute | solution.py:293
  47.9 0.1 pad_maximum_fusion.2.numbers
  48.0 0.0 collective-permute-done.6.peer
  48.0 0.0 collective-permute-done.7.beside
  48.0 1.2 %near.1 = (f32[576,128]{1,0:T(8,128)S(1)}, f32[8,128]{1,0:T(8,128)S(1)}) custom-call(f32[3]{0:T(128)S(1)} %pad_maximum_fusion.2.numbers, bf16[400,128]{1,0:T(8,128)(2,1)S(1)} %scores.3.mine, bf16[400,128]{1,0:T(8,128)(2,1)S(1)} %collective-permute-done.6.peer, bf16[576,128]{1,0:T(8,128)(2,1)S(1)} %get-tuple-element.37.refs_0_.o0, ...), custom_call_target="tpu_custom_call" | custom-call | tf_op jit(solution)/shard_map/near/pallas_call | solution.py:294
  49.2 3.1 %collective-permute-done.5.peer = bf16[272,128]{1,0:T(8,128)(2,1)S(1)} collective-permute-done((bf16[272,128]{1,0:T(8,128)(2,1)S(1)}, bf16[272,128]{1,0:T(8,128)(2,1)S(1)}, u32[]{:S(2)}, u32[]{:S(2)}) %collective-permute-start.5) | collective-permute-done | bytes 69664 | tf_op jit(solution)/shard_map/ppermute | solution.py:293
  52.3 0.0 copy-start.2
  52.3 1.1 far.1
  53.4 3.1 %collective-permute-start.8 = (f32[296,128]{1,0:T(8,128)S(1)}, f32[296,128]{1,0:T(8,128)S(1)}, u32[]{:S(2)}, u32[]{:S(2)}) collective-permute-start(f32[296,128]{1,0:T(8,128)S(1)} %get-tuple-element.29), channel_id=1, source_target_pairs={{0,1},{1,0},{2,3},{3,2},{4,5},{5,4},{6,7},{7,6},{8,9},{9,8},{10,11... | collective-permute-start | bytes 454664 | tf_op jit(solution)/shard_map/ppermute | solution.py:314
  56.5 1.0 collective-permute-done.8.got
  57.5 0.0 copy-done.2
  57.5 0.6 slopes.1
  58.2 6.8 %collective-permute-start.9 = (bf16[576,128]{1,0:T(8,128)(2,1)S(1)}, bf16[576,128]{1,0:T(8,128)(2,1)S(1)}, u32[]{:S(2)}, u32[]{:S(2)}) collective-permute-start(bf16[576,128]{1,0:T(8,128)(2,1)S(1)} %get-tuple-element.33), channel_id=1, source_target_pairs={{0,128},{4,132},{8,136},{12,140},{16,144},{20,148},{24,152},{28,15... | collective-permute-start | bytes 442376 | tf_op jit(solution)/shard_map/ppermute | solution.py:327
  65.0 4.1 %collective-permute-done.9.theirs = bf16[576,128]{1,0:T(8,128)(2,1)S(1)} collective-permute-done((bf16[576,128]{1,0:T(8,128)(2,1)S(1)}, bf16[576,128]{1,0:T(8,128)(2,1)S(1)}, u32[]{:S(2)}, u32[]{:S(2)}) %collective-permute-start.9) | collective-permute-done | bytes 147488 | tf_op jit(solution)/shard_map/ppermute | solution.py:327
  69.1 0.8 gradients.1
  70.0 15.1 %all_to_all.10.got = bf16[8,368,128]{2,1,0:T(8,128)(2,1)S(1)} all-to-all(bf16[8,368,128]{2,1,0:T(8,128)(2,1)S(1)} %gradients.1), channel_id=1, replica_groups={{0,4,256,260,512,516,768,772},{8,12,264,268,520,524,776,780},{16,20,272..., dimensions={0} | all-to-all | bytes 1507328 | tf_op jit(solution)/shard_map/all_to_all | solution.py:346
  85.1 0.4 ring.1
  85.4 0.7 convert_element_type.7
  86.1 19.6 %all-to-all-start.1 = ((f16[16,24,128]{2,1,0:T(8,128)(2,1)}), f16[16,24,128]{2,1,0:T(8,128)(2,1)S(1)}, u32[]{:S(2)}, u32[]{:S(2)}) async-start(f16[16,24,128]{2,1,0:T(8,128)(2,1)} %convert_element_type.7), calls=%async_computation.1 | async-start | bytes 196608 | tf_op jit(solution)/shard_map/all_to_all | solution.py:360
  105.7 0.5 slice_bitcast_fusion
  106.2 10.9 %all-to-all-done.1 = f16[16,24,128]{2,1,0:T(8,128)(2,1)S(1)} async-done(((f16[16,24,128]{2,1,0:T(8,128)(2,1)}), f16[16,24,128]{2,1,0:T(8,128)(2,1)S(1)}, u32[]{:S(2)}, u32[]{:S(2)}) %all-to-all-start.1) | async-done | bytes 98336 | tf_op jit(solution)/shard_map/all_to_all | solution.py:360
  117.2 0.1 fusion.4
  117.3 0.1 fusion.5
  117.3 0.1 reshape.12
  117.4 0.1 reshape.13
  117.5 0.7 broadcast_select_fusion.2
  (7 shorter events, 0.1 us)
Async XLA Ops:
  3.5 3.5 %collective-permute-start = (bf16[576,128]{1,0:T(8,128)(2,1)}, bf16[576,128]{1,0:T(8,128)(2,1)S(1)}, u32[]{:S(2)}, u32[]{:S(2)}) collective-permute-start(bf16[576,128]{1,0:T(8,128)(2,1)} %get-tuple-element.20), channel_id=1, source_target_pairs={{0,1},{1,0},{2,3},{3,2},{4,5},{5,4},{6,7},{7,6},{8,9},{9,8},{10,11... | collective-permute-start | bytes 442376 | tf_op jit(solution)/shard_map/ppermute | solution.py:255
  7.0 9.3 %copy-start = (bf16[128,1152]{1,0:T(8,128)(2,1)S(1)}, bf16[128,1152]{1,0:T(8,128)(2,1)}, u32[]{:S(2)}) copy-start(bf16[128,1152]{1,0:T(8,128)(2,1)} %xi.2) | copy-start | bytes 884740
  7.0 9.3 %copy-start.1 = (bf16[128,1152]{1,0:T(8,128)(2,1)S(1)}, bf16[128,1152]{1,0:T(8,128)(2,1)}, u32[]{:S(2)}) copy-start(bf16[128,1152]{1,0:T(8,128)(2,1)} %xt.2) | copy-start | bytes 884740
  7.1 22.2 %collective-permute-start.1 = (bf16[576,128]{1,0:T(8,128)(2,1)S(1)}, bf16[576,128]{1,0:T(8,128)(2,1)S(1)}, u32[]{:S(2)}, u32[]{:S(2)}) collective-permute-start(bf16[576,128]{1,0:T(8,128)(2,1)S(1)} %get-tuple-element.37.refs_0_.o0), channel_id=1, source_target_pairs={{0,4},{1,1021},{2,6},{3,1023},{4,8},{5,1},{6,10},{7,3},{8,12},{9,5... | collective-permute-start | bytes 442376 | tf_op jit(solution)/shard_map/ppermute | solution.py:39
  11.1 23.1 %collective-permute-start.3 = (bf16[576,128]{1,0:T(8,128)(2,1)S(1)}, bf16[576,128]{1,0:T(8,128)(2,1)S(1)}, u32[]{:S(2)}, u32[]{:S(2)}) collective-permute-start(bf16[576,128]{1,0:T(8,128)(2,1)S(1)} %get-tuple-element.37.refs_0_.o0), channel_id=1, source_target_pairs={{0,8},{1,1017},{2,10},{3,1019},{4,12},{5,1021},{6,14},{7,1023},{8,... | collective-permute-start | bytes 442376 | tf_op jit(solution)/shard_map/ppermute | solution.py:39
  16.7 31.3 %collective-permute-start.7 = (bf16[1280,128]{1,0:T(8,128)(2,1)S(1)}, bf16[1280,128]{1,0:T(8,128)(2,1)S(1)}, u32[]{:S(2)}, u32[]{:S(2)}) collective-permute-start(bf16[1280,128]{1,0:T(8,128)(2,1)S(1)} %get-tuple-element.24), channel_id=1, source_target_pairs={{0,128},{4,132},{8,136},{12,140},{16,144},{20,148},{24,152},{28,15... | collective-permute-start | bytes 983048 | tf_op jit(solution)/shard_map/ppermute | solution.py:276
  29.3 11.6 %collective-permute-start.2 = (bf16[576,128]{1,0:T(8,128)(2,1)S(1)}, bf16[576,128]{1,0:T(8,128)(2,1)S(1)}, u32[]{:S(2)}, u32[]{:S(2)}) collective-permute-start(bf16[576,128]{1,0:T(8,128)(2,1)S(1)} %collective-permute-done.1.refs_1_.o1), channel_id=1, source_target_pairs={{0,8},{1,1017},{2,10},{3,1019},{4,12},{5,1021},{6,14},{7,1023},{8,... | collective-permute-start | bytes 442376 | tf_op jit(solution)/shard_map/ppermute | solution.py:39
  34.2 10.1 %collective-permute-start.4 = (bf16[576,128]{1,0:T(8,128)(2,1)S(1)}, bf16[576,128]{1,0:T(8,128)(2,1)S(1)}, u32[]{:S(2)}, u32[]{:S(2)}) collective-permute-start(bf16[576,128]{1,0:T(8,128)(2,1)S(1)} %collective-permute-done.3.refs_2_.o2), channel_id=1, source_target_pairs={{0,8},{1,1017},{2,10},{3,1019},{4,12},{5,1021},{6,14},{7,1023},{8,... | collective-permute-start | bytes 442376 | tf_op jit(solution)/shard_map/ppermute | solution.py:39
  37.7 10.3 %collective-permute-start.6 = (bf16[400,128]{1,0:T(8,128)(2,1)S(1)}, bf16[400,128]{1,0:T(8,128)(2,1)S(1)}, u32[]{:S(2)}, u32[]{:S(2)}) collective-permute-start(bf16[400,128]{1,0:T(8,128)(2,1)S(1)} %scores.3.mine), channel_id=1, source_target_pairs={{0,2},{1,3},{2,0},{3,1},{4,6},{5,7},{6,4},{7,5},{8,10},{9,11},{10,... | collective-permute-start | bytes 307208 | tf_op jit(solution)/shard_map/ppermute | solution.py:290
  44.6 7.7 %collective-permute-start.5 = (bf16[272,128]{1,0:T(8,128)(2,1)S(1)}, bf16[272,128]{1,0:T(8,128)(2,1)S(1)}, u32[]{:S(2)}, u32[]{:S(2)}) collective-permute-start(bf16[272,128]{1,0:T(8,128)(2,1)S(1)} %scores.2.mine), channel_id=1, source_target_pairs={{0,2},{1,3},{2,0},{3,1},{4,6},{5,7},{6,4},{7,5},{8,10},{9,11},{10,... | collective-permute-start | bytes 208904 | tf_op jit(solution)/shard_map/ppermute | solution.py:293
  52.3 5.2 %copy-start.2 = (f32[576,128]{1,0:T(8,128)S(1)}, f32[576,128]{1,0:T(8,128)}, u32[]{:S(2)}) copy-start(f32[576,128]{1,0:T(8,128)} %get-tuple-element.30.z) | copy-start | bytes 884740
  53.4 4.1 %collective-permute-start.8 = (f32[296,128]{1,0:T(8,128)S(1)}, f32[296,128]{1,0:T(8,128)S(1)}, u32[]{:S(2)}, u32[]{:S(2)}) collective-permute-start(f32[296,128]{1,0:T(8,128)S(1)} %get-tuple-element.29), channel_id=1, source_target_pairs={{0,1},{1,0},{2,3},{3,2},{4,5},{5,4},{6,7},{7,6},{8,9},{9,8},{10,11... | collective-permute-start | bytes 454664 | tf_op jit(solution)/shard_map/ppermute | solution.py:314
  58.2 10.9 %collective-permute-start.9 = (bf16[576,128]{1,0:T(8,128)(2,1)S(1)}, bf16[576,128]{1,0:T(8,128)(2,1)S(1)}, u32[]{:S(2)}, u32[]{:S(2)}) collective-permute-start(bf16[576,128]{1,0:T(8,128)(2,1)S(1)} %get-tuple-element.33), channel_id=1, source_target_pairs={{0,128},{4,132},{8,136},{12,140},{16,144},{20,148},{24,152},{28,15... | collective-permute-start | bytes 442376 | tf_op jit(solution)/shard_map/ppermute | solution.py:327
  86.1 31.0 %all-to-all-start.1 = ((f16[16,24,128]{2,1,0:T(8,128)(2,1)}), f16[16,24,128]{2,1,0:T(8,128)(2,1)S(1)}, u32[]{:S(2)}, u32[]{:S(2)}) async-start(f16[16,24,128]{2,1,0:T(8,128)(2,1)} %convert_element_type.7), calls=%async_computation.1 | async-start | bytes 196608 | tf_op jit(solution)/shard_map/all_to_all | solution.py:360

commit v15 on v14

--- a/solution.py
+++ b/solution.py
@@ -166,7 +166,7 @@
 
 
 def ring_order(places):
-    first = 3 * places // 8
+    first = 5 * places // 8
     near = [m // 2 if m % 2 == 0 else places - 1 - m // 2 for m in range(places)]
     return [first] + [m for m in near if m != first]
 

time: 119 us -> 116 us (0.975); the launches traced: 118 us -> 114 us
  starting transfers between devices: 53.5 us -> 50.8 us
  waiting for transfers between devices: 36 us -> 34.4 us
    all_to_all x1, starting transfers between devices: 19.6 us -> 16.8 us  [shards(): lax.all_to_all(sent, 'dp', 0, 0, axis_index_groups=groups, tiled=True)]
    all_to_all x1, waiting for transfers between devices: 10.9 us -> 9.25 us  [shards(): lax.all_to_all(sent, 'dp', 0, 0, axis_index_groups=groups, tiled=True)]
where the time goes in v15:
time: 116 us; the launch traced here: 114 us
  starting transfers between devices  50.8 us (44%)
  waiting for transfers between devices  34.4 us (30%)
  blocking collectives  15.1 us (13%)
  Pallas kernels  8 us (7%)
  between operations  2.2 us (2%)
  local copies, waits for them, and re-layouts  1.79 us (2%)
  other arithmetic  1.58 us (1%)
    all_to_all x1, starting transfers between devices, shards(): lax.all_to_all(sent, 'dp', 0, 0, axis_index_groups=groups, tiled=True)  16.8 us
    ppermute x4, waiting for transfers between devices, shifted(): return lax.ppermute(block, ('dp', 'tower'), route)  16.3 us
    all_to_all x1, blocking collectives, shards(): lax.all_to_all(grads, 'dp', 0, 0, axis_index_groups=groups, tiled=True)  15.1 us
    ppermute x4, starting transfers between devices, shifted(): return lax.ppermute(block, ('dp', 'tower'), route)  13 us
    all_to_all x1, waiting for transfers between devices, shards(): lax.all_to_all(sent, 'dp', 0, 0, axis_index_groups=groups, tiled=True)  9.25 us
    ppermute x1, starting transfers between devices, shards(): theirs = lax.ppermute(send, 'dp', beside)  6.79 us
    ppermute x1, waiting for transfers between devices, shards(): theirs = lax.ppermute(send, 'dp', beside)  4.14 us
    ppermute x1, starting transfers between devices, shards(): far_peer = lax.ppermute(far, 'tower', to_chip)  3.31 us
  transfers between devices with their start and end apart: 11, of which 8 were waited for; matrix products, arithmetic and copies ran while one was open for 1% of the time, Pallas kernels for 2%

profile of v15, /device:TPU:6, one launch (start us, length us, event | category | flops | bytes accessed | tf_op | source)
XLA Modules:
  0.0 113.8 jit_solution(8152023969524417744)
XLA Ops:
  0.6 2.9 %project.1 = (f32[576,128]{1,0:T(8,128)}, bf16[576,128]{1,0:T(8,128)(2,1)}) custom-call(bf16[128,1152]{1,0:T(8,128)(2,1)} %xi.2, bf16[288,1152]{1,0:T(8,128)(2,1)} %bitcast.7, bf16[128,1152]{1,0:T(8,128)(2,1)} %xt.2, bf16[288,1152]{1,0:T(8,128)(2,1)} %bitcast.8), custom_call_target="tpu_custom_call" | custom-call | tf_op jit(solution)/shard_map/project/pallas_call | solution.py:243
  3.5 1.9 %collective-permute-start = (bf16[576,128]{1,0:T(8,128)(2,1)}, bf16[576,128]{1,0:T(8,128)(2,1)S(1)}, u32[]{:S(2)}, u32[]{:S(2)}) collective-permute-start(bf16[576,128]{1,0:T(8,128)(2,1)} %get-tuple-element.20), channel_id=1, source_target_pairs={{0,1},{1,0},{2,3},{3,2},{4,5},{5,4},{6,7},{7,6},{8,9},{9,8},{10,11... | collective-permute-start | bytes 442376 | tf_op jit(solution)/shard_map/ppermute | solution.py:255
  5.5 0.9 fusion.1
  6.4 0.6 collective-permute-done
  7.0 0.0 copy-start
  7.0 0.0 copy-start.1
  7.1 0.1 broadcast_select_fusion
  7.1 4.0 %collective-permute-start.1 = (bf16[576,128]{1,0:T(8,128)(2,1)S(1)}, bf16[576,128]{1,0:T(8,128)(2,1)S(1)}, u32[]{:S(2)}, u32[]{:S(2)}) collective-permute-start(bf16[576,128]{1,0:T(8,128)(2,1)S(1)} %get-tuple-element.37.refs_0_.o0), channel_id=1, source_target_pairs={{0,4},{1,1021},{2,6},{3,1023},{4,8},{5,1},{6,10},{7,3},{8,12},{9,5... | collective-permute-start | bytes 442376 | tf_op jit(solution)/shard_map/ppermute | solution.py:39
  11.1 5.2 %collective-permute-start.3 = (bf16[576,128]{1,0:T(8,128)(2,1)S(1)}, bf16[576,128]{1,0:T(8,128)(2,1)S(1)}, u32[]{:S(2)}, u32[]{:S(2)}) collective-permute-start(bf16[576,128]{1,0:T(8,128)(2,1)S(1)} %get-tuple-element.37.refs_0_.o0), channel_id=1, source_target_pairs={{0,8},{1,1017},{2,10},{3,1019},{4,12},{5,1021},{6,14},{7,1023},{8,... | collective-permute-start | bytes 442376 | tf_op jit(solution)/shard_map/ppermute | solution.py:39
  16.3 0.0 copy-done
  16.3 0.0 copy-done.1
  16.3 0.3 order.1
  16.7 2.7 %collective-permute-start.7 = (bf16[1280,128]{1,0:T(8,128)(2,1)S(1)}, bf16[1280,128]{1,0:T(8,128)(2,1)S(1)}, u32[]{:S(2)}, u32[]{:S(2)}) collective-permute-start(bf16[1280,128]{1,0:T(8,128)(2,1)S(1)} %get-tuple-element.24), channel_id=1, source_target_pairs={{0,128},{4,132},{8,136},{12,140},{16,144},{20,148},{24,152},{28,15... | collective-permute-start | bytes 983048 | tf_op jit(solution)/shard_map/ppermute | solution.py:276
  19.4 9.9 %collective-permute-done.1.refs_1_.o1 = bf16[576,128]{1,0:T(8,128)(2,1)S(1)} collective-permute-done((bf16[576,128]{1,0:T(8,128)(2,1)S(1)}, bf16[576,128]{1,0:T(8,128)(2,1)S(1)}, u32[]{:S(2)}, u32[]{:S(2)}) %collective-permute-start.1) | collective-permute-done | bytes 147488 | tf_op jit(solution)/shard_map/ppermute | solution.py:39
  29.3 1.9 %collective-permute-start.2 = (bf16[576,128]{1,0:T(8,128)(2,1)S(1)}, bf16[576,128]{1,0:T(8,128)(2,1)S(1)}, u32[]{:S(2)}, u32[]{:S(2)}) collective-permute-start(bf16[576,128]{1,0:T(8,128)(2,1)S(1)} %collective-permute-done.1.refs_1_.o1), channel_id=1, source_target_pairs={{0,8},{1,1017},{2,10},{3,1019},{4,12},{5,1021},{6,14},{7,1023},{8,... | collective-permute-start | bytes 442376 | tf_op jit(solution)/shard_map/ppermute | solution.py:39
  31.2 3.0 %collective-permute-done.3.refs_2_.o2 = bf16[576,128]{1,0:T(8,128)(2,1)S(1)} collective-permute-done((bf16[576,128]{1,0:T(8,128)(2,1)S(1)}, bf16[576,128]{1,0:T(8,128)(2,1)S(1)}, u32[]{:S(2)}, u32[]{:S(2)}) %collective-permute-start.3) | collective-permute-done | bytes 147488 | tf_op jit(solution)/shard_map/ppermute | solution.py:39
  34.2 1.9 %collective-permute-start.4 = (bf16[576,128]{1,0:T(8,128)(2,1)S(1)}, bf16[576,128]{1,0:T(8,128)(2,1)S(1)}, u32[]{:S(2)}, u32[]{:S(2)}) collective-permute-start(bf16[576,128]{1,0:T(8,128)(2,1)S(1)} %collective-permute-done.3.refs_2_.o2), channel_id=1, source_target_pairs={{0,8},{1,1017},{2,10},{3,1019},{4,12},{5,1021},{6,14},{7,1023},{8,... | collective-permute-start | bytes 442376 | tf_op jit(solution)/shard_map/ppermute | solution.py:39
  37.4 0.3 scores.3.mine
  37.7 3.1 %collective-permute-start.6 = (bf16[400,128]{1,0:T(8,128)(2,1)S(1)}, bf16[400,128]{1,0:T(8,128)(2,1)S(1)}, u32[]{:S(2)}, u32[]{:S(2)}) collective-permute-start(bf16[400,128]{1,0:T(8,128)(2,1)S(1)} %scores.3.mine), channel_id=1, source_target_pairs={{0,2},{1,3},{2,0},{3,1},{4,6},{5,7},{6,4},{7,5},{8,10},{9,11},{10,... | collective-permute-start | bytes 307208 | tf_op jit(solution)/shard_map/ppermute | solution.py:290
  40.9 0.0 collective-permute-done.2.refs_0_.o3
  40.9 3.4 %collective-permute-done.4.refs_1_.o4 = bf16[576,128]{1,0:T(8,128)(2,1)S(1)} collective-permute-done((bf16[576,128]{1,0:T(8,128)(2,1)S(1)}, bf16[576,128]{1,0:T(8,128)(2,1)S(1)}, u32[]{:S(2)}, u32[]{:S(2)}) %collective-permute-start.4) | collective-permute-done | bytes 147488 | tf_op jit(solution)/shard_map/ppermute | solution.py:39
  44.3 0.3 scores.2.mine
  44.6 3.3 %collective-permute-start.5 = (bf16[272,128]{1,0:T(8,128)(2,1)S(1)}, bf16[272,128]{1,0:T(8,128)(2,1)S(1)}, u32[]{:S(2)}, u32[]{:S(2)}) collective-permute-start(bf16[272,128]{1,0:T(8,128)(2,1)S(1)} %scores.2.mine), channel_id=1, source_target_pairs={{0,2},{1,3},{2,0},{3,1},{4,6},{5,7},{6,4},{7,5},{8,10},{9,11},{10,... | collective-permute-start | bytes 208904 | tf_op jit(solution)/shard_map/ppermute | solution.py:293
  47.9 0.1 pad_maximum_fusion.2.numbers
  48.0 0.0 collective-permute-done.6.peer
  48.0 0.0 collective-permute-done.7.beside
  48.0 1.2 %near.1 = (f32[576,128]{1,0:T(8,128)S(1)}, f32[8,128]{1,0:T(8,128)S(1)}) custom-call(f32[3]{0:T(128)S(1)} %pad_maximum_fusion.2.numbers, bf16[400,128]{1,0:T(8,128)(2,1)S(1)} %scores.3.mine, bf16[400,128]{1,0:T(8,128)(2,1)S(1)} %collective-permute-done.6.peer, bf16[576,128]{1,0:T(8,128)(2,1)S(1)} %get-tuple-element.37.refs_0_.o0, ...), custom_call_target="tpu_custom_call" | custom-call | tf_op jit(solution)/shard_map/near/pallas_call | solution.py:294
  49.2 3.1 %collective-permute-done.5.peer = bf16[272,128]{1,0:T(8,128)(2,1)S(1)} collective-permute-done((bf16[272,128]{1,0:T(8,128)(2,1)S(1)}, bf16[272,128]{1,0:T(8,128)(2,1)S(1)}, u32[]{:S(2)}, u32[]{:S(2)}) %collective-permute-start.5) | collective-permute-done | bytes 69664 | tf_op jit(solution)/shard_map/ppermute | solution.py:293
  52.3 0.0 copy-start.2
  52.3 1.1 far.1
  53.4 3.1 %collective-permute-start.8 = (f32[296,128]{1,0:T(8,128)S(1)}, f32[296,128]{1,0:T(8,128)S(1)}, u32[]{:S(2)}, u32[]{:S(2)}) collective-permute-start(f32[296,128]{1,0:T(8,128)S(1)} %get-tuple-element.29), channel_id=1, source_target_pairs={{0,1},{1,0},{2,3},{3,2},{4,5},{5,4},{6,7},{7,6},{8,9},{9,8},{10,11... | collective-permute-start | bytes 454664 | tf_op jit(solution)/shard_map/ppermute | solution.py:314
  56.5 1.0 collective-permute-done.8.got
  57.5 0.0 copy-done.2
  57.5 0.6 slopes.1
  58.2 6.8 %collective-permute-start.9 = (bf16[576,128]{1,0:T(8,128)(2,1)S(1)}, bf16[576,128]{1,0:T(8,128)(2,1)S(1)}, u32[]{:S(2)}, u32[]{:S(2)}) collective-permute-start(bf16[576,128]{1,0:T(8,128)(2,1)S(1)} %get-tuple-element.33), channel_id=1, source_target_pairs={{0,128},{4,132},{8,136},{12,140},{16,144},{20,148},{24,152},{28,15... | collective-permute-start | bytes 442376 | tf_op jit(solution)/shard_map/ppermute | solution.py:327
  65.0 4.1 %collective-permute-done.9.theirs = bf16[576,128]{1,0:T(8,128)(2,1)S(1)} collective-permute-done((bf16[576,128]{1,0:T(8,128)(2,1)S(1)}, bf16[576,128]{1,0:T(8,128)(2,1)S(1)}, u32[]{:S(2)}, u32[]{:S(2)}) %collective-permute-start.9) | collective-permute-done | bytes 147488 | tf_op jit(solution)/shard_map/ppermute | solution.py:327
  69.1 0.8 gradients.1
  70.0 15.1 %all_to_all.10.got = bf16[8,368,128]{2,1,0:T(8,128)(2,1)S(1)} all-to-all(bf16[8,368,128]{2,1,0:T(8,128)(2,1)S(1)} %gradients.1), channel_id=1, replica_groups={{0,4,256,260,512,516,768,772},{8,12,264,268,520,524,776,780},{16,20,272..., dimensions={0} | all-to-all | bytes 1507328 | tf_op jit(solution)/shard_map/all_to_all | solution.py:346
  85.1 0.4 ring.1
  85.4 0.7 convert_element_type.7
  86.1 16.8 %all-to-all-start.1 = ((f16[16,24,128]{2,1,0:T(8,128)(2,1)}), f16[16,24,128]{2,1,0:T(8,128)(2,1)S(1)}, u32[]{:S(2)}, u32[]{:S(2)}) async-start(f16[16,24,128]{2,1,0:T(8,128)(2,1)} %convert_element_type.7), calls=%async_computation.1 | async-start | bytes 196608 | tf_op jit(solution)/shard_map/all_to_all | solution.py:360
  102.9 0.5 slice_bitcast_fusion
  103.4 9.3 %all-to-all-done.1 = f16[16,24,128]{2,1,0:T(8,128)(2,1)S(1)} async-done(((f16[16,24,128]{2,1,0:T(8,128)(2,1)}), f16[16,24,128]{2,1,0:T(8,128)(2,1)S(1)}, u32[]{:S(2)}, u32[]{:S(2)}) %all-to-all-start.1) | async-done | bytes 98336 | tf_op jit(solution)/shard_map/all_to_all | solution.py:360
  112.8 0.1 fusion.4
  112.9 0.1 fusion.5
  113.0 0.1 reshape.12
  113.1 0.1 reshape.13
  113.1 0.7 broadcast_select_fusion.2
  (7 shorter events, 0.1 us)
Async XLA Ops:
  3.5 3.5 %collective-permute-start = (bf16[576,128]{1,0:T(8,128)(2,1)}, bf16[576,128]{1,0:T(8,128)(2,1)S(1)}, u32[]{:S(2)}, u32[]{:S(2)}) collective-permute-start(bf16[576,128]{1,0:T(8,128)(2,1)} %get-tuple-element.20), channel_id=1, source_target_pairs={{0,1},{1,0},{2,3},{3,2},{4,5},{5,4},{6,7},{7,6},{8,9},{9,8},{10,11... | collective-permute-start | bytes 442376 | tf_op jit(solution)/shard_map/ppermute | solution.py:255
  7.0 9.3 %copy-start = (bf16[128,1152]{1,0:T(8,128)(2,1)S(1)}, bf16[128,1152]{1,0:T(8,128)(2,1)}, u32[]{:S(2)}) copy-start(bf16[128,1152]{1,0:T(8,128)(2,1)} %xi.2) | copy-start | bytes 884740
  7.0 9.3 %copy-start.1 = (bf16[128,1152]{1,0:T(8,128)(2,1)S(1)}, bf16[128,1152]{1,0:T(8,128)(2,1)}, u32[]{:S(2)}) copy-start(bf16[128,1152]{1,0:T(8,128)(2,1)} %xt.2) | copy-start | bytes 884740
  7.1 22.2 %collective-permute-start.1 = (bf16[576,128]{1,0:T(8,128)(2,1)S(1)}, bf16[576,128]{1,0:T(8,128)(2,1)S(1)}, u32[]{:S(2)}, u32[]{:S(2)}) collective-permute-start(bf16[576,128]{1,0:T(8,128)(2,1)S(1)} %get-tuple-element.37.refs_0_.o0), channel_id=1, source_target_pairs={{0,4},{1,1021},{2,6},{3,1023},{4,8},{5,1},{6,10},{7,3},{8,12},{9,5... | collective-permute-start | bytes 442376 | tf_op jit(solution)/shard_map/ppermute | solution.py:39
  11.1 23.1 %collective-permute-start.3 = (bf16[576,128]{1,0:T(8,128)(2,1)S(1)}, bf16[576,128]{1,0:T(8,128)(2,1)S(1)}, u32[]{:S(2)}, u32[]{:S(2)}) collective-permute-start(bf16[576,128]{1,0:T(8,128)(2,1)S(1)} %get-tuple-element.37.refs_0_.o0), channel_id=1, source_target_pairs={{0,8},{1,1017},{2,10},{3,1019},{4,12},{5,1021},{6,14},{7,1023},{8,... | collective-permute-start | bytes 442376 | tf_op jit(solution)/shard_map/ppermute | solution.py:39
  16.7 31.3 %collective-permute-start.7 = (bf16[1280,128]{1,0:T(8,128)(2,1)S(1)}, bf16[1280,128]{1,0:T(8,128)(2,1)S(1)}, u32[]{:S(2)}, u32[]{:S(2)}) collective-permute-start(bf16[1280,128]{1,0:T(8,128)(2,1)S(1)} %get-tuple-element.24), channel_id=1, source_target_pairs={{0,128},{4,132},{8,136},{12,140},{16,144},{20,148},{24,152},{28,15... | collective-permute-start | bytes 983048 | tf_op jit(solution)/shard_map/ppermute | solution.py:276
  29.3 11.6 %collective-permute-start.2 = (bf16[576,128]{1,0:T(8,128)(2,1)S(1)}, bf16[576,128]{1,0:T(8,128)(2,1)S(1)}, u32[]{:S(2)}, u32[]{:S(2)}) collective-permute-start(bf16[576,128]{1,0:T(8,128)(2,1)S(1)} %collective-permute-done.1.refs_1_.o1), channel_id=1, source_target_pairs={{0,8},{1,1017},{2,10},{3,1019},{4,12},{5,1021},{6,14},{7,1023},{8,... | collective-permute-start | bytes 442376 | tf_op jit(solution)/shard_map/ppermute | solution.py:39
  34.2 10.1 %collective-permute-start.4 = (bf16[576,128]{1,0:T(8,128)(2,1)S(1)}, bf16[576,128]{1,0:T(8,128)(2,1)S(1)}, u32[]{:S(2)}, u32[]{:S(2)}) collective-permute-start(bf16[576,128]{1,0:T(8,128)(2,1)S(1)} %collective-permute-done.3.refs_2_.o2), channel_id=1, source_target_pairs={{0,8},{1,1017},{2,10},{3,1019},{4,12},{5,1021},{6,14},{7,1023},{8,... | collective-permute-start | bytes 442376 | tf_op jit(solution)/shard_map/ppermute | solution.py:39
  37.7 10.3 %collective-permute-start.6 = (bf16[400,128]{1,0:T(8,128)(2,1)S(1)}, bf16[400,128]{1,0:T(8,128)(2,1)S(1)}, u32[]{:S(2)}, u32[]{:S(2)}) collective-permute-start(bf16[400,128]{1,0:T(8,128)(2,1)S(1)} %scores.3.mine), channel_id=1, source_target_pairs={{0,2},{1,3},{2,0},{3,1},{4,6},{5,7},{6,4},{7,5},{8,10},{9,11},{10,... | collective-permute-start | bytes 307208 | tf_op jit(solution)/shard_map/ppermute | solution.py:290
  44.6 7.7 %collective-permute-start.5 = (bf16[272,128]{1,0:T(8,128)(2,1)S(1)}, bf16[272,128]{1,0:T(8,128)(2,1)S(1)}, u32[]{:S(2)}, u32[]{:S(2)}) collective-permute-start(bf16[272,128]{1,0:T(8,128)(2,1)S(1)} %scores.2.mine), channel_id=1, source_target_pairs={{0,2},{1,3},{2,0},{3,1},{4,6},{5,7},{6,4},{7,5},{8,10},{9,11},{10,... | collective-permute-start | bytes 208904 | tf_op jit(solution)/shard_map/ppermute | solution.py:293
  52.3 5.2 %copy-start.2 = (f32[576,128]{1,0:T(8,128)S(1)}, f32[576,128]{1,0:T(8,128)}, u32[]{:S(2)}) copy-start(f32[576,128]{1,0:T(8,128)} %get-tuple-element.30.z) | copy-start | bytes 884740
  53.4 4.1 %collective-permute-start.8 = (f32[296,128]{1,0:T(8,128)S(1)}, f32[296,128]{1,0:T(8,128)S(1)}, u32[]{:S(2)}, u32[]{:S(2)}) collective-permute-start(f32[296,128]{1,0:T(8,128)S(1)} %get-tuple-element.29), channel_id=1, source_target_pairs={{0,1},{1,0},{2,3},{3,2},{4,5},{5,4},{6,7},{7,6},{8,9},{9,8},{10,11... | collective-permute-start | bytes 454664 | tf_op jit(solution)/shard_map/ppermute | solution.py:314
  58.2 10.9 %collective-permute-start.9 = (bf16[576,128]{1,0:T(8,128)(2,1)S(1)}, bf16[576,128]{1,0:T(8,128)(2,1)S(1)}, u32[]{:S(2)}, u32[]{:S(2)}) collective-permute-start(bf16[576,128]{1,0:T(8,128)(2,1)S(1)} %get-tuple-element.33), channel_id=1, source_target_pairs={{0,128},{4,132},{8,136},{12,140},{16,144},{20,148},{24,152},{28,15... | collective-permute-start | bytes 442376 | tf_op jit(solution)/shard_map/ppermute | solution.py:327
  86.1 26.6 %all-to-all-start.1 = ((f16[16,24,128]{2,1,0:T(8,128)(2,1)}), f16[16,24,128]{2,1,0:T(8,128)(2,1)S(1)}, u32[]{:S(2)}, u32[]{:S(2)}) async-start(f16[16,24,128]{2,1,0:T(8,128)(2,1)} %convert_element_type.7), calls=%async_computation.1 | async-start | bytes 196608 | tf_op jit(solution)/shard_map/all_to_all | solution.py:360
